TPU v7x, 32 devices: a whole 2x2x4 slice. The times are simulated.
32 devices in a mesh: dp: 8 (over y, x, core), tensor: 4 (over z).
Axes of the slice: x: 2, y: 2, z: 4, core: 2. Of those that a mesh axis runs over, the one named last changes fastest.
Arguments:
- tokens: bfloat16 [8192, 2048], P('dp', 'tensor'), may hold values from -6 to 6
- cotangent: bfloat16 [8192, 2048], P('dp', 'tensor'), may hold values from -6 to 6
- norm1_gain: bfloat16 [2048], P('tensor'), may hold values from 0.5 to 1.5
- w_query: bfloat16 [2048, 2048], P(None, 'tensor'), may hold values from -0.125 to 0.125
- w_key: bfloat16 [2048, 2048], P(None, 'tensor'), may hold values from -0.125 to 0.125
- w_value: bfloat16 [2048, 2048], P(None, 'tensor'), may hold values from -0.125 to 0.125
- query_gain: bfloat16 [2048], P('tensor'), may hold values from 0.25 to 1.75
- key_gain: bfloat16 [2048], P('tensor'), may hold values from 0.25 to 1.75
- w_output: bfloat16 [2048, 2048], P('tensor'), may hold values from -0.75 to 0.75
- norm2_gain: bfloat16 [2048], P('tensor'), may hold values from 0.5 to 1.5
- router: bfloat16 [2048, 6], replicated, may hold values from -0.09375 to 0.09375
- w_gate: bfloat16 [6, 2048, 1024], P(None, None, 'tensor'), may hold values from -0.125 to 0.125
- w_up: bfloat16 [6, 2048, 1024], P(None, None, 'tensor'), may hold values from -0.125 to 0.125
- w_down: bfloat16 [6, 1024, 2048], P(None, 'tensor'), may hold values from -1 to 1
- routes: int32 [8192, 3], P('dp'), may hold values from 0 to 5, as said below
- prefix: int32 [8], P('dp'), may hold values from 102 to 512
- slot_order: int32 [8, 3072], P('dp'), may hold values from 0 to 3071, each once within a row
Outputs:
- mixed: bfloat16 [8192, 2048], P('dp', 'tensor')
- grad_tokens: float32 [8192, 2048], P('dp', 'tensor')
- grad_norm1_gain: float32 [2048], P('tensor')
- grad_query: float32 [2048, 2048], P(None, 'tensor')
- grad_key: float32 [2048, 2048], P(None, 'tensor')
- grad_value: float32 [2048, 2048], P(None, 'tensor')
- grad_query_gain: float32 [2048], P('tensor')
- grad_key_gain: float32 [2048], P('tensor')
- grad_output: float32 [2048, 2048], P('tensor')
- grad_norm2_gain: float32 [2048], P('tensor')
- grad_router: float32 [2048, 6], replicated
- grad_gate: float32 [6, 2048, 1024], P(None, None, 'tensor')
- grad_up: float32 [6, 2048, 1024], P(None, None, 'tensor')
- grad_down: float32 [6, 1024, 2048], P(None, 'tensor')
Inputs may be any that keep to these rules, and one draw needn't show every extreme that they name: `routes`: each token names 3 different experts. `slot_order`: each row names every pair index of its sequence once.
All inputs are finite; a program needn't handle non-finite values.
Results may differ from a plain program's by a relative error of at most 0.028.
Values may be sent and summed in bfloat16 or wider, within the bound.
No kernel may reach another device: no remote copies, remote signals or barrier semaphores. Data moves between devices by JAX's collectives and lax.ppermute only.
A program may use at most 384 MiB of HBM per device.

v0:
```python
import jax
import jax.numpy as jnp
from jax import lax
from jax.sharding import PartitionSpec as P

HEAD_DIM = 128
EXPERTS = 6
TOP = 3
CAP = 640


EPSILON = 1e-05
ROPE_BASE = 10000.0
MASKED = -1e30


def rope_tables(length, head_size):
    halfway = head_size // 2
    freqs = ROPE_BASE ** (-(jnp.arange(halfway, dtype=jnp.float32) * 2.0 / head_size))
    angles = jnp.arange(length, dtype=jnp.float32)[:, None] * freqs[None, :]
    angles = jnp.concatenate([angles, angles], axis=1)
    return (jnp.cos(angles), jnp.sin(angles))


def turned(field):
    halfway = field.shape[-1] // 2
    return jnp.concatenate([-field[..., halfway:], field[..., :halfway]], axis=-1)


def turned_back(field):
    halfway = field.shape[-1] // 2
    return jnp.concatenate([field[..., halfway:], -field[..., :halfway]], axis=-1)


def rotate(flat_rows, cosine, sine, heads_here):
    length = flat_rows.shape[0]
    field = flat_rows.reshape(length, heads_here, -1)
    return (field * cosine[:, None, :] + turned(field) * sine[:, None, :]).reshape(length, -1)


def unrotate(flat_rows, cosine, sine, heads_here):
    length = flat_rows.shape[0]
    field = flat_rows.reshape(length, heads_here, -1)
    return (field * cosine[:, None, :] + turned_back(field * sine[:, None, :])).reshape(length, -1)


def rms_scale(field):
    return lax.rsqrt(jnp.mean(field * field, axis=1, keepdims=True) + EPSILON)


def softmax_rows(scores):
    highest = jnp.max(scores, axis=-1, keepdims=True)
    exponent = jnp.exp(scores - highest)
    return exponent / jnp.sum(exponent, axis=-1, keepdims=True)


def rounded(field):
    return lax.optimization_barrier(field.astype(jnp.bfloat16)).astype(jnp.float32)


def place(routes_seq, order_seq):
    flat_routes = routes_seq.reshape(-1)
    ordered = flat_routes[order_seq]
    choose = (ordered[:, None] == jnp.arange(EXPERTS, dtype=jnp.int32)[None, :]).astype(jnp.int32)
    slot_ranks = jnp.sum(jnp.cumsum(choose, axis=0) * choose, axis=1) - 1
    slot_index = jnp.zeros_like(flat_routes).at[order_seq].set(slot_ranks)
    target = jnp.where(slot_index < CAP, flat_routes * CAP + slot_index, EXPERTS * CAP)
    pair_ids = jnp.arange(flat_routes.shape[0], dtype=jnp.int32)
    source_pair = (
        jnp.full((EXPERTS * CAP + 1,), flat_routes.shape[0], jnp.int32).at[target].set(pair_ids)
    )
    return (source_pair[: EXPERTS * CAP], target)


def on_device(
    tokens,
    cotangent,
    norm1_gain,
    w_query,
    w_key,
    w_value,
    query_gain,
    key_gain,
    w_output,
    norm2_gain,
    router,
    w_gate,
    w_up,
    w_down,
    routes,
    prefix,
    slot_order,
):
    length = tokens.shape[0]
    shard_cols = tokens.shape[1]
    full_cols = shard_cols * lax.axis_size("tensor")
    heads_here = w_query.shape[1] // HEAD_DIM
    rows_block = min(512, length)
    factor = HEAD_DIM ** (-0.5)
    rows_x, rows_cot, gain_one, gain_two = (
        lax.all_gather(tokens, "tensor", axis=1, tiled=True),
        lax.all_gather(cotangent, "tensor", axis=1, tiled=True),
        lax.all_gather(norm1_gain, "tensor", axis=0, tiled=True),
        lax.all_gather(norm2_gain, "tensor", axis=0, tiled=True),
    )
    tokens_full = rows_x.astype(jnp.float32)
    scale_one = rms_scale(tokens_full)
    normed_one = (tokens_full * scale_one * gain_one.astype(jnp.float32)).astype(jnp.bfloat16)
    query_pre = jnp.dot(normed_one, w_query, preferred_element_type=jnp.float32)
    key_pre = jnp.dot(normed_one, w_key, preferred_element_type=jnp.float32)
    value_rows = jnp.dot(normed_one, w_value, preferred_element_type=jnp.float32).astype(
        jnp.bfloat16
    )
    square_query, square_key = lax.psum(
        (jnp.sum(query_pre * query_pre, axis=1), jnp.sum(key_pre * key_pre, axis=1)), "tensor"
    )
    query_scale = lax.rsqrt(square_query[:, None] / full_cols + EPSILON)
    key_scale = lax.rsqrt(square_key[:, None] / full_cols + EPSILON)
    gain_query = query_gain.astype(jnp.float32)
    gain_key = key_gain.astype(jnp.float32)
    cosine, sine = rope_tables(length, HEAD_DIM)
    query_rot = rotate(query_pre * query_scale * gain_query, cosine, sine, heads_here).astype(
        jnp.bfloat16
    )
    key_rot = rotate(key_pre * key_scale * gain_key, cosine, sine, heads_here).astype(jnp.bfloat16)
    query_heads = query_rot.reshape(length, heads_here, HEAD_DIM)
    key_heads = key_rot.reshape(length, heads_here, HEAD_DIM)
    value_heads = value_rows.reshape(length, heads_here, HEAD_DIM)
    positions = jnp.arange(length, dtype=jnp.int32)
    prefix_len = prefix[0]
    starts = jnp.arange(length // rows_block, dtype=jnp.int32) * rows_block

    def block_scores(offset):
        query_rows = lax.dynamic_slice_in_dim(query_heads, offset, rows_block, 0)
        raw_scores = (
            jnp.einsum("qhd,khd->hqk", query_rows, key_heads, preferred_element_type=jnp.float32)
            * factor
        )
        row_pos = offset + jnp.arange(rows_block, dtype=jnp.int32)
        allowed = (positions[None, :] <= row_pos[:, None]) | (positions[None, :] < prefix_len)
        return (query_rows, jnp.where(allowed[None], raw_scores, MASKED))

    def forward_block(offset):
        query_rows, scores = block_scores(offset)
        highest = jnp.max(scores, axis=2, keepdims=True)
        exponent = jnp.exp(scores - highest)
        row_sums = jnp.sum(exponent, axis=2, keepdims=True)
        weights = (exponent / row_sums).astype(jnp.bfloat16)
        head_rows = jnp.einsum(
            "hqk,khd->qhd", weights, value_heads, preferred_element_type=jnp.float32
        )
        return (head_rows, (highest + jnp.log(row_sums))[:, :, 0])

    head_rows, log_sums = lax.map(forward_block, starts)
    attended = head_rows.reshape(length, shard_cols).astype(jnp.bfloat16)
    attn_terms = jnp.dot(attended, w_output, preferred_element_type=jnp.float32)
    residual = tokens.astype(jnp.float32) + lax.psum_scatter(
        attn_terms.astype(jnp.bfloat16), "tensor", scatter_dimension=1, tiled=True
    ).astype(jnp.float32)
    residual_full = lax.all_gather(
        residual.astype(jnp.bfloat16), "tensor", axis=1, tiled=True
    ).astype(residual.dtype)
    scale_two = rms_scale(residual_full)
    gain_wide = gain_two.astype(jnp.float32)
    normed_two = (residual_full * scale_two * gain_wide).astype(jnp.bfloat16)
    logits = jnp.dot(normed_two, router, preferred_element_type=jnp.float32)
    expert_probs = softmax_rows(logits)
    choose = (routes[:, :, None] == jnp.arange(EXPERTS, dtype=jnp.int32)[None, None, :]).astype(
        jnp.float32
    )
    gates = jnp.sum(choose * expert_probs[:, None, :], axis=2)
    source_pair, target = place(routes, slot_order[0])
    source_token = source_pair // TOP
    padded = jnp.concatenate([normed_two, jnp.zeros((1, full_cols), jnp.bfloat16)], axis=0)
    dispatched = padded[source_token].reshape(EXPERTS, CAP, full_cols)
    pre_gate = jnp.einsum("ecd,edf->ecf", dispatched, w_gate, preferred_element_type=jnp.float32)
    pre_up = jnp.einsum("ecd,edf->ecf", dispatched, w_up, preferred_element_type=jnp.float32)
    sigmoid_gate = jax.nn.sigmoid(pre_gate)
    activated = pre_gate * sigmoid_gate
    hidden = (activated * pre_up).astype(jnp.bfloat16)
    expert_out = jnp.einsum(
        "ecf,efd->ecd", hidden, w_down, preferred_element_type=jnp.float32
    ).reshape(EXPERTS * CAP, full_cols)
    expert_pad = jnp.concatenate([expert_out, jnp.zeros((1, full_cols), jnp.float32)], axis=0)
    paired = expert_pad[target].reshape(length, TOP, full_cols)
    mixture = jnp.sum(gates[:, :, None] * paired, axis=1)
    mixed = (
        residual
        + lax.psum_scatter(
            mixture.astype(jnp.bfloat16), "tensor", scatter_dimension=1, tiled=True
        ).astype(jnp.float32)
    ).astype(jnp.bfloat16)
    cot_full = rows_cot.astype(jnp.float32)
    gate_terms = jnp.sum(paired * cot_full[:, None, :], axis=2)
    slot_gate = jnp.concatenate([gates.reshape(-1), jnp.zeros((1,), jnp.float32)], axis=0)[
        source_pair
    ]
    cot_pad = jnp.concatenate([cot_full, jnp.zeros((1, full_cols), jnp.float32)], axis=0)
    slot_grad = (
        (slot_gate[:, None] * cot_pad[source_token])
        .astype(jnp.bfloat16)
        .reshape(EXPERTS, CAP, full_cols)
    )
    hidden_grad = jnp.einsum("ecd,efd->ecf", slot_grad, w_down, preferred_element_type=jnp.float32)
    grad_pre_gate = (
        hidden_grad * pre_up * sigmoid_gate * (1.0 + pre_gate * (1.0 - sigmoid_gate))
    ).astype(jnp.bfloat16)
    grad_pre_up = (hidden_grad * activated).astype(jnp.bfloat16)
    grad_down = jnp.einsum("ecf,ecd->efd", hidden, slot_grad, preferred_element_type=jnp.float32)
    grad_gate = jnp.einsum(
        "ecd,ecf->edf", dispatched, grad_pre_gate, preferred_element_type=jnp.float32
    )
    grad_up = jnp.einsum(
        "ecd,ecf->edf", dispatched, grad_pre_up, preferred_element_type=jnp.float32
    )
    slot_input = jnp.einsum(
        "ecf,edf->ecd", grad_pre_gate, w_gate, preferred_element_type=jnp.float32
    )
    slot_input = slot_input + jnp.einsum(
        "ecf,edf->ecd", grad_pre_up, w_up, preferred_element_type=jnp.float32
    )
    slot_pad = jnp.concatenate(
        [slot_input.reshape(EXPERTS * CAP, full_cols), jnp.zeros((1, full_cols), jnp.float32)],
        axis=0,
    )
    token_input = jnp.sum(slot_pad[target].reshape(length, TOP, full_cols), axis=1)
    weighted_rows = residual_full * gain_wide
    gate_grads, stat_two = lax.psum(
        (gate_terms, jnp.sum(weighted_rows * token_input, axis=1)), "tensor"
    )
    prob_grad = jnp.sum(gate_grads[:, :, None] * choose, axis=1)
    logit_grad = (
        expert_probs * (prob_grad - jnp.sum(prob_grad * expert_probs, axis=1, keepdims=True))
    ).astype(jnp.bfloat16)
    router_input = jnp.einsum("te,de->td", logit_grad, router, preferred_element_type=jnp.float32)
    grad_router = jnp.einsum(
        "td,te->de", normed_two, logit_grad, preferred_element_type=jnp.float32
    )
    stat_two = stat_two + jnp.sum(weighted_rows * router_input, axis=1)
    column = lax.axis_index("tensor") * shard_cols
    normed_two_grad = lax.psum_scatter(
        token_input.astype(jnp.bfloat16), "tensor", scatter_dimension=1, tiled=True
    ).astype(jnp.float32) + lax.dynamic_slice_in_dim(router_input, column, shard_cols, 1)
    own_gain_two = norm2_gain.astype(jnp.float32)
    grad_norm2_gain = jnp.sum(normed_two_grad * residual * scale_two, axis=0)
    residual_grad = (
        cotangent.astype(jnp.float32)
        + scale_two * own_gain_two * normed_two_grad
        - residual * scale_two**3 * stat_two[:, None] / full_cols
    )
    branch_grad = lax.all_gather(residual_grad.astype(jnp.bfloat16), "tensor", axis=1, tiled=True)
    grad_output = jnp.einsum("tc,td->cd", attended, branch_grad, preferred_element_type=jnp.float32)
    out_grad = jnp.einsum(
        "td,cd->tc", branch_grad, w_output, preferred_element_type=jnp.float32
    ).astype(jnp.bfloat16)
    out_grad = out_grad.reshape(length, heads_here, HEAD_DIM)

    def backward_block(totals, item):
        key_total, value_total = totals
        offset, log_rows = item
        query_rows, scores = block_scores(offset)
        weights = jnp.exp(scores - log_rows[:, :, None])
        grad_rows = lax.dynamic_slice_in_dim(out_grad, offset, rows_block, 0)
        weight_grad = jnp.einsum(
            "qhd,khd->hqk", grad_rows, value_heads, preferred_element_type=jnp.float32
        )
        centred = jnp.sum(weight_grad * weights, axis=2, keepdims=True)
        score_grad = (weights * (weight_grad - centred)).astype(jnp.bfloat16)
        query_grad = (
            jnp.einsum("hqk,khd->qhd", score_grad, key_heads, preferred_element_type=jnp.float32)
            * factor
        )
        key_total = (
            key_total
            + jnp.einsum("hqk,qhd->khd", score_grad, query_rows, preferred_element_type=jnp.float32)
            * factor
        )
        value_total = value_total + jnp.einsum(
            "hqk,qhd->khd",
            weights.astype(jnp.bfloat16),
            grad_rows,
            preferred_element_type=jnp.float32,
        )
        return ((key_total, value_total), query_grad)

    empty_heads = jnp.zeros((length, heads_here, HEAD_DIM), jnp.float32)
    (key_total, value_total), query_grads = lax.scan(
        backward_block, (empty_heads, empty_heads), (starts, log_sums)
    )
    query_normed_grad = unrotate(
        rounded(query_grads.reshape(length, shard_cols)), cosine, sine, heads_here
    )
    key_normed_grad = unrotate(
        rounded(key_total.reshape(length, shard_cols)), cosine, sine, heads_here
    )
    value_grad = value_total.reshape(length, shard_cols).astype(jnp.bfloat16)
    sums_query, sums_key = lax.psum(
        (
            jnp.sum(query_pre * gain_query * query_normed_grad, axis=1),
            jnp.sum(key_pre * gain_key * key_normed_grad, axis=1),
        ),
        "tensor",
    )
    grad_query_gain = jnp.sum(query_normed_grad * query_pre * query_scale, axis=0)
    grad_key_gain = jnp.sum(key_normed_grad * key_pre * key_scale, axis=0)
    query_pre_grad = (
        query_scale * gain_query * query_normed_grad
        - query_pre * query_scale**3 * sums_query[:, None] / full_cols
    ).astype(jnp.bfloat16)
    key_pre_grad = (
        key_scale * gain_key * key_normed_grad
        - key_pre * key_scale**3 * sums_key[:, None] / full_cols
    ).astype(jnp.bfloat16)
    grad_query = jnp.einsum(
        "td,tc->dc", normed_one, query_pre_grad, preferred_element_type=jnp.float32
    )
    grad_key = jnp.einsum("td,tc->dc", normed_one, key_pre_grad, preferred_element_type=jnp.float32)
    grad_value = jnp.einsum("td,tc->dc", normed_one, value_grad, preferred_element_type=jnp.float32)
    input_terms = jnp.einsum(
        "tc,dc->td", query_pre_grad, w_query, preferred_element_type=jnp.float32
    )
    input_terms = input_terms + jnp.einsum(
        "tc,dc->td", key_pre_grad, w_key, preferred_element_type=jnp.float32
    )
    input_terms = input_terms + jnp.einsum(
        "tc,dc->td", value_grad, w_value, preferred_element_type=jnp.float32
    )
    normed_one_grad = lax.psum_scatter(
        input_terms.astype(jnp.bfloat16), "tensor", scatter_dimension=1, tiled=True
    ).astype(jnp.float32)
    own_tokens = tokens.astype(jnp.float32)
    own_gain_one = norm1_gain.astype(jnp.float32)
    stat_one = lax.psum(jnp.sum(own_tokens * own_gain_one * normed_one_grad, axis=1), "tensor")
    grad_norm1_gain = jnp.sum(normed_one_grad * own_tokens * scale_one, axis=0)
    grad_tokens = (
        residual_grad
        + scale_one * own_gain_one * normed_one_grad
        - own_tokens * scale_one**3 * stat_one[:, None] / full_cols
    )
    (
        grad_norm1_gain,
        grad_query,
        grad_key,
        grad_value,
        grad_query_gain,
        grad_key_gain,
        grad_output,
        grad_norm2_gain,
        grad_router,
        grad_gate,
        grad_up,
        grad_down,
    ) = (
        lax.psum(grad_norm1_gain.astype(jnp.bfloat16), "dp").astype(jnp.float32),
        lax.psum(grad_query.astype(jnp.bfloat16), "dp").astype(jnp.float32),
        lax.psum(grad_key.astype(jnp.bfloat16), "dp").astype(jnp.float32),
        lax.psum(grad_value.astype(jnp.bfloat16), "dp").astype(jnp.float32),
        lax.psum(grad_query_gain.astype(jnp.bfloat16), "dp").astype(jnp.float32),
        lax.psum(grad_key_gain.astype(jnp.bfloat16), "dp").astype(jnp.float32),
        lax.psum(grad_output.astype(jnp.bfloat16), "dp").astype(jnp.float32),
        lax.psum(grad_norm2_gain.astype(jnp.bfloat16), "dp").astype(jnp.float32),
        lax.psum(grad_router.astype(jnp.bfloat16), "dp").astype(jnp.float32),
        lax.psum(grad_gate.astype(jnp.bfloat16), "dp").astype(jnp.float32),
        lax.psum(grad_up.astype(jnp.bfloat16), "dp").astype(jnp.float32),
        lax.psum(grad_down.astype(jnp.bfloat16), "dp").astype(jnp.float32),
    )
    return (
        mixed,
        grad_tokens,
        grad_norm1_gain,
        grad_query,
        grad_key,
        grad_value,
        grad_query_gain,
        grad_key_gain,
        grad_output,
        grad_norm2_gain,
        grad_router,
        grad_gate,
        grad_up,
        grad_down,
    )


def solution(mesh):
    return jax.shard_map(
        on_device,
        mesh=mesh,
        in_specs=(
            P("dp", "tensor"),
            P("dp", "tensor"),
            P("tensor"),
            P(None, "tensor"),
            P(None, "tensor"),
            P(None, "tensor"),
            P("tensor"),
            P("tensor"),
            P("tensor", None),
            P("tensor"),
            P(),
            P(None, None, "tensor"),
            P(None, None, "tensor"),
            P(None, "tensor", None),
            P("dp", None),
            P("dp"),
            P("dp", None),
        ),
        out_specs=(
            P("dp", "tensor"),
            P("dp", "tensor"),
            P("tensor"),
            P(None, "tensor"),
            P(None, "tensor"),
            P(None, "tensor"),
            P("tensor"),
            P("tensor"),
            P("tensor", None),
            P("tensor"),
            P(),
            P(None, None, "tensor"),
            P(None, None, "tensor"),
            P(None, "tensor", None),
        ),
        check_vma=False,
    )
```

profile of v0, /device:TPU:0, one launch (start us, length us, event | category | flops | bytes accessed | tf_op | source)
XLA Modules:
  0.0 1687.6 jit_solution(1363458505611487672)
XLA Ops:
  10.0 13.5 all-gather
  25.6 67.5 %all-gather.7.cloned.1.call-done = bf16[1024,2048]{1,0:T(8,128)(2,1)} async-done(((bf16[1024,512]{1,0:T(8,128)(2,1)}), bf16[1024,2048]{1,0:T(8,128)(2,1)}) %all-gather.7.cloned.1.call-update) | async-done | bytes 4194320 | tf_op jit(solution)/shard_map/all_gather | solution.py:101
  96.9 5.1 convolution_convert_fusion.9
  104.3 6.8 multiply_reduce_fusion.8
  115.1 9.3 all-reduce.5
  136.3 28.0 %while.30 = (s32[]{:T(128)}, bf16[2,512,4,128]{3,1,2,0:T(8,128)(2,1)}, f32[2,4,512]{2,1,0:T(4,128)S(1)}, s32[2]{0:T(128)S(1)}, s32[]{:T(128)}, /*index=5*/bf16[1...) while((s32[]{:T(128)}, ...), condition=%wide.region_8.9_spmd.clone.clone, body=%wide.region_5.8_spmd.clone.clone.sunk | while | flops 1099955712 | bytes 43587848 | solution.py:154
  167.8 6.0 convolution_convert_fusion.2
  176.2 73.6 %reduce-scatter.5.cloned.1.call-done = bf16[1024,512]{0,1:T(8,128)(2,1)} async-done(((bf16[1024,2048]{0,1:T(8,128)(2,1)}), bf16[1024,512]{0,1:T(8,128)(2,1)}) %reduce-scatter.5.cloned.1.call-update) | async-done | bytes 1048592 | tf_op jit(solution)/shard_map/reduce_scatter | solution.py:157
  252.4 12.8 all-gather.1
  267.6 17.4 %gather_fusion = s32[3072]{0:T(1024)S(1)} fusion(s32[3072]{0:T(1024)S(1)} %reshape.395, s32[3072]{0:T(1024)S(1)} %broadcast_clamp_fusion.1), kind=kCustom, calls=%fused_computation | custom fusion | bytes 36864 | tf_op jit(solution)/shard_map/gather | solution.py:63
  287.4 11.8 scatter_custom_fusion
  299.8 11.8 scatter_custom_fusion.1
  311.7 21.1 %all-gather.11.cloned.1.call-done = bf16[1024,2048]{1,0:T(8,128)(2,1)} async-done(((bf16[1024,512]{1,0:T(8,128)(2,1)}), bf16[1024,2048]{1,0:T(8,128)(2,1)}) %all-gather.11.cloned.1.call-update) | async-done | bytes 4194320 | tf_op jit(solution)/shard_map/all_gather | solution.py:102
  332.7 6.7 concatenate.48
  339.4 32.7 %gather_fusion.4 = f32[3840,2048]{1,0:T(8,128)} fusion(f32[1025,2048]{1,0:T(8,128)} %concatenate.48, s32[4096]{0:T(1024)S(1)} %pad_clamp_fusion.1), kind=kCustom, calls=%fused_computation.4 | custom fusion | bytes 62929920 | tf_op jit(solution)/shard_map/gather | solution.py:200
  372.1 6.7 convert_element_type.248
  378.8 35.4 %all-gather.9.cloned.1.call-done = bf16[1024,2048]{0,1:T(8,128)(2,1)} async-done(((bf16[1024,512]{0,1:T(8,128)(2,1)}), bf16[1024,2048]{0,1:T(8,128)(2,1)}) %all-gather.9.cloned.1.call-update) | async-done | bytes 4194320 | tf_op jit(solution)/shard_map/all_gather | solution.py:160
  421.1 6.4 copy.190
  432.4 20.2 %gather_fusion.3 = f32[3840]{0:T(1024)S(1)} fusion(f32[3073]{0:T(1024)S(1)} %pad_maximum_fusion.3, s32[4096]{0:T(1024)S(1)} %pad_clamp_fusion), kind=kCustom, calls=%fused_computation.3 | custom fusion | bytes 46080 | tf_op jit(solution)/shard_map/gather | solution.py:195
  452.6 4.8 concatenate.45.clone
  457.4 32.6 %gather_fusion.1 = bf16[3840,2048]{1,0:T(8,128)(2,1)} fusion(bf16[1025,2048]{1,0:T(8,128)(2,1)} %concatenate.45.clone, s32[4096]{0:T(1024)S(1)} %pad_clamp_fusion.1), kind=kCustom, calls=%fused_computation.1 | custom fusion | bytes 31472640 | tf_op jit(solution)/shard_map/gather | solution.py:175
  490.0 13.4 fusion.96
  503.4 13.4 fusion.95
  516.8 20.0 %multiply_convert_fusion.6 = (bf16[6,640,256]{2,1,0:T(8,128)(2,1)}, bf16[6,640,256]{2,1,0:T(8,128)(2,1)}, bf16[6,640,256]{2,1,0:T(8,128)(2,1)}) fusion(f32[6,640,256]{2,1,0:T(8,128)} %fusion.95, f32[6,640,256]{2,1,0:T(8,128)} %fusion.96, bf16[6,256,2048]{2,1,0:T(8,128)(2,1)} %param.34, f32[6,640,2048]{2,1,0:T(8,128)} %bitcast.198, f32[6,640]{1,0:T(8,128)S(1)} %mul.520), kind=kOutput, calls=%fused_computation.88 | convolution fusion | flops 4057006080 | bytes 51526656 | tf_op jit(solution)/shard_map/ecd,efd->ecf/dot_general | solution.py:204
  536.8 18.1 %fusion.98 = f32[6,640,2048]{2,1,0:T(8,128)} fusion(bf16[6,640,256]{2,1,0:T(8,128)(2,1)} %get-tuple-element.483, bf16[6,2048,256]{2,1,0:T(8,128)(2,1)} %param.32), kind=kOutput, calls=%fused_computation.206 | convolution fusion | flops 4026531840 | bytes 39714816 | tf_op jit(solution)/shard_map/ecf,edf->ecd/dot_general | solution.py:216
  554.9 26.0 %convolution_add_fusion = f32[6,640,2048]{2,1,0:T(8,128)} fusion(f32[6,640,2048]{2,1,0:T(8,128)} %fusion.98, bf16[6,640,256]{2,1,0:T(8,128)(2,1)} %get-tuple-element.482, bf16[6,2048,256]{2,1,0:T(8,128)(2,1)} %param.33), kind=kOutput, calls=%fused_computation.62 | convolution fusion | flops 4034396160 | bytes 71172096 | tf_op jit(solution)/shard_map/ecf,edf->ecd/dot_general | solution.py:219
  580.9 21.7 %concatenate.49 = f32[3841,2048]{1,0:T(8,128)} pad(f32[3840,2048]{1,0:T(8,128)} %bitcast.200, f32[]{:T(128)} %constant.41.clone.1), padding=0_1x0_0 | pad | bytes 62922756 | tf_op jit(solution)/shard_map/concatenate | solution.py:222
  602.6 34.0 %gather_fusion.5 = f32[3072,2048]{1,0:T(8,128)} fusion(f32[3841,2048]{1,0:T(8,128)} %concatenate.49, s32[3072]{0:T(1024)S(1)} %copy-done.55), kind=kCustom, calls=%fused_computation.5 | custom fusion | bytes 50343936 | tf_op jit(solution)/shard_map/gather | solution.py:226
  636.5 37.4 %reshape.402 = f32[1024,3,2048]{2,1,0:T(4,128)} reshape(f32[3072,2048]{1,0:T(8,128)} %gather_fusion.5) | data formatting | bytes 50331648 | tf_op jit(solution)/shard_map/reshape | solution.py:226
  673.9 25.8 %reduce_sum.215 = f32[1024,2048]{1,0:T(8,128)} reduce(f32[1024,3,2048]{2,1,0:T(4,128)} %reshape.402, f32[]{:T(128)} %constant.41.clone.1), dimensions={1}, to_apply=%region_21.22 | reduce | flops 4194304 | bytes 33554436 | tf_op jit(solution)/shard_map/reduce_sum | solution.py:226
  699.6 9.6 copy.161
  709.3 18.0 %fusion.97 = f32[6,640,2048]{2,1,0:T(8,128)} fusion(bf16[6,640,256]{2,1,0:T(8,128)(2,1)} %get-tuple-element.484, bf16[6,256,2048]{2,1,0:T(8,128)(2,1)} %param.34), kind=kOutput, calls=%fused_computation.205 | convolution fusion | flops 4026531840 | bytes 39714816 | tf_op jit(solution)/shard_map/ecf,efd->ecd/dot_general | solution.py:181
  727.3 21.6 %concatenate.46 = f32[3841,2048]{1,0:T(8,128)} pad(f32[3840,2048]{1,0:T(8,128)} %bitcast.201, f32[]{:T(128)} %constant.41.clone.1), padding=0_1x0_0 | pad | bytes 62922756 | tf_op jit(solution)/shard_map/concatenate | solution.py:184
  748.9 34.0 %gather_fusion.2 = f32[3072,2048]{1,0:T(8,128)} fusion(f32[3841,2048]{1,0:T(8,128)} %concatenate.46, s32[3072]{0:T(1024)S(1)} %copy-done.55), kind=kCustom, calls=%fused_computation.2 | custom fusion | bytes 50343936 | tf_op jit(solution)/shard_map/gather | solution.py:185
  782.9 37.4 %reshape.399 = f32[1024,3,2048]{2,1,0:T(4,128)} reshape(f32[3072,2048]{1,0:T(8,128)} %gather_fusion.2) | data formatting | bytes 50331648 | tf_op jit(solution)/shard_map/reshape | solution.py:185
  820.4 37.3 %multiply_reduce_fusion.1 = (f32[1024,3]{1,0:T(8,128)S(1)}, bf16[1024,2048]{1,0:T(8,128)(2,1)}) fusion(f32[1024,3,2048]{2,1,0:T(4,128)} %reshape.399, f32[1024,2048]{1,0:T(8,128)} %convert_element_type.248, f32[1024,3]{1,0:T(8,128)S(1)} %copy-done.23), kind=kLoop, calls=%fused_computation.59 | loop fusion | flops 23065600 | bytes 37773312 | tf_op jit(solution)/shard_map/reduce_sum | solution.py:194
  857.7 27.6 %psum.135 = f32[1024,3]{1,0:T(8,128)S(1)} all-reduce(f32[1024,3]{1,0:T(8,128)S(1)} %get-tuple-element.408), channel_id=1, replica_groups=mesh['dp'=8,'tensor'=4] {'tensor'}, use_global_device_ids=true, to_apply=%region_24.25 | all-reduce | flops 3072 | bytes 24576 | tf_op jit(solution)/shard_map/psum | solution.py:228
  885.6 12.5 fusion.42
  901.1 8.9 psum.136
  909.9 63.9 %reduce-scatter.9.cloned.1.call-done = bf16[1024,512]{0,1:T(8,128)(2,1)} async-done(((bf16[1024,2048]{0,1:T(8,128)(2,1)}), bf16[1024,512]{0,1:T(8,128)(2,1)}) %reduce-scatter.9.cloned.1.call-update) | async-done | bytes 1048592 | tf_op jit(solution)/shard_map/reduce_scatter | solution.py:241
  973.8 4.7 fusion.83
  978.6 81.3 %all-gather.13.cloned.1.call-done = bf16[1024,2048]{0,1:T(8,128)(2,1)} async-done(((bf16[1024,512]{0,1:T(8,128)(2,1)}), bf16[1024,2048]{0,1:T(8,128)(2,1)}) %all-gather.13.cloned.1.call-update) | async-done | bytes 4194320 | tf_op jit(solution)/shard_map/all_gather | solution.py:251
  1059.9 6.1 convolution_convert_fusion.8
  1067.2 44.2 %while.31 = (s32[]{:T(128)}, f32[1024,4,128]{0,2,1:T(8,128)}, f32[1024,4,128]{0,2,1:T(8,128)}, bf16[2,512,4,128]{3,1,2,0:T(8,128)(2,1)}, s32[2]{0:T(128)S(1)}, /...) while((s32[]{:T(128)}, f32[1024,4,128]{0,2,1:T(8,128)}, ...), condition=%wide.region_32.33_spmd.clone.clone, body=%wide.region_30.32_spmd.clone.clone.sunk | while | flops 2719743488 | bytes 117504416 | solution.py:287
  1095.4 5.3 bitcast_add_fusion.5
  1125.8 9.1 all-reduce.4
  1135.0 5.3 subtract_convert_fusion
  1145.3 4.7 add_convert_fusion
  1150.0 6.4 copy.158
  1156.5 12.1 convolution_convert_fusion
  1168.6 11.2 convolution_convert_fusion.1
  1179.8 16.4 fusion.51
  1196.2 6.4 convolution_convert_fusion.3
  1207.0 4.4 convolution_convert_fusion.5
  1219.9 6.0 reduce-scatter.11.cloned.1.call-done
  1230.1 25.7 %all-reduce.6 = (bf16[512]{0:T(512)(128)(2,1)S(1)}, bf16[512]{0:T(512)(128)(2,1)S(1)}, bf16[512]{0:T(512)(128)(2,1)S(1)}, bf16[512]{0:T(512)(128)(2,1)S(1)}, bf16[2048,6]{0,1:T(8,128)(2,1)S(1)}) all-reduce(bf16[512]{0:T(512)(128)(2,1)S(1)} %get-tuple-element.416, ...), channel_id=1, replica_groups=mesh['dp'=8,'tensor'=4] {'dp'}, use_global_device_ids=true, to_apply=%region_41.42 | all-reduce | flops 14336 | bytes 57344 | tf_op jit(solution)/shard_map/psum | solution.py:354
  1258.0 12.3 psum.139
  1270.3 36.1 %reduce-scatter.7.cloned.1.call-done = bf16[1024,512]{0,1:T(8,128)(2,1)} async-done(((bf16[1024,2048]{0,1:T(8,128)(2,1)}), bf16[1024,512]{0,1:T(8,128)(2,1)}) %reduce-scatter.7.cloned.1.call-update) | async-done | bytes 1048592 | tf_op jit(solution)/shard_map/reduce_scatter | solution.py:189
  1306.5 6.7 fusion.54
  1318.1 329.5 %all-reduce.10.cloned.1.call-done = (bf16[2048,512]{1,0:T(8,128)(2,1)}, bf16[2048,512]{1,0:T(8,128)(2,1)}, bf16[2048,512]{1,0:T(8,128)(2,1)}, bf16[512,2048]{1,0...) async-done(((bf16[2048,512]{1,0:T(8,128)(2,1)}, bf16[2048,512]{1,0:T(8,128)(2,1)}, ...) | async-done | bytes 27262992 | tf_op jit(solution)/shard_map/psum | solution.py:355
  1647.6 4.3 convert_element_type.273
  1659.8 8.9 convert_element_type.289
  1668.7 5.9 convert_element_type.291
  1674.6 6.3 convert_element_type.293
  (367 shorter events, 166.6 us)
Async XLA Ops:
  7.2 104.0 %copy-start = (bf16[2048,512]{1,0:T(8,128)(2,1)S(1)}, bf16[2048,512]{1,0:T(8,128)(2,1)}, u32[]{:S(2)}) copy-start(bf16[2048,512]{1,0:T(8,128)(2,1)} %param.24) | copy-start | bytes 6291460
  7.2 85.9 %all-gather.7.cloned.1.call-start = ((), (), s32[]{:S(2)}) async-start(), calls=%async_computation.4 | async-start | bytes 5242880 | tf_op jit(solution)/shard_map/all_gather | solution.py:101
  7.9 241.8 %reduce-scatter.5.cloned.1.call-start = ((), (), s32[]{:S(2)}) async-start(), calls=%async_computation.5 | async-start | bytes 5242880 | tf_op jit(solution)/shard_map/reduce_scatter | solution.py:157
  8.7 119.7 %copy-start.71 = (f32[512]{0:T(512)}, f32[512]{0:T(512)S(1)}, u32[]{:S(2)}) copy-start(f32[512]{0:T(512)S(1)} %convert_element_type.228) | copy-start | bytes 6148
  9.4 119.1 %copy-start.73 = (f32[512]{0:T(512)}, f32[512]{0:T(512)S(1)}, u32[]{:S(2)}) copy-start(f32[512]{0:T(512)S(1)} %convert_element_type.230) | copy-start | bytes 6148
  23.6 87.6 %copy-start.87 = (f32[4,1,512]{2,1,0:T(1,128)}, f32[4,1,512]{2,1,0:T(1,128)S(1)}, u32[]{:S(2)}) copy-start(f32[4,1,512]{2,1,0:T(1,128)S(1)} %convert_element_type.297) | copy-start | bytes 24580
  25.6 102.0 %copy-start.24 = (f32[1024,128]{0,1:T(8,128)}, f32[1024,128]{0,1:T(8,128)S(1)}, u32[]{:S(2)}) copy-start(f32[1024,128]{0,1:T(8,128)S(1)} %get-tuple-element.504) | copy-start | bytes 1572868
  25.6 102.8 %copy-start.19 = (f32[1024,128]{0,1:T(8,128)}, f32[1024,128]{0,1:T(8,128)S(1)}, u32[]{:S(2)}) copy-start(f32[1024,128]{0,1:T(8,128)S(1)} %get-tuple-element.503) | copy-start | bytes 1572868
  96.9 14.2 copy-start.75
  104.3 6.8 copy-start.29
  164.3 9.5 copy-start.3
  164.4 9.5 copy-start.65
  164.4 9.5 copy-start.93
  173.8 78.6 %copy-start.89 = (bf16[512]{0:T(512)(128)(2,1)S(1)}, bf16[512]{0:T(512)(128)(2,1)}, u32[]{:S(2)}) copy-start(bf16[512]{0:T(512)(128)(2,1)} %param.30) | copy-start | bytes 3076
  173.8 91.4 %copy-start.51 = (s32[1024,3]{0,1:T(4,128)S(1)}, s32[1024,3]{0,1:T(4,128)}, u32[]{:S(2)}) copy-start(s32[1024,3]{0,1:T(4,128)} %param.35) | copy-start | bytes 36868
  173.9 158.9 %all-gather.11.cloned.1.call-start = ((), (), s32[]{:S(2)}) async-start(), calls=%async_computation.8 | async-start | bytes 5242880 | tf_op jit(solution)/shard_map/all_gather | solution.py:102
  174.6 93.0 %copy-start.86 = (s32[1,3072]{1,0:T(1,128)S(1)}, s32[1,3072]{1,0:T(1,128)}, u32[]{:S(2)}) copy-start(s32[1,3072]{1,0:T(1,128)} %param.37) | copy-start | bytes 36868
  174.6 239.5 %all-gather.9.cloned.1.call-start = ((), (), s32[]{:S(2)}) async-start(), calls=%async_computation.6 | async-start | bytes 5242880 | tf_op jit(solution)/shard_map/all_gather | solution.py:160
  176.2 89.1 %copy-start.13 = (bf16[1024,512]{0,1:T(8,128)(2,1)}, bf16[1024,512]{0,1:T(8,128)(2,1)S(1)}, u32[]{:S(2)}) copy-start(bf16[1024,512]{0,1:T(8,128)(2,1)S(1)} %copy.149) | copy-start | bytes 3145732
  252.4 721.4 %reduce-scatter.9.cloned.1.call-start = ((), (), s32[]{:S(2)}) async-start(), calls=%async_computation.9 | async-start | bytes 5242880 | tf_op jit(solution)/shard_map/reduce_scatter | solution.py:241
  265.2 152.8 %copy-start.67 = (f32[4,1,512]{2,1,0:T(1,128)}, f32[4,1,512]{2,1,0:T(1,128)S(1)}, u32[]{:S(2)}) copy-start(f32[4,1,512]{2,1,0:T(1,128)S(1)} %convert_element_type.298) | copy-start | bytes 24580
  421.1 6.4 copy-start.53
  430.5 22.1 %copy-start.63 = (f32[1024]{0:T(1024)}, f32[1024]{0:T(1024)S(1)}, u32[]{:S(2)}) copy-start(f32[1024]{0:T(1024)S(1)} %get-tuple-element.519) | copy-start | bytes 12292
  430.5 22.1 %copy-start.69 = (f32[1024]{0:T(1024)}, f32[1024]{0:T(1024)S(1)}, u32[]{:S(2)}) copy-start(f32[1024]{0:T(1024)S(1)} %fusion.77) | copy-start | bytes 12292
  452.6 64.2 %copy-start.47 = (f32[6,640]{1,0:T(8,128)}, f32[6,640]{1,0:T(8,128)S(1)}, u32[]{:S(2)}) copy-start(f32[6,640]{1,0:T(8,128)S(1)} %mul.520) | copy-start | bytes 46084
  580.9 21.7 %copy-start.55 = (s32[3072]{0:T(1024)S(1)}, s32[3072]{0:T(1024)}, u32[]{:S(2)}) copy-start(s32[3072]{0:T(1024)} %get-tuple-element.475) | copy-start | bytes 36868
  782.9 37.4 %copy-start.23 = (f32[1024,3]{1,0:T(8,128)S(1)}, f32[1024,3]{1,0:T(8,128)}, u32[]{:S(2)}) copy-start(f32[1024,3]{1,0:T(8,128)} %copy-done.22) | copy-start | bytes 36868
  820.3 65.1 %copy-start.52 = (s32[1024,3]{0,1:T(4,128)S(1)}, s32[1024,3]{0,1:T(4,128)}, u32[]{:S(2)}) copy-start(s32[1024,3]{0,1:T(4,128)} %param.35) | copy-start | bytes 36868
  820.3 65.2 %copy-start.46 = (f32[1024,6]{0,1:T(8,128)S(1)}, f32[1024,6]{0,1:T(8,128)}, u32[]{:S(2)}) copy-start(f32[1024,6]{0,1:T(8,128)} %copy-done.45) | copy-start | bytes 73732
  820.3 65.2 %copy-start.64 = (f32[1024]{0:T(1024)S(1)}, f32[1024]{0:T(1024)}, u32[]{:S(2)}) copy-start(f32[1024]{0:T(1024)} %copy-done.63) | copy-start | bytes 12292
  820.4 65.2 %copy-start.70 = (f32[1024]{0:T(1024)S(1)}, f32[1024]{0:T(1024)}, u32[]{:S(2)}) copy-start(f32[1024]{0:T(1024)} %copy-done.69) | copy-start | bytes 12292
  820.4 65.2 %copy-start.54 = (bf16[2048,6]{0,1:T(8,128)(2,1)S(1)}, bf16[2048,6]{0,1:T(8,128)(2,1)}, u32[]{:S(2)}) copy-start(bf16[2048,6]{0,1:T(8,128)(2,1)} %param.31) | copy-start | bytes 73732
  820.4 65.2 %copy-start.68 = (f32[4,1,512]{2,1,0:T(1,128)S(1)}, f32[4,1,512]{2,1,0:T(1,128)}, u32[]{:S(2)}) copy-start(f32[4,1,512]{2,1,0:T(1,128)} %copy-done.67) | copy-start | bytes 24580
  885.6 12.5 copy-start.49
  898.1 75.7 %copy-start.14 = (bf16[1024,512]{0,1:T(8,128)(2,1)S(1)}, bf16[1024,512]{0,1:T(8,128)(2,1)}, u32[]{:S(2)}) copy-start(bf16[1024,512]{0,1:T(8,128)(2,1)} %copy-done.13) | copy-start | bytes 3145732
  898.1 75.7 %copy-start.57 = (f32[1024]{0:T(1024)S(1)}, f32[1024]{0:T(1024)}, u32[]{:S(2)}) copy-start(f32[1024]{0:T(1024)} %copy-done.56) | copy-start | bytes 12292
  898.1 75.7 %copy-start.77 = (f32[1024]{0:T(1024)S(1)}, f32[1024]{0:T(1024)}, u32[]{:S(2)}) copy-start(f32[1024]{0:T(1024)} %get-tuple-element.513) | copy-start | bytes 12292
  898.2 161.8 %all-gather.13.cloned.1.call-start = ((), (), s32[]{:S(2)}) async-start(), calls=%async_computation.10 | async-start | bytes 5242880 | tf_op jit(solution)/shard_map/all_gather | solution.py:251
  898.8 79.7 %copy-start.81 = (f32[512]{0:T(512)}, f32[512]{0:T(512)S(1)}, u32[]{:S(2)}) copy-start(f32[512]{0:T(512)S(1)} %convert_element_type.247) | copy-start | bytes 6148
  909.9 68.6 %copy-start.79 = (f32[1024]{0:T(1024)}, f32[1024]{0:T(1024)S(1)}, u32[]{:S(2)}) copy-start(f32[1024]{0:T(1024)S(1)} %add.241) | copy-start | bytes 12292
  978.5 247.4 %reduce-scatter.11.cloned.1.call-start = ((), (), s32[]{:S(2)}) async-start(), calls=%async_computation.11 | async-start | bytes 5242880 | tf_op jit(solution)/shard_map/reduce_scatter | solution.py:328
  978.6 88.6 %copy-start.4 = (bf16[1024,4,128]{2,0,1:T(8,128)(2,1)S(1)}, bf16[1024,4,128]{2,0,1:T(8,128)(2,1)}, u32[]{:S(2)}) copy-start(bf16[1024,4,128]{2,0,1:T(8,128)(2,1)} %copy-done.3) | copy-start | bytes 3145732
  978.6 88.6 %copy-start.66 = (f32[2,4,512]{2,1,0:T(4,128)S(1)}, f32[2,4,512]{2,1,0:T(4,128)}, u32[]{:S(2)}) copy-start(f32[2,4,512]{2,1,0:T(4,128)} %copy-done.65) | copy-start | bytes 49156
  978.6 88.6 %copy-start.94 = (s32[2]{0:T(128)S(1)}, s32[2]{0:T(128)}, u32[]{:S(2)}) copy-start(s32[2]{0:T(128)} %copy-done.93) | copy-start | bytes 28
  1114.1 6.6 copy-start.18
  1123.3 11.7 copy-start.84
  1123.3 11.7 copy-start.85
  1150.0 156.5 %reduce-scatter.7.cloned.1.call-start = ((), (), s32[]{:S(2)}) async-start(), calls=%async_computation.7 | async-start | bytes 5242880 | tf_op jit(solution)/shard_map/reduce_scatter | solution.py:189
  1156.5 491.1 %all-reduce.10.cloned.1.call-start = ((), (), s32[]{:S(2)}) async-start(), calls=%async_computation.12 | async-start | bytes 54525952 | tf_op jit(solution)/shard_map/psum | solution.py:355
  1156.5 12.1 copy-start.35
  1168.6 11.2 copy-start.48
  1196.2 6.5 copy-start.30
  1196.2 6.4 copy-start.76
  1196.2 6.4 copy-start.88
  1216.4 9.6 copy-start.15
  1216.4 9.6 copy-start.58
  1219.9 86.6 %copy-start.78 = (f32[1024]{0:T(1024)S(1)}, f32[1024]{0:T(1024)}, u32[]{:S(2)}) copy-start(f32[1024]{0:T(1024)} %get-tuple-element.513) | copy-start | bytes 12292
  1219.9 86.6 %copy-start.80 = (f32[1024]{0:T(1024)S(1)}, f32[1024]{0:T(1024)}, u32[]{:S(2)}) copy-start(f32[1024]{0:T(1024)} %copy-done.79) | copy-start | bytes 12292
  1219.9 86.6 %copy-start.82 = (f32[512]{0:T(512)S(1)}, f32[512]{0:T(512)}, u32[]{:S(2)}) copy-start(f32[512]{0:T(512)} %copy-done.81) | copy-start | bytes 6148
  1219.9 86.6 %copy-start.83 = (f32[1024]{0:T(1024)S(1)}, f32[1024]{0:T(1024)}, u32[]{:S(2)}) copy-start(f32[1024]{0:T(1024)} %get-tuple-element.507) | copy-start | bytes 12292
  1657.1 11.5 slice-start.2
  1659.8 8.9 slice-start.3
  1659.8 14.8 slice-start
  1668.7 5.9 slice-start.1
  (54 other events, 134.9 us)
Sparse Core Ops, SparseCore 0:
  9.6 83.4 all-gather.6
  174.0 75.7 reduce-scatter.4
  251.4 81.2 all-gather.10
  334.8 79.2 all-gather.8
  898.3 75.4 reduce-scatter.8
  978.6 81.2 all-gather.12
  1150.1 75.8 reduce-scatter.10
  1228.9 77.5 reduce-scatter.6
  1312.8 334.6 all-reduce.9
where the time goes:
time: 1700 us; the launch traced here: 1690 us
  waiting for transfers between devices  716 us (42%)
  local copies, waits for them, and re-layouts  388 us (23%)
  matrix products  264 us (16%)
  other arithmetic  177 us (10%)
  blocking collectives  119 us (7%)
    psum x1, waiting for transfers between devices, on_device(): lax.psum(grad_query.astype(jnp.bfloat16), 'dp').astype(jnp.float32)  329 us
    all_gather x1, waiting for transfers between devices, on_device(): lax.all_gather(residual_grad.astype(jnp.bfloat16), 'tensor', axis=1, tile...  81.3 us
    reduce_scatter x1, waiting for transfers between devices, on_device(): lax.psum_scatter(attn_terms.astype(jnp.bfloat16), 'tensor', scatter_dimen...  73.6 us
    all_gather x1, waiting for transfers between devices, on_device(): lax.all_gather(tokens, 'tensor', axis=1, tiled=True)  67.5 us
    reduce_scatter x1, waiting for transfers between devices, on_device(): lax.psum_scatter(token_input.astype(jnp.bfloat16), 'tensor', scatter_dime...  63.9 us
    reshape x1, local copies, waits for them, and re-layouts, on_device(): paired = expert_pad[target].reshape(length, TOP, full_cols)  37.4 us
    reshape x1, local copies, waits for them, and re-layouts, on_device(): slot_pad[target].reshape(length, TOP, full_cols)  37.4 us
    reduce_sum x1, other arithmetic, on_device(): gate_terms = jnp.sum(paired * cot_full[:, None, :], axis=2)  37.3 us
  transfers between devices with their start and end apart: 9, of which 9 were waited for; matrix products, arithmetic and copies ran while one was open for 11% of the time, Pallas kernels for 0%

commit v1 on v0

v1 whole, which is shorter than its diff:
```python
import functools

import jax
import jax.numpy as jnp
from jax import lax
from jax.experimental import pallas as pl
from jax.experimental.pallas import tpu as pltpu
from jax.sharding import PartitionSpec as P

HEAD_DIM = 128
EXPERTS = 6
TOP = 3
CAP = 640
PREFIX_MAX = 512

EPSILON = 1e-05
ROPE_BASE = 10000.0
MASKED = -1e30
BF = jnp.bfloat16
F32 = jnp.float32
VMEM_LIMIT = 56 * 1024 * 1024


def params():
    return pltpu.CompilerParams(vmem_limit_bytes=VMEM_LIMIT)


def cost(flops, nbytes, trans=0):
    return pl.CostEstimate(flops=int(flops), bytes_accessed=int(nbytes), transcendentals=int(trans))


def dot(a, b):
    return jnp.dot(a, b, preferred_element_type=F32)


def dot_t(a, b):
    return lax.dot_general(a, b, (((1,), (1,)), ((), ())), preferred_element_type=F32)


def row_sums(field):
    ones = jnp.ones((8, field.shape[1]), F32)
    return lax.dot_general(
        ones, field, (((1,), (1,)), ((), ())), precision=lax.Precision.HIGHEST,
        preferred_element_type=F32,
    )


def ring(size):
    return [(at, (at + 1) % size) for at in range(size)]


def gather_ring(block, size):
    held = [block]
    for _ in range(size - 1):
        held.append(lax.ppermute(held[-1], "tensor", ring(size)))
    return held


def scatter_ring(part, mine, size):
    received = None
    for step in range(1, size):
        term = part((mine - step) % size)
        if received is not None:
            term = term.astype(F32) + received.astype(F32)
        received = lax.ppermute(term.astype(BF), "tensor", ring(size))
    return part(mine).astype(F32) + received.astype(F32)


def sum_direct(field, size):
    total = field
    for step in range(1, size):
        total = total + lax.ppermute(
            field, "tensor", [(at, (at + step) % size) for at in range(size)]
        )
    return total


def exchange(blocks, mine, size):
    own = lax.dynamic_slice_in_dim(blocks, mine, 1, 0)
    out = lax.dynamic_update_slice_in_dim(jnp.zeros_like(blocks), own, mine, 0)
    for step in range(1, size):
        send = lax.dynamic_slice_in_dim(blocks, (mine + step) % size, 1, 0)
        got = lax.ppermute(send, "tensor", [(at, (at + step) % size) for at in range(size)])
        out = lax.dynamic_update_slice_in_dim(out, got, (mine - step) % size, 0)
    return out


def swap(field, mask, n):
    return lax.ppermute(field, "dp", [(at, at ^ mask) for at in range(n)])


def swap_orders(n):
    masks = [1 << bit for bit in range(n.bit_length() - 1)]
    return masks, masks[:1] + masks[1:][::-1]


def rel_table(order):
    bits = len(order)
    return [
        sum(order[s] for s in range(bits) if (p >> (bits - 1 - s)) & 1) for p in range(1 << bits)
    ]


def dp_sum(send, keep, order, n):
    received = swap(send, order[0], n)
    size = n // 2
    for mask in order[1:]:
        size //= 2
        send = keep[size:] + received[size:]
        keep = keep[:size] + received[:size]
        received = swap(send, mask, n)
    total = keep + received
    for mask in order[1:][::-1]:
        total = jnp.concatenate([total, swap(total, mask, n)], axis=0)
    return total, swap(total, order[0], n)


def dp_sum_small(field, n):
    for mask in swap_orders(n)[0]:
        field = field + swap(field, mask, n)
    return field


def qkv_kernel(x_ref, gain_ref, wq_ref, wk_ref, wv_ref, n1_ref, q_ref, k_ref, v_ref, sums_ref):
    blocks, rows, cols = x_ref.shape
    full = blocks * cols
    fields = [x_ref[t].astype(F32) for t in range(blocks)]
    squares = fields[0] * fields[0]
    for t in range(1, blocks):
        squares = squares + fields[t] * fields[t]
    scale = lax.rsqrt(jnp.sum(squares, axis=1, keepdims=True) / full + EPSILON)
    for t in range(blocks):
        gain = gain_ref[t, 0:1, :].astype(F32)
        n1_ref[:, t * cols : (t + 1) * cols] = (fields[t] * scale * gain).astype(BF)
    normed = n1_ref[...]
    query = dot(normed, wq_ref[...])
    key = dot(normed, wk_ref[...])
    q_ref[...] = query
    k_ref[...] = key
    v_ref[...] = dot(normed, wv_ref[...]).astype(BF)
    which = lax.broadcasted_iota(jnp.int32, (8, rows), 0)
    sums_ref[...] = jnp.where(
        which == 0,
        row_sums(query * query),
        jnp.where(which == 1, row_sums(key * key), row_sums(squares)),
    )


def qkv_call(x_aug, wq, wk, wv, length):
    blocks, _, cols = x_aug.shape
    full = blocks * cols
    out = wq.shape[1]
    rows = min(256, length)
    whole = pl.BlockSpec((full, out), lambda g: (0, 0))
    tile = pl.BlockSpec((rows, out), lambda g: (g, 0))
    return pl.pallas_call(
        qkv_kernel,
        grid=(length // rows,),
        in_specs=[
            pl.BlockSpec((blocks, rows, cols), lambda g: (0, g, 0)),
            pl.BlockSpec((blocks, 16, cols), lambda g: (0, length // 16, 0)),
            whole,
            whole,
            whole,
        ],
        out_specs=[
            pl.BlockSpec((rows, full), lambda g: (g, 0)),
            tile,
            tile,
            tile,
            pl.BlockSpec((8, rows), lambda g: (0, g)),
        ],
        out_shape=[
            jax.ShapeDtypeStruct((length, full), BF),
            jax.ShapeDtypeStruct((length, out), F32),
            jax.ShapeDtypeStruct((length, out), F32),
            jax.ShapeDtypeStruct((length, out), BF),
            jax.ShapeDtypeStruct((8, length), F32),
        ],
        compiler_params=params(),
        cost_estimate=cost(6 * length * full * out, 10 * length * full + 6 * full * out),
    )(x_aug, x_aug, wq, wk, wv)


def head_scales(sums_refs, full):
    total = sums_refs[0][...]
    for ref in sums_refs[1:]:
        total = total + ref[...]
    return jnp.transpose(lax.rsqrt(total / full + EPSILON))


def masked_scores(query, key, first, prefix):
    scores = dot_t(query, key) * (HEAD_DIM**-0.5)
    row = first + lax.broadcasted_iota(jnp.int32, scores.shape, 0)
    col = lax.broadcasted_iota(jnp.int32, scores.shape, 1)
    return jnp.where((col <= row) | (col < prefix), scores, MASKED)


def attn_forward_kernel(full, size, prefix_ref, q_ref, k_ref, v_ref, gq_ref, gk_ref, cos_ref, sin_ref, *rest):
    sums_refs, (att_ref, lse_ref, qr_ref, kr_ref) = rest[:size], rest[size:]
    length = q_ref.shape[0]
    rows = min(256, length)
    scales = head_scales(sums_refs, full)
    cosine, sine = cos_ref[...], sin_ref[...]
    for pre_ref, gain_ref, out_ref, at in ((q_ref, gq_ref, qr_ref, 0), (k_ref, gk_ref, kr_ref, 1)):
        field = pre_ref[...] * scales[:, at : at + 1] * gain_ref[...].astype(F32)
        out_ref[...] = (field * cosine + pltpu.roll(field, HEAD_DIM // 2, 1) * sine).astype(BF)
    prefix = prefix_ref[0]
    for first in range(0, length, rows):
        last = min(length, max(PREFIX_MAX, first + rows))
        scores = masked_scores(qr_ref[first : first + rows, :], kr_ref[:last, :], first, prefix)
        highest = jnp.max(scores, axis=1, keepdims=True)
        exponent = jnp.exp(scores - highest)
        total = jnp.sum(exponent, axis=1, keepdims=True)
        mixed = dot(exponent.astype(BF), v_ref[:last, :])
        att_ref[first : first + rows, :] = (mixed / total).astype(BF)
        lse_ref[first : first + rows, :] = jnp.broadcast_to(
            highest + jnp.log(total), (rows, HEAD_DIM)
        )


def attn_forward(prefix, q_pre, k_pre, v_rows, gq, gk, cosine, sine, sums):
    length, width = q_pre.shape
    full = width * len(sums)
    head = pl.BlockSpec((length, HEAD_DIM), lambda h, *_: (0, h))
    gain = pl.BlockSpec((1, HEAD_DIM), lambda h, *_: (0, h))
    table = pl.BlockSpec((length, HEAD_DIM), lambda h, *_: (0, 0))
    sums_spec = pl.BlockSpec((8, length), lambda h, *_: (0, 0))
    return pl.pallas_call(
        functools.partial(attn_forward_kernel, full, len(sums)),
        grid_spec=pltpu.PrefetchScalarGridSpec(
            num_scalar_prefetch=1,
            grid=(width // HEAD_DIM,),
            in_specs=[head, head, head, gain, gain, table, table] + [sums_spec] * len(sums),
            out_specs=[head] * 4,
        ),
        out_shape=[
            jax.ShapeDtypeStruct((length, width), BF),
            jax.ShapeDtypeStruct((length, width), F32),
            jax.ShapeDtypeStruct((length, width), BF),
            jax.ShapeDtypeStruct((length, width), BF),
        ],
        compiler_params=params(),
        cost_estimate=cost(4 * length * length * width, 20 * length * width, length * length * 4),
    )(prefix, q_pre, k_pre, v_rows, gq, gk, cosine, sine, *sums)


def attn_backward_kernel(
    full, size, prefix_ref, q_ref, k_ref, qr_ref, kr_ref, v_ref, do_ref, lse_ref, gq_ref, gk_ref,
    cos_ref, sin_ref, *rest,
):
    sums_refs, rest = rest[:size], rest[size:]
    dq_ref, dk_ref, dv_ref, gains_ref, rows_ref, kacc, vacc = rest
    head = pl.program_id(0)
    length = q_ref.shape[0]
    rows = min(256, length)
    prefix = prefix_ref[0]
    factor = HEAD_DIM**-0.5
    kacc[...] = jnp.zeros_like(kacc)
    vacc[...] = jnp.zeros_like(vacc)
    contract = (((0,), (0,)), ((), ()))
    for first in range(0, length, rows):
        last = min(length, max(PREFIX_MAX, first + rows))
        here = slice(first, first + rows)
        scores = masked_scores(qr_ref[here, :], kr_ref[:last, :], first, prefix)
        weights = jnp.exp(scores - lse_ref[here, 0:1])
        grad_rows = do_ref[here, :]
        weight_grad = dot_t(grad_rows, v_ref[:last, :])
        centred = jnp.sum(weight_grad * weights, axis=1, keepdims=True)
        score_grad = (weights * (weight_grad - centred)).astype(BF)
        dq_ref[here, :] = dot(score_grad, kr_ref[:last, :]) * factor
        kacc[:last, :] += lax.dot_general(
            score_grad, qr_ref[here, :], contract, preferred_element_type=F32
        )
        vacc[:last, :] += lax.dot_general(
            weights.astype(BF), grad_rows, contract, preferred_element_type=F32
        )
    dv_ref[...] = vacc[...].astype(BF)
    scales = head_scales(sums_refs, full)
    cosine, sine = cos_ref[...], sin_ref[...]
    which = lax.broadcasted_iota(jnp.int32, (8, length), 0)
    lanes = lax.broadcasted_iota(jnp.int32, (8, HEAD_DIM), 0)
    row_terms = jnp.zeros((8, length), F32)
    gain_terms = jnp.zeros((8, HEAD_DIM), F32)
    for at, (pre_ref, gain_ref, out_ref, raw) in enumerate(
        ((q_ref, gq_ref, dq_ref, dq_ref[...]), (k_ref, gk_ref, dk_ref, kacc[...] * factor))
    ):
        raw = raw.astype(BF).astype(F32)
        normed_grad = raw * cosine - pltpu.roll(raw, HEAD_DIM // 2, 1) * sine
        out_ref[...] = normed_grad
        product = normed_grad * pre_ref[...]
        row_terms = jnp.where(
            which == at, row_sums(product * gain_ref[...].astype(F32)), row_terms
        )
        gain_terms = jnp.where(
            lanes == at,
            jnp.sum(product * scales[:, at : at + 1], axis=0, keepdims=True),
            gain_terms,
        )
    gains_ref[...] = gain_terms

    @pl.when(head == 0)
    def _():
        rows_ref[...] = row_terms

    @pl.when(head > 0)
    def _():
        rows_ref[...] += row_terms


def attn_backward(prefix, q_pre, k_pre, q_rot, k_rot, v_rows, out_grad, lse, gq, gk, cosine, sine, sums):
    length, width = q_pre.shape
    full = width * len(sums)
    head = pl.BlockSpec((length, HEAD_DIM), lambda h, *_: (0, h))
    gain = pl.BlockSpec((1, HEAD_DIM), lambda h, *_: (0, h))
    table = pl.BlockSpec((length, HEAD_DIM), lambda h, *_: (0, 0))
    sums_spec = pl.BlockSpec((8, length), lambda h, *_: (0, 0))
    return pl.pallas_call(
        functools.partial(attn_backward_kernel, full, len(sums)),
        grid_spec=pltpu.PrefetchScalarGridSpec(
            num_scalar_prefetch=1,
            grid=(width // HEAD_DIM,),
            in_specs=[head] * 7 + [gain, gain, table, table] + [sums_spec] * len(sums),
            out_specs=[head, head, head, pl.BlockSpec((8, HEAD_DIM), lambda h, *_: (0, h)), sums_spec],
            scratch_shapes=[pltpu.VMEM((length, HEAD_DIM), F32)] * 2,
        ),
        out_shape=[
            jax.ShapeDtypeStruct((length, width), F32),
            jax.ShapeDtypeStruct((length, width), F32),
            jax.ShapeDtypeStruct((length, width), BF),
            jax.ShapeDtypeStruct((8, width), F32),
            jax.ShapeDtypeStruct((8, length), F32),
        ],
        compiler_params=params(),
        cost_estimate=cost(10 * length * length * width, 36 * length * width, length * length * 4),
    )(prefix, q_pre, k_pre, q_rot, k_rot, v_rows, out_grad, lse, gq, gk, cosine, sine, *sums)


def norm_back_kernel(full, size, q_ref, k_ref, v_ref, dq_ref, dk_ref, dv_ref, gq_ref, gk_ref, *rest):
    sums_refs, back_refs, (out_ref, stat_ref) = rest[:size], rest[size : 2 * size], rest[2 * size :]
    width = q_ref.shape[1]
    scales = head_scales(sums_refs, full)
    back = back_refs[0][...]
    for ref in back_refs[1:]:
        back = back + ref[...]
    back = jnp.transpose(back)
    grads = []
    stat = dv_ref[...].astype(F32) * v_ref[...].astype(F32)
    for at, (pre_ref, grad_ref, gain_ref) in enumerate(
        ((q_ref, dq_ref, gq_ref), (k_ref, dk_ref, gk_ref))
    ):
        scale = scales[:, at : at + 1]
        pre = pre_ref[...]
        grad = (
            scale * gain_ref[...].astype(F32) * grad_ref[...]
            - pre * (scale * scale * scale * back[:, at : at + 1] / full)
        ).astype(BF)
        stat = stat + grad.astype(F32) * pre
        grads.append(grad)
    out_ref[:, :width] = grads[0]
    out_ref[:, width : 2 * width] = grads[1]
    out_ref[:, 2 * width :] = dv_ref[...]
    stat_ref[...] = row_sums(stat)


def norm_back(q_pre, k_pre, v_rows, dq, dk, dv, gq, gk, sums, back):
    length, width = q_pre.shape
    full = width * len(sums)
    rows = min(256, length)
    tile = pl.BlockSpec((rows, width), lambda g: (g, 0))
    wide = pl.BlockSpec((rows, 3 * width), lambda g: (g, 0))
    gain = pl.BlockSpec((1, width), lambda g: (0, 0))
    line = pl.BlockSpec((8, rows), lambda g: (0, g))
    return pl.pallas_call(
        functools.partial(norm_back_kernel, full, len(sums)),
        grid=(length // rows,),
        in_specs=[tile] * 6 + [gain, gain] + [line] * (2 * len(sums)),
        out_specs=[wide, line],
        out_shape=[
            jax.ShapeDtypeStruct((length, 3 * width), BF),
            jax.ShapeDtypeStruct((8, length), F32),
        ],
        compiler_params=params(),
        cost_estimate=cost(20 * length * width, 28 * length * width),
    )(q_pre, k_pre, v_rows, dq, dk, dv, gq, gk, *sums, *back)


def expert_kernel(own, aliased, chunk_ref, n2_ref, cot_ref, router_ref, keep_ref, wg_ref, wu_ref, wd_ref, *rest):
    rest = list(rest)
    res_ref = rest.pop(0) if own else None
    rest = rest[aliased:]
    h2t_ref, dg_ref, du_ref, n2t_ref, mix_ref, dn2_ref, gg_ref, probs_ref, mix, dn2, gates = rest
    expert = pl.program_id(0)
    blocks, rows, cols = cot_ref.shape
    lane = lax.broadcasted_iota(jnp.int32, (rows, 128), 1)

    @pl.when(expert == 0)
    def _():
        logits = jnp.where(lane < EXPERTS, dot(n2_ref[...], router_ref[...]), MASKED)
        exponent = jnp.exp(logits - jnp.max(logits, axis=1, keepdims=True))
        probs = exponent / jnp.sum(exponent, axis=1, keepdims=True)
        probs_ref[...] = probs
        gates[...] = probs * keep_ref[...]
        gg_ref[...] = jnp.zeros_like(gg_ref)
        n2t_ref[...] = jnp.transpose(n2_ref[...])
        dn2[...] = jnp.zeros_like(dn2)
        if own:
            mix[...] = res_ref[...]
        else:
            mix[...] = jnp.zeros_like(mix)

    normed = n2_ref[...]
    w_down = wd_ref[0]
    pre_gate = dot(normed, wg_ref[0])
    pre_up = dot(normed, wu_ref[0])
    back = dot_t(cot_ref[0], w_down[:, :cols])
    for t in range(1, blocks):
        back = back + dot_t(cot_ref[t], w_down[:, t * cols : (t + 1) * cols])
    here = lane == expert
    gate = jnp.sum(jnp.where(here, gates[...], 0.0), axis=1, keepdims=True)
    sigmoid = jax.nn.sigmoid(pre_gate)
    activated = pre_gate * sigmoid
    hidden = (activated * pre_up).astype(BF).astype(F32)
    gate_grad = jnp.sum(back * hidden, axis=1, keepdims=True)
    gg_ref[...] += jnp.where(here, gate_grad * keep_ref[...], 0.0)
    back = back * gate
    h2 = (hidden * gate).astype(BF)
    dg = (back * pre_up * sigmoid * (1.0 + pre_gate * (1.0 - sigmoid))).astype(BF)
    du = (back * activated).astype(BF)
    h2t_ref[...] = jnp.transpose(h2)
    dg_ref[...] = dg
    du_ref[...] = du
    mix[...] += dot(h2, w_down)
    dn2[...] += dot_t(dg, wg_ref[0]) + dot_t(du, wu_ref[0])

    @pl.when(expert == EXPERTS - 1)
    def _():
        dn2_ref[...] = dn2[...].astype(BF)
        for t in range(blocks):
            mix_ref[t] = mix[:, t * cols : (t + 1) * cols].astype(BF)


def expert_call(chunk, n2, cot, router, keep, wg, wu, wd, residual, carried):
    rows, full = n2.shape
    blocks, length, cols = cot.shape
    hidden = wg.shape[2]
    own = residual is not None
    in_specs = [
        pl.BlockSpec((rows, full), lambda e, c: (0, 0)),
        pl.BlockSpec((blocks, rows, cols), lambda e, c: (0, c[0], 0)),
        pl.BlockSpec((full, 128), lambda e, c: (0, 0)),
        pl.BlockSpec((rows, 128), lambda e, c: (c[0], 0)),
        pl.BlockSpec((1, full, hidden), lambda e, c: (e, 0, 0)),
        pl.BlockSpec((1, full, hidden), lambda e, c: (e, 0, 0)),
        pl.BlockSpec((1, hidden, full), lambda e, c: (e, 0, 0)),
    ]
    operands = [chunk, n2, cot, router, keep, wg, wu, wd]
    if own:
        in_specs.append(pl.BlockSpec((rows, full), lambda e, c: (0, 0)))
        operands.append(residual)
    aliases = {len(operands) + k: k for k in range(len(carried))}
    in_specs += [pl.BlockSpec(memory_space=pl.ANY)] * len(carried)
    operands += list(carried)
    slab = pl.BlockSpec((rows, hidden), lambda e, c: (c[0], e))
    return pl.pallas_call(
        functools.partial(expert_kernel, own, len(carried)),
        grid_spec=pltpu.PrefetchScalarGridSpec(
            num_scalar_prefetch=1,
            grid=(EXPERTS,),
            in_specs=in_specs,
            out_specs=[
                pl.BlockSpec((hidden, rows), lambda e, c: (e, c[0])),
                slab,
                slab,
                pl.BlockSpec((full, rows), lambda e, c: (0, c[0])),
                pl.BlockSpec((blocks, rows, cols), lambda e, c: (0, c[0], 0)),
                pl.BlockSpec((rows, full), lambda e, c: (0, 0)),
                pl.BlockSpec((rows, 128), lambda e, c: (0, 0)),
                pl.BlockSpec((rows, 128), lambda e, c: (0, 0)),
            ],
            scratch_shapes=[
                pltpu.VMEM((rows, full), F32),
                pltpu.VMEM((rows, full), F32),
                pltpu.VMEM((rows, 128), F32),
            ],
        ),
        out_shape=[
            jax.ShapeDtypeStruct((EXPERTS * hidden, length), BF),
            jax.ShapeDtypeStruct((length, EXPERTS * hidden), BF),
            jax.ShapeDtypeStruct((length, EXPERTS * hidden), BF),
            jax.ShapeDtypeStruct((full, length), BF),
            jax.ShapeDtypeStruct((blocks, length, cols), BF),
            jax.ShapeDtypeStruct((rows, full), BF),
            jax.ShapeDtypeStruct((rows, 128), F32),
            jax.ShapeDtypeStruct((rows, 128), F32),
        ],
        input_output_aliases=aliases,
        compiler_params=params(),
        cost_estimate=cost(
            12 * rows * full * EXPERTS * hidden, 6 * full * EXPERTS * hidden + 10 * rows * full
        ),
    )(*operands)


def gate_up_kernel(n2t_ref, dg_ref, du_ref, gate_ref, up_ref):
    turned = n2t_ref[...]
    gate_ref[0] = dot(turned, dg_ref[...]).astype(BF)
    up_ref[0] = dot(turned, du_ref[...]).astype(BF)


def gate_up_grads(n2t, dg, du):
    full, length = n2t.shape
    hidden = dg.shape[1] // EXPERTS
    slab = pl.BlockSpec((length, hidden), lambda e: (0, e))
    out = pl.BlockSpec((1, full, hidden), lambda e: (e, 0, 0))
    return pl.pallas_call(
        gate_up_kernel,
        grid=(EXPERTS,),
        in_specs=[pl.BlockSpec((full, length), lambda e: (0, 0)), slab, slab],
        out_specs=[out, out],
        out_shape=[jax.ShapeDtypeStruct((EXPERTS, full, hidden), BF)] * 2,
        compiler_params=params(),
        cost_estimate=cost(4 * length * full * EXPERTS * hidden, 10 * full * EXPERTS * hidden),
    )(n2t, dg, du)


def down_kernel(h2t_ref, cot_ref, out_ref):
    product = dot(h2t_ref[...], cot_ref[0]).astype(BF)
    hidden = out_ref.shape[1]
    for e in range(EXPERTS):
        out_ref[e] = product[e * hidden : (e + 1) * hidden]


def down_grads(h2t, cot):
    wide, length = h2t.shape
    blocks, _, cols = cot.shape
    hidden = wide // EXPERTS
    return pl.pallas_call(
        down_kernel,
        grid=(blocks,),
        in_specs=[
            pl.BlockSpec((wide, length), lambda t: (0, 0)),
            pl.BlockSpec((1, length, cols), lambda t: (t, 0, 0)),
        ],
        out_specs=pl.BlockSpec((EXPERTS, hidden, cols), lambda t: (0, 0, t)),
        out_shape=jax.ShapeDtypeStruct((EXPERTS, hidden, blocks * cols), BF),
        compiler_params=params(),
        cost_estimate=cost(2 * length * wide * blocks * cols, 4 * wide * blocks * cols),
    )(h2t, cot)


def middle_kernel(mine_ref, att_ref, wo_ref, x_ref, gain_ref, res_ref, n2_ref):
    step = pl.program_id(0)
    blocks, rows, cols = x_ref.shape

    @pl.when(step == 0)
    def _():
        for t in range(blocks):
            res_ref[:, t * cols : (t + 1) * cols] = x_ref[t].astype(F32)

    res_ref[...] += dot(att_ref[0], wo_ref[...])

    @pl.when(step == blocks - 1)
    def _():
        residual = res_ref[...]
        scale = lax.rsqrt(jnp.mean(residual * residual, axis=1, keepdims=True) + EPSILON)
        for t in range(blocks):
            here = slice(t * cols, (t + 1) * cols)
            gain = gain_ref[t, 1:2, :].astype(F32)
            n2_ref[:, here] = (residual[:, here] * scale * gain).astype(BF)


def middle(mine, att, w_out, x_aug):
    blocks, rows, width = att.shape
    full = w_out.shape[1]
    cols = full // blocks
    last = x_aug.shape[1] // 16 - 1
    return pl.pallas_call(
        middle_kernel,
        grid_spec=pltpu.PrefetchScalarGridSpec(
            num_scalar_prefetch=1,
            grid=(blocks,),
            in_specs=[
                pl.BlockSpec((1, rows, width), lambda t, m: (t, 0, 0)),
                pl.BlockSpec((width, full), lambda t, m: (t, 0)),
                pl.BlockSpec((blocks, rows, cols), lambda t, m: (0, m[0], 0)),
                pl.BlockSpec((blocks, 16, cols), lambda t, m: (0, last, 0)),
            ],
            out_specs=[pl.BlockSpec((rows, full), lambda t, m: (0, 0))] * 2,
        ),
        out_shape=[
            jax.ShapeDtypeStruct((rows, full), F32),
            jax.ShapeDtypeStruct((rows, full), BF),
        ],
        compiler_params=params(),
        cost_estimate=cost(2 * rows * full * full, 2 * full * full),
    )(mine, att, w_out, x_aug, x_aug)


def middle_back_kernel(
    size, mine_ref, own_ref, received_ref, probs_ref, router_ref, res_ref, n2_ref, cot_ref, gain_ref, wo_ref, *rest
):
    grads_refs, (branch_ref, out_ref, parts_ref) = rest[:size], rest[size:]
    step = pl.program_id(0)
    blocks, rows, cols = cot_ref.shape
    full = blocks * cols

    @pl.when(step == 0)
    def _():
        probs = probs_ref[...]
        prob_grad = grads_refs[0][...]
        for ref in grads_refs[1:]:
            prob_grad = prob_grad + ref[...]
        centred = jnp.sum(prob_grad * probs, axis=1, keepdims=True)
        logit_grad = (probs * (prob_grad - centred)).astype(BF)
        grad = (
            own_ref[...].astype(F32)
            + received_ref[...].astype(F32)
            + dot_t(logit_grad, router_ref[...])
        )
        residual = res_ref[...]
        scale = lax.rsqrt(jnp.mean(residual * residual, axis=1, keepdims=True) + EPSILON)
        stat = jnp.zeros((rows, 1), F32)
        for t in range(blocks):
            here = slice(t * cols, (t + 1) * cols)
            gain = gain_ref[t, 1:2, :].astype(F32)
            stat = stat + jnp.sum(residual[:, here] * gain * grad[:, here], axis=1, keepdims=True)
        stat = scale * scale * scale * stat / full
        for t in range(blocks):
            here = slice(t * cols, (t + 1) * cols)
            gain = gain_ref[t, 1:2, :].astype(F32)
            branch_ref[:, here] = (
                cot_ref[t].astype(F32) + scale * gain * grad[:, here] - residual[:, here] * stat
            ).astype(BF)
        router_part = lax.dot_general(
            logit_grad, n2_ref[...], (((0,), (0,)), ((), ())), preferred_element_type=F32
        )[:8]
        norm_part = jnp.sum(grad * residual * scale, axis=0, keepdims=True)
        which = lax.broadcasted_iota(jnp.int32, (8, full), 0)
        parts_ref[...] = jnp.where(which == EXPERTS, norm_part, router_part)

    out_ref[0] = dot_t(branch_ref[...], wo_ref[...]).astype(BF)


def middle_back(mine, own, received, probs, router, residual, n2, cot, x_aug, w_out, gate_grads):
    blocks, _, cols = cot.shape
    rows, full = residual.shape
    width = full // blocks
    last = x_aug.shape[1] // 16 - 1
    whole = pl.BlockSpec((rows, full), lambda t, m: (0, 0))
    lanes = pl.BlockSpec((rows, 128), lambda t, m: (0, 0))
    return pl.pallas_call(
        functools.partial(middle_back_kernel, len(gate_grads)),
        grid_spec=pltpu.PrefetchScalarGridSpec(
            num_scalar_prefetch=1,
            grid=(blocks,),
            in_specs=[
                whole,
                whole,
                lanes,
                pl.BlockSpec((full, 128), lambda t, m: (0, 0)),
                whole,
                whole,
                pl.BlockSpec((blocks, rows, cols), lambda t, m: (0, m[0], 0)),
                pl.BlockSpec((blocks, 16, cols), lambda t, m: (0, last, 0)),
                pl.BlockSpec((width, full), lambda t, m: (t, 0)),
            ]
            + [lanes] * len(gate_grads),
            out_specs=[
                whole,
                pl.BlockSpec((1, rows, width), lambda t, m: (t, 0, 0)),
                pl.BlockSpec((8, full), lambda t, m: (0, 0)),
            ],
        ),
        out_shape=[
            jax.ShapeDtypeStruct((rows, full), BF),
            jax.ShapeDtypeStruct((blocks, rows, width), BF),
            jax.ShapeDtypeStruct((8, full), F32),
        ],
        compiler_params=params(),
        cost_estimate=cost(2 * rows * full * full, 2 * full * full),
    )(mine, own, received, probs, router, residual, n2, cot, x_aug, w_out, *gate_grads)


def reversed_bits(at, bits):
    return sum(((at >> b) & 1) << (bits - 1 - b) for b in range(bits)) if bits else at


def column_grad_kernel(table_ref, left_ref, right_ref, a_ref, b_ref):
    product = dot(jnp.transpose(left_ref[...]), right_ref[...]).astype(BF)
    half = a_ref.shape[2]
    a_ref[0] = product[:, :half]
    b_ref[0] = product[:, half:]


def column_grads(table, left, right, n):
    length, full = left.shape
    width = right.shape[1]
    half = width // 2
    piece = full // n
    bits = n.bit_length() - 2
    steps = n // 2
    return pl.pallas_call(
        column_grad_kernel,
        grid_spec=pltpu.PrefetchScalarGridSpec(
            num_scalar_prefetch=1,
            grid=(steps,),
            in_specs=[
                pl.BlockSpec((length, piece), lambda g, t: (0, t[g])),
                pl.BlockSpec((length, width), lambda g, t: (0, 0)),
            ],
            out_specs=[
                pl.BlockSpec((1, piece, half), lambda g, t: (g, 0, 0)),
                pl.BlockSpec((1, piece, half), lambda g, t: (reversed_bits(g, bits), 0, 0)),
            ],
        ),
        out_shape=[jax.ShapeDtypeStruct((steps, piece, half), BF)] * 2,
        compiler_params=params(),
        cost_estimate=cost(
            2 * length * piece * steps * width, 2 * length * (piece * steps + width)
        ),
    )(table, left, right)


def row_grad_kernel(table_ref, left_ref, right_ref, a_ref, b_ref, turned_left):
    @pl.when(pl.program_id(0) == 0)
    def _():
        turned_left[...] = jnp.transpose(left_ref[...])

    right = right_ref[0] if len(right_ref.shape) == 3 else right_ref[...]
    product = dot(turned_left[...], right).astype(BF)
    half = a_ref.shape[1]
    a_ref[0] = product[:half]
    b_ref[0] = product[half:]


def row_grads(table, left, right, n):
    length, width = left.shape
    full = right.shape[-1] * (right.shape[0] if right.ndim == 3 else 1)
    piece = full // n
    bits = n.bit_length() - 2
    steps = n // 2
    if right.ndim == 3:
        per = right.shape[2] // piece
        right_spec = pl.BlockSpec(
            (1, length, piece), lambda g, t: (t[g] // per, 0, lax.rem(t[g], per))
        )
    else:
        right_spec = pl.BlockSpec((length, piece), lambda g, t: (0, t[g]))
    half = width // 2
    return pl.pallas_call(
        row_grad_kernel,
        grid_spec=pltpu.PrefetchScalarGridSpec(
            num_scalar_prefetch=1,
            grid=(steps,),
            in_specs=[pl.BlockSpec((length, width), lambda g, t: (0, 0)), right_spec],
            out_specs=[
                pl.BlockSpec((1, half, piece), lambda g, t: (g, 0, 0)),
                pl.BlockSpec((1, half, piece), lambda g, t: (reversed_bits(g, bits), 0, 0)),
            ],
            scratch_shapes=[pltpu.VMEM((width, length), BF)],
        ),
        out_shape=[jax.ShapeDtypeStruct((steps, half, piece), BF)] * 2,
        compiler_params=params(),
        cost_estimate=cost(
            2 * length * piece * steps * width, 2 * length * (piece * steps + width)
        ),
    )(table, left, right)


def piece_specs(shape, steps, row):
    block = (1,) + shape
    return [
        pl.BlockSpec(block, lambda a, pos: (jnp.minimum(pos[row, a], steps - 1), 0, 0)),
        pl.BlockSpec(block, lambda a, pos: (jnp.maximum(pos[row, a] - steps, 0), 0, 0)),
    ]


def pick(pos_ref, row, steps, low_ref, high_ref):
    low = pos_ref[row, pl.program_id(0)] < steps
    return jnp.where(low, low_ref[0].astype(F32), high_ref[0].astype(F32))


def projections_kernel(steps, pos_ref, la_ref, ha_ref, lb_ref, hb_ref, q_ref, k_ref, v_ref):
    first = pick(pos_ref, 0, steps, la_ref, ha_ref)
    second = pick(pos_ref, 1, steps, lb_ref, hb_ref)
    width = q_ref.shape[1]
    half = width // 2
    q_ref[...] = first[:, :width]
    k_ref[:, :half] = first[:, width:]
    k_ref[:, half:] = second[:, :half]
    v_ref[...] = second[:, half:]


def widen_projections(pos, a, b, n):
    steps, piece, width = a[0].shape
    out = 2 * width // 3
    return pl.pallas_call(
        functools.partial(projections_kernel, steps),
        grid_spec=pltpu.PrefetchScalarGridSpec(
            num_scalar_prefetch=1,
            grid=(n,),
            in_specs=piece_specs((piece, width), steps, 0) + piece_specs((piece, width), steps, 1),
            out_specs=[pl.BlockSpec((piece, out), lambda g, pos: (g, 0))] * 3,
        ),
        out_shape=[jax.ShapeDtypeStruct((piece * n, out), F32)] * 3,
        compiler_params=params(),
        cost_estimate=cost(0, 18 * n * piece * out),
    )(pos, *a, *b)


def rows_kernel(steps, pos_ref, la_ref, ha_ref, lb_ref, hb_ref, out_ref):
    half = la_ref.shape[1]
    out_ref[:half, :] = pick(pos_ref, 0, steps, la_ref, ha_ref)
    out_ref[half:, :] = pick(pos_ref, 1, steps, lb_ref, hb_ref)


def widen_rows(pos, a, b, n):
    steps, half, piece = a[0].shape
    return pl.pallas_call(
        functools.partial(rows_kernel, steps),
        grid_spec=pltpu.PrefetchScalarGridSpec(
            num_scalar_prefetch=1,
            grid=(n,),
            in_specs=piece_specs((half, piece), steps, 0) + piece_specs((half, piece), steps, 1),
            out_specs=pl.BlockSpec((2 * half, piece), lambda g, pos: (0, g)),
        ),
        out_shape=jax.ShapeDtypeStruct((2 * half, piece * n), F32),
        compiler_params=params(),
        cost_estimate=cost(0, 12 * n * piece * half),
    )(pos, *a, *b)


def kept_experts(routes, order):
    length = routes.shape[0]
    token, which = order // TOP, order % TOP
    onehot = (token[:, None] == jnp.arange(length, dtype=jnp.int32)[None, :]).astype(BF)
    named = (routes[:, :, None] == jnp.arange(8, dtype=jnp.int32)).astype(BF).reshape(length, TOP * 8)
    ordered = dot(onehot, named).reshape(-1, TOP, 8)
    choose = jnp.sum(
        jnp.where(which[:, None, None] == jnp.arange(TOP)[None, :, None], ordered, 0.0), axis=1
    )
    kept = jnp.where(jnp.cumsum(choose, axis=0) <= CAP, choose, 0.0).astype(BF)
    kept = jnp.pad(kept, ((0, 0), (0, 120)))
    return lax.dot_general(onehot, kept, (((0,), (0,)), ((), ())), preferred_element_type=F32)


def stacked(blocks, mine):
    size = len(blocks)
    out = jnp.zeros((size,) + blocks[0].shape, blocks[0].dtype)
    for step, block in enumerate(blocks):
        out = lax.dynamic_update_slice_in_dim(out, block[None], (mine - step) % size, 0)
    return out


def on_device(
    tokens, cotangent, norm1_gain, w_query, w_key, w_value, query_gain, key_gain, w_output,
    norm2_gain, router, w_gate, w_up, w_down, routes, prefix, slot_order,
):
    size, n = lax.axis_size("tensor"), lax.axis_size("dp")
    mine, group = lax.axis_index("tensor"), lax.axis_index("dp")
    length, cols = tokens.shape
    full = cols * size
    rows = length // size

    order_a, order_b = swap_orders(n)
    rel_a, rel_b = rel_table(order_a), rel_table(order_b)
    table = jnp.asarray(rel_a, jnp.int32) ^ group
    positions = jnp.stack(
        [
            jnp.asarray([rel.index(v) for v in range(n)], jnp.int32)[
                jnp.arange(n, dtype=jnp.int32) ^ group
            ]
            for rel in (rel_a, rel_b)
        ]
    )
    half = n // 2

    part = w_output.shape[0] // n
    w_piece = lax.dynamic_slice_in_dim(w_output, group * part, part, 0)
    w_out = lax.all_gather(w_piece, ("tensor", "dp"), axis=0, tiled=True)
    extra = jnp.zeros((14, cols), BF)
    block = jnp.concatenate([tokens, norm1_gain[None], norm2_gain[None], extra], axis=0)
    x_blocks = gather_ring(block, size)
    x_blocks[-1], late_cot = lax.optimization_barrier((x_blocks[-1], cotangent))
    x_aug = stacked(x_blocks, mine)
    cot = lax.all_gather(late_cot, "tensor", axis=0)
    normed_one, q_pre, k_pre, v_rows, own_sums = qkv_call(x_aug, w_query, w_key, w_value, length)
    keep = kept_experts(routes, slot_order[0])
    router_wide = jnp.pad(router, ((0, 0), (0, 128 - EXPERTS)))
    here = mine.astype(jnp.int32)[None]

    def everyone(field):
        return [field] + [
            lax.ppermute(field, "tensor", [(at, (at + step) % size) for at in range(size)])
            for step in range(1, size)
        ]

    sums = everyone(own_sums)

    halfway = HEAD_DIM // 2
    freqs = ROPE_BASE ** (-(jnp.arange(halfway, dtype=F32) * 2.0 / HEAD_DIM))
    angles = jnp.arange(length, dtype=F32)[:, None] * freqs[None, :]
    cosine = jnp.concatenate([jnp.cos(angles)] * 2, axis=1)
    sine = jnp.concatenate([-jnp.sin(angles), jnp.sin(angles)], axis=1)
    gq, gk = query_gain[None], key_gain[None]
    attended, lse, q_rot, k_rot = attn_forward(
        prefix, q_pre, k_pre, v_rows, gq, gk, cosine, sine, sums
    )

    att_rows = exchange(attended.reshape(size, rows, -1), mine, size)
    residual, normed_two = middle(here, att_rows, w_out, x_aug)

    chunks = gather_ring(normed_two, size)
    carried = ()
    received = None
    gate_grads = []
    for step, chunk in enumerate(chunks):
        at = ((mine - step) % size).astype(jnp.int32)
        outs = expert_call(
            at[None], chunk, cot, router_wide, keep, w_gate, w_up, w_down,
            residual if step == 0 else None, carried,
        )
        carried, (dn2, gg, probs) = outs[:5], outs[5:]
        if step == 0:
            own_dn2, gate_grads, expert_probs = dn2, [gg], probs
            continue
        term = dn2 if received is None else dn2 + received
        received = lax.ppermute(term, "tensor", ring(size))
        gate_grads.append(
            lax.ppermute(gg, "tensor", [(i, (i - step) % size) for i in range(size)])
        )
    h2t, dg, du, n2t, mix = carried

    grad_gate, grad_up = gate_up_grads(n2t, dg, du)
    grad_down = down_grads(h2t, cot)
    grad_gate, grad_up, grad_down = lax.psum((grad_gate, grad_up, grad_down), "dp")

    branch_rows, out_rows, small = middle_back(
        here, own_dn2, received, expert_probs, router_wide, residual, normed_two, cot, x_aug,
        w_out, gate_grads,
    )
    small = sum_direct(small, size)

    out_grad = exchange(out_rows, mine, size).reshape(length, -1)
    branch = stacked(gather_ring(branch_rows, size), mine).reshape(length, full)
    dq, dk, dv, gain_grads, own_back = attn_backward(
        prefix, q_pre, k_pre, q_rot, k_rot, v_rows, out_grad, lse, gq, gk, cosine, sine, sums
    )
    back = everyone(own_back)
    send_out = row_grads(table[half:], attended, branch, n)
    keep_out = row_grads(table[:half], attended, branch, n)
    sum_out_a = dp_sum(send_out[0], keep_out[0], order_a, n)
    sum_out_b = dp_sum(send_out[1], keep_out[1], order_b, n)
    grad_qkv, own_stat = norm_back(q_pre, k_pre, v_rows, dq, dk, dv, gq, gk, sums, back)
    stat_one = sum_direct(own_stat, size)[0]

    w_all = jnp.concatenate([w_query, w_key, w_value], axis=1)

    def input_part(at):
        return dot_t(grad_qkv, lax.dynamic_slice_in_dim(w_all, at * cols, cols, 0))

    send_in = column_grads(table[half:], normed_one, grad_qkv, n)
    keep_in = column_grads(table[:half], normed_one, grad_qkv, n)
    sum_in_a = dp_sum(send_in[0], keep_in[0], order_a, n)
    sum_in_b = dp_sum(send_in[1], keep_in[1], order_b, n)
    normed_one_grad = scatter_ring(input_part, mine, size)

    own_tokens = tokens.astype(F32)
    gain_one = norm1_gain.astype(F32)[None]
    scale_one = lax.rsqrt(own_sums[2] / full + EPSILON)
    stat_row = (stat_one / full) * scale_one * scale_one
    own_branch = lax.dynamic_slice_in_dim(branch, mine * cols, cols, 1).astype(F32)
    grad_tokens = (
        own_branch
        + scale_one[:, None] * gain_one * normed_one_grad
        - own_tokens * stat_row[:, None]
    )
    norm1_part = jnp.sum(normed_one_grad * own_tokens * scale_one[:, None], axis=0)

    mixed = scatter_ring(
        lambda at: lax.dynamic_index_in_dim(mix, at, 0, keepdims=False), mine, size
    ).astype(BF)

    own_norm2 = lax.dynamic_slice_in_dim(small[EXPERTS], mine * cols, cols, 0)
    packed = jnp.concatenate(
        [small[:EXPERTS].reshape(-1), own_norm2, gain_grads[0], gain_grads[1]]
    )
    packed = dp_sum_small(packed.reshape(-1, 128), n).reshape(-1)
    grad_norm1_gain = dp_sum_small(norm1_part, n)
    marks = [EXPERTS * full, EXPERTS * full + cols, EXPERTS * full + 2 * cols]
    grad_router = packed[: marks[0]].reshape(EXPERTS, full).T
    grad_norm2_gain = packed[marks[0] : marks[1]]
    grad_query_gain = packed[marks[1] : marks[2]]
    grad_key_gain = packed[marks[2] :]

    grad_output = widen_rows(positions, sum_out_a, sum_out_b, n)
    grad_query, grad_key, grad_value = widen_projections(positions, sum_in_a, sum_in_b, n)
    return (
        mixed, grad_tokens, grad_norm1_gain, grad_query, grad_key, grad_value, grad_query_gain,
        grad_key_gain, grad_output, grad_norm2_gain, grad_router, grad_gate.astype(F32), grad_up.astype(F32),
        grad_down.astype(F32),
    )


def solution(mesh):
    rows, weight_cols, weight_rows = P("dp", "tensor"), P(None, "tensor"), P("tensor", None)
    vector, expert_cols, expert_rows = P("tensor"), P(None, None, "tensor"), P(None, "tensor", None)
    return jax.shard_map(
        on_device,
        mesh=mesh,
        in_specs=(
            rows, rows, vector, weight_cols, weight_cols, weight_cols, vector, vector, weight_rows,
            vector, P(), expert_cols, expert_cols, expert_rows, P("dp", None), P("dp"),
            P("dp", None),
        ),
        out_specs=(
            rows, rows, vector, weight_cols, weight_cols, weight_cols, vector, vector, weight_rows,
            vector, P(), expert_cols, expert_cols, expert_rows,
        ),
        check_vma=False,
    )
```

time: 1700 us -> 847 us (0.50)
  local copies, waits for them, and re-layouts: 388 us -> 45.2 us
  waiting for transfers between devices: 716 us -> 395 us
  matrix products: 264 us -> 26.2 us
  Pallas kernels: 0 us -> 223 us
  other arithmetic: 177 us -> 46.5 us
  blocking collectives: 119 us -> 0 us
  starting transfers between devices: 0.37 us -> 85.4 us
    ppermute x0 -> x69, waiting for transfers between devices: none -> 395 us  [the longest x9 174 us: gather_ring(): held.append(lax.ppermute(held[-1], 'tensor', ring(size)))]
    psum x1, waiting for transfers between devices: 329 us -> 0.01 us  [on_device(): lax.psum((grad_gate, grad_up, grad_down), 'dp')]
    dot_general x38 -> x6, matrix products: 264 us -> 26.2 us  [the longest x4 20.6 us: dot_t(): lax.dot_general(a, b, (((1,), (1,)), ((), ())), preferred_element_type=F32)]
    pallas_call x0 -> x18, Pallas kernels: none -> 223 us  [the longest x4 71.7 us: expert_call(): pl.pallas_call(functools.partial(expert_kernel, own, len(carried)), grid_...]
    all_gather x4 -> x2, waiting for transfers between devices: 205 us -> 0.02 us  [the longest x1 0.02 us: on_device(): w_out = lax.all_gather(w_piece, ('tensor', 'dp'), axis=0, tiled=True)]
    reduce_scatter x4 -> x0, waiting for transfers between devices: 180 us -> none  [the longest x1 73.6 us: on_device(): lax.psum_scatter(attn_terms.astype(jnp.bfloat16), 'tensor', scatter_dimen...]
    gather x6 -> x2, local copies, waits for them, and re-layouts: 171 us -> 1.29 us  [on_device(): jnp.asarray([rel.index(v) for v in range(n)], jnp.int32)]
    psum x6 -> x0, blocking collectives: 92.8 us -> none  [the longest x2 36.5 us: on_device(): lax.psum((gate_terms, jnp.sum(weighted_rows * token_input, axis=1)), 'ten...]
  transfers between devices with their start and end apart: 9 -> 72, of which waited for: 9 -> 34; matrix products, arithmetic and copies ran while one was open for 11% -> 10% of each run, Pallas kernels for 0% -> 27%
where the time goes in v1:
time: 847 us; the launch traced here: 837 us
  waiting for transfers between devices  395 us (47%)
  Pallas kernels  223 us (26%)
  starting transfers between devices  85.4 us (10%)
  other arithmetic  46.5 us (5%)
  local copies, waits for them, and re-layouts  45.2 us (5%)
  matrix products  26.2 us (3%)
  between operations  15.7 us (2%)
    ppermute x9, waiting for transfers between devices, gather_ring(): held.append(lax.ppermute(held[-1], 'tensor', ring(size)))  174 us
    ppermute x6, waiting for transfers between devices, exchange(): lax.ppermute(send, 'tensor', [(at, (at + step) % size) for at in range(si...  80 us
    ppermute x30, waiting for transfers between devices, swap(): return lax.ppermute(field, 'dp', [(at, at ^ mask) for at in range(n)])  74.6 us
    pallas_call x4, Pallas kernels, expert_call(): pl.pallas_call(functools.partial(expert_kernel, own, len(carried)), grid_...  71.7 us
    ppermute x6, waiting for transfers between devices, scatter_ring(): received = lax.ppermute(term.astype(BF), 'tensor', ring(size))  30.6 us
    ppermute x30, starting transfers between devices, swap(): return lax.ppermute(field, 'dp', [(at, at ^ mask) for at in range(n)])  26.5 us
    ppermute x9, starting transfers between devices, gather_ring(): held.append(lax.ppermute(held[-1], 'tensor', ring(size)))  21.1 us
    dot_general x4, matrix products, dot_t(): lax.dot_general(a, b, (((1,), (1,)), ((), ())), preferred_element_type=F32)  20.6 us
  transfers between devices with their start and end apart: 72, of which 34 were waited for; matrix products, arithmetic and copies ran while one was open for 10% of the time, Pallas kernels for 27%

profile of v1, /device:TPU:0, one launch (start us, length us, event | category | flops | bytes accessed | tf_op | source)
XLA Modules:
  0.0 836.7 jit_solution(3221757440069903106)
XLA Ops:
  10.9 3.9 concatenate.43
  14.9 3.1 collective-permute-start
  18.0 31.1 %collective-permute-done = bf16[1040,512]{1,0:T(8,128)(2,1)S(1)} collective-permute-done((bf16[1040,512]{1,0:T(8,128)(2,1)S(1)}, bf16[1040,512]{1,0:T(8,128)(2,1)S(1)}, u32[]{:S(2)}, u32[]{:S(2)}) %collective-permute-start) | collective-permute-done | bytes 1064992 | tf_op jit(solution)/shard_map/ppermute | solution.py:55
  50.8 36.3 %collective-permute-done.1 = bf16[1040,512]{1,0:T(8,128)(2,1)} collective-permute-done((bf16[1040,512]{1,0:T(8,128)(2,1)S(1)}, bf16[1040,512]{1,0:T(8,128)(2,1)}, u32[]{:S(2)}, u32[]{:S(2)}) %collective-permute-start.1) | collective-permute-done | bytes 1064992 | tf_op jit(solution)/shard_map/ppermute | solution.py:55
  87.1 2.4 fusion.34
  94.2 39.1 %collective-permute-done.2 = bf16[1040,512]{1,0:T(8,128)(2,1)} collective-permute-done((bf16[1040,512]{1,0:T(8,128)(2,1)}, bf16[1040,512]{1,0:T(8,128)(2,1)}, u32[]{:S(2)}, u32[]{:S(2)}) %collective-permute-start.2) | collective-permute-done | bytes 1064992 | tf_op jit(solution)/shard_map/ppermute | solution.py:55
  135.8 2.7 copy-done.23
  138.4 3.2 fusion.4.keep_ref
  147.7 16.7 %shard_map.299 = (bf16[1024,2048]{1,0:T(8,128)(2,1)}, f32[1024,512]{1,0:T(8,128)}, f32[1024,512]{1,0:T(8,128)}, bf16[1024,512]{1,0:T(8,128)(2,1)}, f32[8,1024]{1,0:T(8,128)}) custom-call(bf16[4,1040,512]{2,1,0:T(8,128)(2,1)} %copy-done.4, bf16[4,1040,512]{2,1,0:T(8,128)(2,1)} %copy-done.4, bf16[2048,512]{1,0:T(8,128)(2,1)} %wq_ref.1, ...), custom_call_target="tpu_custom_call" | custom-call | flops 6442450944 | bytes 27262976 | tf_op jit(solution)/shard_map/pallas_call | solution.py:156
  165.0 3.5 collective-permute-start.5
  174.1 14.0 %shard_map.300 = (bf16[1024,512]{1,0:T(8,128)(2,1)}, f32[1024,512]{1,0:T(8,128)}, bf16[1024,512]{1,0:T(8,128)(2,1)}, bf16[1024,512]{1,0:T(8,128)(2,1)}) custom-call(s32[1]{0:T(128)S(6)} %copy.93.prefix_ref, f32[1024,512]{1,0:T(8,128)} %get-tuple-element.80.q_ref, f32[1024,512]{1,0:T(8,128)} %get-tuple-element.81.k_ref, ...), custom_call_target="tpu_custom_call" | custom-call | flops 2147483648 | bytes 10485760 | tf_op jit(solution)/shard_map/pallas_call | solution.py:229
  193.4 2.3 collective-permute-start.8
  198.3 8.0 collective-permute-done.6
  206.3 17.6 %collective-permute-done.7 = bf16[1,256,512]{2,1,0:T(8,128)(2,1)S(1)} collective-permute-done((bf16[1,256,512]{2,1,0:T(8,128)(2,1)S(1)}, bf16[1,256,512]{2,1,0:T(8,128)(2,1)S(1)}, u32[]{:S(2)}, u32[]{:S(2)}) %collective-permute-start.7) | collective-permute-done | bytes 262176 | tf_op jit(solution)/shard_map/ppermute | solution.py:83
  226.9 8.1 shard_map.301
  235.0 12.5 %collective-permute-start.9 = (bf16[256,2048]{1,0:T(8,128)(2,1)}, bf16[256,2048]{1,0:T(8,128)(2,1)S(1)}, u32[]{:S(2)}, u32[]{:S(2)}) collective-permute-start(bf16[256,2048]{1,0:T(8,128)(2,1)} %get-tuple-element.85.n2_ref), channel_id=1, source_target_pairs={{0,1},{1,2},{2,3},{3,0},{4,5},{5,6},{6,7},{7,4},{8,9},{9,10},{10,1... | collective-permute-start | bytes 3145736 | tf_op jit(solution)/shard_map/ppermute | solution.py:55
  247.4 18.5 %shard_map.302 = (bf16[1536,1024]{1,0:T(8,128)(2,1)}, bf16[1024,1536]{1,0:T(8,128)(2,1)}, bf16[1024,1536]{1,0:T(8,128)(2,1)}, bf16[2048,1024]{1,0:T(8,128)(2,1)}...) custom-call(s32[1]{0:T(128)} %bitcast.18.chunk_ref, ...), custom_call_target="tpu_custom_call" | custom-call | flops 9663676416 | bytes 24117248 | tf_op jit(solution)/shard_map/pallas_call | solution.py:465
  265.9 4.8 collective-permute-done.9.n2_ref
  272.6 17.8 %shard_map.303 = (bf16[1536,1024]{1,0:T(8,128)(2,1)}, bf16[1024,1536]{1,0:T(8,128)(2,1)}, bf16[1024,1536]{1,0:T(8,128)(2,1)}, bf16[2048,1024]{1,0:T(8,128)(2,1)}...) custom-call(s32[1]{0:T(128)} %bitcast.17.chunk_ref, ...), custom_call_target="tpu_custom_call", output_to_operand_aliasing={{0}: (8, {}), {1}: (9, {}), {2}: (10, {}), {3}: (11, {}), {... | custom-call | flops 9663676416 | bytes 24117248 | tf_op jit(solution)/shard_map/pallas_call | solution.py:465
  292.0 6.6 collective-permute-done.10.n2_ref
  299.6 17.7 %shard_map.304 = (bf16[1536,1024]{1,0:T(8,128)(2,1)}, bf16[1024,1536]{1,0:T(8,128)(2,1)}, bf16[1024,1536]{1,0:T(8,128)(2,1)}, bf16[2048,1024]{1,0:T(8,128)(2,1)}...) custom-call(s32[1]{0:T(128)} %bitcast.16.chunk_ref, ...), custom_call_target="tpu_custom_call", output_to_operand_aliasing={{0}: (8, {}), {1}: (9, {}), {2}: (10, {}), {3}: (11, {}), {... | custom-call | flops 9663676416 | bytes 24117248 | tf_op jit(solution)/shard_map/pallas_call | solution.py:465
  317.3 3.8 collective-permute-done.15
  323.6 3.8 collective-permute-start.18
  327.4 16.3 %collective-permute-done.11.n2_ref = bf16[256,2048]{1,0:T(8,128)(2,1)S(1)} collective-permute-done((bf16[256,2048]{1,0:T(8,128)(2,1)S(1)}, bf16[256,2048]{1,0:T(8,128)(2,1)S(1)}, u32[]{:S(2)}, u32[]{:S(2)}) %collective-permute-start.11) | collective-permute-done | bytes 1048608 | tf_op jit(solution)/shard_map/ppermute | solution.py:55
  344.7 17.7 %shard_map.305 = (bf16[1536,1024]{1,0:T(8,128)(2,1)}, bf16[1024,1536]{1,0:T(8,128)(2,1)}, bf16[1024,1536]{1,0:T(8,128)(2,1)}, bf16[2048,1024]{1,0:T(8,128)(2,1)}...) custom-call(s32[1]{0:T(128)} %bitcast.chunk_ref, ...), custom_call_target="tpu_custom_call", output_to_operand_aliasing={{0}: (8, {}), {1}: (9, {}), {2}: (10, {}), {3}: (11, {}), {... | custom-call | flops 9663676416 | bytes 24117248 | tf_op jit(solution)/shard_map/pallas_call | solution.py:465
  369.4 3.1 collective-permute-start.20
  372.6 18.1 %shard_map.315 = (bf16[6,2048,256]{2,1,0:T(8,128)(2,1)}, bf16[6,2048,256]{2,1,0:T(8,128)(2,1)}) custom-call(bf16[2048,1024]{1,0:T(8,128)(2,1)} %get-tuple-element.138.n2t_ref, bf16[1024,1536]{1,0:T(8,128)(2,1)} %get-tuple-element.139.dg_ref, bf16[1024,1536]{1,0:T(8,128)(2,1)} %get-tuple-element.140.du_ref), custom_call_target="tpu_custom_call" | custom-call | flops 12884901888 | bytes 31457280 | tf_op jit(solution)/shard_map/pallas_call | solution.py:516
  390.7 10.7 %shard_map.316 = bf16[6,256,2048]{2,1,0:T(8,128)(2,1)} custom-call(bf16[1536,1024]{1,0:T(8,128)(2,1)} %get-tuple-element.143.h2t_ref, bf16[4,1024,512]{2,1,0:T(8,128)(2,1)} %bitcast.102), custom_call_target="tpu_custom_call" | custom-call | flops 6442450944 | bytes 12582912 | tf_op jit(solution)/shard_map/pallas_call | solution.py:538
  401.4 19.5 %collective-permute-done.19.rest_2_ = f32[256,128]{1,0:T(8,128)S(1)} collective-permute-done((f32[256,128]{1,0:T(8,128)}, f32[256,128]{1,0:T(8,128)S(1)}, u32[]{:S(2)}, u32[]{:S(2)}) %collective-permute-start.19) | collective-permute-done | bytes 131104 | tf_op jit(solution)/shard_map/ppermute | solution.py:931
  422.0 10.3 %shard_map.306 = (bf16[256,2048]{1,0:T(8,128)(2,1)}, bf16[4,256,512]{2,1,0:T(8,128)(2,1)}, f32[8,2048]{1,0:T(8,128)}) custom-call(s32[1]{0:T(128)} %bitcast.1.mine_ref, bf16[256,2048]{1,0:T(8,128)(2,1)} %get-tuple-element.104.own_ref, bf16[256,2048]{1,0:T(8,128)(2,1)} %copy-done.17, f32[256,128]{1,0:T(8,128)} %get-tuple-element.108.probs_ref, ...), custom_call_target="tpu_custom_call" | custom-call | flops 2147483648 | bytes 8388608 | tf_op jit(solution)/shard_map/pallas_call | solution.py:652
  434.4 3.0 fusion.14
  440.7 2.5 broadcast_in_dim.108
  446.4 2.5 collective-permute-start.25
  450.4 43.3 %collective-permute-done.24 = bf16[1,256,512]{2,1,0:T(8,128)(2,1)S(1)} collective-permute-done((bf16[1,256,512]{2,1,0:T(8,128)(2,1)}, bf16[1,256,512]{2,1,0:T(8,128)(2,1)S(1)}, u32[]{:S(2)}, u32[]{:S(2)}) %collective-permute-start.24) | collective-permute-done | bytes 262176 | tf_op jit(solution)/shard_map/ppermute | solution.py:83
  494.4 9.1 %collective-permute-done.25 = bf16[1,256,512]{2,1,0:T(8,128)(2,1)S(1)} collective-permute-done((bf16[1,256,512]{2,1,0:T(8,128)(2,1)}, bf16[1,256,512]{2,1,0:T(8,128)(2,1)S(1)}, u32[]{:S(2)}, u32[]{:S(2)}) %collective-permute-start.25) | collective-permute-done | bytes 262176 | tf_op jit(solution)/shard_map/ppermute | solution.py:83
  505.0 20.3 %shard_map.307 = (f32[1024,512]{1,0:T(8,128)}, f32[1024,512]{1,0:T(8,128)}, bf16[1024,512]{1,0:T(8,128)(2,1)}, f32[8,512]{1,0:T(8,128)}, f32[8,1024]{1,0:T(8,128)}) custom-call(s32[1]{0:T(128)S(6)} %copy.93.prefix_ref, f32[1024,512]{1,0:T(8,128)} %get-tuple-element.80.q_ref, f32[1024,512]{1,0:T(8,128)} %get-tuple-element.81.k_ref, ...), custom_call_target="tpu_custom_call" | custom-call | flops 5368709120 | bytes 18874368 | tf_op jit(solution)/shard_map/pallas_call | solution.py:318
  525.4 5.3 collective-permute-start.27
  537.8 8.0 shard_map.308
  548.0 5.1 fusion.27
  553.1 7.8 shard_map.310
  561.0 8.4 %shard_map.309 = (bf16[4,256,768]{2,1,0:T(8,128)(2,1)}, bf16[4,256,768]{2,1,0:T(8,128)(2,1)}) custom-call(s32[4]{0:T(128)} %get-tuple-element.174.table_ref, bf16[1024,2048]{1,0:T(8,128)(2,1)} %get-tuple-element.124.left_ref, bf16[1024,1536]{1,0:T(8,128)(2,1)} %get-tuple-element.122.right_ref), custom_call_target="tpu_custom_call" | custom-call | flops 3221225472 | bytes 5242880 | tf_op jit(solution)/shard_map/pallas_call | solution.py:703
  570.6 4.5 collective-permute-done.33
  578.4 2.8 fusion.15
  584.9 18.3 %collective-permute-done.30 = bf16[1024,512]{1,0:T(8,128)(2,1)S(1)} collective-permute-done((bf16[1024,512]{1,0:T(8,128)(2,1)}, bf16[1024,512]{1,0:T(8,128)(2,1)S(1)}, u32[]{:S(2)}, u32[]{:S(2)}) %collective-permute-start.30) | collective-permute-done | bytes 1048608 | tf_op jit(solution)/shard_map/ppermute | solution.py:65
  603.2 4.2 add_convert_fusion.1
  607.4 18.3 %collective-permute-done.22 = bf16[256,2048]{1,0:T(8,128)(2,1)S(1)} collective-permute-done((bf16[256,2048]{1,0:T(8,128)(2,1)S(1)}, bf16[256,2048]{1,0:T(8,128)(2,1)S(1)}, u32[]{:S(2)}, u32[]{:S(2)}) %collective-permute-start.22) | collective-permute-done | bytes 1048608 | tf_op jit(solution)/shard_map/ppermute | solution.py:55
  630.0 15.2 %collective-permute-done.41 = bf16[1,256,768]{2,1,0:T(8,128)(2,1)S(1)} collective-permute-done((bf16[1,256,768]{2,1,0:T(8,128)(2,1)S(1)}, bf16[1,256,768]{2,1,0:T(8,128)(2,1)S(1)}, u32[]{:S(2)}, u32[]{:S(2)}) %collective-permute-start.41) | collective-permute-done | bytes 393248 | tf_op jit(solution)/shard_map/ppermute | solution.py:89
  647.1 21.8 %collective-permute-done.23 = bf16[256,2048]{1,0:T(8,128)(2,1)S(1)} collective-permute-done((bf16[256,2048]{1,0:T(8,128)(2,1)S(1)}, bf16[256,2048]{1,0:T(8,128)(2,1)S(1)}, u32[]{:S(2)}, u32[]{:S(2)}) %collective-permute-start.23) | collective-permute-done | bytes 1048608 | tf_op jit(solution)/shard_map/ppermute | solution.py:55
  670.0 5.7 shard_map.313
  675.7 5.5 add_convert_fusion
  682.0 5.7 shard_map.312
  692.8 7.0 collective-permute-done.48
  701.4 19.9 %collective-permute-done.58 = bf16[2,256,256]{2,1,0:T(8,128)(2,1)S(1)} collective-permute-done((bf16[2,256,256]{2,1,0:T(8,128)(2,1)S(1)}, bf16[2,256,256]{2,1,0:T(8,128)(2,1)S(1)}, u32[]{:S(2)}, u32[]{:S(2)}) %collective-permute-start.58) | collective-permute-done | bytes 262176 | tf_op jit(solution)/shard_map/ppermute | solution.py:89
  723.5 19.3 %collective-permute-done.59 = bf16[1,256,256]{2,1,0:T(8,128)(2,1)S(1)} collective-permute-done((bf16[1,256,256]{2,1,0:T(8,128)(2,1)S(1)}, bf16[1,256,256]{2,1,0:T(8,128)(2,1)S(1)}, u32[]{:S(2)}, u32[]{:S(2)}) %collective-permute-start.59) | collective-permute-done | bytes 131104 | tf_op jit(solution)/shard_map/ppermute | solution.py:89
  744.4 3.4 collective-permute-done.65
  753.1 5.8 fusion.13
  761.3 6.8 collective-permute-done.61
  774.6 12.3 %collective-permute-done.14 = bf16[1024,512]{1,0:T(8,128)(2,1)} collective-permute-done((bf16[1024,512]{1,0:T(8,128)(2,1)}, bf16[1024,512]{1,0:T(8,128)(2,1)}, u32[]{:S(2)}, u32[]{:S(2)}) %collective-permute-start.14) | collective-permute-done | bytes 1048608 | tf_op jit(solution)/shard_map/ppermute | solution.py:65
  787.4 2.8 fusion.16
  791.0 7.2 shard_map.314
  798.2 10.1 %shard_map.311 = (f32[2048,512]{1,0:T(8,128)}, f32[2048,512]{1,0:T(8,128)}, f32[2048,512]{1,0:T(8,128)}) custom-call(s32[2,8]{1,0:T(2,128)} %pad_add_fusion.pos_ref, bf16[4,256,768]{2,1,0:T(8,128)(2,1)} %copy-done.6, bf16[4,256,768]{2,1,0:T(8,128)(2,1)} %collective-permute-done.44.ha_ref, bf16[4,256,768]{2,1,0:T(8,128)(2,1)} %pad_maximum_fusion.1.lb_ref, ...), custom_call_target="tpu_custom_call" | custom-call | bytes 18874368 | tf_op jit(solution)/shard_map/pallas_call | solution.py:798
  808.4 9.1 %convert_element_type.103 = f32[6,2048,256]{2,1,0:T(8,128)} convert(bf16[6,2048,256]{2,1,0:T(8,128)(2,1)} %get-tuple-element.144) | non-fusion elementwise | flops 3145728 | bytes 18874368 | tf_op jit(solution)/shard_map/convert_element_type | solution.py:1001
  817.5 5.9 convert_element_type.104
  823.4 6.3 convert_element_type.105
  (302 shorter events, 114.3 us)
Async XLA Ops:
  7.2 218.7 %all-gather.4.cloned.1.call-start = ((), (), s32[]{:S(2)}) async-start(), calls=%async_computation | async-start | bytes 8650752 | tf_op jit(solution)/shard_map/all_gather | solution.py:881
  9.5 237.9 %all-gather.6.cloned.1.call-start = ((), (), s32[]{:S(2)}) async-start(), calls=%async_computation.1 | async-start | bytes 5242880 | tf_op jit(solution)/shard_map/all_gather | solution.py:887
  14.9 34.2 %collective-permute-start = (bf16[1040,512]{1,0:T(8,128)(2,1)S(1)}, bf16[1040,512]{1,0:T(8,128)(2,1)S(1)}, u32[]{:S(2)}, u32[]{:S(2)}) collective-permute-start(bf16[1040,512]{1,0:T(8,128)(2,1)S(1)} %concatenate.43), channel_id=1, source_target_pairs={{0,1},{1,2},{2,3},{3,0},{4,5},{5,6},{6,7},{7,4},{8,9},{9,10},{10,1... | collective-permute-start | bytes 3194888 | tf_op jit(solution)/shard_map/ppermute | solution.py:55
  49.1 37.9 %collective-permute-start.1 = (bf16[1040,512]{1,0:T(8,128)(2,1)S(1)}, bf16[1040,512]{1,0:T(8,128)(2,1)}, u32[]{:S(2)}, u32[]{:S(2)}) collective-permute-start(bf16[1040,512]{1,0:T(8,128)(2,1)S(1)} %collective-permute-done), channel_id=1, source_target_pairs={{0,1},{1,2},{2,3},{3,0},{4,5},{5,6},{6,7},{7,4},{8,9},{9,10},{10,1... | collective-permute-start | bytes 3194888 | tf_op jit(solution)/shard_map/ppermute | solution.py:55
  87.0 46.3 %collective-permute-start.2 = (bf16[1040,512]{1,0:T(8,128)(2,1)}, bf16[1040,512]{1,0:T(8,128)(2,1)}, u32[]{:S(2)}, u32[]{:S(2)}) collective-permute-start(bf16[1040,512]{1,0:T(8,128)(2,1)} %collective-permute-done.1), channel_id=1, source_target_pairs={{0,1},{1,2},{2,3},{3,0},{4,5},{5,6},{6,7},{7,4},{8,9},{9,10},{10,1... | collective-permute-start | bytes 3194888 | tf_op jit(solution)/shard_map/ppermute | solution.py:55
  133.3 675.0 %all-reduce.5.cloned.1.call-start = ((), (), s32[]{:S(2)}) async-start(), calls=%async_computation.2 | async-start | bytes 37748736 | tf_op jit(solution)/shard_map/psum | solution.py:937
  164.4 7.3 collective-permute-start.3
  164.4 9.1 %collective-permute-start.4 = (f32[8,1024]{1,0:T(8,128)}, f32[8,1024]{1,0:T(8,128)S(1)}, u32[]{:S(2)}, u32[]{:S(2)}) collective-permute-start(f32[8,1024]{1,0:T(8,128)} %get-tuple-element.83.rest_0_), channel_id=1, source_target_pairs={{0,2},{1,3},{2,0},{3,1},{4,6},{5,7},{6,4},{7,5},{8,10},{9,11},{10,... | collective-permute-start | bytes 98312 | tf_op jit(solution)/shard_map/ppermute | solution.py:895
  165.0 8.6 %collective-permute-start.5 = (f32[8,1024]{1,0:T(8,128)}, f32[8,1024]{1,0:T(8,128)S(1)}, u32[]{:S(2)}, u32[]{:S(2)}) collective-permute-start(f32[8,1024]{1,0:T(8,128)} %get-tuple-element.83.rest_0_), channel_id=1, source_target_pairs={{0,3},{1,0},{2,1},{3,2},{4,7},{5,4},{6,5},{7,6},{8,11},{9,8},{10,9... | collective-permute-start | bytes 98312 | tf_op jit(solution)/shard_map/ppermute | solution.py:895
  189.7 16.6 %collective-permute-start.6 = (bf16[1,256,512]{2,1,0:T(8,128)(2,1)S(1)}, bf16[1,256,512]{2,1,0:T(8,128)(2,1)S(1)}, u32[]{:S(2)}, u32[]{:S(2)}) collective-permute-start(bf16[1,256,512]{2,1,0:T(8,128)(2,1)S(1)} %get-tuple-element.163), channel_id=1, source_target_pairs={{0,1},{1,2},{2,3},{3,0},{4,5},{5,6},{6,7},{7,4},{8,9},{9,10},{10,1... | collective-permute-start | bytes 786440 | tf_op jit(solution)/shard_map/ppermute | solution.py:83
  193.0 30.9 %collective-permute-start.7 = (bf16[1,256,512]{2,1,0:T(8,128)(2,1)S(1)}, bf16[1,256,512]{2,1,0:T(8,128)(2,1)S(1)}, u32[]{:S(2)}, u32[]{:S(2)}) collective-permute-start(bf16[1,256,512]{2,1,0:T(8,128)(2,1)S(1)} %get-tuple-element.162), channel_id=1, source_target_pairs={{0,2},{1,3},{2,0},{3,1},{4,6},{5,7},{6,4},{7,5},{8,10},{9,11},{10,... | collective-permute-start | bytes 786440 | tf_op jit(solution)/shard_map/ppermute | solution.py:83
  193.4 32.5 %collective-permute-start.8 = (bf16[1,256,512]{2,1,0:T(8,128)(2,1)S(1)}, bf16[1,256,512]{2,1,0:T(8,128)(2,1)S(1)}, u32[]{:S(2)}, u32[]{:S(2)}) collective-permute-start(bf16[1,256,512]{2,1,0:T(8,128)(2,1)S(1)} %get-tuple-element.161), channel_id=1, source_target_pairs={{0,3},{1,0},{2,1},{3,2},{4,7},{5,4},{6,5},{7,6},{8,11},{9,8},{10,9... | collective-permute-start | bytes 786440 | tf_op jit(solution)/shard_map/ppermute | solution.py:83
  235.0 35.7 %collective-permute-start.9 = (bf16[256,2048]{1,0:T(8,128)(2,1)}, bf16[256,2048]{1,0:T(8,128)(2,1)S(1)}, u32[]{:S(2)}, u32[]{:S(2)}) collective-permute-start(bf16[256,2048]{1,0:T(8,128)(2,1)} %get-tuple-element.85.n2_ref), channel_id=1, source_target_pairs={{0,1},{1,2},{2,3},{3,0},{4,5},{5,6},{6,7},{7,4},{8,9},{9,10},{10,1... | collective-permute-start | bytes 3145736 | tf_op jit(solution)/shard_map/ppermute | solution.py:55
  270.7 27.9 %collective-permute-start.10 = (bf16[256,2048]{1,0:T(8,128)(2,1)S(1)}, bf16[256,2048]{1,0:T(8,128)(2,1)S(1)}, u32[]{:S(2)}, u32[]{:S(2)}) collective-permute-start(bf16[256,2048]{1,0:T(8,128)(2,1)S(1)} %collective-permute-done.9.n2_ref), channel_id=1, source_target_pairs={{0,1},{1,2},{2,3},{3,0},{4,5},{5,6},{6,7},{7,4},{8,9},{9,10},{10,1... | collective-permute-start | bytes 3145736 | tf_op jit(solution)/shard_map/ppermute | solution.py:55
  290.3 30.7 %collective-permute-start.15 = (bf16[256,2048]{1,0:T(8,128)(2,1)}, bf16[256,2048]{1,0:T(8,128)(2,1)S(1)}, u32[]{:S(2)}, u32[]{:S(2)}) collective-permute-start(bf16[256,2048]{1,0:T(8,128)(2,1)} %get-tuple-element.107), channel_id=1, source_target_pairs={{0,1},{1,2},{2,3},{3,0},{4,5},{5,6},{6,7},{7,4},{8,9},{9,10},{10,1... | collective-permute-start | bytes 3145736 | tf_op jit(solution)/shard_map/ppermute | solution.py:929
  298.6 45.1 %collective-permute-start.11 = (bf16[256,2048]{1,0:T(8,128)(2,1)S(1)}, bf16[256,2048]{1,0:T(8,128)(2,1)S(1)}, u32[]{:S(2)}, u32[]{:S(2)}) collective-permute-start(bf16[256,2048]{1,0:T(8,128)(2,1)S(1)} %collective-permute-done.10.n2_ref), channel_id=1, source_target_pairs={{0,1},{1,2},{2,3},{3,0},{4,5},{5,6},{6,7},{7,4},{8,9},{9,10},{10,1... | collective-permute-start | bytes 3145736 | tf_op jit(solution)/shard_map/ppermute | solution.py:55
  322.7 43.4 %collective-permute-start.16 = (bf16[256,2048]{1,0:T(8,128)(2,1)S(1)}, bf16[256,2048]{1,0:T(8,128)(2,1)S(1)}, u32[]{:S(2)}, u32[]{:S(2)}) collective-permute-start(bf16[256,2048]{1,0:T(8,128)(2,1)S(1)} %add.318), channel_id=1, source_target_pairs={{0,1},{1,2},{2,3},{3,0},{4,5},{5,6},{6,7},{7,4},{8,9},{9,10},{10,1... | collective-permute-start | bytes 3145736 | tf_op jit(solution)/shard_map/ppermute | solution.py:929
  323.6 77.8 %collective-permute-start.18 = (f32[256,128]{1,0:T(8,128)}, f32[256,128]{1,0:T(8,128)S(1)}, u32[]{:S(2)}, u32[]{:S(2)}) collective-permute-start(f32[256,128]{1,0:T(8,128)} %get-tuple-element.110), channel_id=1, source_target_pairs={{0,3},{1,0},{2,1},{3,2},{4,7},{5,4},{6,5},{7,6},{8,11},{9,8},{10,9... | collective-permute-start | bytes 393224 | tf_op jit(solution)/shard_map/ppermute | solution.py:931
  327.4 93.5 %collective-permute-start.19 = (f32[256,128]{1,0:T(8,128)}, f32[256,128]{1,0:T(8,128)S(1)}, u32[]{:S(2)}, u32[]{:S(2)}) collective-permute-start(f32[256,128]{1,0:T(8,128)} %get-tuple-element.111), channel_id=1, source_target_pairs={{0,2},{1,3},{2,0},{3,1},{4,6},{5,7},{6,4},{7,5},{8,10},{9,11},{10,... | collective-permute-start | bytes 393224 | tf_op jit(solution)/shard_map/ppermute | solution.py:931
  363.7 70.6 %collective-permute-start.12 = (bf16[1024,512]{1,0:T(8,128)(2,1)S(1)}, bf16[1024,512]{1,0:T(8,128)(2,1)}, u32[]{:S(2)}, u32[]{:S(2)}) collective-permute-start(bf16[1024,512]{1,0:T(8,128)(2,1)S(1)} %dynamic-slice_bitcast_fusion), channel_id=1, source_target_pairs={{0,1},{1,2},{2,3},{3,0},{4,5},{5,6},{6,7},{7,4},{8,9},{9,10},{10,1... | collective-permute-start | bytes 3145736 | tf_op jit(solution)/shard_map/ppermute | solution.py:65
  367.7 53.2 %collective-permute-start.17 = (bf16[256,2048]{1,0:T(8,128)(2,1)S(1)}, bf16[256,2048]{1,0:T(8,128)(2,1)S(1)}, u32[]{:S(2)}, u32[]{:S(2)}) collective-permute-start(bf16[256,2048]{1,0:T(8,128)(2,1)S(1)} %add.319), channel_id=1, source_target_pairs={{0,1},{1,2},{2,3},{3,0},{4,5},{5,6},{6,7},{7,4},{8,9},{9,10},{10,1... | collective-permute-start | bytes 3145736 | tf_op jit(solution)/shard_map/ppermute | solution.py:929
  369.4 51.5 %collective-permute-start.20 = (f32[256,128]{1,0:T(8,128)}, f32[256,128]{1,0:T(8,128)S(1)}, u32[]{:S(2)}, u32[]{:S(2)}) collective-permute-start(f32[256,128]{1,0:T(8,128)} %get-tuple-element.112), channel_id=1, source_target_pairs={{0,1},{1,2},{2,3},{3,0},{4,5},{5,6},{6,7},{7,4},{8,9},{9,10},{10,1... | collective-permute-start | bytes 393224 | tf_op jit(solution)/shard_map/ppermute | solution.py:931
  432.3 14.0 %collective-permute-start.53 = (f32[8,2048]{1,0:T(8,128)}, f32[8,2048]{1,0:T(8,128)S(1)}, u32[]{:S(2)}, u32[]{:S(2)}) collective-permute-start(f32[8,2048]{1,0:T(8,128)} %get-tuple-element.132), channel_id=1, source_target_pairs={{0,3},{1,0},{2,1},{3,2},{4,7},{5,4},{6,5},{7,6},{8,11},{9,8},{10,9... | collective-permute-start | bytes 196616 | tf_op jit(solution)/shard_map/ppermute | solution.py:72
  432.3 14.1 %collective-permute-start.52 = (f32[8,2048]{1,0:T(8,128)}, f32[8,2048]{1,0:T(8,128)S(1)}, u32[]{:S(2)}, u32[]{:S(2)}) collective-permute-start(f32[8,2048]{1,0:T(8,128)} %get-tuple-element.132), channel_id=1, source_target_pairs={{0,2},{1,3},{2,0},{3,1},{4,6},{5,7},{6,4},{7,5},{8,10},{9,11},{10,... | collective-permute-start | bytes 196616 | tf_op jit(solution)/shard_map/ppermute | solution.py:72
  432.4 16.5 %collective-permute-start.51 = (f32[8,2048]{1,0:T(8,128)}, f32[8,2048]{1,0:T(8,128)S(1)}, u32[]{:S(2)}, u32[]{:S(2)}) collective-permute-start(f32[8,2048]{1,0:T(8,128)} %get-tuple-element.132), channel_id=1, source_target_pairs={{0,1},{1,2},{2,3},{3,0},{4,5},{5,6},{6,7},{7,4},{8,9},{9,10},{10,1... | collective-permute-start | bytes 196616 | tf_op jit(solution)/shard_map/ppermute | solution.py:72
  437.4 137.8 %collective-permute-start.13 = (bf16[1024,512]{1,0:T(8,128)(2,1)}, bf16[1024,512]{1,0:T(8,128)(2,1)}, u32[]{:S(2)}, u32[]{:S(2)}) collective-permute-start(bf16[1024,512]{1,0:T(8,128)(2,1)} %fusion.14), channel_id=1, source_target_pairs={{0,1},{1,2},{2,3},{3,0},{4,5},{5,6},{6,7},{7,4},{8,9},{9,10},{10,1... | collective-permute-start | bytes 3145736 | tf_op jit(solution)/shard_map/ppermute | solution.py:65
  438.9 138.0 %collective-permute-start.21 = (bf16[256,2048]{1,0:T(8,128)(2,1)S(1)}, bf16[256,2048]{1,0:T(8,128)(2,1)S(1)}, u32[]{:S(2)}, u32[]{:S(2)}) collective-permute-start(bf16[256,2048]{1,0:T(8,128)(2,1)S(1)} %copy-done.20), channel_id=1, source_target_pairs={{0,1},{1,2},{2,3},{3,0},{4,5},{5,6},{6,7},{7,4},{8,9},{9,10},{10,1... | collective-permute-start | bytes 3145736 | tf_op jit(solution)/shard_map/ppermute | solution.py:55
  446.3 47.4 %collective-permute-start.24 = (bf16[1,256,512]{2,1,0:T(8,128)(2,1)}, bf16[1,256,512]{2,1,0:T(8,128)(2,1)S(1)}, u32[]{:S(2)}, u32[]{:S(2)}) collective-permute-start(bf16[1,256,512]{2,1,0:T(8,128)(2,1)} %get-tuple-element.159), channel_id=1, source_target_pairs={{0,1},{1,2},{2,3},{3,0},{4,5},{5,6},{6,7},{7,4},{8,9},{9,10},{10,1... | collective-permute-start | bytes 786440 | tf_op jit(solution)/shard_map/ppermute | solution.py:83
  446.4 57.2 %collective-permute-start.25 = (bf16[1,256,512]{2,1,0:T(8,128)(2,1)}, bf16[1,256,512]{2,1,0:T(8,128)(2,1)S(1)}, u32[]{:S(2)}, u32[]{:S(2)}) collective-permute-start(bf16[1,256,512]{2,1,0:T(8,128)(2,1)} %get-tuple-element.158), channel_id=1, source_target_pairs={{0,2},{1,3},{2,0},{3,1},{4,6},{5,7},{6,4},{7,5},{8,10},{9,11},{10,... | collective-permute-start | bytes 786440 | tf_op jit(solution)/shard_map/ppermute | solution.py:83
  448.9 55.4 %collective-permute-start.26 = (bf16[1,256,512]{2,1,0:T(8,128)(2,1)S(1)}, bf16[1,256,512]{2,1,0:T(8,128)(2,1)S(1)}, u32[]{:S(2)}, u32[]{:S(2)}) collective-permute-start(bf16[1,256,512]{2,1,0:T(8,128)(2,1)S(1)} %get-tuple-element.157), channel_id=1, source_target_pairs={{0,3},{1,0},{2,1},{3,2},{4,7},{5,4},{6,5},{7,6},{8,11},{9,8},{10,9... | collective-permute-start | bytes 786440 | tf_op jit(solution)/shard_map/ppermute | solution.py:83
  525.4 9.3 %collective-permute-start.27 = (f32[8,1024]{1,0:T(8,128)}, f32[8,1024]{1,0:T(8,128)S(1)}, u32[]{:S(2)}, u32[]{:S(2)}) collective-permute-start(f32[8,1024]{1,0:T(8,128)} %get-tuple-element.121.rest_4_), channel_id=1, source_target_pairs={{0,1},{1,2},{2,3},{3,0},{4,5},{5,6},{6,7},{7,4},{8,9},{9,10},{10,1... | collective-permute-start | bytes 98312 | tf_op jit(solution)/shard_map/ppermute | solution.py:895
  534.7 26.2 %collective-permute-start.54 = (f32[108,128]{1,0:T(8,128)S(1)}, f32[108,128]{1,0:T(8,128)S(1)}, u32[]{:S(2)}, u32[]{:S(2)}) collective-permute-start(f32[108,128]{1,0:T(8,128)S(1)} %maximum_bitcast_fusion), channel_id=1, source_target_pairs={{0,4},{4,0},{8,12},{12,8},{16,20},{20,16},{24,28},{28,24},{1,5},{5... | collective-permute-start | bytes 165896 | tf_op jit(solution)/shard_map/ppermute | solution.py:89
  545.9 23.5 %collective-permute-start.35 = (f32[8,1024]{1,0:T(8,128)}, f32[8,1024]{1,0:T(8,128)S(1)}, u32[]{:S(2)}, u32[]{:S(2)}) collective-permute-start(f32[8,1024]{1,0:T(8,128)} %get-tuple-element.123), channel_id=1, source_target_pairs={{0,3},{1,0},{2,1},{3,2},{4,7},{5,4},{6,5},{7,6},{8,11},{9,8},{10,9... | collective-permute-start | bytes 98312 | tf_op jit(solution)/shard_map/ppermute | solution.py:72
  548.0 22.4 %collective-permute-start.34 = (f32[8,1024]{1,0:T(8,128)}, f32[8,1024]{1,0:T(8,128)S(1)}, u32[]{:S(2)}, u32[]{:S(2)}) collective-permute-start(f32[8,1024]{1,0:T(8,128)} %get-tuple-element.123), channel_id=1, source_target_pairs={{0,2},{1,3},{2,0},{3,1},{4,6},{5,7},{6,4},{7,5},{8,10},{9,11},{10,... | collective-permute-start | bytes 98312 | tf_op jit(solution)/shard_map/ppermute | solution.py:72
  560.9 21.3 %collective-permute-start.39 = (bf16[4,256,768]{2,1,0:T(8,128)(2,1)}, bf16[4,256,768]{2,1,0:T(8,128)(2,1)S(1)}, u32[]{:S(2)}, u32[]{:S(2)}) collective-permute-start(bf16[4,256,768]{2,1,0:T(8,128)(2,1)} %get-tuple-element.126), channel_id=1, source_target_pairs={{0,4},{4,0},{8,12},{12,8},{16,20},{20,16},{24,28},{28,24},{1,5},{5... | collective-permute-start | bytes 4718600 | tf_op jit(solution)/shard_map/ppermute | solution.py:89
  570.4 12.7 %collective-permute-start.45 = (bf16[4,256,768]{2,1,0:T(8,128)(2,1)}, bf16[4,256,768]{2,1,0:T(8,128)(2,1)S(1)}, u32[]{:S(2)}, u32[]{:S(2)}) collective-permute-start(bf16[4,256,768]{2,1,0:T(8,128)(2,1)} %get-tuple-element.128), channel_id=1, source_target_pairs={{0,4},{4,0},{8,12},{12,8},{16,20},{20,16},{24,28},{28,24},{1,5},{5... | collective-permute-start | bytes 4718600 | tf_op jit(solution)/shard_map/ppermute | solution.py:89
  575.1 28.1 %collective-permute-start.30 = (bf16[1024,512]{1,0:T(8,128)(2,1)}, bf16[1024,512]{1,0:T(8,128)(2,1)S(1)}, u32[]{:S(2)}, u32[]{:S(2)}) collective-permute-start(bf16[1024,512]{1,0:T(8,128)(2,1)} %fusion.27), channel_id=1, source_target_pairs={{0,1},{1,2},{2,3},{3,0},{4,5},{5,6},{6,7},{7,4},{8,9},{9,10},{10,1... | collective-permute-start | bytes 3145736 | tf_op jit(solution)/shard_map/ppermute | solution.py:65
  575.2 184.1 %collective-permute-start.55 = (f32[108,128]{1,0:T(8,128)S(1)}, f32[108,128]{1,0:T(8,128)S(1)}, u32[]{:S(2)}, u32[]{:S(2)}) collective-permute-start(f32[108,128]{1,0:T(8,128)S(1)} %fusion.57), channel_id=1, source_target_pairs={{0,8},{4,12},{8,0},{12,4},{16,24},{20,28},{24,16},{28,20},{1,9},{5... | collective-permute-start | bytes 165896 | tf_op jit(solution)/shard_map/ppermute | solution.py:89
  576.9 48.8 %collective-permute-start.22 = (bf16[256,2048]{1,0:T(8,128)(2,1)S(1)}, bf16[256,2048]{1,0:T(8,128)(2,1)S(1)}, u32[]{:S(2)}, u32[]{:S(2)}) collective-permute-start(bf16[256,2048]{1,0:T(8,128)(2,1)S(1)} %collective-permute-done.21), channel_id=1, source_target_pairs={{0,1},{1,2},{2,3},{3,0},{4,5},{5,6},{6,7},{7,4},{8,9},{9,10},{10,1... | collective-permute-start | bytes 3145736 | tf_op jit(solution)/shard_map/ppermute | solution.py:55
  582.5 43.2 %collective-permute-start.40 = (bf16[2,256,768]{2,1,0:T(8,128)(2,1)S(1)}, bf16[2,256,768]{2,1,0:T(8,128)(2,1)S(1)}, u32[]{:S(2)}, u32[]{:S(2)}) collective-permute-start(bf16[2,256,768]{2,1,0:T(8,128)(2,1)S(1)} %get-tuple-element.152), channel_id=1, source_target_pairs={{0,8},{4,12},{8,0},{12,4},{16,24},{20,28},{24,16},{28,20},{1,9},{5... | collective-permute-start | bytes 2359304 | tf_op jit(solution)/shard_map/ppermute | solution.py:89
  583.3 45.4 %collective-permute-start.46 = (bf16[2,256,768]{2,1,0:T(8,128)(2,1)S(1)}, bf16[2,256,768]{2,1,0:T(8,128)(2,1)S(1)}, u32[]{:S(2)}, u32[]{:S(2)}) collective-permute-start(bf16[2,256,768]{2,1,0:T(8,128)(2,1)S(1)} %get-tuple-element.150), channel_id=1, source_target_pairs={{0,16},{4,20},{8,24},{12,28},{16,0},{20,4},{24,8},{28,12},{1,17},{... | collective-permute-start | bytes 2359304 | tf_op jit(solution)/shard_map/ppermute | solution.py:89
  607.4 68.2 %collective-permute-start.31 = (bf16[1024,512]{1,0:T(8,128)(2,1)}, bf16[1024,512]{1,0:T(8,128)(2,1)}, u32[]{:S(2)}, u32[]{:S(2)}) collective-permute-start(bf16[1024,512]{1,0:T(8,128)(2,1)} %add_convert_fusion.1), channel_id=1, source_target_pairs={{0,1},{1,2},{2,3},{3,0},{4,5},{5,6},{6,7},{7,4},{8,9},{9,10},{10,1... | collective-permute-start | bytes 3145736 | tf_op jit(solution)/shard_map/ppermute | solution.py:65
  625.7 43.2 %collective-permute-start.23 = (bf16[256,2048]{1,0:T(8,128)(2,1)S(1)}, bf16[256,2048]{1,0:T(8,128)(2,1)S(1)}, u32[]{:S(2)}, u32[]{:S(2)}) collective-permute-start(bf16[256,2048]{1,0:T(8,128)(2,1)S(1)} %collective-permute-done.22), channel_id=1, source_target_pairs={{0,1},{1,2},{2,3},{3,0},{4,5},{5,6},{6,7},{7,4},{8,9},{9,10},{10,1... | collective-permute-start | bytes 3145736 | tf_op jit(solution)/shard_map/ppermute | solution.py:55
  625.8 19.5 %collective-permute-start.41 = (bf16[1,256,768]{2,1,0:T(8,128)(2,1)S(1)}, bf16[1,256,768]{2,1,0:T(8,128)(2,1)S(1)}, u32[]{:S(2)}, u32[]{:S(2)}) collective-permute-start(bf16[1,256,768]{2,1,0:T(8,128)(2,1)S(1)} %slice_add_fusion.6), channel_id=1, source_target_pairs={{0,16},{4,20},{8,24},{12,28},{16,0},{20,4},{24,8},{28,12},{1,17},{... | collective-permute-start | bytes 1179656 | tf_op jit(solution)/shard_map/ppermute | solution.py:89
  628.7 52.7 %collective-permute-start.47 = (bf16[1,256,768]{2,1,0:T(8,128)(2,1)S(1)}, bf16[1,256,768]{2,1,0:T(8,128)(2,1)S(1)}, u32[]{:S(2)}, u32[]{:S(2)}) collective-permute-start(bf16[1,256,768]{2,1,0:T(8,128)(2,1)S(1)} %slice_add_fusion.4), channel_id=1, source_target_pairs={{0,8},{4,12},{8,0},{12,4},{16,24},{20,28},{24,16},{28,20},{1,9},{5... | collective-permute-start | bytes 1179656 | tf_op jit(solution)/shard_map/ppermute | solution.py:89
  645.3 42.4 %collective-permute-start.42 = (bf16[1,256,768]{2,1,0:T(8,128)(2,1)S(1)}, bf16[1,256,768]{2,1,0:T(8,128)(2,1)S(1)}, u32[]{:S(2)}, u32[]{:S(2)}) collective-permute-start(bf16[1,256,768]{2,1,0:T(8,128)(2,1)S(1)} %fusion.41), channel_id=1, source_target_pairs={{0,16},{4,20},{8,24},{12,28},{16,0},{20,4},{24,8},{28,12},{1,17},{... | collective-permute-start | bytes 1179656 | tf_op jit(solution)/shard_map/ppermute | solution.py:89
  675.7 13.8 %collective-permute-start.57 = (bf16[4,256,256]{2,1,0:T(8,128)(2,1)}, bf16[4,256,256]{2,1,0:T(8,128)(2,1)S(1)}, u32[]{:S(2)}, u32[]{:S(2)}) collective-permute-start(bf16[4,256,256]{2,1,0:T(8,128)(2,1)} %get-tuple-element.135), channel_id=1, source_target_pairs={{0,4},{4,0},{8,12},{12,8},{16,20},{20,16},{24,28},{28,24},{1,5},{5... | collective-permute-start | bytes 1572872 | tf_op jit(solution)/shard_map/ppermute | solution.py:89
  681.2 71.6 %collective-permute-start.32 = (bf16[1024,512]{1,0:T(8,128)(2,1)}, bf16[1024,512]{1,0:T(8,128)(2,1)}, u32[]{:S(2)}, u32[]{:S(2)}) collective-permute-start(bf16[1024,512]{1,0:T(8,128)(2,1)} %add_convert_fusion), channel_id=1, source_target_pairs={{0,1},{1,2},{2,3},{3,0},{4,5},{5,6},{6,7},{7,4},{8,9},{9,10},{10,1... | collective-permute-start | bytes 3145736 | tf_op jit(solution)/shard_map/ppermute | solution.py:65
  681.4 9.6 %collective-permute-start.63 = (bf16[4,256,256]{2,1,0:T(8,128)(2,1)S(1)}, bf16[4,256,256]{2,1,0:T(8,128)(2,1)S(1)}, u32[]{:S(2)}, u32[]{:S(2)}) collective-permute-start(bf16[4,256,256]{2,1,0:T(8,128)(2,1)S(1)} %copy-done.42), channel_id=1, source_target_pairs={{0,4},{4,0},{8,12},{12,8},{16,20},{20,16},{24,28},{28,24},{1,5},{5... | collective-permute-start | bytes 1572872 | tf_op jit(solution)/shard_map/ppermute | solution.py:89
  687.7 12.0 %collective-permute-start.48 = (bf16[1,256,768]{2,1,0:T(8,128)(2,1)S(1)}, bf16[1,256,768]{2,1,0:T(8,128)(2,1)S(1)}, u32[]{:S(2)}, u32[]{:S(2)}) collective-permute-start(bf16[1,256,768]{2,1,0:T(8,128)(2,1)S(1)} %fusion.40), channel_id=1, source_target_pairs={{0,8},{4,12},{8,0},{12,4},{16,24},{20,28},{24,16},{28,20},{1,9},{5... | collective-permute-start | bytes 1179656 | tf_op jit(solution)/shard_map/ppermute | solution.py:89
  689.4 60.0 %collective-permute-start.43 = (bf16[2,256,768]{2,1,0:T(8,128)(2,1)S(1)}, bf16[2,256,768]{2,1,0:T(8,128)(2,1)S(1)}, u32[]{:S(2)}, u32[]{:S(2)}) collective-permute-start(bf16[2,256,768]{2,1,0:T(8,128)(2,1)S(1)} %pad_maximum_fusion.2), channel_id=1, source_target_pairs={{0,8},{4,12},{8,0},{12,4},{16,24},{20,28},{24,16},{28,20},{1,9},{5... | collective-permute-start | bytes 2359304 | tf_op jit(solution)/shard_map/ppermute | solution.py:89
  691.1 30.3 %collective-permute-start.58 = (bf16[2,256,256]{2,1,0:T(8,128)(2,1)S(1)}, bf16[2,256,256]{2,1,0:T(8,128)(2,1)S(1)}, u32[]{:S(2)}, u32[]{:S(2)}) collective-permute-start(bf16[2,256,256]{2,1,0:T(8,128)(2,1)S(1)} %get-tuple-element.156), channel_id=1, source_target_pairs={{0,8},{4,12},{8,0},{12,4},{16,24},{20,28},{24,16},{28,20},{1,9},{5... | collective-permute-start | bytes 786440 | tf_op jit(solution)/shard_map/ppermute | solution.py:89
  699.8 23.2 %collective-permute-start.64 = (bf16[2,256,256]{2,1,0:T(8,128)(2,1)S(1)}, bf16[2,256,256]{2,1,0:T(8,128)(2,1)S(1)}, u32[]{:S(2)}, u32[]{:S(2)}) collective-permute-start(bf16[2,256,256]{2,1,0:T(8,128)(2,1)S(1)} %get-tuple-element.154), channel_id=1, source_target_pairs={{0,16},{4,20},{8,24},{12,28},{16,0},{20,4},{24,8},{28,12},{1,17},{... | collective-permute-start | bytes 786440 | tf_op jit(solution)/shard_map/ppermute | solution.py:89
  721.4 29.8 %collective-permute-start.49 = (bf16[2,256,768]{2,1,0:T(8,128)(2,1)S(1)}, bf16[2,256,768]{2,1,0:T(8,128)(2,1)S(1)}, u32[]{:S(2)}, u32[]{:S(2)}) collective-permute-start(bf16[2,256,768]{2,1,0:T(8,128)(2,1)S(1)} %pad_maximum_fusion.3), channel_id=1, source_target_pairs={{0,16},{4,20},{8,24},{12,28},{16,0},{20,4},{24,8},{28,12},{1,17},{... | collective-permute-start | bytes 2359304 | tf_op jit(solution)/shard_map/ppermute | solution.py:89
  723.0 19.8 %collective-permute-start.59 = (bf16[1,256,256]{2,1,0:T(8,128)(2,1)S(1)}, bf16[1,256,256]{2,1,0:T(8,128)(2,1)S(1)}, u32[]{:S(2)}, u32[]{:S(2)}) collective-permute-start(bf16[1,256,256]{2,1,0:T(8,128)(2,1)S(1)} %slice_add_fusion.14), channel_id=1, source_target_pairs={{0,16},{4,20},{8,24},{12,28},{16,0},{20,4},{24,8},{28,12},{1,17},{... | collective-permute-start | bytes 393224 | tf_op jit(solution)/shard_map/ppermute | solution.py:89
  747.8 11.1 %collective-permute-start.60 = (bf16[1,256,256]{2,1,0:T(8,128)(2,1)S(1)}, bf16[1,256,256]{2,1,0:T(8,128)(2,1)S(1)}, u32[]{:S(2)}, u32[]{:S(2)}) collective-permute-start(bf16[1,256,256]{2,1,0:T(8,128)(2,1)S(1)} %fusion.44), channel_id=1, source_target_pairs={{0,16},{4,20},{8,24},{12,28},{16,0},{20,4},{24,8},{28,12},{1,17},{... | collective-permute-start | bytes 393224 | tf_op jit(solution)/shard_map/ppermute | solution.py:89
  749.5 9.8 %collective-permute-start.66 = (bf16[1,256,256]{2,1,0:T(8,128)(2,1)S(1)}, bf16[1,256,256]{2,1,0:T(8,128)(2,1)S(1)}, u32[]{:S(2)}, u32[]{:S(2)}) collective-permute-start(bf16[1,256,256]{2,1,0:T(8,128)(2,1)S(1)} %fusion.43), channel_id=1, source_target_pairs={{0,8},{4,12},{8,0},{12,4},{16,24},{20,28},{24,16},{28,20},{1,9},{5... | collective-permute-start | bytes 393224 | tf_op jit(solution)/shard_map/ppermute | solution.py:89
  751.1 47.1 %collective-permute-start.44 = (bf16[4,256,768]{2,1,0:T(8,128)(2,1)S(1)}, bf16[4,256,768]{2,1,0:T(8,128)(2,1)}, u32[]{:S(2)}, u32[]{:S(2)}) collective-permute-start(bf16[4,256,768]{2,1,0:T(8,128)(2,1)S(1)} %pad_maximum_fusion.la_ref), channel_id=1, source_target_pairs={{0,4},{4,0},{8,12},{12,8},{16,20},{20,16},{24,28},{28,24},{1,5},{5... | collective-permute-start | bytes 4718600 | tf_op jit(solution)/shard_map/ppermute | solution.py:89
  752.8 45.4 %collective-permute-start.50 = (bf16[4,256,768]{2,1,0:T(8,128)(2,1)}, bf16[4,256,768]{2,1,0:T(8,128)(2,1)}, u32[]{:S(2)}, u32[]{:S(2)}) collective-permute-start(bf16[4,256,768]{2,1,0:T(8,128)(2,1)} %pad_maximum_fusion.1.lb_ref), channel_id=1, source_target_pairs={{0,4},{4,0},{8,12},{12,8},{16,20},{20,16},{24,28},{28,24},{1,5},{5... | collective-permute-start | bytes 4718600 | tf_op jit(solution)/shard_map/ppermute | solution.py:89
  758.9 28.0 %collective-permute-start.14 = (bf16[1024,512]{1,0:T(8,128)(2,1)}, bf16[1024,512]{1,0:T(8,128)(2,1)}, u32[]{:S(2)}, u32[]{:S(2)}) collective-permute-start(bf16[1024,512]{1,0:T(8,128)(2,1)} %fusion.15), channel_id=1, source_target_pairs={{0,1},{1,2},{2,3},{3,0},{4,5},{5,6},{6,7},{7,4},{8,9},{9,10},{10,1... | collective-permute-start | bytes 3145736 | tf_op jit(solution)/shard_map/ppermute | solution.py:65
  759.3 8.7 %collective-permute-start.61 = (bf16[2,256,256]{2,1,0:T(8,128)(2,1)S(1)}, bf16[2,256,256]{2,1,0:T(8,128)(2,1)S(1)}, u32[]{:S(2)}, u32[]{:S(2)}) collective-permute-start(bf16[2,256,256]{2,1,0:T(8,128)(2,1)S(1)} %pad_maximum_fusion.8), channel_id=1, source_target_pairs={{0,8},{4,12},{8,0},{12,4},{16,24},{20,28},{24,16},{28,20},{1,9},{5... | collective-permute-start | bytes 786440 | tf_op jit(solution)/shard_map/ppermute | solution.py:89
  760.5 8.4 %collective-permute-start.67 = (bf16[2,256,256]{2,1,0:T(8,128)(2,1)S(1)}, bf16[2,256,256]{2,1,0:T(8,128)(2,1)S(1)}, u32[]{:S(2)}, u32[]{:S(2)}) collective-permute-start(bf16[2,256,256]{2,1,0:T(8,128)(2,1)S(1)} %pad_maximum_fusion.9), channel_id=1, source_target_pairs={{0,16},{4,20},{8,24},{12,28},{16,0},{20,4},{24,8},{28,12},{1,17},{... | collective-permute-start | bytes 786440 | tf_op jit(solution)/shard_map/ppermute | solution.py:89
  772.2 18.8 %collective-permute-start.62 = (bf16[4,256,256]{2,1,0:T(8,128)(2,1)S(1)}, bf16[4,256,256]{2,1,0:T(8,128)(2,1)}, u32[]{:S(2)}, u32[]{:S(2)}) collective-permute-start(bf16[4,256,256]{2,1,0:T(8,128)(2,1)S(1)} %pad_maximum_fusion.6.la_ref), channel_id=1, source_target_pairs={{0,4},{4,0},{8,12},{12,8},{16,20},{20,16},{24,28},{28,24},{1,5},{5... | collective-permute-start | bytes 1572872 | tf_op jit(solution)/shard_map/ppermute | solution.py:89
  772.4 18.5 %collective-permute-start.68 = (bf16[4,256,256]{2,1,0:T(8,128)(2,1)S(1)}, bf16[4,256,256]{2,1,0:T(8,128)(2,1)}, u32[]{:S(2)}, u32[]{:S(2)}) collective-permute-start(bf16[4,256,256]{2,1,0:T(8,128)(2,1)S(1)} %pad_maximum_fusion.7.lb_ref), channel_id=1, source_target_pairs={{0,4},{4,0},{8,12},{12,8},{16,20},{20,16},{24,28},{28,24},{1,5},{5... | collective-permute-start | bytes 1572872 | tf_op jit(solution)/shard_map/ppermute | solution.py:89
  (54 other events, 446.0 us)
Sparse Core Ops, SparseCore 0:
  11.5 118.8 all-gather.3
  133.4 104.7 all-gather.5
  401.5 272.6 all-reduce.4

commit v2 on v1

v2 whole, which is shorter than its diff:
```python
import functools

import jax
import jax.numpy as jnp
from jax import lax
from jax.experimental import pallas as pl
from jax.experimental.pallas import tpu as pltpu
from jax.sharding import PartitionSpec as P

HEAD_DIM = 128
EXPERTS = 6
TOP = 3
CAP = 640
PREFIX_MAX = 512

EPSILON = 1e-05
ROPE_BASE = 10000.0
MASKED = -1e30
GROUP = 8
LONG = 2e13
BF = jnp.bfloat16
F32 = jnp.float32
VMEM_LIMIT = 56 * 1024 * 1024


class Chain:
    token = None


def launch(
    body, operands, *, grid, in_specs, out_specs, out_shape, work=1, prefetch=0, scratch=(), aliases=None,
    token=0, others=(),
):
    operands = list(operands)
    unread = [field for field in (Chain.token, *others) if field is not None]
    unread = [field for field in unread if all(field is not own for own in operands)]
    first, last = len(operands), len(operands) + len(unread)

    def kernel(*refs):
        body(*refs[:first], *refs[last:])

    out = pl.pallas_call(
        kernel,
        grid_spec=pltpu.PrefetchScalarGridSpec(
            num_scalar_prefetch=prefetch,
            grid=grid,
            in_specs=list(in_specs) + [pl.BlockSpec(memory_space=pl.ANY)] * len(unread),
            out_specs=out_specs,
            scratch_shapes=list(scratch),
        ),
        out_shape=out_shape,
        input_output_aliases=aliases or {},
        compiler_params=pltpu.CompilerParams(vmem_limit_bytes=VMEM_LIMIT),
        cost_estimate=pl.CostEstimate(flops=int(work), bytes_accessed=1, transcendentals=0),
    )(*operands, *unread)
    Chain.token = out[token] if isinstance(out, (list, tuple)) else out
    return out


def dot(a, b):
    return jnp.dot(a, b, preferred_element_type=F32)


def dot_t(a, b):
    return lax.dot_general(a, b, (((1,), (1,)), ((), ())), preferred_element_type=F32)


def row_sums(field):
    folded = field[:, :128]
    for at in range(128, field.shape[1], 128):
        folded = folded + field[:, at : at + 128]
    return jnp.sum(jnp.transpose(folded), axis=0, keepdims=True)


def ring(size):
    return [(at, (at + 1) % size) for at in range(size)]


def send(value, step, size):
    return lax.ppermute(value, "tensor", [(at, (at + step) % size) for at in range(size)])


def swap(value, mask, n):
    return lax.ppermute(value, "dp", [(at, at ^ mask) for at in range(n)])


def take(blocks, at):
    return lax.dynamic_slice_in_dim(blocks, at, 1, 0)


def place(size, received, mine, own):
    out = lax.dynamic_update_slice_in_dim(jnp.zeros((size,) + own.shape[1:], own.dtype), own, mine, 0)
    for step, block in enumerate(received, 1):
        out = lax.dynamic_update_slice_in_dim(out, block, (mine - step) % size, 0)
    return out


def swap(field, mask, n):
    return lax.ppermute(field, "dp", [(at, at ^ mask) for at in range(n)])


def swap_masks(n):
    return [1 << bit for bit in range(n.bit_length() - 1)]


def rel_table(masks):
    bits = len(masks)
    return [
        sum(masks[s] for s in range(bits) if (p >> (bits - 1 - s)) & 1) for p in range(1 << bits)
    ]


def blockwise(body, ins, outs, others=(), work=1):
    chunks = max(c for c in (1, 2, 3, 4) if ins[0].shape[1] % (16 * c) == 0)

    def spec(shape):
        return pl.BlockSpec((shape[0], shape[1] // chunks, shape[2]), lambda g: (0, g, 0))

    def kernel(*refs):
        body(refs[: len(ins)], refs[len(ins) :])

    return launch(
        kernel,
        [*ins],
        grid=(chunks,),
        in_specs=[spec(field.shape) for field in ins],
        out_specs=[spec(shape) for shape in outs],
        out_shape=[jax.ShapeDtypeStruct(shape, BF) for shape in outs],
        others=others,
        work=work,
    )


def added(a, b):
    return (a.astype(F32) + b.astype(F32)).astype(BF)


def copied(field, others=()):
    def body(ins, outs):
        outs[0][...] = ins[0][...]

    return blockwise(body, [field[None]], [(1,) + field.shape], others)[0][0]


def side_by_side(fields):
    def body(ins, outs):
        at = 0
        for ref in ins:
            outs[0][:, :, at : at + ref.shape[2]] = ref[...]
            at += ref.shape[2]

    width = sum(field.shape[1] for field in fields)
    return blockwise(body, [field[None] for field in fields], [(1, fields[0].shape[0], width)])[0][0]


def add_blocks(a, b, work=1):
    def body(ins, outs):
        outs[0][...] = added(ins[0][...], ins[1][...])

    return blockwise(body, [a, b], [a.shape], work=work)[0]


class Sum:
    def __init__(self, n, parts, first):
        self.n, self.parts = n, parts
        self.masks = swap_masks(n)
        self.stage = 0
        self.flying = [swap(first, self.masks[0], n)]

    def send(self, fields, stage):
        self.flying = []
        for part, field in enumerate(fields):
            mask = self.masks[stage] if part == 0 else self.masks[-stage]
            self.flying.append(swap(field, mask, self.n))

    def split(self, keeps, received):
        count, rows, width = keeps[0].shape
        wide = width // self.parts if len(keeps) < self.parts else width

        def body(ins, outs):
            for part in range(self.parts):
                at = part if len(keeps) == self.parts else 0
                here = slice(part * wide, (part + 1) * wide) if at != part else slice(0, wide)
                for i in range(count):
                    total = added(ins[2 * at][i, :, here], ins[2 * at + 1][i, :, here])
                    if part == 0:
                        away, place_at = i >= count // 2, i % (count // 2)
                    else:
                        away, place_at = i % 2 == 1, i // 2
                    outs[2 * part + (0 if away else 1)][place_at] = total

        ins = [field for pair in zip(keeps, received, strict=True) for field in pair]
        outs = blockwise(body, ins, [(count // 2, rows, wide)] * (2 * self.parts))
        return outs[0::2], outs[1::2]

    def total(self, keeps, received):
        def body(ins, outs):
            for part, out in enumerate(outs):
                out[...] = added(ins[2 * part][...], ins[2 * part + 1][...])

        ins = [field for pair in zip(keeps, received, strict=True) for field in pair]
        return blockwise(body, ins, [field.shape for field in keeps])

    def joined(self, last, keeps, received):
        count, rows, wide = keeps[0].shape

        def body(ins, outs):
            for part in range(self.parts):
                out = outs[0] if last else outs[part]
                here = slice(part * wide, (part + 1) * wide) if last else slice(0, wide)
                for i in range(count):
                    low, high = (i, count + i) if part == 0 else (2 * i, 2 * i + 1)
                    out[low, :, here] = ins[2 * part][i]
                    out[high, :, here] = ins[2 * part + 1][i]

        ins = [field for pair in zip(keeps, received, strict=True) for field in pair]
        if last:
            return blockwise(body, ins, [(2 * count, rows, wide * self.parts)])
        return blockwise(body, ins, [(2 * count, rows, wide)] * self.parts)

    def step(self):
        bits = len(self.masks)
        if self.stage == 2 * bits - 1:
            return
        received = self.flying
        self.stage += 1
        if self.stage < bits:
            keep = [self.keep] if self.stage == 1 else self.keep
            away, self.keep = self.split(keep, received)
            self.send(away, self.stage)
            return
        back = 2 * bits - 1 - self.stage
        if self.stage == bits:
            self.keep = self.total(self.keep, received)
        else:
            self.keep = self.joined(back == 0, self.keep, received)
        if back:
            self.send(self.keep, back)
        else:
            self.keep = self.keep[0]
            self.flying = [swap(self.keep, self.masks[0], self.n)]

    def finish(self):
        return self.keep, self.flying[0]


def copied_pair(first, second, work):
    fold = second.shape[0] // first.shape[0]

    def body(ins, outs):
        outs[0][...] = ins[0][...]
        outs[1][...] = ins[1][...]

    folded = second.reshape(fold, first.shape[0], second.shape[1])
    a, b = blockwise(
        body, [first[None], folded], [(1,) + first.shape, folded.shape], work=work
    )
    return a[0], b.reshape(second.shape)


def qkv_kernel(owners_ref, *refs):
    blocks, refs = refs[:-9], refs[-9:]
    gain_ref, wq_ref, wk_ref, wv_ref, n1_ref, q_ref, k_ref, v_ref, sums_ref = refs
    rows, cols = blocks[0].shape
    full = len(blocks) * cols
    fields = [block[...].astype(F32) for block in blocks]
    squares = fields[0] * fields[0]
    for field in fields[1:]:
        squares = squares + field * field
    scale = lax.rsqrt(jnp.sum(squares, axis=1, keepdims=True) / full + EPSILON)
    for k, field in enumerate(fields):
        at = owners_ref[k]
        gain = gain_ref[at, 0:1, :].astype(F32)
        first = pl.multiple_of(at * cols, 128)
        n1_ref[:, pl.ds(first, cols)] = (field * scale * gain).astype(BF)
    normed = n1_ref[...]
    query = dot(normed, wq_ref[...])
    key = dot(normed, wk_ref[...])
    q_ref[...] = query
    k_ref[...] = key
    v_ref[...] = dot(normed, wv_ref[...]).astype(BF)
    which = lax.broadcasted_iota(jnp.int32, (8, rows), 0)
    sums_ref[...] = jnp.where(
        which == 0,
        row_sums(query * query),
        jnp.where(which == 1, row_sums(key * key), row_sums(squares)),
    )


def qkv_call(owners, blocks, gains, wq, wk, wv):
    length, cols = blocks[0].shape
    full = cols * len(blocks)
    out = wq.shape[1]
    rows = min(256, length)
    whole = pl.BlockSpec((full, out), lambda g, o: (0, 0))
    tile = pl.BlockSpec((rows, out), lambda g, o: (g, 0))
    return launch(
        qkv_kernel,
        [owners, *blocks, gains, wq, wk, wv],
        prefetch=1,
        grid=(length // rows,),
        in_specs=[pl.BlockSpec((rows, cols), lambda g, o: (g, 0))] * len(blocks)
        + [pl.BlockSpec((len(blocks), 16, cols), lambda g, o: (0, 0, 0)), whole, whole, whole],
        out_specs=[
            pl.BlockSpec((rows, full), lambda g, o: (g, 0)),
            tile,
            tile,
            tile,
            pl.BlockSpec((8, rows), lambda g, o: (0, g)),
        ],
        out_shape=[
            jax.ShapeDtypeStruct((length, full), BF),
            jax.ShapeDtypeStruct((length, out), F32),
            jax.ShapeDtypeStruct((length, out), F32),
            jax.ShapeDtypeStruct((length, out), BF),
            jax.ShapeDtypeStruct((8, length), F32),
        ],
    )


def head_scales(sums_refs, full):
    total = sums_refs[0][...]
    for ref in sums_refs[1:]:
        total = total + ref[...]
    return jnp.transpose(lax.rsqrt(total / full + EPSILON))


def masked_scores(query, key, first, prefix):
    scores = dot_t(query, key) * (HEAD_DIM**-0.5)
    row = first + lax.broadcasted_iota(jnp.int32, scores.shape, 0)
    col = lax.broadcasted_iota(jnp.int32, scores.shape, 1)
    return jnp.where((col <= row) | (col < prefix), scores, MASKED)


def attn_forward_kernel(full, size, prefix_ref, q_ref, k_ref, v_ref, gq_ref, gk_ref, cos_ref, sin_ref, *rest):
    sums_refs, (att_ref, lse_ref, qr_ref, kr_ref) = rest[:size], rest[size:]
    length = q_ref.shape[0]
    rows = min(256, length)
    scales = head_scales(sums_refs, full)
    cosine, sine = cos_ref[...], sin_ref[...]
    for pre_ref, gain_ref, out_ref, at in ((q_ref, gq_ref, qr_ref, 0), (k_ref, gk_ref, kr_ref, 1)):
        field = pre_ref[...] * scales[:, at : at + 1] * gain_ref[...].astype(F32)
        out_ref[...] = (field * cosine + pltpu.roll(field, HEAD_DIM // 2, 1) * sine).astype(BF)
    prefix = prefix_ref[0]
    for first in range(0, length, rows):
        last = min(length, max(PREFIX_MAX, first + rows))
        scores = masked_scores(qr_ref[first : first + rows, :], kr_ref[:last, :], first, prefix)
        highest = jnp.max(scores, axis=1, keepdims=True)
        exponent = jnp.exp(scores - highest)
        total = jnp.sum(exponent, axis=1, keepdims=True)
        mixed = dot(exponent.astype(BF), v_ref[:last, :])
        att_ref[first : first + rows, :] = (mixed / total).astype(BF)
        lse_ref[first : first + rows, :] = jnp.broadcast_to(
            highest + jnp.log(total), (rows, HEAD_DIM)
        )


def attn_forward(prefix, q_pre, k_pre, v_rows, gq, gk, cosine, sine, sums):
    length, width = q_pre.shape
    full = width * len(sums)
    head = pl.BlockSpec((length, HEAD_DIM), lambda h, *_: (0, h))
    gain = pl.BlockSpec((1, HEAD_DIM), lambda h, *_: (0, h))
    table = pl.BlockSpec((length, HEAD_DIM), lambda h, *_: (0, 0))
    sums_spec = pl.BlockSpec((8, length), lambda h, *_: (0, 0))
    return launch(
        functools.partial(attn_forward_kernel, full, len(sums)),
        [prefix, q_pre, k_pre, v_rows, gq, gk, cosine, sine, *sums],
        prefetch=1,
            grid=(width // HEAD_DIM,),
            in_specs=[head, head, head, gain, gain, table, table] + [sums_spec] * len(sums),
            out_specs=[head] * 4,
        out_shape=[
            jax.ShapeDtypeStruct((length, width), BF),
            jax.ShapeDtypeStruct((length, width), F32),
            jax.ShapeDtypeStruct((length, width), BF),
            jax.ShapeDtypeStruct((length, width), BF),
        ],
    )


def attn_backward_kernel(
    full, size, prefix_ref, q_ref, k_ref, qr_ref, kr_ref, v_ref, do_ref, lse_ref, gq_ref, gk_ref,
    cos_ref, sin_ref, *rest,
):
    sums_refs, rest = rest[:size], rest[size:]
    dq_ref, dk_ref, dv_ref, gains_ref, rows_ref, kacc, vacc = rest
    head = pl.program_id(0)
    length = q_ref.shape[0]
    rows = min(256, length)
    prefix = prefix_ref[0]
    factor = HEAD_DIM**-0.5
    kacc[...] = jnp.zeros_like(kacc)
    vacc[...] = jnp.zeros_like(vacc)
    contract = (((0,), (0,)), ((), ()))
    for first in range(0, length, rows):
        last = min(length, max(PREFIX_MAX, first + rows))
        here = slice(first, first + rows)
        scores = masked_scores(qr_ref[here, :], kr_ref[:last, :], first, prefix)
        weights = jnp.exp(scores - lse_ref[here, 0:1])
        grad_rows = do_ref[here, :]
        weight_grad = dot_t(grad_rows, v_ref[:last, :])
        centred = jnp.sum(weight_grad * weights, axis=1, keepdims=True)
        score_grad = (weights * (weight_grad - centred)).astype(BF)
        dq_ref[here, :] = dot(score_grad, kr_ref[:last, :]) * factor
        kacc[:last, :] += lax.dot_general(
            score_grad, qr_ref[here, :], contract, preferred_element_type=F32
        )
        vacc[:last, :] += lax.dot_general(
            weights.astype(BF), grad_rows, contract, preferred_element_type=F32
        )
    dv_ref[...] = vacc[...].astype(BF)
    scales = head_scales(sums_refs, full)
    cosine, sine = cos_ref[...], sin_ref[...]
    which = lax.broadcasted_iota(jnp.int32, (8, length), 0)
    lanes = lax.broadcasted_iota(jnp.int32, (8, HEAD_DIM), 0)
    row_terms = jnp.zeros((8, length), F32)
    gain_terms = jnp.zeros((8, HEAD_DIM), F32)
    for at, (pre_ref, gain_ref, out_ref, raw) in enumerate(
        ((q_ref, gq_ref, dq_ref, dq_ref[...]), (k_ref, gk_ref, dk_ref, kacc[...] * factor))
    ):
        raw = raw.astype(BF).astype(F32)
        normed_grad = raw * cosine - pltpu.roll(raw, HEAD_DIM // 2, 1) * sine
        out_ref[...] = normed_grad
        product = normed_grad * pre_ref[...]
        row_terms = jnp.where(
            which == at, row_sums(product * gain_ref[...].astype(F32)), row_terms
        )
        gain_terms = jnp.where(
            lanes == at,
            jnp.sum(product * scales[:, at : at + 1], axis=0, keepdims=True),
            gain_terms,
        )
    gains_ref[...] = gain_terms
    product = dv_ref[...].astype(F32) * v_ref[...].astype(F32)
    row_terms = jnp.where(which == 2, row_sums(product), row_terms)

    @pl.when(head == 0)
    def _():
        rows_ref[...] = row_terms

    @pl.when(head > 0)
    def _():
        rows_ref[...] += row_terms


def attn_backward(
    prefix, q_pre, k_pre, q_rot, k_rot, v_rows, out_grad, lse, gq, gk, cosine, sine, sums, others=()
):
    length, width = q_pre.shape
    full = width * len(sums)
    head = pl.BlockSpec((length, HEAD_DIM), lambda h, *_: (0, h))
    gain = pl.BlockSpec((1, HEAD_DIM), lambda h, *_: (0, h))
    table = pl.BlockSpec((length, HEAD_DIM), lambda h, *_: (0, 0))
    sums_spec = pl.BlockSpec((8, length), lambda h, *_: (0, 0))
    return launch(
        functools.partial(attn_backward_kernel, full, len(sums)),
        [prefix, q_pre, k_pre, q_rot, k_rot, v_rows, out_grad, lse, gq, gk, cosine, sine, *sums],
        prefetch=1,
            grid=(width // HEAD_DIM,),
            in_specs=[head] * 7 + [gain, gain, table, table] + [sums_spec] * len(sums),
            out_specs=[head, head, head, pl.BlockSpec((8, HEAD_DIM), lambda h, *_: (0, h)), sums_spec],
            scratch=[pltpu.VMEM((length, HEAD_DIM), F32)] * 2,
        out_shape=[
            jax.ShapeDtypeStruct((length, width), F32),
            jax.ShapeDtypeStruct((length, width), F32),
            jax.ShapeDtypeStruct((length, width), BF),
            jax.ShapeDtypeStruct((8, width), F32),
            jax.ShapeDtypeStruct((8, length), F32),
        ],
        others=others,
    )


def norm_back_kernel(
    full, size, q_ref, k_ref, dq_ref, dk_ref, dv_ref, gq_ref, gk_ref, branch_ref, *rest
):
    sums_refs, back_refs, (out_ref, stat_ref, copy_ref) = rest[:size], rest[size : 2 * size], rest[2 * size :]
    copy_ref[...] = branch_ref[...]
    width = q_ref.shape[1]
    scales = head_scales(sums_refs, full)
    back = back_refs[0][...]
    squares = sums_refs[0][...]
    for ref, sums_ref in zip(back_refs[1:], sums_refs[1:], strict=True):
        back = back + ref[...]
        squares = squares + sums_ref[...]
    scale = lax.rsqrt(squares / full + EPSILON)
    along = scale * back - scale * scale * scale * (back / full) * squares
    stat_ref[...] = jnp.broadcast_to(along[0:1] + along[1:2] + back[2:3], stat_ref.shape)
    back = jnp.transpose(back)
    grads = []
    for at, (pre_ref, grad_ref, gain_ref) in enumerate(
        ((q_ref, dq_ref, gq_ref), (k_ref, dk_ref, gk_ref))
    ):
        scale = scales[:, at : at + 1]
        pre = pre_ref[...]
        grad = (
            scale * gain_ref[...].astype(F32) * grad_ref[...]
            - pre * (scale * scale * scale * back[:, at : at + 1] / full)
        ).astype(BF)
        grads.append(grad)
    out_ref[:, :width] = grads[0]
    out_ref[:, width : 2 * width] = grads[1]
    out_ref[:, 2 * width :] = dv_ref[...]


def norm_back(q_pre, k_pre, dq, dk, dv, gq, gk, branch, sums, back):
    length, width = q_pre.shape
    full = width * len(sums)
    rows = min(256, length)
    tile = pl.BlockSpec((rows, width), lambda g: (g, 0))
    wide = pl.BlockSpec((rows, 3 * width), lambda g: (g, 0))
    gain = pl.BlockSpec((1, width), lambda g: (0, 0))
    chunk = branch.shape[0] * rows // length
    part = pl.BlockSpec((chunk, branch.shape[1]), lambda g: (g, 0))
    line = pl.BlockSpec((8, rows), lambda g: (0, g))
    return launch(
        functools.partial(norm_back_kernel, full, len(sums)),
        [q_pre, k_pre, dq, dk, dv, gq, gk, branch, *sums, *back],
        grid=(length // rows,),
        in_specs=[tile] * 5 + [gain, gain, part] + [line] * (2 * len(sums)),
        out_specs=[wide, line, part],
        out_shape=[
            jax.ShapeDtypeStruct((length, 3 * width), BF),
            jax.ShapeDtypeStruct((8, length), F32),
            jax.ShapeDtypeStruct(branch.shape, BF),
        ],

    )


def expert_kernel(step, aliased, chunk_ref, n2_ref, cot_ref, router_ref, keep_ref, wg_ref, wu_ref, wd_ref, *rest):
    rest = list(rest)
    own = step == 0
    res_ref = rest.pop(0) if own else None
    rest = rest[aliased:]
    h2t_ref, dg_ref, du_ref, n2t_ref, mix_ref, dn2_ref, probs_ref, mix, dn2, gates, gate_grads = rest
    expert = pl.program_id(0)
    blocks, rows, cols = cot_ref.shape
    lane = lax.broadcasted_iota(jnp.int32, (rows, 128), 1)

    @pl.when(expert == 0)
    def _():
        logits = jnp.where(lane < EXPERTS, dot(n2_ref[...], router_ref[...]), MASKED)
        exponent = jnp.exp(logits - jnp.max(logits, axis=1, keepdims=True))
        probs = exponent / jnp.sum(exponent, axis=1, keepdims=True)
        probs_ref[...] = probs
        gates[...] = probs * keep_ref[...]
        gate_grads[...] = jnp.zeros_like(gate_grads)
        n2t_ref[...] = jnp.transpose(n2_ref[...])
        dn2[...] = jnp.zeros_like(dn2)
        if own:
            mix[...] = res_ref[...]
        else:
            mix[...] = jnp.zeros_like(mix)

    normed = n2_ref[...]
    w_down = wd_ref[0]
    pre_gate = dot(normed, wg_ref[0])
    pre_up = dot(normed, wu_ref[0])
    back = dot_t(cot_ref[0], w_down[:, :cols])
    for t in range(1, blocks):
        back = back + dot_t(cot_ref[t], w_down[:, t * cols : (t + 1) * cols])
    here = lane == expert
    gate = jnp.sum(jnp.where(here, gates[...], 0.0), axis=1, keepdims=True)
    sigmoid = jax.nn.sigmoid(pre_gate)
    activated = pre_gate * sigmoid
    hidden = (activated * pre_up).astype(BF).astype(F32)
    gate_grad = jnp.sum(back * hidden, axis=1, keepdims=True)
    gate_grads[...] += jnp.where(here, gate_grad * keep_ref[...], 0.0)
    back = back * gate
    h2 = (hidden * gate).astype(BF)
    dg = (back * pre_up * sigmoid * (1.0 + pre_gate * (1.0 - sigmoid))).astype(BF)
    du = (back * activated).astype(BF)
    h2t_ref[...] = jnp.transpose(h2)
    dg_ref[...] = dg
    du_ref[...] = du
    mix[...] += dot(h2, w_down)
    dn2[...] += dot_t(dg, wg_ref[0]) + dot_t(du, wu_ref[0])

    @pl.when(expert == EXPERTS - 1)
    def _():
        dn2_ref[:, : blocks * cols] = dn2[...].astype(BF)
        high = gate_grads[...].astype(BF).astype(F32)
        low = gate_grads[...] - high
        if step:
            high = pltpu.roll(high, GROUP * 2 * step, 1)
        low = pltpu.roll(low, GROUP * (2 * step + 1), 1)
        dn2_ref[:, blocks * cols :] = (high + low).astype(BF)
        for t in range(blocks):
            mix_ref[t] = mix[:, t * cols : (t + 1) * cols].astype(BF)


def expert_call(step, chunk, n2, cot, router, keep, wg, wu, wd, residual, carried):
    rows, full = n2.shape
    blocks, length, cols = cot.shape
    hidden = wg.shape[2]
    own = step == 0
    in_specs = [
        pl.BlockSpec((rows, full), lambda e, c: (0, 0)),
        pl.BlockSpec((blocks, rows, cols), lambda e, c: (0, c[0], 0)),
        pl.BlockSpec((full, 128), lambda e, c: (0, 0)),
        pl.BlockSpec((rows, 128), lambda e, c: (c[0], 0)),
        pl.BlockSpec((1, full, hidden), lambda e, c: (e, 0, 0)),
        pl.BlockSpec((1, full, hidden), lambda e, c: (e, 0, 0)),
        pl.BlockSpec((1, hidden, full), lambda e, c: (e, 0, 0)),
    ]
    operands = [chunk, n2, cot, router, keep, wg, wu, wd]
    if own:
        in_specs.append(pl.BlockSpec((rows, full), lambda e, c: (0, 0)))
        operands.append(residual)
    aliases = {len(operands) + k: k for k in range(len(carried))}
    in_specs += [pl.BlockSpec(memory_space=pl.ANY)] * len(carried)
    operands += list(carried)
    slab = pl.BlockSpec((rows, hidden), lambda e, c: (c[0], e))
    return launch(
        functools.partial(expert_kernel, step, len(carried)),
        [*operands],
        prefetch=1,
            grid=(EXPERTS,),
            in_specs=in_specs,
            out_specs=[
                pl.BlockSpec((hidden, rows), lambda e, c: (e, c[0])),
                slab,
                slab,
                pl.BlockSpec((full, rows), lambda e, c: (0, c[0])),
                pl.BlockSpec((blocks, rows, cols), lambda e, c: (0, c[0], 0)),
                pl.BlockSpec((rows, full + 128), lambda e, c: (0, 0)),
                pl.BlockSpec((rows, 128), lambda e, c: (0, 0)),
            ],
            scratch=[
                pltpu.VMEM((rows, full), F32),
                pltpu.VMEM((rows, full), F32),
                pltpu.VMEM((rows, 128), F32),
                pltpu.VMEM((rows, 128), F32),
            ],
        out_shape=[
            jax.ShapeDtypeStruct((EXPERTS * hidden, length), BF),
            jax.ShapeDtypeStruct((length, EXPERTS * hidden), BF),
            jax.ShapeDtypeStruct((length, EXPERTS * hidden), BF),
            jax.ShapeDtypeStruct((full, length), BF),
            jax.ShapeDtypeStruct((blocks, length, cols), BF),
            jax.ShapeDtypeStruct((rows, full + 128), BF),
            jax.ShapeDtypeStruct((rows, 128), F32),
        ],
        aliases=aliases,

        token=6,
    )


def arrange_kernel(owners_ref, *refs):
    blocks, (branch_ref, rows_ref, out_ref) = refs[:-3], refs[-3:]
    for k, ref in enumerate(blocks):
        rows_ref[owners_ref[k]] = ref[...]
    out_ref[...] = branch_ref[...]


def arrange(owners, blocks, branch):
    rows, width = blocks[0].shape
    full = branch.shape[1]
    chunk = rows // 4
    return launch(
        arrange_kernel,
        [owners, *blocks, branch],
        prefetch=1,
        grid=(4,),
        in_specs=[pl.BlockSpec((chunk, width), lambda g, o: (g, 0))] * len(blocks)
        + [pl.BlockSpec((chunk, full), lambda g, o: (g, 0))],
        out_specs=[
            pl.BlockSpec((len(blocks), chunk, width), lambda g, o: (0, g, 0)),
            pl.BlockSpec((chunk, full), lambda g, o: (g, 0)),
        ],
        out_shape=[
            jax.ShapeDtypeStruct((len(blocks), rows, width), BF),
            jax.ShapeDtypeStruct((rows, full), BF),
        ],
    )


def gate_up_kernel(n2t_ref, dg_ref, du_ref, out_ref):
    turned = n2t_ref[...]
    out_ref[0, 0] = dot(turned, dg_ref[...]).astype(BF)
    out_ref[1, 0] = dot(turned, du_ref[...]).astype(BF)


def gate_up_grads(n2t, dg, du):
    full, length = n2t.shape
    hidden = dg.shape[1] // EXPERTS
    slab = pl.BlockSpec((length, hidden), lambda e: (0, e))
    return launch(
        gate_up_kernel,
        [n2t, dg, du],
        grid=(EXPERTS,),
        in_specs=[pl.BlockSpec((full, length), lambda e: (0, 0)), slab, slab],
        out_specs=pl.BlockSpec((2, 1, full, hidden), lambda e: (0, e, 0, 0)),
        out_shape=jax.ShapeDtypeStruct((2, EXPERTS, full, hidden), BF),
    )


def down_kernel(table_ref, h2t_ref, cot_ref, out_ref):
    cols = cot_ref.shape[2]
    for t in range(cot_ref.shape[0]):
        out_ref[0, :, t * cols : (t + 1) * cols] = dot(h2t_ref[...], cot_ref[t]).astype(BF)


def down_grads(table, h2t, cot, n):
    wide, length = h2t.shape
    blocks, _, cols = cot.shape
    rows = wide // n
    steps = n // 2
    return launch(
        down_kernel,
        [table, h2t, cot],
        prefetch=1,
        grid=(steps,),
        in_specs=[
            pl.BlockSpec((rows, length), lambda g, t: (t[g], 0)),
            pl.BlockSpec((blocks, length, cols), lambda g, t: (0, 0, 0)),
        ],
        out_specs=pl.BlockSpec((1, rows, blocks * cols), lambda g, t: (g, 0, 0)),
        out_shape=jax.ShapeDtypeStruct((steps, rows, blocks * cols), BF),
    )


def middle_kernel(size, owners_ref, *refs):
    heads, x_refs = refs[:size], refs[size : 2 * size]
    wo_ref, gain_ref, res_ref, n2_ref = refs[2 * size :]
    step = pl.program_id(0)
    cols = x_refs[0].shape[1]
    width = heads[0].shape[1]

    @pl.when(step == 0)
    def _():
        for k, ref in enumerate(x_refs):
            first = pl.multiple_of(owners_ref[k] * cols, 128)
            res_ref[:, pl.ds(first, cols)] = ref[...].astype(F32)

    weights = wo_ref[...].reshape(width, -1)
    for k, ref in enumerate(heads):

        @pl.when(step == k)
        def _(ref=ref):
            res_ref[...] += dot(ref[...], weights)

    @pl.when(step == size - 1)
    def _():
        residual = res_ref[...]
        scale = lax.rsqrt(jnp.mean(residual * residual, axis=1, keepdims=True) + EPSILON)
        for t in range(size):
            here = slice(t * cols, (t + 1) * cols)
            gain = gain_ref[t, 1:2, :].astype(F32)
            n2_ref[:, here] = (residual[:, here] * scale * gain).astype(BF)


def middle(owners, attended, received, w_out, x_blocks, gains):
    size = len(x_blocks)
    groups, _, part, full = w_out.shape
    width, cols = groups * part, full // size
    rows = attended.shape[0] // size
    return launch(
        functools.partial(middle_kernel, size),
        [owners, attended, *received, *x_blocks, w_out, gains],
        prefetch=1,
        grid=(size,),
        in_specs=[pl.BlockSpec((rows, width), lambda t, o: (o[0], 0))]
        + [pl.BlockSpec((rows, width), lambda t, o: (0, 0))] * (size - 1)
        + [pl.BlockSpec((rows, cols), lambda t, o: (o[0], 0))] * size
        + [
            pl.BlockSpec((groups, 1, part, full), lambda t, o: (0, o[t], 0, 0)),
            pl.BlockSpec((size, 16, cols), lambda t, o: (0, 0, 0)),
        ],
        out_specs=[pl.BlockSpec((rows, full), lambda t, o: (0, 0))] * 2,
        out_shape=[
            jax.ShapeDtypeStruct((rows, full), F32),
            jax.ShapeDtypeStruct((rows, full), BF),
        ],
    )


def middle_back_kernel(
    mine_ref, own_ref, received_ref, probs_ref, router_ref, res_ref, n2_ref, cot_ref, gain_ref, wo_ref,
    branch_ref, out_ref, parts_ref,
):
    step = pl.program_id(0)
    blocks, rows, cols = cot_ref.shape
    full = blocks * cols

    @pl.when(step == 0)
    def _():
        probs = probs_ref[...]
        parts = own_ref[:, full:].astype(F32) + received_ref[:, full:].astype(F32)
        prob_grad = parts
        for group in range(1, 2 * blocks):
            prob_grad = prob_grad + pltpu.roll(parts, 128 - GROUP * group, 1)
        lane = lax.broadcasted_iota(jnp.int32, (rows, 128), 1)
        prob_grad = jnp.where(lane < EXPERTS, prob_grad, 0.0)
        centred = jnp.sum(prob_grad * probs, axis=1, keepdims=True)
        logit_grad = (probs * (prob_grad - centred)).astype(BF)
        grad = (
            own_ref[:, :full].astype(F32)
            + received_ref[:, :full].astype(F32)
            + dot_t(logit_grad, router_ref[...])
        )
        residual = res_ref[...]
        scale = lax.rsqrt(jnp.mean(residual * residual, axis=1, keepdims=True) + EPSILON)
        stat = jnp.zeros((rows, 1), F32)
        for t in range(blocks):
            here = slice(t * cols, (t + 1) * cols)
            gain = gain_ref[t, 1:2, :].astype(F32)
            stat = stat + jnp.sum(residual[:, here] * gain * grad[:, here], axis=1, keepdims=True)
        stat = scale * scale * scale * stat / full
        for t in range(blocks):
            here = slice(t * cols, (t + 1) * cols)
            gain = gain_ref[t, 1:2, :].astype(F32)
            branch_ref[:, here] = (
                cot_ref[t].astype(F32) + scale * gain * grad[:, here] - residual[:, here] * stat
            ).astype(BF)
        router_part = lax.dot_general(
            logit_grad, n2_ref[...], (((0,), (0,)), ((), ())), preferred_element_type=F32
        )[:8]
        norm_part = jnp.sum(grad * residual * scale, axis=0, keepdims=True)
        which = lax.broadcasted_iota(jnp.int32, (8, full), 0)
        parts_ref[...] = jnp.where(which == EXPERTS, norm_part, router_part)

    out_ref[0] = dot_t(branch_ref[...], wo_ref[...].reshape(-1, full)).astype(BF)


def middle_back(mine, own, received, probs, router, residual, n2, cot, gains, w_out):
    blocks, _, cols = cot.shape
    rows, full = residual.shape
    groups, _, part, _ = w_out.shape
    width = groups * part
    whole = pl.BlockSpec((rows, full), lambda t, m: (0, 0))
    wide = pl.BlockSpec((rows, full + 128), lambda t, m: (0, 0))
    lanes = pl.BlockSpec((rows, 128), lambda t, m: (0, 0))
    return launch(
        middle_back_kernel,
        [mine, own, received, probs, router, residual, n2, cot, gains, w_out],
        prefetch=1,
            grid=(blocks,),
            in_specs=[
                wide,
                wide,
                lanes,
                pl.BlockSpec((full, 128), lambda t, m: (0, 0)),
                whole,
                whole,
                pl.BlockSpec((blocks, rows, cols), lambda t, m: (0, m[0], 0)),
                pl.BlockSpec((blocks, 16, cols), lambda t, m: (0, 0, 0)),
                pl.BlockSpec((groups, 1, part, full), lambda t, m: (0, lax.rem(m[0] + t, blocks), 0, 0)),
            ],
            out_specs=[
                whole,
                pl.BlockSpec((1, rows, width), lambda t, m: (t, 0, 0)),
                pl.BlockSpec((8, full), lambda t, m: (0, 0)),
            ],
        out_shape=[
            jax.ShapeDtypeStruct((rows, full), BF),
            jax.ShapeDtypeStruct((blocks, rows, width), BF),
            jax.ShapeDtypeStruct((8, full), F32),
        ],
    )


def reversed_bits(at, bits):
    return sum(((at >> b) & 1) << (bits - 1 - b) for b in range(bits)) if bits else at


def column_grad_kernel(left_ref, right_ref, w_ref, out_ref, gain_ref):
    product = dot(jnp.transpose(left_ref[...]), right_ref[...])
    out_ref[...] = product.astype(BF)
    gain_ref[...] = jnp.broadcast_to(row_sums(product * w_ref[...].astype(F32)), gain_ref.shape)


def column_grads(left, right, weights):
    length, full = left.shape
    width = right.shape[1]
    piece = min(512, full)
    tile = pl.BlockSpec((piece, width), lambda g: (g, 0))
    return launch(
        column_grad_kernel,
        [left, right, weights],
        grid=(full // piece,),
        in_specs=[
            pl.BlockSpec((length, piece), lambda g: (0, g)),
            pl.BlockSpec((length, width), lambda g: (0, 0)),
            tile,
        ],
        out_specs=[tile, pl.BlockSpec((8, piece), lambda g: (0, g))],
        out_shape=[
            jax.ShapeDtypeStruct((full, width), BF),
            jax.ShapeDtypeStruct((8, full), F32),
        ],
    )


def row_grad_kernel(rows_ref, left_ref, *rest):
    blocks, (out_ref, turned_left) = rest[:-2], rest[-2:]
    rows = blocks[0].shape[0]

    @pl.when(pl.program_id(0) == 0)
    def _():
        for k in range(len(blocks)):
            first = pl.multiple_of(rows_ref[k] * rows, rows)
            turned_left[:, k * rows : (k + 1) * rows] = jnp.transpose(
                left_ref[pl.ds(first, rows), :]
            )

    total = None
    for k, block in enumerate(blocks):
        term = dot(turned_left[:, k * rows : (k + 1) * rows], block[...])
        total = term if total is None else total + term
    out_ref[...] = total.astype(BF)


def row_grads(owners, left, blocks):
    length, width = left.shape
    rows, full = blocks[0].shape
    piece = min(512, full)
    return launch(
        row_grad_kernel,
        [owners, left, *blocks],
        prefetch=1,
        grid=(full // piece,),
        in_specs=[pl.BlockSpec((length, width), lambda g, o: (0, 0))]
        + [pl.BlockSpec((rows, piece), lambda g, o: (0, g))] * len(blocks),
        out_specs=pl.BlockSpec((width, piece), lambda g, o: (0, g)),
        out_shape=jax.ShapeDtypeStruct((width, full), BF),
        scratch=[pltpu.VMEM((width, length), BF)],
    )


def input_kernel(owner_ref, grad_ref, w_ref, *rest):
    total = dot_t(grad_ref[...], w_ref[...])
    if len(rest) == 2:
        total = total + rest[0][...].astype(F32)
    rest[-1][...] = total.astype(BF)


def input_grads(owner, cols, grad, w_all, received=None, work=1):
    length, width = grad.shape
    rows = min(256, length)
    tile = pl.BlockSpec((rows, cols), lambda g, o: (g, 0))
    return launch(
        input_kernel,
        [owner, grad, w_all, *([] if received is None else [received])],
        prefetch=1,
            grid=(length // rows,),
            in_specs=[
                pl.BlockSpec((rows, width), lambda g, o: (g, 0)),
                pl.BlockSpec((cols, width), lambda g, o: (o[0], 0)),
            ]
            + ([] if received is None else [tile]),
            out_specs=tile,
        out_shape=jax.ShapeDtypeStruct((length, cols), BF),

        work=work,
    )


def mix_kernel(owner_ref, mix_ref, *rest):
    if len(rest) == 1:
        rest[0][...] = mix_ref[0]
    else:
        rest[1][...] = added(mix_ref[0], rest[0][...])


def mix_block(owner, mix, received=None, work=1):
    blocks, length, cols = mix.shape
    chunk = length // 4
    tile = pl.BlockSpec((chunk, cols), lambda g, o: (g, 0))
    return launch(
        mix_kernel,
        [owner, mix, *([] if received is None else [received])],
        prefetch=1,
            grid=(4,),
            in_specs=[pl.BlockSpec((1, chunk, cols), lambda g, o: (o[0], g, 0))]
            + ([] if received is None else [tile]),
            out_specs=tile,
        out_shape=jax.ShapeDtypeStruct((length, cols), BF),
        work=work,
    )


def final_kernel(
    full, owners_ref, grad_ref, w_ref, received_ref, tokens_ref, sums_ref, stat_ref, gain_ref, *rest
):
    blocks, out_ref = rest[:-1], rest[-1]
    step = pl.program_id(0)
    branch = blocks[0][...]
    for k in range(1, len(blocks)):
        branch = jnp.where(step == k, blocks[k][...], branch)
    scale = lax.rsqrt(sums_ref[...] / full + EPSILON)
    scale_one = jnp.transpose(scale)[:, 2:3]
    stat = jnp.transpose(stat_ref[...])[:, 0:1] / full * scale_one * scale_one
    normed_grad = dot_t(grad_ref[...], w_ref[...]) + received_ref[...].astype(F32)
    out_ref[...] = (
        branch.astype(F32)
        + scale_one * gain_ref[...].astype(F32) * normed_grad
        - tokens_ref[...].astype(F32) * stat
    )


def final_grads(owners, grad, w_all, received, tokens, sums, stat, gain, blocks):
    length, cols = tokens.shape
    width = grad.shape[1]
    rows = length // len(blocks)
    tile = pl.BlockSpec((rows, cols), lambda k, o: (o[k], 0))
    line = pl.BlockSpec((8, rows), lambda k, o: (0, o[k]))
    return launch(
        functools.partial(final_kernel, cols * len(blocks)),
        [owners, grad, w_all, received, tokens, sums, stat, gain, *blocks],
        prefetch=1,
            grid=(len(blocks),),
            in_specs=[
                pl.BlockSpec((rows, width), lambda k, o: (o[k], 0)),
                pl.BlockSpec((cols, width), lambda k, o: (o[0], 0)),
                tile,
                tile,
                line,
                line,
                pl.BlockSpec((1, cols), lambda k, o: (0, 0)),
            ]
            + [pl.BlockSpec((rows, cols), lambda k, o: (0, o[0]))] * len(blocks),
            out_specs=tile,
        out_shape=jax.ShapeDtypeStruct((length, cols), F32),
    )


def piece_specs(shape, steps):
    block = (1,) + shape
    return [
        pl.BlockSpec(block, lambda a, pos: (jnp.minimum(pos[a], steps - 1), 0, 0)),
        pl.BlockSpec(block, lambda a, pos: (jnp.maximum(pos[a] - steps, 0), 0, 0)),
    ]


def pieces_kernel(steps, pos_ref, low_ref, high_ref, out_ref):
    low = pos_ref[pl.program_id(0)] < steps
    out_ref[...] = jnp.where(low, low_ref[0].astype(F32), high_ref[0].astype(F32))


def widen_pieces(pos, halves, n):
    steps, rows, width = halves[0].shape
    return launch(
        functools.partial(pieces_kernel, steps),
        [pos, *halves],
        prefetch=1,
        grid=(n,),
        in_specs=piece_specs((rows, width), steps),
        out_specs=pl.BlockSpec((rows, width), lambda a, pos: (a, 0)),
        out_shape=jax.ShapeDtypeStruct((rows * n, width), F32),
    )


def projections_kernel(sum_ref, q_ref, k_ref, v_ref):
    width = q_ref.shape[1]
    for at, out_ref in enumerate((q_ref, k_ref, v_ref)):
        out_ref[...] = sum_ref[:, at * width : (at + 1) * width].astype(F32)


def widen_projections(total):
    full, width = total.shape
    out = width // 3
    piece = min(256, full)
    tile = pl.BlockSpec((piece, out), lambda g: (g, 0))
    return launch(
        projections_kernel,
        [total],
        grid=(full // piece,),
        in_specs=[pl.BlockSpec((piece, width), lambda g: (g, 0))],
        out_specs=[tile] * 3,
        out_shape=[jax.ShapeDtypeStruct((full, out), F32)] * 3,
    )


def experts_kernel(held_ref, gate_ref, up_ref):
    gate_ref[0] = held_ref[0, 0].astype(F32)
    up_ref[0] = held_ref[1, 0].astype(F32)


def widen_experts(held):
    _, experts, full, hidden = held.shape
    tall = pl.BlockSpec((1, full, hidden), lambda e: (e, 0, 0))
    return launch(
        experts_kernel,
        [held],
        grid=(experts,),
        in_specs=[pl.BlockSpec((2, 1, full, hidden), lambda e: (0, e, 0, 0))],
        out_specs=[tall, tall],
        out_shape=[jax.ShapeDtypeStruct((experts, full, hidden), F32)] * 2,
    )


def kept_experts(routes, order):
    length = routes.shape[0]
    token, which = order // TOP, order % TOP
    onehot = (token[:, None] == jnp.arange(length, dtype=jnp.int32)[None, :]).astype(BF)
    named = (routes[:, :, None] == jnp.arange(8, dtype=jnp.int32)).astype(BF).reshape(length, TOP * 8)
    ordered = dot(onehot, named).reshape(-1, TOP, 8)
    choose = jnp.sum(
        jnp.where(which[:, None, None] == jnp.arange(TOP)[None, :, None], ordered, 0.0), axis=1
    )
    kept = jnp.where(jnp.cumsum(choose, axis=0) <= CAP, choose, 0.0).astype(BF)
    kept = jnp.pad(kept, ((0, 0), (0, 120)))
    return lax.dot_general(onehot, kept, (((0,), (0,)), ((), ())), preferred_element_type=F32)


def on_device(
    tokens, cotangent, norm1_gain, w_query, w_key, w_value, query_gain, key_gain, w_output,
    norm2_gain, router, w_gate, w_up, w_down, routes, prefix, slot_order,
):
    size, n = lax.axis_size("tensor"), lax.axis_size("dp")
    mine, group = lax.axis_index("tensor"), lax.axis_index("dp")
    length, cols = tokens.shape
    full = cols * size
    rows = length // size
    steps = range(1, size)
    Chain.token = None

    def add(*terms):
        return functools.reduce(jnp.add, terms)

    here = mine.astype(jnp.int32)[None]

    rel = rel_table(swap_masks(n))
    table = jnp.asarray(rel, jnp.int32) ^ group
    positions = jnp.asarray([rel.index(v) for v in range(n)], jnp.int32)[
        jnp.arange(n, dtype=jnp.int32) ^ group
    ]
    half = n // 2
    owners = ((mine - jnp.arange(size)) % size).astype(jnp.int32)

    def owner(step):
        return owners[step : step + 1]

    def by_owner(own, *others):
        return place(size, [b[None] for b in others], mine, own[None])

    part = w_output.shape[0] // n
    gains = jnp.concatenate([norm1_gain[None], norm2_gain[None], jnp.zeros((14, cols), BF)])
    w_piece = jnp.concatenate(
        [
            lax.dynamic_slice_in_dim(w_output, group * part, part, 0),
            jnp.pad(gains, ((0, 0), (0, full - cols))),
        ]
    )
    w_blocks, x_blocks = [w_piece], [tokens]
    for step in steps:
        w_blocks.append(send(w_blocks[-1], 1, size))
    w_mixed = by_owner(*w_blocks)
    w_out = lax.all_gather(w_mixed[:, :part], "dp", axis=0)
    gains = w_mixed[:, part:, :cols]
    w_all = side_by_side([w_query, w_key, w_value])
    keep = kept_experts(routes, slot_order[0])
    router_wide = jnp.pad(router, ((0, 0), (0, 128 - EXPERTS)))
    halfway = HEAD_DIM // 2
    freqs = ROPE_BASE ** (-(jnp.arange(halfway, dtype=F32) * 2.0 / HEAD_DIM))
    angles = jnp.arange(length, dtype=F32)[:, None] * freqs[None, :]
    cosine = jnp.concatenate([jnp.cos(angles)] * 2, axis=1)
    sine = jnp.concatenate([-jnp.sin(angles), jnp.sin(angles)], axis=1)
    for step in steps:
        x_blocks.append(send(x_blocks[-1], 1, size))
    late_cot = copied(cotangent, (x_blocks[-1], keep, router_wide, cosine, sine))
    cot = lax.all_gather(late_cot, "tensor", axis=0)
    normed_one, q_pre, k_pre, v_rows, own_sums = qkv_call(
        owners, x_blocks, gains, w_query, w_key, w_value
    )
    sums = [own_sums] + [send(own_sums, step, size) for step in steps]

    gq, gk = query_gain[None], key_gain[None]
    attended, lse, q_rot, k_rot = attn_forward(
        prefix, q_pre, k_pre, v_rows, gq, gk, cosine, sine, sums
    )

    received = [
        send(lax.dynamic_slice_in_dim(attended, (mine + step) % size * rows, rows, 0), step, size)
        for step in steps
    ]
    residual, normed_two = middle(owners, attended, received, w_out, x_blocks, gains)

    def add_wide(a, b, work=1):
        return add_blocks(a[None], b[None], work)[0]

    chunks = [copied(normed_two, (cot,))]
    chunks.append(send(chunks[0], 1, size))
    carried, later, dn2_flying = (), [], None
    for step in range(size):
        outs = expert_call(
            step, owner(step), chunks[step], cot, router_wide, keep, w_gate, w_up, w_down,
            residual if step == 0 else None, carried,
        )
        carried = outs[:5]
        if step < size - 2:
            chunks.append(send(copied(chunks[-1]), 1, size))
        if step == 0:
            own_dn2, expert_probs = outs[5:]
        else:
            later.append(outs[5])
        if step > 3:
            dn2_flying = send(add_wide(later.pop(0), dn2_flying), 1, size)
        elif step == min(3, size - 1):
            dn2_flying = send(copied(later.pop(0)), 1, size)
    h2t, dg, du, n2t, mix = carried

    expert_grads = lax.psum(gate_up_grads(n2t, dg, du), "dp")
    dn2_flying = send(add_wide(later.pop(0), dn2_flying, LONG), 1, size)
    sum_down = Sum(n, 2, down_grads(table[half:], h2t, cot, n))
    sum_down.keep = down_grads(table[:half], h2t, cot, n)
    for term in later:
        dn2_flying = send(add_wide(term, dn2_flying), 1, size)
    sum_down.step()

    branch_rows, out_rows, small = middle_back(
        here, own_dn2, dn2_flying, expert_probs, router_wide, residual, normed_two, cot, gains, w_out
    )

    received = [send(out_rows[step], step, size) for step in steps]
    out_grad, branch_rows = arrange(owners, [out_rows[0]] + received, branch_rows)
    branch_blocks = [branch_rows, send(branch_rows, 1, size)]
    dq, dk, dv, gain_grads, own_back = attn_backward(
        prefix, q_pre, k_pre, q_rot, k_rot, v_rows, out_grad.reshape(length, -1), lse, gq, gk,
        cosine, sine, sums,
    )
    back = [own_back] + [send(own_back, step, size) for step in steps]
    sum_down.step()
    grad_qkv, stat_one, branch_copy = norm_back(
        q_pre, k_pre, dq, dk, dv, gq, gk, branch_blocks[1], sums, back
    )
    branch_blocks.append(send(branch_copy, 1, size))
    in_grads, gain_part = column_grads(normed_one, grad_qkv, w_all)
    small = jnp.concatenate([small[:7], gain_part[7:]])
    small = add(small, *[send(small, step, size) for step in steps])
    dn1 = input_grads(owner(1), cols, grad_qkv, w_all)
    branch_copy, dn1 = copied_pair(branch_blocks[2], dn1, 1)
    branch_blocks.append(send(branch_copy, 1, size))
    dn1_flying = send(dn1, 1, size)
    sum_down.step()
    for step in range(4, size):
        branch_blocks.append(send(copied(branch_blocks[-1]), 1, size))
    out_grads = row_grads(owners, attended, branch_blocks)
    packed = jnp.concatenate([small, gain_grads], axis=1)
    width = 3 * w_query.shape[1]
    extra = jnp.pad(packed.reshape(-1), (0, 32 * width - packed.size)).astype(BF).reshape(32, width)
    extra = copied(extra, (expert_grads,))
    in_grads, out_grads, extra = lax.psum((in_grads, out_grads, extra), "dp")
    mix_flying = send(mix_block(owner(1), mix, work=LONG), 1, size)
    for step in range(2, size):
        dn1_flying = send(input_grads(owner(step), cols, grad_qkv, w_all, dn1_flying), 1, size)
        sum_down.step()
        mix_flying = send(mix_block(owner(step), mix, mix_flying), 1, size)
    for _ in range(2 * len(swap_masks(n))):
        sum_down.step()

    grad_tokens = final_grads(
        owners, grad_qkv, w_all, dn1_flying, tokens, own_sums, stat_one, norm1_gain[None],
        branch_blocks,
    )
    grad_gate, grad_up = widen_experts(expert_grads)
    grad_down = widen_pieces(positions, sum_down.finish(), n).reshape(w_down.shape)

    mixed = mix_block(owner(0), mix, mix_flying)
    grad_query, grad_key, grad_value = widen_projections(in_grads)
    packed = extra.astype(F32).reshape(-1)[: packed.size].reshape(packed.shape)
    gain_total, packed = packed[:2, full:], packed[:, :full]
    grad_output = out_grads.astype(F32)

    grad_router = packed[:EXPERTS].T
    own = lax.dynamic_slice_in_dim(packed[EXPERTS:], mine * cols, cols, 1)
    grad_norm2_gain = own[0]
    grad_norm1_gain = own[1] / norm1_gain.astype(F32)
    grad_query_gain, grad_key_gain = gain_total[0], gain_total[1]
    return (
        mixed, grad_tokens, grad_norm1_gain, grad_query, grad_key, grad_value, grad_query_gain,
        grad_key_gain, grad_output, grad_norm2_gain, grad_router, grad_gate, grad_up, grad_down,
    )


def solution(mesh):
    rows, weight_cols, weight_rows = P("dp", "tensor"), P(None, "tensor"), P("tensor", None)
    vector, expert_cols, expert_rows = P("tensor"), P(None, None, "tensor"), P(None, "tensor", None)
    return jax.shard_map(
        on_device,
        mesh=mesh,
        in_specs=(
            rows, rows, vector, weight_cols, weight_cols, weight_cols, vector, vector, weight_rows,
            vector, P(), expert_cols, expert_cols, expert_rows, P("dp", None), P("dp"),
            P("dp", None),
        ),
        out_specs=(
            rows, rows, vector, weight_cols, weight_cols, weight_cols, vector, vector, weight_rows,
            vector, P(), expert_cols, expert_cols, expert_rows,
        ),
        check_vma=False,
    )
```

time: 847 us -> 787 us (0.929)
  Pallas kernels: 223 us -> 342 us
  waiting for transfers between devices: 395 us -> 317 us
  starting transfers between devices: 85.4 us -> 43.2 us
  other arithmetic: 46.5 us -> 13.4 us
  matrix products: 26.2 us -> 5.64 us
    pallas_call x18 -> x42, Pallas kernels: 223 us -> 342 us  [launch(): pl.pallas_call(kernel, grid_spec=pltpu.PrefetchScalarGridSpec(num_scalar_...]
    ppermute x30 -> x10, waiting for transfers between devices: 74.6 us -> 4.95 us  [swap(): return lax.ppermute(field, 'dp', [(at, at ^ mask) for at in range(n)])]
    convert_element_type x7 -> x1, other arithmetic: 30 us -> 4.14 us  [on_device(): grad_output = out_grads.astype(F32)]
    ppermute x39 -> x36, starting transfers between devices: 58.7 us -> 34.2 us  [send(): lax.ppermute(value, 'tensor', [(at, (at + step) % size) for at in range(s...]
    ppermute x39 -> x36, waiting for transfers between devices: 320 us -> 298 us  [send(): lax.ppermute(value, 'tensor', [(at, (at + step) % size) for at in range(s...]
    dot_general x4 -> x0, matrix products: 20.6 us -> none  [dot_t(): lax.dot_general(a, b, (((1,), (1,)), ((), ())), preferred_element_type=F32)]
    ppermute x30 -> x10, starting transfers between devices: 26.5 us -> 8.93 us  [swap(): return lax.ppermute(field, 'dp', [(at, at ^ mask) for at in range(n)])]
    all_gather x1, waiting for transfers between devices: 0.01 us -> 14.3 us  [on_device(): cot = lax.all_gather(late_cot, 'tensor', axis=0)]
  transfers between devices with their start and end apart: 72 -> 50, of which waited for: 34 -> 29; matrix products, arithmetic and copies ran while one was open for 10% -> 3% of each run, Pallas kernels for 27% -> 37%
where the time goes in v2:
time: 787 us; the launch traced here: 775 us
  Pallas kernels  342 us (43%)
  waiting for transfers between devices  317 us (40%)
  starting transfers between devices  43.2 us (5%)
  local copies, waits for them, and re-layouts  38.2 us (5%)
  between operations  15.5 us (2%)
  other arithmetic  13.4 us (2%)
    pallas_call x42, Pallas kernels, launch(): pl.pallas_call(kernel, grid_spec=pltpu.PrefetchScalarGridSpec(num_scalar_...  342 us
    ppermute x36, waiting for transfers between devices, send(): lax.ppermute(value, 'tensor', [(at, (at + step) % size) for at in range(s...  298 us
    ppermute x36, starting transfers between devices, send(): lax.ppermute(value, 'tensor', [(at, (at + step) % size) for at in range(s...  34.2 us
    unnamed x114, local copies, waits for them, and re-layouts  21.4 us
  transfers between devices with their start and end apart: 50, of which 29 were waited for; matrix products, arithmetic and copies ran while one was open for 3% of the time, Pallas kernels for 37%

profile of v2, /device:TPU:0, one launch (start us, length us, event | category | flops | bytes accessed | tf_op | source)
XLA Modules:
  0.0 775.2 jit_solution(7093048046150000989)
XLA Ops:
  13.9 8.5 %collective-permute-done.3 = bf16[80,2048]{1,0:T(8,128)(2,1)S(1)} collective-permute-done((bf16[80,2048]{1,0:T(8,128)(2,1)S(1)}, bf16[80,2048]{1,0:T(8,128)(2,1)S(1)}, u32[]{:S(2)}, u32[]{:S(2)}) %collective-permute-start.3) | collective-permute-done | bytes 327712 | tf_op jit(solution)/shard_map/ppermute | solution.py:80
  22.4 10.7 %collective-permute-done.4 = bf16[80,2048]{1,0:T(8,128)(2,1)S(1)} collective-permute-done((bf16[80,2048]{1,0:T(8,128)(2,1)S(1)}, bf16[80,2048]{1,0:T(8,128)(2,1)S(1)}, u32[]{:S(2)}, u32[]{:S(2)}) %collective-permute-start.4) | collective-permute-done | bytes 327712 | tf_op jit(solution)/shard_map/ppermute | solution.py:80
  33.1 9.7 %collective-permute-done.5 = bf16[80,2048]{1,0:T(8,128)(2,1)S(1)} collective-permute-done((bf16[80,2048]{1,0:T(8,128)(2,1)S(1)}, bf16[80,2048]{1,0:T(8,128)(2,1)S(1)}, u32[]{:S(2)}, u32[]{:S(2)}) %collective-permute-start.5) | collective-permute-done | bytes 327712 | tf_op jit(solution)/shard_map/ppermute | solution.py:80
  44.2 24.1 %collective-permute-done.refs_2_.refs_6_ = bf16[1024,512]{1,0:T(8,128)(2,1)S(1)} collective-permute-done((bf16[1024,512]{1,0:T(8,128)(2,1)S(1)}, bf16[1024,512]{1,0:T(8,128)(2,1)S(1)}, u32[]{:S(2)}, u32[]{:S(2)}) %collective-permute-start) | collective-permute-done | bytes 1048608 | tf_op jit(solution)/shard_map/ppermute | solution.py:80
  75.7 16.1 %collective-permute-done.1.refs_3_.refs_7_ = bf16[1024,512]{1,0:T(8,128)(2,1)} collective-permute-done((bf16[1024,512]{1,0:T(8,128)(2,1)S(1)}, bf16[1024,512]{1,0:T(8,128)(2,1)}, u32[]{:S(2)}, u32[]{:S(2)}) %collective-permute-start.1) | collective-permute-done | bytes 1048608 | tf_op jit(solution)/shard_map/ppermute | solution.py:80
  93.1 5.8 shard_map.290.refs_1_
  103.4 11.1 %collective-permute-done.2.refs_2_.refs_4_.refs_8_ = bf16[1024,512]{1,0:T(8,128)(2,1)S(1)} collective-permute-done((bf16[1024,512]{1,0:T(8,128)(2,1)}, bf16[1024,512]{1,0:T(8,128)(2,1)S(1)}, u32[]{:S(2)}, u32[]{:S(2)}) %collective-permute-start.2) | collective-permute-done | bytes 1048608 | tf_op jit(solution)/shard_map/ppermute | solution.py:80
  120.1 14.6 %shard_map.292 = (bf16[1024,2048]{1,0:T(8,128)(2,1)}, f32[1024,512]{1,0:T(8,128)}, f32[1024,512]{1,0:T(8,128)}, bf16[1024,512]{1,0:T(8,128)(2,1)}, f32[8,1024]{1,0:T(8,128)}) custom-call(s32[4]{0:T(128)} %and_select_fusion.refs_0_, bf16[1024,512]{1,0:T(8,128)(2,1)} %refs_4_.1, bf16[1024,512]{1,0:T(8,128)(2,1)} %copy-done.8, ...), custom_call_target="tpu_custom_call" | custom-call | flops 1 | bytes 1 | tf_op jit(solution)/shard_map/pallas_call | solution.py:42
  134.8 4.2 collective-permute-start.8
  143.3 14.1 %shard_map.293 = (bf16[1024,512]{1,0:T(8,128)(2,1)}, f32[1024,512]{1,0:T(8,128)}, bf16[1024,512]{1,0:T(8,128)(2,1)}, bf16[1024,512]{1,0:T(8,128)(2,1)}) custom-call(s32[1]{0:T(128)S(6)} %copy.79.refs_0_, f32[1024,512]{1,0:T(8,128)} %get-tuple-element.87.refs_1_.refs_0_, f32[1024,512]{1,0:T(8,128)} %get-tuple-element.88.refs_2_.refs_1_, ...), custom_call_target="tpu_custom_call" | custom-call | flops 1 | bytes 1 | tf_op jit(solution)/shard_map/pallas_call | solution.py:42
  161.2 3.5 collective-permute-start.11
  164.7 21.6 %collective-permute-done.10.refs_3_ = bf16[256,512]{1,0:T(8,128)(2,1)S(1)} collective-permute-done((bf16[256,512]{1,0:T(8,128)(2,1)S(1)}, bf16[256,512]{1,0:T(8,128)(2,1)S(1)}, u32[]{:S(2)}, u32[]{:S(2)}) %collective-permute-start.10) | collective-permute-done | bytes 262176 | tf_op jit(solution)/shard_map/ppermute | solution.py:80
  186.3 11.1 %collective-permute-done.9.refs_2_ = bf16[256,512]{1,0:T(8,128)(2,1)S(1)} collective-permute-done((bf16[256,512]{1,0:T(8,128)(2,1)S(1)}, bf16[256,512]{1,0:T(8,128)(2,1)S(1)}, u32[]{:S(2)}, u32[]{:S(2)}) %collective-permute-start.9) | collective-permute-done | bytes 262176 | tf_op jit(solution)/shard_map/ppermute | solution.py:80
  198.1 9.3 %shard_map.294 = (f32[256,2048]{1,0:T(8,128)}, bf16[256,2048]{1,0:T(8,128)(2,1)}) custom-call(s32[4]{0:T(128)} %and_select_fusion.refs_0_, bf16[1024,512]{1,0:T(8,128)(2,1)} %get-tuple-element.92.refs_1_, bf16[256,512]{1,0:T(8,128)(2,1)} %copy-done.36, bf16[256,512]{1,0:T(8,128)(2,1)} %copy-done.34, bf16[256,512]{1,0:T(8,128)(2,1)} %copy-done.35, ...), custom_call_target="tpu_custom_call" | custom-call | flops 1 | bytes 1 | tf_op jit(solution)/shard_map/pallas_call | solution.py:42
  207.4 14.3 %all-gather.4.cloned.1.call-done.refs_2_.refs_7_ = bf16[4,1024,512]{2,1,0:T(8,128)(2,1)} async-done(((bf16[1,1024,512]{2,1,0:T(8,128)(2,1)}), bf16[4,1024,512]{2,1,0:T(8,128)(2,1)}) %all-gather.4.cloned.1.call-update) | async-done | bytes 4194320 | tf_op jit(solution)/shard_map/all_gather | solution.py:1165
  225.7 19.2 %shard_map.296 = (bf16[1536,1024]{1,0:T(8,128)(2,1)}, bf16[1024,1536]{1,0:T(8,128)(2,1)}, bf16[1024,1536]{1,0:T(8,128)(2,1)}, bf16[2048,1024]{1,0:T(8,128)(2,1)}...) custom-call(s32[1]{0:T(128)} %get-tuple-element.183.refs_0_, ...), custom_call_target="tpu_custom_call" | custom-call | flops 1 | bytes 1 | tf_op jit(solution)/shard_map/pallas_call | solution.py:42
  244.9 7.0 collective-permute-done.12.refs_1_
  256.3 18.4 %shard_map.298 = (bf16[1536,1024]{1,0:T(8,128)(2,1)}, bf16[1024,1536]{1,0:T(8,128)(2,1)}, bf16[1024,1536]{1,0:T(8,128)(2,1)}, bf16[2048,1024]{1,0:T(8,128)(2,1)}...) custom-call(s32[1]{0:T(128)} %get-tuple-element.181.refs_0_, ...), custom_call_target="tpu_custom_call", output_to_operand_aliasing={{0}: (8, {}), {1}: (9, {}), {2}: (10, {}), {3}: (11, {}), {... | custom-call | flops 1 | bytes 1 | tf_op jit(solution)/shard_map/pallas_call | solution.py:42
  274.7 7.7 collective-permute-done.13.refs_1_
  286.9 18.5 %shard_map.300 = (bf16[1536,1024]{1,0:T(8,128)(2,1)}, bf16[1024,1536]{1,0:T(8,128)(2,1)}, bf16[1024,1536]{1,0:T(8,128)(2,1)}, bf16[2048,1024]{1,0:T(8,128)(2,1)}...) custom-call(s32[1]{0:T(128)} %get-tuple-element.180.refs_0_, ...), custom_call_target="tpu_custom_call", output_to_operand_aliasing={{0}: (8, {}), {1}: (9, {}), {2}: (10, {}), {3}: (11, {}), {... | custom-call | flops 1 | bytes 1 | tf_op jit(solution)/shard_map/pallas_call | solution.py:42
  305.4 6.6 collective-permute-done.14.refs_1_
  313.0 18.5 %shard_map.301 = (bf16[1536,1024]{1,0:T(8,128)(2,1)}, bf16[1024,1536]{1,0:T(8,128)(2,1)}, bf16[1024,1536]{1,0:T(8,128)(2,1)}, bf16[2048,1024]{1,0:T(8,128)(2,1)}...) custom-call(s32[1]{0:T(128)} %get-tuple-element.182.refs_0_, ...), custom_call_target="tpu_custom_call", output_to_operand_aliasing={{0}: (8, {}), {1}: (9, {}), {2}: (10, {}), {3}: (11, {}), {... | custom-call | flops 1 | bytes 1 | tf_op jit(solution)/shard_map/pallas_call | solution.py:42
  335.4 18.1 %shard_map.303.refs_2_ = bf16[2,6,2048,256]{3,2,1,0:T(8,128)(2,1)} custom-call(bf16[2048,1024]{1,0:T(8,128)(2,1)} %get-tuple-element.119.refs_0_, bf16[1024,1536]{1,0:T(8,128)(2,1)} %get-tuple-element.120.refs_1_, bf16[1024,1536]{1,0:T(8,128)(2,1)} %get-tuple-element.121.refs_2_, bf16[1,256,2176]{2,1,0:T(8,128)(2,1)} %shard_map.302.refs_3_), custom_call_target="tpu_custom_call" | custom-call | flops 1 | bytes 1 | tf_op jit(solution)/shard_map/pallas_call | solution.py:42
  353.5 6.9 collective-permute-done.15
  361.4 3.7 shard_map.304.refs_3_
  365.1 8.2 %shard_map.305.refs_3_ = bf16[4,192,2048]{2,1,0:T(8,128)(2,1)} custom-call(s32[4]{0:T(128)} %get-tuple-element.178.refs_0_, bf16[1536,1024]{1,0:T(8,128)(2,1)} %get-tuple-element.122.refs_1_, bf16[4,1024,512]{2,1,0:T(8,128)(2,1)} %all-gather.4.cloned.1.call-done.refs_2_.refs_7_, bf16[1,256,2176]{2,1,0:T(8,128)(2,1)} %shard_map.304.refs_3_), custom_call_target="tpu_custom_call" | custom-call | flops 1 | bytes 1 | tf_op jit(solution)/shard_map/pallas_call | solution.py:42
  374.5 8.6 %shard_map.306.refs_2_.refs_0_ = bf16[4,192,2048]{2,1,0:T(8,128)(2,1)} custom-call(s32[4]{0:T(128)} %get-tuple-element.179.refs_0_, bf16[1536,1024]{1,0:T(8,128)(2,1)} %get-tuple-element.122.refs_1_, bf16[4,1024,512]{2,1,0:T(8,128)(2,1)} %all-gather.4.cloned.1.call-done.refs_2_.refs_7_, bf16[4,192,2048]{2,1,0:T(8,128)(2,1)} %shard_map.305.refs_3_), custom_call_target="tpu_custom_call" | custom-call | flops 1 | bytes 1 | tf_op jit(solution)/shard_map/pallas_call | solution.py:42
  383.1 19.0 %collective-permute-done.16 = bf16[256,2176]{1,0:T(8,128)(2,1)S(1)} collective-permute-done((bf16[256,2176]{1,0:T(8,128)(2,1)S(1)}, bf16[256,2176]{1,0:T(8,128)(2,1)S(1)}, u32[]{:S(2)}, u32[]{:S(2)}) %collective-permute-start.16) | collective-permute-done | bytes 1114144 | tf_op jit(solution)/shard_map/ppermute | solution.py:80
  403.2 3.7 shard_map.307.refs_2_
  407.1 5.2 shard_map.308
  412.3 21.8 %collective-permute-done.17.refs_2_ = bf16[256,2176]{1,0:T(8,128)(2,1)S(1)} collective-permute-done((bf16[256,2176]{1,0:T(8,128)(2,1)}, bf16[256,2176]{1,0:T(8,128)(2,1)S(1)}, u32[]{:S(2)}, u32[]{:S(2)}) %collective-permute-start.17) | collective-permute-done | bytes 1114144 | tf_op jit(solution)/shard_map/ppermute | solution.py:80
  435.2 11.5 %shard_map.309 = (bf16[256,2048]{1,0:T(8,128)(2,1)}, bf16[4,256,512]{2,1,0:T(8,128)(2,1)}, f32[8,2048]{1,0:T(8,128)}) custom-call(s32[1]{0:T(128)} %bitcast.23.refs_0_, bf16[256,2176]{1,0:T(8,128)(2,1)} %get-tuple-element.114.refs_1_, bf16[256,2176]{1,0:T(8,128)(2,1)} %copy-done.15, f32[256,128]{1,0:T(8,128)} %get-tuple-element.95.refs_1_.refs_3_, ...), custom_call_target="tpu_custom_call" | custom-call | flops 1 | bytes 1 | tf_op jit(solution)/shard_map/pallas_call | solution.py:42
  448.7 3.8 collective-permute-start.21
  452.5 7.3 collective-permute-done.19.refs_2_
  459.8 7.1 collective-permute-done.20.refs_3_
  467.7 4.5 shard_map.310
  472.2 5.0 collective-permute-start.22
  479.7 19.0 %shard_map.311 = (f32[1024,512]{1,0:T(8,128)}, f32[1024,512]{1,0:T(8,128)}, bf16[1024,512]{1,0:T(8,128)(2,1)}, f32[8,512]{1,0:T(8,128)}, f32[8,1024]{1,0:T(8,128)}) custom-call(s32[1]{0:T(128)S(6)} %copy.79.refs_0_, f32[1024,512]{1,0:T(8,128)} %get-tuple-element.87.refs_1_.refs_0_, f32[1024,512]{1,0:T(8,128)} %get-tuple-element.88.refs_2_.refs_1_, ...), custom_call_target="tpu_custom_call" | custom-call | flops 1 | bytes 1 | tf_op jit(solution)/shard_map/pallas_call | solution.py:42
  504.7 4.0 shard_map.312
  509.7 7.1 shard_map.313
  516.9 12.6 %shard_map.314 = (bf16[2048,1536]{1,0:T(8,128)(2,1)}, f32[8,2048]{1,0:T(8,128)}) custom-call(bf16[1024,2048]{1,0:T(8,128)(2,1)} %get-tuple-element.91.refs_12_.refs_0_, bf16[1024,1536]{1,0:T(8,128)(2,1)} %get-tuple-element.140.refs_1_, bf16[2048,1536]{1,0:T(8,128)(2,1)} %bitcast.87), custom_call_target="tpu_custom_call" | custom-call | flops 1 | bytes 1 | tf_op jit(solution)/shard_map/pallas_call | solution.py:42
  529.5 6.2 shard_map.315.refs_2_
  536.6 6.5 collective-permute-done.31.refs_4_.refs_10_
  544.1 3.7 shard_map.316
  547.9 4.4 collective-permute-start.29
  553.8 22.3 %collective-permute-done.28 = f32[8,2048]{1,0:T(8,128)S(1)} collective-permute-done((f32[8,2048]{1,0:T(8,128)S(1)}, f32[8,2048]{1,0:T(8,128)S(1)}, u32[]{:S(2)}, u32[]{:S(2)}) %collective-permute-start.28) | collective-permute-done | bytes 65568 | tf_op jit(solution)/shard_map/ppermute | solution.py:80
  591.3 7.1 shard_map.318.refs_1_
  601.6 4.0 shard_map.320.refs_4_
  605.8 6.4 shard_map.321.refs_4_
  613.3 3.7 shard_map.322
  619.2 14.5 %collective-permute-done.35.refs_2_ = bf16[1024,512]{1,0:T(8,128)(2,1)S(1)} collective-permute-done((bf16[1024,512]{1,0:T(8,128)(2,1)}, bf16[1024,512]{1,0:T(8,128)(2,1)S(1)}, u32[]{:S(2)}, u32[]{:S(2)}) %collective-permute-start.35) | collective-permute-done | bytes 1048608 | tf_op jit(solution)/shard_map/ppermute | solution.py:80
  634.7 4.3 shard_map.323.refs_4_
  639.0 12.0 %collective-permute-done.42.refs_3_ = bf16[1024,512]{1,0:T(8,128)(2,1)S(1)} collective-permute-done((bf16[1024,512]{1,0:T(8,128)(2,1)}, bf16[1024,512]{1,0:T(8,128)(2,1)S(1)}, u32[]{:S(2)}, u32[]{:S(2)}) %collective-permute-start.42) | collective-permute-done | bytes 1048608 | tf_op jit(solution)/shard_map/ppermute | solution.py:80
  652.0 6.4 shard_map.324.refs_4_
  660.2 4.2 shard_map.325.refs_3_.refs_1_
  664.6 27.6 %collective-permute-done.39.refs_2_ = bf16[1024,512]{1,0:T(8,128)(2,1)S(1)} collective-permute-done((bf16[1024,512]{1,0:T(8,128)(2,1)S(1)}, bf16[1024,512]{1,0:T(8,128)(2,1)S(1)}, u32[]{:S(2)}, u32[]{:S(2)}) %collective-permute-start.39) | collective-permute-done | bytes 1048608 | tf_op jit(solution)/shard_map/ppermute | solution.py:80
  693.2 4.3 shard_map.326.refs_12_
  698.7 16.1 %collective-permute-done.45.refs_3_ = bf16[1024,512]{1,0:T(8,128)(2,1)S(1)} collective-permute-done((bf16[1024,512]{1,0:T(8,128)(2,1)S(1)}, bf16[1024,512]{1,0:T(8,128)(2,1)S(1)}, u32[]{:S(2)}, u32[]{:S(2)}) %collective-permute-start.45) | collective-permute-done | bytes 1048608 | tf_op jit(solution)/shard_map/ppermute | solution.py:80
  715.7 7.5 shard_map.327.refs_1_
  723.2 14.2 %shard_map.328 = (f32[6,2048,256]{2,1,0:T(8,128)}, f32[6,2048,256]{2,1,0:T(8,128)}) custom-call(bf16[2,6,2048,256]{3,2,1,0:T(8,128)(2,1)} %all-reduce.8.cloned.1.call-done.refs_2_.refs_0_, f32[1024,512]{1,0:T(8,128)} %shard_map.327.refs_1_), custom_call_target="tpu_custom_call" | custom-call | flops 1 | bytes 1 | tf_op jit(solution)/shard_map/pallas_call | solution.py:42
  737.5 10.5 %shard_map.329.refs_3_ = f32[1536,2048]{1,0:T(8,128)} custom-call(s32[8]{0:T(128)} %gather_fusion, bf16[4,192,2048]{2,1,0:T(8,128)(2,1)} %shard_map.325.refs_3_.refs_1_, bf16[4,192,2048]{2,1,0:T(8,128)(2,1)} %collective-permute-done.44.refs_2_, f32[6,2048,256]{2,1,0:T(8,128)} %get-tuple-element.84.refs_3_), custom_call_target="tpu_custom_call" | custom-call | flops 1 | bytes 1 | tf_op jit(solution)/shard_map/pallas_call | solution.py:42
  747.9 4.3 shard_map.330.refs_1_
  754.3 4.1 convert_element_type.23
  759.6 8.7 %shard_map.331 = (f32[2048,512]{1,0:T(8,128)}, f32[2048,512]{1,0:T(8,128)}, f32[2048,512]{1,0:T(8,128)}) custom-call(bf16[2048,1536]{1,0:T(8,128)(2,1)} %get-tuple-element.161.refs_0_, bf16[1024,512]{1,0:T(8,128)(2,1)} %shard_map.330.refs_1_), custom_call_target="tpu_custom_call" | custom-call | flops 1 | bytes 1 | tf_op jit(solution)/shard_map/pallas_call | solution.py:42
  (255 shorter events, 105.0 us)
Async XLA Ops:
  7.2 190.2 %all-gather.6.cloned.1.call-start = ((), (), s32[]{:S(2)}) async-start(), calls=%async_computation.2 | async-start | bytes 9437184 | tf_op jit(solution)/shard_map/all_gather | solution.py:1152
  9.5 12.8 %collective-permute-start.3 = (bf16[80,2048]{1,0:T(8,128)(2,1)S(1)}, bf16[80,2048]{1,0:T(8,128)(2,1)S(1)}, u32[]{:S(2)}, u32[]{:S(2)}) collective-permute-start(bf16[80,2048]{1,0:T(8,128)(2,1)S(1)} %fusion.18), channel_id=1, source_target_pairs={{0,1},{1,2},{2,3},{3,0},{4,5},{5,6},{6,7},{7,4},{8,9},{9,10},{10,1... | collective-permute-start | bytes 983048 | tf_op jit(solution)/shard_map/ppermute | solution.py:80
  12.8 31.2 %copy-start.4 = (bf16[1024,512]{1,0:T(8,128)(2,1)S(1)}, bf16[1024,512]{1,0:T(8,128)(2,1)}, u32[]{:S(2)}) copy-start(bf16[1024,512]{1,0:T(8,128)(2,1)} %refs_4_.1) | copy-start | bytes 3145732
  12.8 31.3 %copy-start.41 = (s32[1,3072]{1,0:T(1,128)S(1)}, s32[1,3072]{1,0:T(1,128)}, u32[]{:S(2)}) copy-start(s32[1,3072]{1,0:T(1,128)} %param.35) | copy-start | bytes 36868
  12.8 55.7 %copy-start.55 = (s32[1024,3]{0,1:T(4,128)S(1)}, s32[1024,3]{0,1:T(4,128)}, u32[]{:S(2)}) copy-start(s32[1024,3]{0,1:T(4,128)} %param.33) | copy-start | bytes 36868
  22.4 10.7 %collective-permute-start.4 = (bf16[80,2048]{1,0:T(8,128)(2,1)S(1)}, bf16[80,2048]{1,0:T(8,128)(2,1)S(1)}, u32[]{:S(2)}, u32[]{:S(2)}) collective-permute-start(bf16[80,2048]{1,0:T(8,128)(2,1)S(1)} %collective-permute-done.3), channel_id=1, source_target_pairs={{0,1},{1,2},{2,3},{3,0},{4,5},{5,6},{6,7},{7,4},{8,9},{9,10},{10,1... | collective-permute-start | bytes 983048 | tf_op jit(solution)/shard_map/ppermute | solution.py:80
  33.1 9.8 %collective-permute-start.5 = (bf16[80,2048]{1,0:T(8,128)(2,1)S(1)}, bf16[80,2048]{1,0:T(8,128)(2,1)S(1)}, u32[]{:S(2)}, u32[]{:S(2)}) collective-permute-start(bf16[80,2048]{1,0:T(8,128)(2,1)S(1)} %collective-permute-done.4), channel_id=1, source_target_pairs={{0,1},{1,2},{2,3},{3,0},{4,5},{5,6},{6,7},{7,4},{8,9},{9,10},{10,1... | collective-permute-start | bytes 983048 | tf_op jit(solution)/shard_map/ppermute | solution.py:80
  43.9 177.7 %all-gather.4.cloned.1.call-start = ((), (), s32[]{:S(2)}) async-start(), calls=%async_computation | async-start | bytes 5242880 | tf_op jit(solution)/shard_map/all_gather | solution.py:1165
  44.0 24.4 %collective-permute-start = (bf16[1024,512]{1,0:T(8,128)(2,1)S(1)}, bf16[1024,512]{1,0:T(8,128)(2,1)S(1)}, u32[]{:S(2)}, u32[]{:S(2)}) collective-permute-start(bf16[1024,512]{1,0:T(8,128)(2,1)S(1)} %copy-done.4), channel_id=1, source_target_pairs={{0,1},{1,2},{2,3},{3,0},{4,5},{5,6},{6,7},{7,4},{8,9},{9,10},{10,1... | collective-permute-start | bytes 3145736 | tf_op jit(solution)/shard_map/ppermute | solution.py:80
  68.3 23.5 %collective-permute-start.1 = (bf16[1024,512]{1,0:T(8,128)(2,1)S(1)}, bf16[1024,512]{1,0:T(8,128)(2,1)}, u32[]{:S(2)}, u32[]{:S(2)}) collective-permute-start(bf16[1024,512]{1,0:T(8,128)(2,1)S(1)} %collective-permute-done.refs_2_.refs_6_), channel_id=1, source_target_pairs={{0,1},{1,2},{2,3},{3,0},{4,5},{5,6},{6,7},{7,4},{8,9},{9,10},{10,1... | collective-permute-start | bytes 3145736 | tf_op jit(solution)/shard_map/ppermute | solution.py:80
  91.8 22.7 %collective-permute-start.2 = (bf16[1024,512]{1,0:T(8,128)(2,1)}, bf16[1024,512]{1,0:T(8,128)(2,1)S(1)}, u32[]{:S(2)}, u32[]{:S(2)}) collective-permute-start(bf16[1024,512]{1,0:T(8,128)(2,1)} %collective-permute-done.1.refs_3_.refs_7_), channel_id=1, source_target_pairs={{0,1},{1,2},{2,3},{3,0},{4,5},{5,6},{6,7},{7,4},{8,9},{9,10},{10,1... | collective-permute-start | bytes 3145736 | tf_op jit(solution)/shard_map/ppermute | solution.py:80
  120.1 18.9 %copy-start.50 = (bf16[512]{0:T(512)(128)(2,1)S(1)}, bf16[512]{0:T(512)(128)(2,1)}, u32[]{:S(2)}) copy-start(bf16[512]{0:T(512)(128)(2,1)} %param.25) | copy-start | bytes 3076
  120.1 19.5 %copy-start.51 = (bf16[512]{0:T(512)(128)(2,1)S(1)}, bf16[512]{0:T(512)(128)(2,1)}, u32[]{:S(2)}) copy-start(bf16[512]{0:T(512)(128)(2,1)} %param.26) | copy-start | bytes 3076
  134.7 6.7 collective-permute-start.6
  134.7 6.6 collective-permute-start.7
  134.8 7.8 %collective-permute-start.8 = (f32[8,1024]{1,0:T(8,128)}, f32[8,1024]{1,0:T(8,128)S(1)}, u32[]{:S(2)}, u32[]{:S(2)}) collective-permute-start(f32[8,1024]{1,0:T(8,128)} %get-tuple-element.90.refs_8_.refs_12_.refs_5_), channel_id=1, source_target_pairs={{0,3},{1,0},{2,1},{3,2},{4,7},{5,4},{6,5},{7,6},{8,11},{9,8},{10,9... | collective-permute-start | bytes 98312 | tf_op jit(solution)/shard_map/ppermute | solution.py:80
  158.5 27.8 %collective-permute-start.10 = (bf16[256,512]{1,0:T(8,128)(2,1)S(1)}, bf16[256,512]{1,0:T(8,128)(2,1)S(1)}, u32[]{:S(2)}, u32[]{:S(2)}) collective-permute-start(bf16[256,512]{1,0:T(8,128)(2,1)S(1)} %get-tuple-element.168), channel_id=1, source_target_pairs={{0,2},{1,3},{2,0},{3,1},{4,6},{5,7},{6,4},{7,5},{8,10},{9,11},{10,... | collective-permute-start | bytes 786440 | tf_op jit(solution)/shard_map/ppermute | solution.py:80
  161.2 25.1 %collective-permute-start.11 = (bf16[256,512]{1,0:T(8,128)(2,1)S(1)}, bf16[256,512]{1,0:T(8,128)(2,1)S(1)}, u32[]{:S(2)}, u32[]{:S(2)}) collective-permute-start(bf16[256,512]{1,0:T(8,128)(2,1)S(1)} %get-tuple-element.167), channel_id=1, source_target_pairs={{0,3},{1,0},{2,1},{3,2},{4,7},{5,4},{6,5},{7,6},{8,11},{9,8},{10,9... | collective-permute-start | bytes 786440 | tf_op jit(solution)/shard_map/ppermute | solution.py:80
  164.7 32.7 %collective-permute-start.9 = (bf16[256,512]{1,0:T(8,128)(2,1)S(1)}, bf16[256,512]{1,0:T(8,128)(2,1)S(1)}, u32[]{:S(2)}, u32[]{:S(2)}) collective-permute-start(bf16[256,512]{1,0:T(8,128)(2,1)S(1)} %get-tuple-element.169), channel_id=1, source_target_pairs={{0,1},{1,2},{2,3},{3,0},{4,5},{5,6},{6,7},{7,4},{8,9},{9,10},{10,1... | collective-permute-start | bytes 786440 | tf_op jit(solution)/shard_map/ppermute | solution.py:80
  186.3 11.1 %copy-start.34 = (bf16[256,512]{1,0:T(8,128)(2,1)}, bf16[256,512]{1,0:T(8,128)(2,1)S(1)}, u32[]{:S(2)}) copy-start(bf16[256,512]{1,0:T(8,128)(2,1)S(1)} %collective-permute-done.10.refs_3_) | copy-start | bytes 786436
  225.0 26.9 %collective-permute-start.12 = (bf16[256,2048]{1,0:T(8,128)(2,1)}, bf16[256,2048]{1,0:T(8,128)(2,1)S(1)}, u32[]{:S(2)}, u32[]{:S(2)}) collective-permute-start(bf16[256,2048]{1,0:T(8,128)(2,1)} %bitcast.97), channel_id=1, source_target_pairs={{0,1},{1,2},{2,3},{3,0},{4,5},{5,6},{6,7},{7,4},{8,9},{9,10},{10,1... | collective-permute-start | bytes 3145736 | tf_op jit(solution)/shard_map/ppermute | solution.py:80
  256.3 26.0 %collective-permute-start.13 = (bf16[256,2048]{1,0:T(8,128)(2,1)}, bf16[256,2048]{1,0:T(8,128)(2,1)S(1)}, u32[]{:S(2)}, u32[]{:S(2)}) collective-permute-start(bf16[256,2048]{1,0:T(8,128)(2,1)} %bitcast.108), channel_id=1, source_target_pairs={{0,1},{1,2},{2,3},{3,0},{4,5},{5,6},{6,7},{7,4},{8,9},{9,10},{10,1... | collective-permute-start | bytes 3145736 | tf_op jit(solution)/shard_map/ppermute | solution.py:80
  286.7 25.3 %collective-permute-start.14 = (bf16[256,2048]{1,0:T(8,128)(2,1)}, bf16[256,2048]{1,0:T(8,128)(2,1)S(1)}, u32[]{:S(2)}, u32[]{:S(2)}) collective-permute-start(bf16[256,2048]{1,0:T(8,128)(2,1)} %bitcast.107), channel_id=1, source_target_pairs={{0,1},{1,2},{2,3},{3,0},{4,5},{5,6},{6,7},{7,4},{8,9},{9,10},{10,1... | collective-permute-start | bytes 3145736 | tf_op jit(solution)/shard_map/ppermute | solution.py:80
  312.9 21.9 %copy-start.2 = (s32[8]{0:T(128)S(1)}, s32[8]{0:T(128)}, u32[]{:S(2)}) copy-start(s32[8]{0:T(128)} %constant.112.clone) | copy-start | bytes 100
  334.8 25.6 %collective-permute-start.15 = (bf16[256,2176]{1,0:T(8,128)(2,1)}, bf16[256,2176]{1,0:T(8,128)(2,1)S(1)}, u32[]{:S(2)}, u32[]{:S(2)}) collective-permute-start(bf16[256,2176]{1,0:T(8,128)(2,1)} %bitcast.103), channel_id=1, source_target_pairs={{0,1},{1,2},{2,3},{3,0},{4,5},{5,6},{6,7},{7,4},{8,9},{9,10},{10,1... | collective-permute-start | bytes 3342344 | tf_op jit(solution)/shard_map/ppermute | solution.py:80
  365.1 233.4 %all-reduce.8.cloned.1.call-start = ((), (), s32[]{:S(2)}) async-start(), calls=%async_computation.1 | async-start | bytes 25165824 | tf_op jit(solution)/shard_map/psum | solution.py:1206
  373.3 33.8 %collective-permute-start.18 = (bf16[4,192,2048]{2,1,0:T(8,128)(2,1)}, bf16[4,192,2048]{2,1,0:T(8,128)(2,1)}, u32[]{:S(2)}, u32[]{:S(2)}) collective-permute-start(bf16[4,192,2048]{2,1,0:T(8,128)(2,1)} %shard_map.305.refs_3_), channel_id=1, source_target_pairs={{0,4},{4,0},{8,12},{12,8},{16,20},{20,16},{24,28},{28,24},{1,5},{5... | collective-permute-start | bytes 9437192 | tf_op jit(solution)/shard_map/ppermute | solution.py:99
  373.3 378.9 %all-reduce.10.cloned.1.call-start = ((), (), s32[]{:S(2)}) async-start(), calls=%async_computation.3 | async-start | bytes 16973824 | tf_op jit(solution)/shard_map/psum | solution.py:1246
  374.5 27.7 %collective-permute-start.16 = (bf16[256,2176]{1,0:T(8,128)(2,1)S(1)}, bf16[256,2176]{1,0:T(8,128)(2,1)S(1)}, u32[]{:S(2)}, u32[]{:S(2)}) collective-permute-start(bf16[256,2176]{1,0:T(8,128)(2,1)S(1)} %bitcast.111), channel_id=1, source_target_pairs={{0,1},{1,2},{2,3},{3,0},{4,5},{5,6},{6,7},{7,4},{8,9},{9,10},{10,1... | collective-permute-start | bytes 3342344 | tf_op jit(solution)/shard_map/ppermute | solution.py:80
  406.9 27.3 %collective-permute-start.17 = (bf16[256,2176]{1,0:T(8,128)(2,1)}, bf16[256,2176]{1,0:T(8,128)(2,1)S(1)}, u32[]{:S(2)}, u32[]{:S(2)}) collective-permute-start(bf16[256,2176]{1,0:T(8,128)(2,1)} %bitcast.102), channel_id=1, source_target_pairs={{0,1},{1,2},{2,3},{3,0},{4,5},{5,6},{6,7},{7,4},{8,9},{9,10},{10,1... | collective-permute-start | bytes 3342344 | tf_op jit(solution)/shard_map/ppermute | solution.py:80
  446.6 30.6 %copy-start.23 = (bf16[2,192,1024]{2,1,0:T(8,128)(2,1)S(1)}, bf16[2,192,1024]{2,1,0:T(8,128)(2,1)}, u32[]{:S(2)}) copy-start(bf16[2,192,1024]{2,1,0:T(8,128)(2,1)} %get-tuple-element.123.refs_10_) | copy-start | bytes 2359300
  446.6 31.8 %copy-start.53 = (bf16[2,192,1024]{2,1,0:T(8,128)(2,1)S(1)}, bf16[2,192,1024]{2,1,0:T(8,128)(2,1)}, u32[]{:S(2)}) copy-start(bf16[2,192,1024]{2,1,0:T(8,128)(2,1)} %get-tuple-element.138) | copy-start | bytes 2359300
  448.7 11.1 %collective-permute-start.19 = (bf16[256,512]{1,0:T(8,128)(2,1)S(1)}, bf16[256,512]{1,0:T(8,128)(2,1)S(1)}, u32[]{:S(2)}, u32[]{:S(2)}) collective-permute-start(bf16[256,512]{1,0:T(8,128)(2,1)S(1)} %get-tuple-element.165), channel_id=1, source_target_pairs={{0,1},{1,2},{2,3},{3,0},{4,5},{5,6},{6,7},{7,4},{8,9},{9,10},{10,1... | collective-permute-start | bytes 786440 | tf_op jit(solution)/shard_map/ppermute | solution.py:80
  448.7 18.2 %collective-permute-start.20 = (bf16[256,512]{1,0:T(8,128)(2,1)S(1)}, bf16[256,512]{1,0:T(8,128)(2,1)S(1)}, u32[]{:S(2)}, u32[]{:S(2)}) collective-permute-start(bf16[256,512]{1,0:T(8,128)(2,1)S(1)} %get-tuple-element.164), channel_id=1, source_target_pairs={{0,2},{1,3},{2,0},{3,1},{4,6},{5,7},{6,4},{7,5},{8,10},{9,11},{10,... | collective-permute-start | bytes 786440 | tf_op jit(solution)/shard_map/ppermute | solution.py:80
  448.7 18.2 %collective-permute-start.21 = (bf16[256,512]{1,0:T(8,128)(2,1)S(1)}, bf16[256,512]{1,0:T(8,128)(2,1)S(1)}, u32[]{:S(2)}, u32[]{:S(2)}) collective-permute-start(bf16[256,512]{1,0:T(8,128)(2,1)S(1)} %get-tuple-element.163), channel_id=1, source_target_pairs={{0,3},{1,0},{2,1},{3,2},{4,7},{5,4},{6,5},{7,6},{8,11},{9,8},{10,9... | collective-permute-start | bytes 786440 | tf_op jit(solution)/shard_map/ppermute | solution.py:80
  472.2 36.5 %collective-permute-start.22 = (bf16[256,2048]{1,0:T(8,128)(2,1)}, bf16[256,2048]{1,0:T(8,128)(2,1)S(1)}, u32[]{:S(2)}, u32[]{:S(2)}) collective-permute-start(bf16[256,2048]{1,0:T(8,128)(2,1)} %get-tuple-element.134.refs_2_.refs_8_), channel_id=1, source_target_pairs={{0,1},{1,2},{2,3},{3,0},{4,5},{5,6},{6,7},{7,4},{8,9},{9,10},{10,1... | collective-permute-start | bytes 3145736 | tf_op jit(solution)/shard_map/ppermute | solution.py:80
  477.2 23.2 %collective-permute-start.26 = (bf16[2,192,1024]{2,1,0:T(8,128)(2,1)S(1)}, bf16[2,192,1024]{2,1,0:T(8,128)(2,1)S(1)}, u32[]{:S(2)}, u32[]{:S(2)}) collective-permute-start(bf16[2,192,1024]{2,1,0:T(8,128)(2,1)S(1)} %copy-done.23), channel_id=1, source_target_pairs={{0,8},{4,12},{8,0},{12,4},{16,24},{20,28},{24,16},{28,20},{1,9},{5... | collective-permute-start | bytes 2359304 | tf_op jit(solution)/shard_map/ppermute | solution.py:99
  478.4 25.3 %collective-permute-start.27 = (bf16[2,192,1024]{2,1,0:T(8,128)(2,1)S(1)}, bf16[2,192,1024]{2,1,0:T(8,128)(2,1)S(1)}, u32[]{:S(2)}, u32[]{:S(2)}) collective-permute-start(bf16[2,192,1024]{2,1,0:T(8,128)(2,1)S(1)} %copy-done.53), channel_id=1, source_target_pairs={{0,16},{4,20},{8,24},{12,28},{16,0},{20,4},{24,8},{28,12},{1,17},{... | collective-permute-start | bytes 2359304 | tf_op jit(solution)/shard_map/ppermute | solution.py:99
  498.7 10.0 %collective-permute-start.23 = (f32[8,1024]{1,0:T(8,128)}, f32[8,1024]{1,0:T(8,128)S(1)}, u32[]{:S(2)}, u32[]{:S(2)}) collective-permute-start(f32[8,1024]{1,0:T(8,128)} %get-tuple-element.135.refs_12_), channel_id=1, source_target_pairs={{0,1},{1,2},{2,3},{3,0},{4,5},{5,6},{6,7},{7,4},{8,9},{9,10},{10,1... | collective-permute-start | bytes 98312 | tf_op jit(solution)/shard_map/ppermute | solution.py:80
  498.8 9.9 %collective-permute-start.24 = (f32[8,1024]{1,0:T(8,128)}, f32[8,1024]{1,0:T(8,128)S(1)}, u32[]{:S(2)}, u32[]{:S(2)}) collective-permute-start(f32[8,1024]{1,0:T(8,128)} %get-tuple-element.135.refs_12_), channel_id=1, source_target_pairs={{0,2},{1,3},{2,0},{3,1},{4,6},{5,7},{6,4},{7,5},{8,10},{9,11},{10,... | collective-permute-start | bytes 98312 | tf_op jit(solution)/shard_map/ppermute | solution.py:80
  500.4 8.3 %collective-permute-start.25 = (f32[8,1024]{1,0:T(8,128)}, f32[8,1024]{1,0:T(8,128)S(1)}, u32[]{:S(2)}, u32[]{:S(2)}) collective-permute-start(f32[8,1024]{1,0:T(8,128)} %get-tuple-element.135.refs_12_), channel_id=1, source_target_pairs={{0,3},{1,0},{2,1},{3,2},{4,7},{5,4},{6,5},{7,6},{8,11},{9,8},{10,9... | collective-permute-start | bytes 98312 | tf_op jit(solution)/shard_map/ppermute | solution.py:80
  516.8 26.3 %collective-permute-start.31 = (bf16[256,2048]{1,0:T(8,128)(2,1)}, bf16[256,2048]{1,0:T(8,128)(2,1)S(1)}, u32[]{:S(2)}, u32[]{:S(2)}) collective-permute-start(bf16[256,2048]{1,0:T(8,128)(2,1)} %get-tuple-element.143), channel_id=1, source_target_pairs={{0,1},{1,2},{2,3},{3,0},{4,5},{5,6},{6,7},{7,4},{8,9},{9,10},{10,1... | collective-permute-start | bytes 3145736 | tf_op jit(solution)/shard_map/ppermute | solution.py:80
  535.7 12.1 %copy-start.40 = (f32[8,2048]{1,0:T(8,128)S(1)}, f32[8,2048]{1,0:T(8,128)}, u32[]{:S(2)}) copy-start(f32[8,2048]{1,0:T(8,128)} %get-tuple-element.124) | copy-start | bytes 196612
  535.7 16.6 %copy-start.48 = (f32[8,512]{1,0:T(8,128)S(1)}, f32[8,512]{1,0:T(8,128)}, u32[]{:S(2)}) copy-start(f32[8,512]{1,0:T(8,128)} %get-tuple-element.142) | copy-start | bytes 49156
  535.7 16.6 %copy-start.28 = (bf16[1,192,1024]{2,1,0:T(8,128)(2,1)S(1)}, bf16[1,192,1024]{2,1,0:T(8,128)(2,1)}, u32[]{:S(2)}) copy-start(bf16[1,192,1024]{2,1,0:T(8,128)(2,1)} %get-tuple-element.139.refs_16_) | copy-start | bytes 1179652
  535.7 40.4 %copy-start.54 = (bf16[1,192,1024]{2,1,0:T(8,128)(2,1)S(1)}, bf16[1,192,1024]{2,1,0:T(8,128)(2,1)}, u32[]{:S(2)}) copy-start(bf16[1,192,1024]{2,1,0:T(8,128)(2,1)} %get-tuple-element.148) | copy-start | bytes 1179652
  547.8 42.5 %collective-permute-start.32 = (bf16[256,2048]{1,0:T(8,128)(2,1)}, bf16[256,2048]{1,0:T(8,128)(2,1)S(1)}, u32[]{:S(2)}, u32[]{:S(2)}) collective-permute-start(bf16[256,2048]{1,0:T(8,128)(2,1)} %bitcast.114), channel_id=1, source_target_pairs={{0,1},{1,2},{2,3},{3,0},{4,5},{5,6},{6,7},{7,4},{8,9},{9,10},{10,1... | collective-permute-start | bytes 3145736 | tf_op jit(solution)/shard_map/ppermute | solution.py:80
  547.9 28.3 %collective-permute-start.28 = (f32[8,2048]{1,0:T(8,128)S(1)}, f32[8,2048]{1,0:T(8,128)S(1)}, u32[]{:S(2)}, u32[]{:S(2)}) collective-permute-start(f32[8,2048]{1,0:T(8,128)S(1)} %pad_maximum_fusion.2), channel_id=1, source_target_pairs={{0,1},{1,2},{2,3},{3,0},{4,5},{5,6},{6,7},{7,4},{8,9},{9,10},{10,1... | collective-permute-start | bytes 196616 | tf_op jit(solution)/shard_map/ppermute | solution.py:80
  547.9 29.6 %collective-permute-start.29 = (f32[8,2048]{1,0:T(8,128)S(1)}, f32[8,2048]{1,0:T(8,128)S(1)}, u32[]{:S(2)}, u32[]{:S(2)}) collective-permute-start(f32[8,2048]{1,0:T(8,128)S(1)} %pad_maximum_fusion.2), channel_id=1, source_target_pairs={{0,2},{1,3},{2,0},{3,1},{4,6},{5,7},{6,4},{7,5},{8,10},{9,11},{10,... | collective-permute-start | bytes 196616 | tf_op jit(solution)/shard_map/ppermute | solution.py:80
  552.3 25.3 %collective-permute-start.30 = (f32[8,2048]{1,0:T(8,128)S(1)}, f32[8,2048]{1,0:T(8,128)S(1)}, u32[]{:S(2)}, u32[]{:S(2)}) collective-permute-start(f32[8,2048]{1,0:T(8,128)S(1)} %pad_maximum_fusion.2), channel_id=1, source_target_pairs={{0,3},{1,0},{2,1},{3,2},{4,7},{5,4},{6,5},{7,6},{8,11},{9,8},{10,9... | collective-permute-start | bytes 196616 | tf_op jit(solution)/shard_map/ppermute | solution.py:80
  552.3 28.3 %collective-permute-start.33 = (bf16[1,192,1024]{2,1,0:T(8,128)(2,1)S(1)}, bf16[1,192,1024]{2,1,0:T(8,128)(2,1)S(1)}, u32[]{:S(2)}, u32[]{:S(2)}) collective-permute-start(bf16[1,192,1024]{2,1,0:T(8,128)(2,1)S(1)} %copy-done.28), channel_id=1, source_target_pairs={{0,16},{4,20},{8,24},{12,28},{16,0},{20,4},{24,8},{28,12},{1,17},{... | collective-permute-start | bytes 1179656 | tf_op jit(solution)/shard_map/ppermute | solution.py:99
  576.1 7.8 %collective-permute-start.34 = (bf16[1,192,1024]{2,1,0:T(8,128)(2,1)S(1)}, bf16[1,192,1024]{2,1,0:T(8,128)(2,1)S(1)}, u32[]{:S(2)}, u32[]{:S(2)}) collective-permute-start(bf16[1,192,1024]{2,1,0:T(8,128)(2,1)S(1)} %copy-done.54), channel_id=1, source_target_pairs={{0,8},{4,12},{8,0},{12,4},{16,24},{20,28},{24,16},{28,20},{1,9},{5... | collective-permute-start | bytes 1179656 | tf_op jit(solution)/shard_map/ppermute | solution.py:99
  578.5 27.3 %collective-permute-start.38 = (bf16[1024,512]{1,0:T(8,128)(2,1)}, bf16[1024,512]{1,0:T(8,128)(2,1)}, u32[]{:S(2)}, u32[]{:S(2)}) collective-permute-start(bf16[1024,512]{1,0:T(8,128)(2,1)} %bitcast.129), channel_id=1, source_target_pairs={{0,1},{1,2},{2,3},{3,0},{4,5},{5,6},{6,7},{7,4},{8,9},{9,10},{10,1... | collective-permute-start | bytes 3145736 | tf_op jit(solution)/shard_map/ppermute | solution.py:80
  588.2 25.2 %collective-permute-start.36 = (bf16[1,192,1024]{2,1,0:T(8,128)(2,1)}, bf16[1,192,1024]{2,1,0:T(8,128)(2,1)}, u32[]{:S(2)}, u32[]{:S(2)}) collective-permute-start(bf16[1,192,1024]{2,1,0:T(8,128)(2,1)} %get-tuple-element.149.refs_6_.refs_0_), channel_id=1, source_target_pairs={{0,16},{4,20},{8,24},{12,28},{16,0},{20,4},{24,8},{28,12},{1,17},{... | collective-permute-start | bytes 1179656 | tf_op jit(solution)/shard_map/ppermute | solution.py:99
  589.6 23.8 %collective-permute-start.37 = (bf16[1,192,1024]{2,1,0:T(8,128)(2,1)}, bf16[1,192,1024]{2,1,0:T(8,128)(2,1)}, u32[]{:S(2)}, u32[]{:S(2)}) collective-permute-start(bf16[1,192,1024]{2,1,0:T(8,128)(2,1)} %get-tuple-element.150.refs_2_), channel_id=1, source_target_pairs={{0,8},{4,12},{8,0},{12,4},{16,24},{20,28},{24,16},{28,20},{1,9},{5... | collective-permute-start | bytes 1179656 | tf_op jit(solution)/shard_map/ppermute | solution.py:99
  605.6 28.1 %collective-permute-start.35 = (bf16[1024,512]{1,0:T(8,128)(2,1)}, bf16[1024,512]{1,0:T(8,128)(2,1)S(1)}, u32[]{:S(2)}, u32[]{:S(2)}) collective-permute-start(bf16[1024,512]{1,0:T(8,128)(2,1)} %shard_map.320.refs_4_), channel_id=1, source_target_pairs={{0,1},{1,2},{2,3},{3,0},{4,5},{5,6},{6,7},{7,4},{8,9},{9,10},{10,1... | collective-permute-start | bytes 3145736 | tf_op jit(solution)/shard_map/ppermute | solution.py:80
  612.2 38.9 %collective-permute-start.42 = (bf16[1024,512]{1,0:T(8,128)(2,1)}, bf16[1024,512]{1,0:T(8,128)(2,1)S(1)}, u32[]{:S(2)}, u32[]{:S(2)}) collective-permute-start(bf16[1024,512]{1,0:T(8,128)(2,1)} %shard_map.321.refs_4_), channel_id=1, source_target_pairs={{0,1},{1,2},{2,3},{3,0},{4,5},{5,6},{6,7},{7,4},{8,9},{9,10},{10,1... | collective-permute-start | bytes 3145736 | tf_op jit(solution)/shard_map/ppermute | solution.py:80
  617.1 41.3 %collective-permute-start.40 = (bf16[2,192,1024]{2,1,0:T(8,128)(2,1)}, bf16[2,192,1024]{2,1,0:T(8,128)(2,1)S(1)}, u32[]{:S(2)}, u32[]{:S(2)}) collective-permute-start(bf16[2,192,1024]{2,1,0:T(8,128)(2,1)} %get-tuple-element.152.refs_3_.refs_0_), channel_id=1, source_target_pairs={{0,8},{4,12},{8,0},{12,4},{16,24},{20,28},{24,16},{28,20},{1,9},{5... | collective-permute-start | bytes 2359304 | tf_op jit(solution)/shard_map/ppermute | solution.py:99
  617.4 41.0 %collective-permute-start.41 = (bf16[2,192,1024]{2,1,0:T(8,128)(2,1)}, bf16[2,192,1024]{2,1,0:T(8,128)(2,1)S(1)}, u32[]{:S(2)}, u32[]{:S(2)}) collective-permute-start(bf16[2,192,1024]{2,1,0:T(8,128)(2,1)} %get-tuple-element.153.refs_2_), channel_id=1, source_target_pairs={{0,16},{4,20},{8,24},{12,28},{16,0},{20,4},{24,8},{28,12},{1,17},{... | collective-permute-start | bytes 2359304 | tf_op jit(solution)/shard_map/ppermute | solution.py:99
  664.4 33.1 %copy-start.3 = (s32[8]{0:T(128)S(1)}, s32[8]{0:T(128)}, u32[]{:S(2)}) copy-start(s32[8]{0:T(128)} %constant.112.clone) | copy-start | bytes 100
  664.4 73.0 %collective-permute-start.44 = (bf16[4,192,2048]{2,1,0:T(8,128)(2,1)}, bf16[4,192,2048]{2,1,0:T(8,128)(2,1)}, u32[]{:S(2)}, u32[]{:S(2)}) collective-permute-start(bf16[4,192,2048]{2,1,0:T(8,128)(2,1)} %shard_map.325.refs_3_.refs_1_), channel_id=1, source_target_pairs={{0,4},{4,0},{8,12},{12,8},{16,20},{20,16},{24,28},{28,24},{1,5},{5... | collective-permute-start | bytes 9437192 | tf_op jit(solution)/shard_map/ppermute | solution.py:99
  664.4 27.8 %collective-permute-start.39 = (bf16[1024,512]{1,0:T(8,128)(2,1)S(1)}, bf16[1024,512]{1,0:T(8,128)(2,1)S(1)}, u32[]{:S(2)}, u32[]{:S(2)}) collective-permute-start(bf16[1024,512]{1,0:T(8,128)(2,1)S(1)} %copy-done.10), channel_id=1, source_target_pairs={{0,1},{1,2},{2,3},{3,0},{4,5},{5,6},{6,7},{7,4},{8,9},{9,10},{10,1... | collective-permute-start | bytes 3145736 | tf_op jit(solution)/shard_map/ppermute | solution.py:80
  664.5 50.2 %collective-permute-start.45 = (bf16[1024,512]{1,0:T(8,128)(2,1)S(1)}, bf16[1024,512]{1,0:T(8,128)(2,1)S(1)}, u32[]{:S(2)}, u32[]{:S(2)}) collective-permute-start(bf16[1024,512]{1,0:T(8,128)(2,1)S(1)} %copy-done.9), channel_id=1, source_target_pairs={{0,1},{1,2},{2,3},{3,0},{4,5},{5,6},{6,7},{7,4},{8,9},{9,10},{10,1... | collective-permute-start | bytes 3145736 | tf_op jit(solution)/shard_map/ppermute | solution.py:80
  697.5 50.5 %collective-permute-start.43 = (bf16[1024,512]{1,0:T(8,128)(2,1)}, bf16[1024,512]{1,0:T(8,128)(2,1)}, u32[]{:S(2)}, u32[]{:S(2)}) collective-permute-start(bf16[1024,512]{1,0:T(8,128)(2,1)} %shard_map.326.refs_12_), channel_id=1, source_target_pairs={{0,1},{1,2},{2,3},{3,0},{4,5},{5,6},{6,7},{7,4},{8,9},{9,10},{10,1... | collective-permute-start | bytes 3145736 | tf_op jit(solution)/shard_map/ppermute | solution.py:80
  (42 other events, 95.9 us)
Sparse Core Ops, SparseCore 0:
  44.0 52.0 all-gather.5
  119.0 102.6 all-gather.3
  373.4 180.0 all-reduce.7
  601.7 142.4 all-reduce.9

commit v3 on v2

--- a/solution.py
+++ b/solution.py
@@ -242,20 +242,6 @@
 
     def finish(self):
         return self.keep, self.flying[0]
-
-
-def copied_pair(first, second, work):
-    fold = second.shape[0] // first.shape[0]
-
-    def body(ins, outs):
-        outs[0][...] = ins[0][...]
-        outs[1][...] = ins[1][...]
-
-    folded = second.reshape(fold, first.shape[0], second.shape[1])
-    a, b = blockwise(
-        body, [first[None], folded], [(1,) + first.shape, folded.shape], work=work
-    )
-    return a[0], b.reshape(second.shape)
 
 
 def qkv_kernel(owners_ref, *refs):
@@ -471,11 +457,8 @@
     )
 
 
-def norm_back_kernel(
-    full, size, q_ref, k_ref, dq_ref, dk_ref, dv_ref, gq_ref, gk_ref, branch_ref, *rest
-):
-    sums_refs, back_refs, (out_ref, stat_ref, copy_ref) = rest[:size], rest[size : 2 * size], rest[2 * size :]
-    copy_ref[...] = branch_ref[...]
+def norm_back_kernel(full, size, q_ref, k_ref, dq_ref, dk_ref, dv_ref, gq_ref, gk_ref, *rest):
+    sums_refs, back_refs, (out_ref, stat_ref) = rest[:size], rest[size : 2 * size], rest[2 * size :]
     width = q_ref.shape[1]
     scales = head_scales(sums_refs, full)
     back = back_refs[0][...]
@@ -503,26 +486,23 @@
     out_ref[:, 2 * width :] = dv_ref[...]
 
 
-def norm_back(q_pre, k_pre, dq, dk, dv, gq, gk, branch, sums, back):
+def norm_back(q_pre, k_pre, dq, dk, dv, gq, gk, sums, back):
     length, width = q_pre.shape
     full = width * len(sums)
     rows = min(256, length)
     tile = pl.BlockSpec((rows, width), lambda g: (g, 0))
     wide = pl.BlockSpec((rows, 3 * width), lambda g: (g, 0))
     gain = pl.BlockSpec((1, width), lambda g: (0, 0))
-    chunk = branch.shape[0] * rows // length
-    part = pl.BlockSpec((chunk, branch.shape[1]), lambda g: (g, 0))
     line = pl.BlockSpec((8, rows), lambda g: (0, g))
     return launch(
         functools.partial(norm_back_kernel, full, len(sums)),
-        [q_pre, k_pre, dq, dk, dv, gq, gk, branch, *sums, *back],
+        [q_pre, k_pre, dq, dk, dv, gq, gk, *sums, *back],
         grid=(length // rows,),
-        in_specs=[tile] * 5 + [gain, gain, part] + [line] * (2 * len(sums)),
-        out_specs=[wide, line, part],
+        in_specs=[tile] * 5 + [gain, gain] + [line] * (2 * len(sums)),
+        out_specs=[wide, line],
         out_shape=[
             jax.ShapeDtypeStruct((length, 3 * width), BF),
             jax.ShapeDtypeStruct((8, length), F32),
-            jax.ShapeDtypeStruct(branch.shape, BF),
         ],
 
     )
@@ -779,7 +759,7 @@
 
 def middle_back_kernel(
     mine_ref, own_ref, received_ref, probs_ref, router_ref, res_ref, n2_ref, cot_ref, gain_ref, wo_ref,
-    branch_ref, out_ref, parts_ref,
+    branch_ref, parts_ref, *out_refs,
 ):
     step = pl.program_id(0)
     blocks, rows, cols = cot_ref.shape
@@ -822,7 +802,12 @@
         which = lax.broadcasted_iota(jnp.int32, (8, full), 0)
         parts_ref[...] = jnp.where(which == EXPERTS, norm_part, router_part)
 
-    out_ref[0] = dot_t(branch_ref[...], wo_ref[...].reshape(-1, full)).astype(BF)
+    product = dot_t(branch_ref[...], wo_ref[...].reshape(-1, full)).astype(BF)
+    for k, ref in enumerate(out_refs):
+
+        @pl.when(step == k)
+        def _(ref=ref):
+            ref[...] = product
 
 
 def middle_back(mine, own, received, probs, router, residual, n2, cot, gains, w_out):
@@ -851,14 +836,14 @@
             ],
             out_specs=[
                 whole,
-                pl.BlockSpec((1, rows, width), lambda t, m: (t, 0, 0)),
                 pl.BlockSpec((8, full), lambda t, m: (0, 0)),
-            ],
+            ]
+            + [pl.BlockSpec((rows, width), lambda t, m: (0, 0))] * blocks,
         out_shape=[
             jax.ShapeDtypeStruct((rows, full), BF),
-            jax.ShapeDtypeStruct((blocks, rows, width), BF),
             jax.ShapeDtypeStruct((8, full), F32),
-        ],
+        ]
+        + [jax.ShapeDtypeStruct((rows, width), BF)] * blocks,
     )
 
 
@@ -1204,67 +1189,68 @@
     h2t, dg, du, n2t, mix = carried
 
     expert_grads = lax.psum(gate_up_grads(n2t, dg, du), "dp")
+    sum_down = Sum(n, 2, down_grads(table[half:], h2t, cot, n))
     dn2_flying = send(add_wide(later.pop(0), dn2_flying, LONG), 1, size)
-    sum_down = Sum(n, 2, down_grads(table[half:], h2t, cot, n))
     sum_down.keep = down_grads(table[:half], h2t, cot, n)
     for term in later:
         dn2_flying = send(add_wide(term, dn2_flying), 1, size)
     sum_down.step()
 
-    branch_rows, out_rows, small = middle_back(
+    branch_rows, small, *out_rows = middle_back(
         here, own_dn2, dn2_flying, expert_probs, router_wide, residual, normed_two, cot, gains, w_out
     )
 
     received = [send(out_rows[step], step, size) for step in steps]
     out_grad, branch_rows = arrange(owners, [out_rows[0]] + received, branch_rows)
     branch_blocks = [branch_rows, send(branch_rows, 1, size)]
+    sum_down.step()
     dq, dk, dv, gain_grads, own_back = attn_backward(
         prefix, q_pre, k_pre, q_rot, k_rot, v_rows, out_grad.reshape(length, -1), lse, gq, gk,
         cosine, sine, sums,
     )
     back = [own_back] + [send(own_back, step, size) for step in steps]
     sum_down.step()
-    grad_qkv, stat_one, branch_copy = norm_back(
-        q_pre, k_pre, dq, dk, dv, gq, gk, branch_blocks[1], sums, back
-    )
-    branch_blocks.append(send(branch_copy, 1, size))
+    branch_blocks.append(send(copied(branch_blocks[1], tuple(back[1:])), 1, size))
+    grad_qkv, stat_one = norm_back(q_pre, k_pre, dq, dk, dv, gq, gk, sums, back)
     in_grads, gain_part = column_grads(normed_one, grad_qkv, w_all)
-    small = jnp.concatenate([small[:7], gain_part[7:]])
-    small = add(small, *[send(small, step, size) for step in steps])
-    dn1 = input_grads(owner(1), cols, grad_qkv, w_all)
-    branch_copy, dn1 = copied_pair(branch_blocks[2], dn1, 1)
-    branch_blocks.append(send(branch_copy, 1, size))
-    dn1_flying = send(dn1, 1, size)
     sum_down.step()
-    for step in range(4, size):
+    for step in range(3, size):
         branch_blocks.append(send(copied(branch_blocks[-1]), 1, size))
-    out_grads = row_grads(owners, attended, branch_blocks)
-    packed = jnp.concatenate([small, gain_grads], axis=1)
+    packed = jnp.concatenate([jnp.concatenate([small[:7], gain_part[7:]]), gain_grads], axis=1)
     width = 3 * w_query.shape[1]
     extra = jnp.pad(packed.reshape(-1), (0, 32 * width - packed.size)).astype(BF).reshape(32, width)
+    out_grads = row_grads(owners, attended, branch_blocks)
     extra = copied(extra, (expert_grads,))
     in_grads, out_grads, extra = lax.psum((in_grads, out_grads, extra), "dp")
-    mix_flying = send(mix_block(owner(1), mix, work=LONG), 1, size)
+    dn1_flying = send(input_grads(owner(1), cols, grad_qkv, w_all, work=LONG), 1, size)
+    mix_flying = send(mix_block(owner(1), mix), 1, size)
+    sum_down.step()
     for step in range(2, size):
         dn1_flying = send(input_grads(owner(step), cols, grad_qkv, w_all, dn1_flying), 1, size)
         sum_down.step()
-        mix_flying = send(mix_block(owner(step), mix, mix_flying), 1, size)
-    for _ in range(2 * len(swap_masks(n))):
-        sum_down.step()
+        if step == 2:
+            grad_gate, grad_up = widen_experts(expert_grads)
+        if step < size - 1:
+            mix_flying = send(mix_block(owner(step), mix, mix_flying), 1, size)
+    mix_flying = send(mix_block(owner(size - 1), mix, mix_flying), 1, size)
 
     grad_tokens = final_grads(
         owners, grad_qkv, w_all, dn1_flying, tokens, own_sums, stat_one, norm1_gain[None],
         branch_blocks,
     )
-    grad_gate, grad_up = widen_experts(expert_grads)
+    for _ in range(2 * len(swap_masks(n))):
+        sum_down.step()
     grad_down = widen_pieces(positions, sum_down.finish(), n).reshape(w_down.shape)
 
     mixed = mix_block(owner(0), mix, mix_flying)
-    grad_query, grad_key, grad_value = widen_projections(in_grads)
+    extra = copied(extra)
     packed = extra.astype(F32).reshape(-1)[: packed.size].reshape(packed.shape)
     gain_total, packed = packed[:2, full:], packed[:, :full]
+    packed = [packed] + [send(packed, step, size) for step in steps]
+    grad_query, grad_key, grad_value = widen_projections(in_grads)
     grad_output = out_grads.astype(F32)
 
+    packed = add(*packed)
     grad_router = packed[:EXPERTS].T
     own = lax.dynamic_slice_in_dim(packed[EXPERTS:], mine * cols, cols, 1)
     grad_norm2_gain = own[0]

time: 787 us -> 763 us (0.970)
  waiting for transfers between devices: 317 us -> 294 us
    ppermute x36, waiting for transfers between devices: 298 us -> 258 us  [send(): lax.ppermute(value, 'tensor', [(at, (at + step) % size) for at in range(s...]
    ppermute x10, waiting for transfers between devices: 4.95 us -> 20.5 us  [swap(): return lax.ppermute(field, 'dp', [(at, at ^ mask) for at in range(n)])]
    pallas_call x42 -> x44, Pallas kernels: 342 us -> 345 us  [launch(): pl.pallas_call(kernel, grid_spec=pltpu.PrefetchScalarGridSpec(num_scalar_...]
    unnamed x114 -> x120, local copies, waits for them, and re-layouts: 21.4 us -> 22.8 us
  transfers between devices with their start and end apart: 50 -> 50, of which waited for: 29 -> 25; matrix products, arithmetic and copies ran while one was open for 3% -> 3% of each run, Pallas kernels for 37% -> 41%
where the time goes in v3:
time: 763 us; the launch traced here: 752 us
  Pallas kernels  345 us (45%)
  waiting for transfers between devices  294 us (39%)
  starting transfers between devices  43.3 us (6%)
  local copies, waits for them, and re-layouts  36.8 us (5%)
  between operations  15.5 us (2%)
  other arithmetic  11 us (1%)
    pallas_call x44, Pallas kernels, launch(): pl.pallas_call(kernel, grid_spec=pltpu.PrefetchScalarGridSpec(num_scalar_...  345 us
    ppermute x36, waiting for transfers between devices, send(): lax.ppermute(value, 'tensor', [(at, (at + step) % size) for at in range(s...  258 us
    ppermute x36, starting transfers between devices, send(): lax.ppermute(value, 'tensor', [(at, (at + step) % size) for at in range(s...  33.6 us
    unnamed x120, local copies, waits for them, and re-layouts  22.8 us
    ppermute x10, waiting for transfers between devices, swap(): return lax.ppermute(field, 'dp', [(at, at ^ mask) for at in range(n)])  20.5 us
  transfers between devices with their start and end apart: 50, of which 25 were waited for; matrix products, arithmetic and copies ran while one was open for 3% of the time, Pallas kernels for 41%

profile of v3, /device:TPU:0, one launch (start us, length us, event | category | flops | bytes accessed | tf_op | source)
XLA Modules:
  0.0 751.6 jit_solution(12148281589829727951)
XLA Ops:
  13.9 8.5 %collective-permute-done.3 = bf16[80,2048]{1,0:T(8,128)(2,1)S(1)} collective-permute-done((bf16[80,2048]{1,0:T(8,128)(2,1)S(1)}, bf16[80,2048]{1,0:T(8,128)(2,1)S(1)}, u32[]{:S(2)}, u32[]{:S(2)}) %collective-permute-start.3) | collective-permute-done | bytes 327712 | tf_op jit(solution)/shard_map/ppermute | solution.py:80
  22.4 10.7 %collective-permute-done.4 = bf16[80,2048]{1,0:T(8,128)(2,1)S(1)} collective-permute-done((bf16[80,2048]{1,0:T(8,128)(2,1)S(1)}, bf16[80,2048]{1,0:T(8,128)(2,1)S(1)}, u32[]{:S(2)}, u32[]{:S(2)}) %collective-permute-start.4) | collective-permute-done | bytes 327712 | tf_op jit(solution)/shard_map/ppermute | solution.py:80
  33.1 9.7 %collective-permute-done.5 = bf16[80,2048]{1,0:T(8,128)(2,1)S(1)} collective-permute-done((bf16[80,2048]{1,0:T(8,128)(2,1)S(1)}, bf16[80,2048]{1,0:T(8,128)(2,1)S(1)}, u32[]{:S(2)}, u32[]{:S(2)}) %collective-permute-start.5) | collective-permute-done | bytes 327712 | tf_op jit(solution)/shard_map/ppermute | solution.py:80
  44.2 24.1 %collective-permute-done.refs_2_.refs_6_ = bf16[1024,512]{1,0:T(8,128)(2,1)S(1)} collective-permute-done((bf16[1024,512]{1,0:T(8,128)(2,1)S(1)}, bf16[1024,512]{1,0:T(8,128)(2,1)S(1)}, u32[]{:S(2)}, u32[]{:S(2)}) %collective-permute-start) | collective-permute-done | bytes 1048608 | tf_op jit(solution)/shard_map/ppermute | solution.py:80
  75.7 16.1 %collective-permute-done.1.refs_3_.refs_7_ = bf16[1024,512]{1,0:T(8,128)(2,1)} collective-permute-done((bf16[1024,512]{1,0:T(8,128)(2,1)S(1)}, bf16[1024,512]{1,0:T(8,128)(2,1)}, u32[]{:S(2)}, u32[]{:S(2)}) %collective-permute-start.1) | collective-permute-done | bytes 1048608 | tf_op jit(solution)/shard_map/ppermute | solution.py:80
  93.1 5.8 shard_map.290.refs_1_
  103.4 11.1 %collective-permute-done.2.refs_2_.refs_4_.refs_8_ = bf16[1024,512]{1,0:T(8,128)(2,1)S(1)} collective-permute-done((bf16[1024,512]{1,0:T(8,128)(2,1)}, bf16[1024,512]{1,0:T(8,128)(2,1)S(1)}, u32[]{:S(2)}, u32[]{:S(2)}) %collective-permute-start.2) | collective-permute-done | bytes 1048608 | tf_op jit(solution)/shard_map/ppermute | solution.py:80
  115.5 3.4 shard_map.291.refs_9_
  120.1 14.6 %shard_map.292 = (bf16[1024,2048]{1,0:T(8,128)(2,1)}, f32[1024,512]{1,0:T(8,128)}, f32[1024,512]{1,0:T(8,128)}, bf16[1024,512]{1,0:T(8,128)(2,1)}, f32[8,1024]{1,0:T(8,128)}) custom-call(s32[4]{0:T(128)} %and_select_fusion.refs_0_, bf16[1024,512]{1,0:T(8,128)(2,1)} %refs_4_.1, bf16[1024,512]{1,0:T(8,128)(2,1)} %copy-done.8, ...), custom_call_target="tpu_custom_call" | custom-call | flops 1 | bytes 1 | tf_op jit(solution)/shard_map/pallas_call | solution.py:42
  134.8 4.2 collective-permute-start.8
  143.3 14.0 %shard_map.293 = (bf16[1024,512]{1,0:T(8,128)(2,1)}, f32[1024,512]{1,0:T(8,128)}, bf16[1024,512]{1,0:T(8,128)(2,1)}, bf16[1024,512]{1,0:T(8,128)(2,1)}) custom-call(s32[1]{0:T(128)S(6)} %copy.79.refs_0_, f32[1024,512]{1,0:T(8,128)} %get-tuple-element.87.refs_1_.refs_0_, f32[1024,512]{1,0:T(8,128)} %get-tuple-element.88.refs_2_.refs_1_, ...), custom_call_target="tpu_custom_call" | custom-call | flops 1 | bytes 1 | tf_op jit(solution)/shard_map/pallas_call | solution.py:42
  161.1 3.5 collective-permute-start.11
  164.7 21.7 %collective-permute-done.10.refs_3_ = bf16[256,512]{1,0:T(8,128)(2,1)S(1)} collective-permute-done((bf16[256,512]{1,0:T(8,128)(2,1)S(1)}, bf16[256,512]{1,0:T(8,128)(2,1)S(1)}, u32[]{:S(2)}, u32[]{:S(2)}) %collective-permute-start.10) | collective-permute-done | bytes 262176 | tf_op jit(solution)/shard_map/ppermute | solution.py:80
  186.3 11.0 %collective-permute-done.9.refs_2_ = bf16[256,512]{1,0:T(8,128)(2,1)S(1)} collective-permute-done((bf16[256,512]{1,0:T(8,128)(2,1)S(1)}, bf16[256,512]{1,0:T(8,128)(2,1)S(1)}, u32[]{:S(2)}, u32[]{:S(2)}) %collective-permute-start.9) | collective-permute-done | bytes 262176 | tf_op jit(solution)/shard_map/ppermute | solution.py:80
  198.0 9.3 %shard_map.294 = (f32[256,2048]{1,0:T(8,128)}, bf16[256,2048]{1,0:T(8,128)(2,1)}) custom-call(s32[4]{0:T(128)} %and_select_fusion.refs_0_, bf16[1024,512]{1,0:T(8,128)(2,1)} %get-tuple-element.92.refs_1_, bf16[256,512]{1,0:T(8,128)(2,1)} %copy-done.40, bf16[256,512]{1,0:T(8,128)(2,1)} %copy-done.38, bf16[256,512]{1,0:T(8,128)(2,1)} %copy-done.39, ...), custom_call_target="tpu_custom_call" | custom-call | flops 1 | bytes 1 | tf_op jit(solution)/shard_map/pallas_call | solution.py:42
  207.3 14.3 %all-gather.4.cloned.1.call-done.refs_2_.refs_7_ = bf16[4,1024,512]{2,1,0:T(8,128)(2,1)} async-done(((bf16[1,1024,512]{2,1,0:T(8,128)(2,1)}), bf16[4,1024,512]{2,1,0:T(8,128)(2,1)}) %all-gather.4.cloned.1.call-update) | async-done | bytes 4194320 | tf_op jit(solution)/shard_map/all_gather | solution.py:1150
  225.6 19.2 %shard_map.296 = (bf16[1536,1024]{1,0:T(8,128)(2,1)}, bf16[1024,1536]{1,0:T(8,128)(2,1)}, bf16[1024,1536]{1,0:T(8,128)(2,1)}, bf16[2048,1024]{1,0:T(8,128)(2,1)}...) custom-call(s32[1]{0:T(128)} %get-tuple-element.179.refs_0_, ...), custom_call_target="tpu_custom_call" | custom-call | flops 1 | bytes 1 | tf_op jit(solution)/shard_map/pallas_call | solution.py:42
  244.8 7.1 collective-permute-done.12.refs_1_
  256.3 18.4 %shard_map.298 = (bf16[1536,1024]{1,0:T(8,128)(2,1)}, bf16[1024,1536]{1,0:T(8,128)(2,1)}, bf16[1024,1536]{1,0:T(8,128)(2,1)}, bf16[2048,1024]{1,0:T(8,128)(2,1)}...) custom-call(s32[1]{0:T(128)} %get-tuple-element.177.refs_0_, ...), custom_call_target="tpu_custom_call", output_to_operand_aliasing={{0}: (8, {}), {1}: (9, {}), {2}: (10, {}), {3}: (11, {}), {... | custom-call | flops 1 | bytes 1 | tf_op jit(solution)/shard_map/pallas_call | solution.py:42
  274.7 7.7 %collective-permute-done.13.refs_1_ = bf16[256,2048]{1,0:T(8,128)(2,1)S(1)} collective-permute-done((bf16[256,2048]{1,0:T(8,128)(2,1)}, bf16[256,2048]{1,0:T(8,128)(2,1)S(1)}, u32[]{:S(2)}, u32[]{:S(2)}) %collective-permute-start.13) | collective-permute-done | bytes 1048608 | tf_op jit(solution)/shard_map/ppermute | solution.py:80
  286.8 18.4 %shard_map.300 = (bf16[1536,1024]{1,0:T(8,128)(2,1)}, bf16[1024,1536]{1,0:T(8,128)(2,1)}, bf16[1024,1536]{1,0:T(8,128)(2,1)}, bf16[2048,1024]{1,0:T(8,128)(2,1)}...) custom-call(s32[1]{0:T(128)} %get-tuple-element.176.refs_0_, ...), custom_call_target="tpu_custom_call", output_to_operand_aliasing={{0}: (8, {}), {1}: (9, {}), {2}: (10, {}), {3}: (11, {}), {... | custom-call | flops 1 | bytes 1 | tf_op jit(solution)/shard_map/pallas_call | solution.py:42
  305.2 6.7 collective-permute-done.14.refs_1_
  312.9 18.4 %shard_map.301 = (bf16[1536,1024]{1,0:T(8,128)(2,1)}, bf16[1024,1536]{1,0:T(8,128)(2,1)}, bf16[1024,1536]{1,0:T(8,128)(2,1)}, bf16[2048,1024]{1,0:T(8,128)(2,1)}...) custom-call(s32[1]{0:T(128)} %get-tuple-element.178.refs_0_, ...), custom_call_target="tpu_custom_call", output_to_operand_aliasing={{0}: (8, {}), {1}: (9, {}), {2}: (10, {}), {3}: (11, {}), {... | custom-call | flops 1 | bytes 1 | tf_op jit(solution)/shard_map/pallas_call | solution.py:42
  331.3 3.4 shard_map.302.refs_3_
  335.2 18.1 %shard_map.303.refs_3_ = bf16[2,6,2048,256]{3,2,1,0:T(8,128)(2,1)} custom-call(bf16[2048,1024]{1,0:T(8,128)(2,1)} %get-tuple-element.122.refs_0_, bf16[1024,1536]{1,0:T(8,128)(2,1)} %get-tuple-element.123.refs_1_, bf16[1024,1536]{1,0:T(8,128)(2,1)} %get-tuple-element.124.refs_2_, bf16[1,256,2176]{2,1,0:T(8,128)(2,1)} %shard_map.302.refs_3_), custom_call_target="tpu_custom_call" | custom-call | flops 1 | bytes 1 | tf_op jit(solution)/shard_map/pallas_call | solution.py:42
  353.3 8.2 %shard_map.304.refs_2_ = bf16[4,192,2048]{2,1,0:T(8,128)(2,1)} custom-call(s32[4]{0:T(128)} %get-tuple-element.175.refs_0_, bf16[1536,1024]{1,0:T(8,128)(2,1)} %get-tuple-element.121.refs_1_, bf16[4,1024,512]{2,1,0:T(8,128)(2,1)} %all-gather.4.cloned.1.call-done.refs_2_.refs_7_, bf16[2,6,2048,256]{3,2,1,0:T(8,128)(2,1)} %shard_map.303.refs_3_), custom_call_target="tpu_custom_call" | custom-call | flops 1 | bytes 1 | tf_op jit(solution)/shard_map/pallas_call | solution.py:42
  363.3 3.7 shard_map.305.refs_3_
  366.9 8.2 %shard_map.306.refs_2_.refs_0_ = bf16[4,192,2048]{2,1,0:T(8,128)(2,1)} custom-call(s32[4]{0:T(128)} %get-tuple-element.174.refs_0_, bf16[1536,1024]{1,0:T(8,128)(2,1)} %get-tuple-element.121.refs_1_, bf16[4,1024,512]{2,1,0:T(8,128)(2,1)} %all-gather.4.cloned.1.call-done.refs_2_.refs_7_, bf16[1,256,2176]{2,1,0:T(8,128)(2,1)} %shard_map.305.refs_3_), custom_call_target="tpu_custom_call" | custom-call | flops 1 | bytes 1 | tf_op jit(solution)/shard_map/pallas_call | solution.py:42
  375.1 20.4 %collective-permute-done.16 = bf16[256,2176]{1,0:T(8,128)(2,1)S(1)} collective-permute-done((bf16[256,2176]{1,0:T(8,128)(2,1)}, bf16[256,2176]{1,0:T(8,128)(2,1)S(1)}, u32[]{:S(2)}, u32[]{:S(2)}) %collective-permute-start.16) | collective-permute-done | bytes 1114144 | tf_op jit(solution)/shard_map/ppermute | solution.py:80
  396.5 3.7 shard_map.307.refs_2_
  400.4 5.2 shard_map.308
  405.6 22.6 %collective-permute-done.17.refs_2_ = bf16[256,2176]{1,0:T(8,128)(2,1)S(1)} collective-permute-done((bf16[256,2176]{1,0:T(8,128)(2,1)}, bf16[256,2176]{1,0:T(8,128)(2,1)S(1)}, u32[]{:S(2)}, u32[]{:S(2)}) %collective-permute-start.17) | collective-permute-done | bytes 1114144 | tf_op jit(solution)/shard_map/ppermute | solution.py:80
  429.2 11.1 %shard_map.309 = (bf16[256,2048]{1,0:T(8,128)(2,1)}, f32[8,2048]{1,0:T(8,128)}, bf16[256,512]{1,0:T(8,128)(2,1)}, bf16[256,512]{1,0:T(8,128)(2,1)}, bf16[256,512]{1,0:T(8,128)(2,1)}, /*index=5*/bf16[256,512]{1,0:T(8,128)(2,1)}) custom-call(s32[1]{0:T(128)} %bitcast.23.refs_0_, bf16[256,2176]{1,0:T(8,128)(2,1)} %get-tuple-element.116.refs_1_, ...), custom_call_target="tpu_custom_call" | custom-call | flops 1 | bytes 1 | tf_op jit(solution)/shard_map/pallas_call | solution.py:42
  446.9 4.7 collective-permute-done.19.refs_2_
  451.6 8.7 %collective-permute-done.20.refs_3_ = bf16[256,512]{1,0:T(8,128)(2,1)S(1)} collective-permute-done((bf16[256,512]{1,0:T(8,128)(2,1)}, bf16[256,512]{1,0:T(8,128)(2,1)S(1)}, u32[]{:S(2)}, u32[]{:S(2)}) %collective-permute-start.20) | collective-permute-done | bytes 262176 | tf_op jit(solution)/shard_map/ppermute | solution.py:80
  461.1 4.5 shard_map.310
  465.6 5.1 collective-permute-start.27
  471.9 4.0 shard_map.311
  478.6 19.0 %shard_map.312 = (f32[1024,512]{1,0:T(8,128)}, f32[1024,512]{1,0:T(8,128)}, bf16[1024,512]{1,0:T(8,128)(2,1)}, f32[8,512]{1,0:T(8,128)}, f32[8,1024]{1,0:T(8,128)}) custom-call(s32[1]{0:T(128)S(6)} %copy.79.refs_0_, f32[1024,512]{1,0:T(8,128)} %get-tuple-element.87.refs_1_.refs_0_, f32[1024,512]{1,0:T(8,128)} %get-tuple-element.88.refs_2_.refs_1_, ...), custom_call_target="tpu_custom_call" | custom-call | flops 1 | bytes 1 | tf_op jit(solution)/shard_map/pallas_call | solution.py:42
  502.3 3.6 shard_map.313
  506.9 3.4 shard_map.314.refs_15_
  512.2 6.5 shard_map.315
  518.7 12.3 %shard_map.316 = (bf16[2048,1536]{1,0:T(8,128)(2,1)}, f32[8,2048]{1,0:T(8,128)}) custom-call(bf16[1024,2048]{1,0:T(8,128)(2,1)} %get-tuple-element.91.refs_12_.refs_0_, bf16[1024,1536]{1,0:T(8,128)(2,1)} %get-tuple-element.146.refs_1_, bf16[2048,1536]{1,0:T(8,128)(2,1)} %bitcast.78), custom_call_target="tpu_custom_call" | custom-call | flops 1 | bytes 1 | tf_op jit(solution)/shard_map/pallas_call | solution.py:42
  531.9 3.6 shard_map.317
  536.5 3.4 shard_map.318.refs_6_
  543.5 20.5 %collective-permute-done.33.refs_5_.refs_11_ = bf16[256,2048]{1,0:T(8,128)(2,1)S(1)} collective-permute-done((bf16[256,2048]{1,0:T(8,128)(2,1)}, bf16[256,2048]{1,0:T(8,128)(2,1)S(1)}, u32[]{:S(2)}, u32[]{:S(2)}) %collective-permute-start.33) | collective-permute-done | bytes 1048608 | tf_op jit(solution)/shard_map/ppermute | solution.py:80
  565.0 7.1 shard_map.319.refs_1_
  573.6 6.1 shard_map.321.refs_2_
  583.5 3.9 shard_map.322.refs_4_
  587.8 18.2 %collective-permute-done.36.refs_1_ = bf16[2,192,1024]{2,1,0:T(8,128)(2,1)S(1)} collective-permute-done((bf16[2,192,1024]{2,1,0:T(8,128)(2,1)S(1)}, bf16[2,192,1024]{2,1,0:T(8,128)(2,1)S(1)}, u32[]{:S(2)}, u32[]{:S(2)}) %collective-permute-start.36) | collective-permute-done | bytes 786464 | tf_op jit(solution)/shard_map/ppermute | solution.py:99
  609.2 4.3 shard_map.323.refs_4_.refs_1_
  614.5 6.6 shard_map.324.refs_1_
  621.1 14.0 %shard_map.325 = (f32[6,2048,256]{2,1,0:T(8,128)}, f32[6,2048,256]{2,1,0:T(8,128)}) custom-call(bf16[2,6,2048,256]{3,2,1,0:T(8,128)(2,1)} %all-reduce.8.cloned.1.call-done.refs_2_.refs_0_, bf16[1024,512]{1,0:T(8,128)(2,1)} %shard_map.324.refs_1_), custom_call_target="tpu_custom_call" | custom-call | flops 1 | bytes 1 | tf_op jit(solution)/shard_map/pallas_call | solution.py:42
  636.1 4.3 shard_map.326.refs_4_
  640.4 12.7 %collective-permute-done.39.refs_3_ = bf16[1024,512]{1,0:T(8,128)(2,1)S(1)} collective-permute-done((bf16[1024,512]{1,0:T(8,128)(2,1)}, bf16[1024,512]{1,0:T(8,128)(2,1)S(1)}, u32[]{:S(2)}, u32[]{:S(2)}) %collective-permute-start.39) | collective-permute-done | bytes 1048608 | tf_op jit(solution)/shard_map/ppermute | solution.py:80
  654.0 6.5 shard_map.327.refs_3_
  660.5 15.0 %collective-permute-done.38.refs_2_ = bf16[1024,512]{1,0:T(8,128)(2,1)S(1)} collective-permute-done((bf16[1024,512]{1,0:T(8,128)(2,1)}, bf16[1024,512]{1,0:T(8,128)(2,1)S(1)}, u32[]{:S(2)}, u32[]{:S(2)}) %collective-permute-start.38) | collective-permute-done | bytes 1048608 | tf_op jit(solution)/shard_map/ppermute | solution.py:80
  676.5 4.3 shard_map.328.refs_12_
  682.0 16.0 %collective-permute-done.42.refs_3_ = bf16[1024,512]{1,0:T(8,128)(2,1)S(1)} collective-permute-done((bf16[1024,512]{1,0:T(8,128)(2,1)}, bf16[1024,512]{1,0:T(8,128)(2,1)S(1)}, u32[]{:S(2)}, u32[]{:S(2)}) %collective-permute-start.42) | collective-permute-done | bytes 1048608 | tf_op jit(solution)/shard_map/ppermute | solution.py:80
  698.9 7.6 %shard_map.329.refs_3_ = f32[1024,512]{1,0:T(8,128)} custom-call(s32[4]{0:T(128)} %and_select_fusion.refs_0_, bf16[1024,1536]{1,0:T(8,128)(2,1)} %get-tuple-element.146.refs_1_, bf16[2048,1536]{1,0:T(8,128)(2,1)} %bitcast.82, bf16[1024,512]{1,0:T(8,128)(2,1)} %copy-done.18, bf16[1024,512]{1,0:T(8,128)(2,1)} %refs_4_.1, ...), custom_call_target="tpu_custom_call" | custom-call | flops 1 | bytes 1 | tf_op jit(solution)/shard_map/pallas_call | solution.py:42
  706.5 10.5 %shard_map.330.refs_3_ = f32[1536,2048]{1,0:T(8,128)} custom-call(s32[8]{0:T(128)} %gather_fusion, bf16[4,192,2048]{2,1,0:T(8,128)(2,1)} %shard_map.323.refs_4_.refs_1_, bf16[4,192,2048]{2,1,0:T(8,128)(2,1)} %collective-permute-done.41.refs_2_, f32[1024,512]{1,0:T(8,128)} %shard_map.329.refs_3_), custom_call_target="tpu_custom_call" | custom-call | flops 1 | bytes 1 | tf_op jit(solution)/shard_map/pallas_call | solution.py:42
  719.2 4.3 shard_map.331.refs_1_
  726.4 3.4 collective-permute-start.45
  730.5 9.7 %shard_map.333 = (f32[2048,512]{1,0:T(8,128)}, f32[2048,512]{1,0:T(8,128)}, f32[2048,512]{1,0:T(8,128)}) custom-call(bf16[2048,1536]{1,0:T(8,128)(2,1)} %get-tuple-element.161.refs_0_, bf16[1,32,1536]{2,1,0:T(8,128)(2,1)} %shard_map.332.refs_1_), custom_call_target="tpu_custom_call" | custom-call | flops 1 | bytes 1 | tf_op jit(solution)/shard_map/pallas_call | solution.py:42
  (263 shorter events, 100.0 us)
Async XLA Ops:
  7.2 190.1 %all-gather.6.cloned.1.call-start = ((), (), s32[]{:S(2)}) async-start(), calls=%async_computation.2 | async-start | bytes 9437184 | tf_op jit(solution)/shard_map/all_gather | solution.py:1137
  9.5 12.8 %collective-permute-start.3 = (bf16[80,2048]{1,0:T(8,128)(2,1)S(1)}, bf16[80,2048]{1,0:T(8,128)(2,1)S(1)}, u32[]{:S(2)}, u32[]{:S(2)}) collective-permute-start(bf16[80,2048]{1,0:T(8,128)(2,1)S(1)} %fusion.18), channel_id=1, source_target_pairs={{0,1},{1,2},{2,3},{3,0},{4,5},{5,6},{6,7},{7,4},{8,9},{9,10},{10,1... | collective-permute-start | bytes 983048 | tf_op jit(solution)/shard_map/ppermute | solution.py:80
  12.8 31.2 %copy-start.4 = (bf16[1024,512]{1,0:T(8,128)(2,1)S(1)}, bf16[1024,512]{1,0:T(8,128)(2,1)}, u32[]{:S(2)}) copy-start(bf16[1024,512]{1,0:T(8,128)(2,1)} %refs_4_.1) | copy-start | bytes 3145732
  12.8 31.3 %copy-start.47 = (s32[1,3072]{1,0:T(1,128)S(1)}, s32[1,3072]{1,0:T(1,128)}, u32[]{:S(2)}) copy-start(s32[1,3072]{1,0:T(1,128)} %param.35) | copy-start | bytes 36868
  12.8 55.7 %copy-start.58 = (s32[1024,3]{0,1:T(4,128)S(1)}, s32[1024,3]{0,1:T(4,128)}, u32[]{:S(2)}) copy-start(s32[1024,3]{0,1:T(4,128)} %param.33) | copy-start | bytes 36868
  22.4 10.7 %collective-permute-start.4 = (bf16[80,2048]{1,0:T(8,128)(2,1)S(1)}, bf16[80,2048]{1,0:T(8,128)(2,1)S(1)}, u32[]{:S(2)}, u32[]{:S(2)}) collective-permute-start(bf16[80,2048]{1,0:T(8,128)(2,1)S(1)} %collective-permute-done.3), channel_id=1, source_target_pairs={{0,1},{1,2},{2,3},{3,0},{4,5},{5,6},{6,7},{7,4},{8,9},{9,10},{10,1... | collective-permute-start | bytes 983048 | tf_op jit(solution)/shard_map/ppermute | solution.py:80
  33.1 9.8 %collective-permute-start.5 = (bf16[80,2048]{1,0:T(8,128)(2,1)S(1)}, bf16[80,2048]{1,0:T(8,128)(2,1)S(1)}, u32[]{:S(2)}, u32[]{:S(2)}) collective-permute-start(bf16[80,2048]{1,0:T(8,128)(2,1)S(1)} %collective-permute-done.4), channel_id=1, source_target_pairs={{0,1},{1,2},{2,3},{3,0},{4,5},{5,6},{6,7},{7,4},{8,9},{9,10},{10,1... | collective-permute-start | bytes 983048 | tf_op jit(solution)/shard_map/ppermute | solution.py:80
  43.9 177.7 %all-gather.4.cloned.1.call-start = ((), (), s32[]{:S(2)}) async-start(), calls=%async_computation | async-start | bytes 5242880 | tf_op jit(solution)/shard_map/all_gather | solution.py:1150
  44.0 24.4 %collective-permute-start = (bf16[1024,512]{1,0:T(8,128)(2,1)S(1)}, bf16[1024,512]{1,0:T(8,128)(2,1)S(1)}, u32[]{:S(2)}, u32[]{:S(2)}) collective-permute-start(bf16[1024,512]{1,0:T(8,128)(2,1)S(1)} %copy-done.4), channel_id=1, source_target_pairs={{0,1},{1,2},{2,3},{3,0},{4,5},{5,6},{6,7},{7,4},{8,9},{9,10},{10,1... | collective-permute-start | bytes 3145736 | tf_op jit(solution)/shard_map/ppermute | solution.py:80
  68.3 23.5 %collective-permute-start.1 = (bf16[1024,512]{1,0:T(8,128)(2,1)S(1)}, bf16[1024,512]{1,0:T(8,128)(2,1)}, u32[]{:S(2)}, u32[]{:S(2)}) collective-permute-start(bf16[1024,512]{1,0:T(8,128)(2,1)S(1)} %collective-permute-done.refs_2_.refs_6_), channel_id=1, source_target_pairs={{0,1},{1,2},{2,3},{3,0},{4,5},{5,6},{6,7},{7,4},{8,9},{9,10},{10,1... | collective-permute-start | bytes 3145736 | tf_op jit(solution)/shard_map/ppermute | solution.py:80
  91.8 22.7 %collective-permute-start.2 = (bf16[1024,512]{1,0:T(8,128)(2,1)}, bf16[1024,512]{1,0:T(8,128)(2,1)S(1)}, u32[]{:S(2)}, u32[]{:S(2)}) collective-permute-start(bf16[1024,512]{1,0:T(8,128)(2,1)} %collective-permute-done.1.refs_3_.refs_7_), channel_id=1, source_target_pairs={{0,1},{1,2},{2,3},{3,0},{4,5},{5,6},{6,7},{7,4},{8,9},{9,10},{10,1... | collective-permute-start | bytes 3145736 | tf_op jit(solution)/shard_map/ppermute | solution.py:80
  120.1 18.9 %copy-start.54 = (bf16[512]{0:T(512)(128)(2,1)S(1)}, bf16[512]{0:T(512)(128)(2,1)}, u32[]{:S(2)}) copy-start(bf16[512]{0:T(512)(128)(2,1)} %param.25) | copy-start | bytes 3076
  120.1 19.5 %copy-start.55 = (bf16[512]{0:T(512)(128)(2,1)S(1)}, bf16[512]{0:T(512)(128)(2,1)}, u32[]{:S(2)}) copy-start(bf16[512]{0:T(512)(128)(2,1)} %param.26) | copy-start | bytes 3076
  134.6 6.7 collective-permute-start.6
  134.7 6.6 collective-permute-start.7
  134.8 7.9 %collective-permute-start.8 = (f32[8,1024]{1,0:T(8,128)}, f32[8,1024]{1,0:T(8,128)S(1)}, u32[]{:S(2)}, u32[]{:S(2)}) collective-permute-start(f32[8,1024]{1,0:T(8,128)} %get-tuple-element.90.refs_8_.refs_12_.refs_7_.refs_5_), channel_id=1, source_target_pairs={{0,3},{1,0},{2,1},{3,2},{4,7},{5,4},{6,5},{7,6},{8,11},{9,8},{10,9... | collective-permute-start | bytes 98312 | tf_op jit(solution)/shard_map/ppermute | solution.py:80
  158.5 27.9 %collective-permute-start.10 = (bf16[256,512]{1,0:T(8,128)(2,1)S(1)}, bf16[256,512]{1,0:T(8,128)(2,1)S(1)}, u32[]{:S(2)}, u32[]{:S(2)}) collective-permute-start(bf16[256,512]{1,0:T(8,128)(2,1)S(1)} %get-tuple-element.164), channel_id=1, source_target_pairs={{0,2},{1,3},{2,0},{3,1},{4,6},{5,7},{6,4},{7,5},{8,10},{9,11},{10,... | collective-permute-start | bytes 786440 | tf_op jit(solution)/shard_map/ppermute | solution.py:80
  161.1 25.2 %collective-permute-start.11 = (bf16[256,512]{1,0:T(8,128)(2,1)S(1)}, bf16[256,512]{1,0:T(8,128)(2,1)S(1)}, u32[]{:S(2)}, u32[]{:S(2)}) collective-permute-start(bf16[256,512]{1,0:T(8,128)(2,1)S(1)} %get-tuple-element.163), channel_id=1, source_target_pairs={{0,3},{1,0},{2,1},{3,2},{4,7},{5,4},{6,5},{7,6},{8,11},{9,8},{10,9... | collective-permute-start | bytes 786440 | tf_op jit(solution)/shard_map/ppermute | solution.py:80
  164.6 32.7 %collective-permute-start.9 = (bf16[256,512]{1,0:T(8,128)(2,1)S(1)}, bf16[256,512]{1,0:T(8,128)(2,1)S(1)}, u32[]{:S(2)}, u32[]{:S(2)}) collective-permute-start(bf16[256,512]{1,0:T(8,128)(2,1)S(1)} %get-tuple-element.165), channel_id=1, source_target_pairs={{0,1},{1,2},{2,3},{3,0},{4,5},{5,6},{6,7},{7,4},{8,9},{9,10},{10,1... | collective-permute-start | bytes 786440 | tf_op jit(solution)/shard_map/ppermute | solution.py:80
  186.3 11.0 %copy-start.38 = (bf16[256,512]{1,0:T(8,128)(2,1)}, bf16[256,512]{1,0:T(8,128)(2,1)S(1)}, u32[]{:S(2)}) copy-start(bf16[256,512]{1,0:T(8,128)(2,1)S(1)} %collective-permute-done.10.refs_3_) | copy-start | bytes 786436
  186.3 11.0 %copy-start.39 = (bf16[256,512]{1,0:T(8,128)(2,1)}, bf16[256,512]{1,0:T(8,128)(2,1)S(1)}, u32[]{:S(2)}) copy-start(bf16[256,512]{1,0:T(8,128)(2,1)S(1)} %collective-permute-done.11.refs_4_) | copy-start | bytes 786436
  225.0 26.9 %collective-permute-start.12 = (bf16[256,2048]{1,0:T(8,128)(2,1)}, bf16[256,2048]{1,0:T(8,128)(2,1)S(1)}, u32[]{:S(2)}, u32[]{:S(2)}) collective-permute-start(bf16[256,2048]{1,0:T(8,128)(2,1)} %bitcast.88), channel_id=1, source_target_pairs={{0,1},{1,2},{2,3},{3,0},{4,5},{5,6},{6,7},{7,4},{8,9},{9,10},{10,1... | collective-permute-start | bytes 3145736 | tf_op jit(solution)/shard_map/ppermute | solution.py:80
  256.3 26.0 %collective-permute-start.13 = (bf16[256,2048]{1,0:T(8,128)(2,1)}, bf16[256,2048]{1,0:T(8,128)(2,1)S(1)}, u32[]{:S(2)}, u32[]{:S(2)}) collective-permute-start(bf16[256,2048]{1,0:T(8,128)(2,1)} %bitcast.99), channel_id=1, source_target_pairs={{0,1},{1,2},{2,3},{3,0},{4,5},{5,6},{6,7},{7,4},{8,9},{9,10},{10,1... | collective-permute-start | bytes 3145736 | tf_op jit(solution)/shard_map/ppermute | solution.py:80
  286.6 25.3 %collective-permute-start.14 = (bf16[256,2048]{1,0:T(8,128)(2,1)}, bf16[256,2048]{1,0:T(8,128)(2,1)S(1)}, u32[]{:S(2)}, u32[]{:S(2)}) collective-permute-start(bf16[256,2048]{1,0:T(8,128)(2,1)} %bitcast.98), channel_id=1, source_target_pairs={{0,1},{1,2},{2,3},{3,0},{4,5},{5,6},{6,7},{7,4},{8,9},{9,10},{10,1... | collective-permute-start | bytes 3145736 | tf_op jit(solution)/shard_map/ppermute | solution.py:80
  312.9 21.8 %copy-start.2 = (s32[8]{0:T(128)S(1)}, s32[8]{0:T(128)}, u32[]{:S(2)}) copy-start(s32[8]{0:T(128)} %constant.112.clone) | copy-start | bytes 100
  334.7 27.6 %collective-permute-start.15 = (bf16[256,2176]{1,0:T(8,128)(2,1)}, bf16[256,2176]{1,0:T(8,128)(2,1)S(1)}, u32[]{:S(2)}, u32[]{:S(2)}) collective-permute-start(bf16[256,2176]{1,0:T(8,128)(2,1)} %bitcast.94), channel_id=1, source_target_pairs={{0,1},{1,2},{2,3},{3,0},{4,5},{5,6},{6,7},{7,4},{8,9},{9,10},{10,1... | collective-permute-start | bytes 3342344 | tf_op jit(solution)/shard_map/ppermute | solution.py:80
  361.5 210.6 %all-reduce.8.cloned.1.call-start = ((), (), s32[]{:S(2)}) async-start(), calls=%async_computation.1 | async-start | bytes 25165824 | tf_op jit(solution)/shard_map/psum | solution.py:1191
  361.5 38.8 %collective-permute-start.18 = (bf16[4,192,2048]{2,1,0:T(8,128)(2,1)}, bf16[4,192,2048]{2,1,0:T(8,128)(2,1)}, u32[]{:S(2)}, u32[]{:S(2)}) collective-permute-start(bf16[4,192,2048]{2,1,0:T(8,128)(2,1)} %shard_map.304.refs_2_), channel_id=1, source_target_pairs={{0,4},{4,0},{8,12},{12,8},{16,20},{20,16},{24,28},{28,24},{1,5},{5... | collective-permute-start | bytes 9437192 | tf_op jit(solution)/shard_map/ppermute | solution.py:99
  366.9 28.6 %collective-permute-start.16 = (bf16[256,2176]{1,0:T(8,128)(2,1)}, bf16[256,2176]{1,0:T(8,128)(2,1)S(1)}, u32[]{:S(2)}, u32[]{:S(2)}) collective-permute-start(bf16[256,2176]{1,0:T(8,128)(2,1)} %bitcast.104), channel_id=1, source_target_pairs={{0,1},{1,2},{2,3},{3,0},{4,5},{5,6},{6,7},{7,4},{8,9},{9,10},{10,1... | collective-permute-start | bytes 3342344 | tf_op jit(solution)/shard_map/ppermute | solution.py:80
  400.2 28.0 %collective-permute-start.17 = (bf16[256,2176]{1,0:T(8,128)(2,1)}, bf16[256,2176]{1,0:T(8,128)(2,1)S(1)}, u32[]{:S(2)}, u32[]{:S(2)}) collective-permute-start(bf16[256,2176]{1,0:T(8,128)(2,1)} %bitcast.93), channel_id=1, source_target_pairs={{0,1},{1,2},{2,3},{3,0},{4,5},{5,6},{6,7},{7,4},{8,9},{9,10},{10,1... | collective-permute-start | bytes 3342344 | tf_op jit(solution)/shard_map/ppermute | solution.py:80
  405.6 38.5 %copy-start.25 = (bf16[2,192,1024]{2,1,0:T(8,128)(2,1)S(1)}, bf16[2,192,1024]{2,1,0:T(8,128)(2,1)}, u32[]{:S(2)}) copy-start(bf16[2,192,1024]{2,1,0:T(8,128)(2,1)} %get-tuple-element.125.refs_10_) | copy-start | bytes 2359300
  405.6 39.9 %copy-start.57 = (bf16[2,192,1024]{2,1,0:T(8,128)(2,1)S(1)}, bf16[2,192,1024]{2,1,0:T(8,128)(2,1)}, u32[]{:S(2)}) copy-start(bf16[2,192,1024]{2,1,0:T(8,128)(2,1)} %get-tuple-element.135) | copy-start | bytes 2359300
  440.2 11.4 %collective-permute-start.19 = (bf16[256,512]{1,0:T(8,128)(2,1)}, bf16[256,512]{1,0:T(8,128)(2,1)S(1)}, u32[]{:S(2)}, u32[]{:S(2)}) collective-permute-start(bf16[256,512]{1,0:T(8,128)(2,1)} %get-tuple-element.127), channel_id=1, source_target_pairs={{0,1},{1,2},{2,3},{3,0},{4,5},{5,6},{6,7},{7,4},{8,9},{9,10},{10,1... | collective-permute-start | bytes 786440 | tf_op jit(solution)/shard_map/ppermute | solution.py:80
  440.2 20.1 %collective-permute-start.20 = (bf16[256,512]{1,0:T(8,128)(2,1)}, bf16[256,512]{1,0:T(8,128)(2,1)S(1)}, u32[]{:S(2)}, u32[]{:S(2)}) collective-permute-start(bf16[256,512]{1,0:T(8,128)(2,1)} %get-tuple-element.128), channel_id=1, source_target_pairs={{0,2},{1,3},{2,0},{3,1},{4,6},{5,7},{6,4},{7,5},{8,10},{9,11},{10,... | collective-permute-start | bytes 786440 | tf_op jit(solution)/shard_map/ppermute | solution.py:80
  441.3 19.0 %collective-permute-start.21 = (bf16[256,512]{1,0:T(8,128)(2,1)}, bf16[256,512]{1,0:T(8,128)(2,1)S(1)}, u32[]{:S(2)}, u32[]{:S(2)}) collective-permute-start(bf16[256,512]{1,0:T(8,128)(2,1)} %get-tuple-element.129), channel_id=1, source_target_pairs={{0,3},{1,0},{2,1},{3,2},{4,7},{5,4},{6,5},{7,6},{8,11},{9,8},{10,9... | collective-permute-start | bytes 786440 | tf_op jit(solution)/shard_map/ppermute | solution.py:80
  444.1 26.6 %collective-permute-start.22 = (bf16[2,192,1024]{2,1,0:T(8,128)(2,1)S(1)}, bf16[2,192,1024]{2,1,0:T(8,128)(2,1)S(1)}, u32[]{:S(2)}, u32[]{:S(2)}) collective-permute-start(bf16[2,192,1024]{2,1,0:T(8,128)(2,1)S(1)} %copy-done.25), channel_id=1, source_target_pairs={{0,8},{4,12},{8,0},{12,4},{16,24},{20,28},{24,16},{28,20},{1,9},{5... | collective-permute-start | bytes 2359304 | tf_op jit(solution)/shard_map/ppermute | solution.py:99
  445.5 25.2 %collective-permute-start.23 = (bf16[2,192,1024]{2,1,0:T(8,128)(2,1)S(1)}, bf16[2,192,1024]{2,1,0:T(8,128)(2,1)S(1)}, u32[]{:S(2)}, u32[]{:S(2)}) collective-permute-start(bf16[2,192,1024]{2,1,0:T(8,128)(2,1)S(1)} %copy-done.57), channel_id=1, source_target_pairs={{0,16},{4,20},{8,24},{12,28},{16,0},{20,4},{24,8},{28,12},{1,17},{... | collective-permute-start | bytes 2359304 | tf_op jit(solution)/shard_map/ppermute | solution.py:99
  465.6 40.4 %collective-permute-start.27 = (bf16[256,2048]{1,0:T(8,128)(2,1)}, bf16[256,2048]{1,0:T(8,128)(2,1)S(1)}, u32[]{:S(2)}, u32[]{:S(2)}) collective-permute-start(bf16[256,2048]{1,0:T(8,128)(2,1)} %get-tuple-element.141.refs_2_.refs_8_), channel_id=1, source_target_pairs={{0,1},{1,2},{2,3},{3,0},{4,5},{5,6},{6,7},{7,4},{8,9},{9,10},{10,1... | collective-permute-start | bytes 3145736 | tf_op jit(solution)/shard_map/ppermute | solution.py:80
  475.8 23.1 %collective-permute-start.28 = (bf16[1,192,1024]{2,1,0:T(8,128)(2,1)}, bf16[1,192,1024]{2,1,0:T(8,128)(2,1)S(1)}, u32[]{:S(2)}, u32[]{:S(2)}) collective-permute-start(bf16[1,192,1024]{2,1,0:T(8,128)(2,1)} %get-tuple-element.136.refs_16_), channel_id=1, source_target_pairs={{0,16},{4,20},{8,24},{12,28},{16,0},{20,4},{24,8},{28,12},{1,17},{... | collective-permute-start | bytes 1179656 | tf_op jit(solution)/shard_map/ppermute | solution.py:99
  477.3 24.2 %collective-permute-start.29 = (bf16[1,192,1024]{2,1,0:T(8,128)(2,1)}, bf16[1,192,1024]{2,1,0:T(8,128)(2,1)S(1)}, u32[]{:S(2)}, u32[]{:S(2)}) collective-permute-start(bf16[1,192,1024]{2,1,0:T(8,128)(2,1)} %get-tuple-element.144), channel_id=1, source_target_pairs={{0,8},{4,12},{8,0},{12,4},{16,24},{20,28},{24,16},{28,20},{1,9},{5... | collective-permute-start | bytes 1179656 | tf_op jit(solution)/shard_map/ppermute | solution.py:99
  497.6 8.3 %collective-permute-start.24 = (f32[8,1024]{1,0:T(8,128)}, f32[8,1024]{1,0:T(8,128)S(1)}, u32[]{:S(2)}, u32[]{:S(2)}) collective-permute-start(f32[8,1024]{1,0:T(8,128)} %get-tuple-element.140.refs_11_), channel_id=1, source_target_pairs={{0,1},{1,2},{2,3},{3,0},{4,5},{5,6},{6,7},{7,4},{8,9},{9,10},{10,1... | collective-permute-start | bytes 98312 | tf_op jit(solution)/shard_map/ppermute | solution.py:80
  497.7 8.2 %collective-permute-start.25 = (f32[8,1024]{1,0:T(8,128)}, f32[8,1024]{1,0:T(8,128)S(1)}, u32[]{:S(2)}, u32[]{:S(2)}) collective-permute-start(f32[8,1024]{1,0:T(8,128)} %get-tuple-element.140.refs_11_), channel_id=1, source_target_pairs={{0,2},{1,3},{2,0},{3,1},{4,6},{5,7},{6,4},{7,5},{8,10},{9,11},{10,... | collective-permute-start | bytes 98312 | tf_op jit(solution)/shard_map/ppermute | solution.py:80
  498.9 7.0 collective-permute-start.26
  510.3 25.2 %collective-permute-start.30 = (bf16[256,2048]{1,0:T(8,128)(2,1)}, bf16[256,2048]{1,0:T(8,128)(2,1)S(1)}, u32[]{:S(2)}, u32[]{:S(2)}) collective-permute-start(bf16[256,2048]{1,0:T(8,128)(2,1)} %bitcast.95), channel_id=1, source_target_pairs={{0,1},{1,2},{2,3},{3,0},{4,5},{5,6},{6,7},{7,4},{8,9},{9,10},{10,1... | collective-permute-start | bytes 3145736 | tf_op jit(solution)/shard_map/ppermute | solution.py:80
  510.9 20.1 %collective-permute-start.31 = (bf16[1,192,1024]{2,1,0:T(8,128)(2,1)}, bf16[1,192,1024]{2,1,0:T(8,128)(2,1)S(1)}, u32[]{:S(2)}, u32[]{:S(2)}) collective-permute-start(bf16[1,192,1024]{2,1,0:T(8,128)(2,1)} %get-tuple-element.145.refs_1_.refs_0_), channel_id=1, source_target_pairs={{0,16},{4,20},{8,24},{12,28},{16,0},{20,4},{24,8},{28,12},{1,17},{... | collective-permute-start | bytes 1179656 | tf_op jit(solution)/shard_map/ppermute | solution.py:99
  511.7 19.3 %collective-permute-start.32 = (bf16[1,192,1024]{2,1,0:T(8,128)(2,1)}, bf16[1,192,1024]{2,1,0:T(8,128)(2,1)S(1)}, u32[]{:S(2)}, u32[]{:S(2)}) collective-permute-start(bf16[1,192,1024]{2,1,0:T(8,128)(2,1)} %get-tuple-element.150.refs_2_), channel_id=1, source_target_pairs={{0,8},{4,12},{8,0},{12,4},{16,24},{20,28},{24,16},{28,20},{1,9},{5... | collective-permute-start | bytes 1179656 | tf_op jit(solution)/shard_map/ppermute | solution.py:99
  531.0 10.7 %copy-start.52 = (f32[8,2048]{1,0:T(8,128)S(1)}, f32[8,2048]{1,0:T(8,128)}, u32[]{:S(2)}) copy-start(f32[8,2048]{1,0:T(8,128)} %get-tuple-element.147) | copy-start | bytes 196612
  531.0 10.7 %copy-start.51 = (f32[8,512]{1,0:T(8,128)S(1)}, f32[8,512]{1,0:T(8,128)}, u32[]{:S(2)}) copy-start(f32[8,512]{1,0:T(8,128)} %get-tuple-element.149) | copy-start | bytes 49156
  539.8 24.2 %collective-permute-start.33 = (bf16[256,2048]{1,0:T(8,128)(2,1)}, bf16[256,2048]{1,0:T(8,128)(2,1)S(1)}, u32[]{:S(2)}, u32[]{:S(2)}) collective-permute-start(bf16[256,2048]{1,0:T(8,128)(2,1)} %bitcast.100), channel_id=1, source_target_pairs={{0,1},{1,2},{2,3},{3,0},{4,5},{5,6},{6,7},{7,4},{8,9},{9,10},{10,1... | collective-permute-start | bytes 3145736 | tf_op jit(solution)/shard_map/ppermute | solution.py:80
  579.7 143.8 %all-reduce.10.cloned.1.call-start = ((), (), s32[]{:S(2)}) async-start(), calls=%async_computation.3 | async-start | bytes 16973824 | tf_op jit(solution)/shard_map/psum | solution.py:1224
  580.8 25.3 %collective-permute-start.36 = (bf16[2,192,1024]{2,1,0:T(8,128)(2,1)S(1)}, bf16[2,192,1024]{2,1,0:T(8,128)(2,1)S(1)}, u32[]{:S(2)}, u32[]{:S(2)}) collective-permute-start(bf16[2,192,1024]{2,1,0:T(8,128)(2,1)S(1)} %copy-done.12), channel_id=1, source_target_pairs={{0,8},{4,12},{8,0},{12,4},{16,24},{20,28},{24,16},{28,20},{1,9},{5... | collective-permute-start | bytes 2359304 | tf_op jit(solution)/shard_map/ppermute | solution.py:99
  582.2 26.1 %collective-permute-start.37 = (bf16[2,192,1024]{2,1,0:T(8,128)(2,1)S(1)}, bf16[2,192,1024]{2,1,0:T(8,128)(2,1)S(1)}, u32[]{:S(2)}, u32[]{:S(2)}) collective-permute-start(bf16[2,192,1024]{2,1,0:T(8,128)(2,1)S(1)} %copy-done.26), channel_id=1, source_target_pairs={{0,16},{4,20},{8,24},{12,28},{16,0},{20,4},{24,8},{28,12},{1,17},{... | collective-permute-start | bytes 2359304 | tf_op jit(solution)/shard_map/ppermute | solution.py:99
  583.5 30.0 %collective-permute-start.35 = (bf16[1024,512]{1,0:T(8,128)(2,1)S(1)}, bf16[1024,512]{1,0:T(8,128)(2,1)S(1)}, u32[]{:S(2)}, u32[]{:S(2)}) collective-permute-start(bf16[1024,512]{1,0:T(8,128)(2,1)S(1)} %copy-done.17), channel_id=1, source_target_pairs={{0,1},{1,2},{2,3},{3,0},{4,5},{5,6},{6,7},{7,4},{8,9},{9,10},{10,1... | collective-permute-start | bytes 3145736 | tf_op jit(solution)/shard_map/ppermute | solution.py:80
  587.4 47.7 %collective-permute-start.34 = (bf16[1024,512]{1,0:T(8,128)(2,1)}, bf16[1024,512]{1,0:T(8,128)(2,1)S(1)}, u32[]{:S(2)}, u32[]{:S(2)}) collective-permute-start(bf16[1024,512]{1,0:T(8,128)(2,1)} %shard_map.322.refs_4_), channel_id=1, source_target_pairs={{0,1},{1,2},{2,3},{3,0},{4,5},{5,6},{6,7},{7,4},{8,9},{9,10},{10,1... | collective-permute-start | bytes 3145736 | tf_op jit(solution)/shard_map/ppermute | solution.py:80
  613.5 93.1 %collective-permute-start.41 = (bf16[4,192,2048]{2,1,0:T(8,128)(2,1)}, bf16[4,192,2048]{2,1,0:T(8,128)(2,1)}, u32[]{:S(2)}, u32[]{:S(2)}) collective-permute-start(bf16[4,192,2048]{2,1,0:T(8,128)(2,1)} %shard_map.323.refs_4_.refs_1_), channel_id=1, source_target_pairs={{0,4},{4,0},{8,12},{12,8},{16,20},{20,16},{24,28},{28,24},{1,5},{5... | collective-permute-start | bytes 9437192 | tf_op jit(solution)/shard_map/ppermute | solution.py:99
  621.1 31.9 %collective-permute-start.39 = (bf16[1024,512]{1,0:T(8,128)(2,1)}, bf16[1024,512]{1,0:T(8,128)(2,1)S(1)}, u32[]{:S(2)}, u32[]{:S(2)}) collective-permute-start(bf16[1024,512]{1,0:T(8,128)(2,1)} %shard_map.324.refs_1_), channel_id=1, source_target_pairs={{0,1},{1,2},{2,3},{3,0},{4,5},{5,6},{6,7},{7,4},{8,9},{9,10},{10,1... | collective-permute-start | bytes 3145736 | tf_op jit(solution)/shard_map/ppermute | solution.py:80
  640.4 35.1 %collective-permute-start.38 = (bf16[1024,512]{1,0:T(8,128)(2,1)}, bf16[1024,512]{1,0:T(8,128)(2,1)S(1)}, u32[]{:S(2)}, u32[]{:S(2)}) collective-permute-start(bf16[1024,512]{1,0:T(8,128)(2,1)} %shard_map.326.refs_4_), channel_id=1, source_target_pairs={{0,1},{1,2},{2,3},{3,0},{4,5},{5,6},{6,7},{7,4},{8,9},{9,10},{10,1... | collective-permute-start | bytes 3145736 | tf_op jit(solution)/shard_map/ppermute | solution.py:80
  660.5 20.3 %copy-start.3 = (s32[8]{0:T(128)S(1)}, s32[8]{0:T(128)}, u32[]{:S(2)}) copy-start(s32[8]{0:T(128)} %constant.112.clone) | copy-start | bytes 100
  660.5 37.5 %collective-permute-start.42 = (bf16[1024,512]{1,0:T(8,128)(2,1)}, bf16[1024,512]{1,0:T(8,128)(2,1)S(1)}, u32[]{:S(2)}, u32[]{:S(2)}) collective-permute-start(bf16[1024,512]{1,0:T(8,128)(2,1)} %shard_map.327.refs_3_), channel_id=1, source_target_pairs={{0,1},{1,2},{2,3},{3,0},{4,5},{5,6},{6,7},{7,4},{8,9},{9,10},{10,1... | collective-permute-start | bytes 3145736 | tf_op jit(solution)/shard_map/ppermute | solution.py:80
  680.8 37.4 %collective-permute-start.40 = (bf16[1024,512]{1,0:T(8,128)(2,1)}, bf16[1024,512]{1,0:T(8,128)(2,1)S(1)}, u32[]{:S(2)}, u32[]{:S(2)}) collective-permute-start(bf16[1024,512]{1,0:T(8,128)(2,1)} %shard_map.328.refs_12_), channel_id=1, source_target_pairs={{0,1},{1,2},{2,3},{3,0},{4,5},{5,6},{6,7},{7,4},{8,9},{9,10},{10,1... | collective-permute-start | bytes 3145736 | tf_op jit(solution)/shard_map/ppermute | solution.py:80
  726.0 16.7 %collective-permute-start.43 = (f32[8,2048]{1,0:T(8,128)S(1)}, f32[8,2048]{1,0:T(8,128)S(1)}, u32[]{:S(2)}, u32[]{:S(2)}) collective-permute-start(f32[8,2048]{1,0:T(8,128)S(1)} %slice.101), channel_id=1, source_target_pairs={{0,1},{1,2},{2,3},{3,0},{4,5},{5,6},{6,7},{7,4},{8,9},{9,10},{10,1... | collective-permute-start | bytes 196616 | tf_op jit(solution)/shard_map/ppermute | solution.py:80
  726.1 16.7 %collective-permute-start.44 = (f32[8,2048]{1,0:T(8,128)S(1)}, f32[8,2048]{1,0:T(8,128)S(1)}, u32[]{:S(2)}, u32[]{:S(2)}) collective-permute-start(f32[8,2048]{1,0:T(8,128)S(1)} %slice.101), channel_id=1, source_target_pairs={{0,2},{1,3},{2,0},{3,1},{4,6},{5,7},{6,4},{7,5},{8,10},{9,11},{10,... | collective-permute-start | bytes 196616 | tf_op jit(solution)/shard_map/ppermute | solution.py:80
  726.4 16.3 %collective-permute-start.45 = (f32[8,2048]{1,0:T(8,128)S(1)}, f32[8,2048]{1,0:T(8,128)S(1)}, u32[]{:S(2)}, u32[]{:S(2)}) collective-permute-start(f32[8,2048]{1,0:T(8,128)S(1)} %slice.101), channel_id=1, source_target_pairs={{0,3},{1,0},{2,1},{3,2},{4,7},{5,4},{6,5},{7,6},{8,11},{9,8},{10,9... | collective-permute-start | bytes 196616 | tf_op jit(solution)/shard_map/ppermute | solution.py:80
  730.5 14.1 %copy-start.1 = (bf16[512,2048]{1,0:T(8,128)(2,1)S(1)}, bf16[512,2048]{1,0:T(8,128)(2,1)}, u32[]{:S(2)}) copy-start(bf16[512,2048]{1,0:T(8,128)(2,1)} %param.27) | copy-start | bytes 6291460
  (45 other events, 81.4 us)
Sparse Core Ops, SparseCore 0:
  44.0 52.0 all-gather.5
  119.0 102.6 all-gather.3
  366.4 199.6 all-reduce.7
  585.3 131.0 all-reduce.9

commit v4 on v3

--- a/solution.py
+++ b/solution.py
@@ -111,7 +111,7 @@
 
 
 def blockwise(body, ins, outs, others=(), work=1):
-    chunks = max(c for c in (1, 2, 3, 4) if ins[0].shape[1] % (16 * c) == 0)
+    chunks = 2 if ins[0].shape[1] % 32 == 0 else 1
 
     def spec(shape):
         return pl.BlockSpec((shape[0], shape[1] // chunks, shape[2]), lambda g: (0, g, 0))
@@ -258,13 +258,14 @@
         at = owners_ref[k]
         gain = gain_ref[at, 0:1, :].astype(F32)
         first = pl.multiple_of(at * cols, 128)
-        n1_ref[:, pl.ds(first, cols)] = (field * scale * gain).astype(BF)
-    normed = n1_ref[...]
-    query = dot(normed, wq_ref[...])
-    key = dot(normed, wk_ref[...])
+        normed = (field * scale * gain).astype(BF)
+        n1_ref[:, pl.ds(first, cols)] = normed
+        terms = [dot(normed, ref[pl.ds(first, cols), :]) for ref in (wq_ref, wk_ref, wv_ref)]
+        total = terms if k == 0 else [a + b for a, b in zip(total, terms, strict=True)]
+    query, key, value = total
     q_ref[...] = query
     k_ref[...] = key
-    v_ref[...] = dot(normed, wv_ref[...]).astype(BF)
+    v_ref[...] = value.astype(BF)
     which = lax.broadcasted_iota(jnp.int32, (8, rows), 0)
     sums_ref[...] = jnp.where(
         which == 0,
@@ -372,7 +373,7 @@
     dq_ref, dk_ref, dv_ref, gains_ref, rows_ref, kacc, vacc = rest
     head = pl.program_id(0)
     length = q_ref.shape[0]
-    rows = min(256, length)
+    rows = min(512, length)
     prefix = prefix_ref[0]
     factor = HEAD_DIM**-0.5
     kacc[...] = jnp.zeros_like(kacc)
@@ -638,12 +639,12 @@
 def arrange(owners, blocks, branch):
     rows, width = blocks[0].shape
     full = branch.shape[1]
-    chunk = rows // 4
+    chunk = rows // 2
     return launch(
         arrange_kernel,
         [owners, *blocks, branch],
         prefetch=1,
-        grid=(4,),
+        grid=(2,),
         in_specs=[pl.BlockSpec((chunk, width), lambda g, o: (g, 0))] * len(blocks)
         + [pl.BlockSpec((chunk, full), lambda g, o: (g, 0))],
         out_specs=[
@@ -952,13 +953,13 @@
 
 def mix_block(owner, mix, received=None, work=1):
     blocks, length, cols = mix.shape
-    chunk = length // 4
+    chunk = length // 2
     tile = pl.BlockSpec((chunk, cols), lambda g, o: (g, 0))
     return launch(
         mix_kernel,
         [owner, mix, *([] if received is None else [received])],
         prefetch=1,
-            grid=(4,),
+            grid=(2,),
             in_specs=[pl.BlockSpec((1, chunk, cols), lambda g, o: (o[0], g, 0))]
             + ([] if received is None else [tile]),
             out_specs=tile,
@@ -1146,7 +1147,7 @@
     sine = jnp.concatenate([-jnp.sin(angles), jnp.sin(angles)], axis=1)
     for step in steps:
         x_blocks.append(send(x_blocks[-1], 1, size))
-    late_cot = copied(cotangent, (x_blocks[-1], keep, router_wide, cosine, sine))
+    late_cot = copied(cotangent, (x_blocks[-2], keep, router_wide, cosine, sine))
     cot = lax.all_gather(late_cot, "tensor", axis=0)
     normed_one, q_pre, k_pre, v_rows, own_sums = qkv_call(
         owners, x_blocks, gains, w_query, w_key, w_value

time: 763 us -> 739 us (0.969)
  Pallas kernels: 345 us -> 322 us
  waiting for transfers between devices: 294 us -> 279 us
  starting transfers between devices: 43.3 us -> 53.3 us
    pallas_call x44, Pallas kernels: 345 us -> 322 us  [launch(): pl.pallas_call(kernel, grid_spec=pltpu.PrefetchScalarGridSpec(num_scalar_...]
    all_gather x1, waiting for transfers between devices: 14.3 us -> 0.01 us  [on_device(): cot = lax.all_gather(late_cot, 'tensor', axis=0)]
    ppermute x36, starting transfers between devices: 33.6 us -> 42.7 us  [send(): lax.ppermute(value, 'tensor', [(at, (at + step) % size) for at in range(s...]
    unnamed x120 -> x124, local copies, waits for them, and re-layouts: 22.8 us -> 26.1 us
  transfers between devices with their start and end apart: 50 -> 50, of which waited for: 25 -> 25; matrix products, arithmetic and copies ran while one was open for 3% -> 4% of each run, Pallas kernels for 41% -> 39%
where the time goes in v4:
time: 739 us; the launch traced here: 729 us
  Pallas kernels  322 us (44%)
  waiting for transfers between devices  279 us (38%)
  starting transfers between devices  53.3 us (7%)
  local copies, waits for them, and re-layouts  41.2 us (6%)
  between operations  15.6 us (2%)
  other arithmetic  12.8 us (2%)
    pallas_call x44, Pallas kernels, launch(): pl.pallas_call(kernel, grid_spec=pltpu.PrefetchScalarGridSpec(num_scalar_...  322 us
    ppermute x36, waiting for transfers between devices, send(): lax.ppermute(value, 'tensor', [(at, (at + step) % size) for at in range(s...  253 us
    ppermute x36, starting transfers between devices, send(): lax.ppermute(value, 'tensor', [(at, (at + step) % size) for at in range(s...  42.7 us
    unnamed x124, local copies, waits for them, and re-layouts  26.1 us
    ppermute x10, waiting for transfers between devices, swap(): return lax.ppermute(field, 'dp', [(at, at ^ mask) for at in range(n)])  24.1 us
  transfers between devices with their start and end apart: 50, of which 25 were waited for; matrix products, arithmetic and copies ran while one was open for 4% of the time, Pallas kernels for 39%

profile of v4, /device:TPU:0, one launch (start us, length us, event | category | flops | bytes accessed | tf_op | source)
XLA Modules:
  0.0 728.7 jit_solution(1666811419965398952)
XLA Ops:
  9.5 3.1 collective-permute-start.3
  13.9 8.5 %collective-permute-done.3 = bf16[80,2048]{1,0:T(8,128)(2,1)S(1)} collective-permute-done((bf16[80,2048]{1,0:T(8,128)(2,1)S(1)}, bf16[80,2048]{1,0:T(8,128)(2,1)S(1)}, u32[]{:S(2)}, u32[]{:S(2)}) %collective-permute-start.3) | collective-permute-done | bytes 327712 | tf_op jit(solution)/shard_map/ppermute | solution.py:80
  22.4 10.7 %collective-permute-done.4 = bf16[80,2048]{1,0:T(8,128)(2,1)S(1)} collective-permute-done((bf16[80,2048]{1,0:T(8,128)(2,1)S(1)}, bf16[80,2048]{1,0:T(8,128)(2,1)S(1)}, u32[]{:S(2)}, u32[]{:S(2)}) %collective-permute-start.4) | collective-permute-done | bytes 327712 | tf_op jit(solution)/shard_map/ppermute | solution.py:80
  33.1 9.7 %collective-permute-done.5 = bf16[80,2048]{1,0:T(8,128)(2,1)S(1)} collective-permute-done((bf16[80,2048]{1,0:T(8,128)(2,1)S(1)}, bf16[80,2048]{1,0:T(8,128)(2,1)S(1)}, u32[]{:S(2)}, u32[]{:S(2)}) %collective-permute-start.5) | collective-permute-done | bytes 327712 | tf_op jit(solution)/shard_map/ppermute | solution.py:80
  44.3 2.4 fusion.11
  47.4 4.3 reduce-window.6
  54.1 14.2 %collective-permute-done.refs_2_.refs_6_ = bf16[1024,512]{1,0:T(8,128)(2,1)S(1)} collective-permute-done((bf16[1024,512]{1,0:T(8,128)(2,1)S(1)}, bf16[1024,512]{1,0:T(8,128)(2,1)S(1)}, u32[]{:S(2)}, u32[]{:S(2)}) %collective-permute-start) | collective-permute-done | bytes 1048608 | tf_op jit(solution)/shard_map/ppermute | solution.py:80
  69.7 5.5 shard_map.290.refs_1_
  79.0 3.2 fusion.4.refs_3_.refs_4_
  82.2 9.6 %collective-permute-done.1.refs_2_.refs_3_.refs_7_ = bf16[1024,512]{1,0:T(8,128)(2,1)S(1)} collective-permute-done((bf16[1024,512]{1,0:T(8,128)(2,1)S(1)}, bf16[1024,512]{1,0:T(8,128)(2,1)S(1)}, u32[]{:S(2)}, u32[]{:S(2)}) %collective-permute-start.1) | collective-permute-done | bytes 1048608 | tf_op jit(solution)/shard_map/ppermute | solution.py:80
  96.0 33.2 %collective-permute-done.2.refs_4_.refs_8_ = bf16[1024,512]{1,0:T(8,128)(2,1)S(1)} collective-permute-done((bf16[1024,512]{1,0:T(8,128)(2,1)}, bf16[1024,512]{1,0:T(8,128)(2,1)S(1)}, u32[]{:S(2)}, u32[]{:S(2)}) %collective-permute-start.2) | collective-permute-done | bytes 1048608 | tf_op jit(solution)/shard_map/ppermute | solution.py:80
  130.1 13.6 %shard_map.292 = (bf16[1024,2048]{1,0:T(8,128)(2,1)}, f32[1024,512]{1,0:T(8,128)}, f32[1024,512]{1,0:T(8,128)}, bf16[1024,512]{1,0:T(8,128)(2,1)}, f32[8,1024]{1,0:T(8,128)}) custom-call(s32[4]{0:T(128)} %and_select_fusion.refs_0_, bf16[1024,512]{1,0:T(8,128)(2,1)} %refs_4_.1, bf16[1024,512]{1,0:T(8,128)(2,1)} %copy-done.8, bf16[1024,512]{1,0:T(8,128)(2,1)} %copy-done.7, ...), custom_call_target="tpu_custom_call" | custom-call | flops 1 | bytes 1 | tf_op jit(solution)/shard_map/pallas_call | solution.py:42
  145.7 2.4 collective-permute-start.8
  151.4 2.6 collective-permute-done.8.refs_11_.refs_15_.refs_10_
  154.6 14.0 %shard_map.293 = (bf16[1024,512]{1,0:T(8,128)(2,1)}, f32[1024,512]{1,0:T(8,128)}, bf16[1024,512]{1,0:T(8,128)(2,1)}, bf16[1024,512]{1,0:T(8,128)(2,1)}) custom-call(s32[1]{0:T(128)S(6)} %copy.79.refs_0_, f32[1024,512]{1,0:T(8,128)} %get-tuple-element.87.refs_1_.refs_0_, f32[1024,512]{1,0:T(8,128)} %get-tuple-element.88.refs_2_.refs_1_, ...), custom_call_target="tpu_custom_call" | custom-call | flops 1 | bytes 1 | tf_op jit(solution)/shard_map/pallas_call | solution.py:42
  171.9 29.6 %collective-permute-done.10.refs_3_ = bf16[256,512]{1,0:T(8,128)(2,1)S(1)} collective-permute-done((bf16[256,512]{1,0:T(8,128)(2,1)S(1)}, bf16[256,512]{1,0:T(8,128)(2,1)S(1)}, u32[]{:S(2)}, u32[]{:S(2)}) %collective-permute-start.10) | collective-permute-done | bytes 262176 | tf_op jit(solution)/shard_map/ppermute | solution.py:80
  202.4 9.3 %shard_map.294 = (f32[256,2048]{1,0:T(8,128)}, bf16[256,2048]{1,0:T(8,128)(2,1)}) custom-call(s32[4]{0:T(128)} %and_select_fusion.refs_0_, bf16[1024,512]{1,0:T(8,128)(2,1)} %get-tuple-element.92.refs_1_, bf16[256,512]{1,0:T(8,128)(2,1)} %copy-done.43, bf16[256,512]{1,0:T(8,128)(2,1)} %copy-done.41, bf16[256,512]{1,0:T(8,128)(2,1)} %copy-done.42, ...), custom_call_target="tpu_custom_call" | custom-call | flops 1 | bytes 1 | tf_op jit(solution)/shard_map/pallas_call | solution.py:42
  213.8 8.9 %collective-permute-start.12 = (bf16[256,2048]{1,0:T(8,128)(2,1)}, bf16[256,2048]{1,0:T(8,128)(2,1)S(1)}, u32[]{:S(2)}, u32[]{:S(2)}) collective-permute-start(bf16[256,2048]{1,0:T(8,128)(2,1)} %bitcast.88), channel_id=1, source_target_pairs={{0,1},{1,2},{2,3},{3,0},{4,5},{5,6},{6,7},{7,4},{8,9},{9,10},{10,1... | collective-permute-start | bytes 3145736 | tf_op jit(solution)/shard_map/ppermute | solution.py:80
  223.3 19.2 %shard_map.296 = (bf16[1536,1024]{1,0:T(8,128)(2,1)}, bf16[1024,1536]{1,0:T(8,128)(2,1)}, bf16[1024,1536]{1,0:T(8,128)(2,1)}, bf16[2048,1024]{1,0:T(8,128)(2,1)}...) custom-call(s32[1]{0:T(128)} %get-tuple-element.179.refs_0_, ...), custom_call_target="tpu_custom_call" | custom-call | flops 1 | bytes 1 | tf_op jit(solution)/shard_map/pallas_call | solution.py:42
  245.6 18.5 %shard_map.298 = (bf16[1536,1024]{1,0:T(8,128)(2,1)}, bf16[1024,1536]{1,0:T(8,128)(2,1)}, bf16[1024,1536]{1,0:T(8,128)(2,1)}, bf16[2048,1024]{1,0:T(8,128)(2,1)}...) custom-call(s32[1]{0:T(128)} %get-tuple-element.177.refs_0_, ...), custom_call_target="tpu_custom_call", output_to_operand_aliasing={{0}: (8, {}), {1}: (9, {}), {2}: (10, {}), {3}: (11, {}), {... | custom-call | flops 1 | bytes 1 | tf_op jit(solution)/shard_map/pallas_call | solution.py:42
  264.0 4.1 collective-permute-done.13.refs_1_
  271.3 18.4 %shard_map.300 = (bf16[1536,1024]{1,0:T(8,128)(2,1)}, bf16[1024,1536]{1,0:T(8,128)(2,1)}, bf16[1024,1536]{1,0:T(8,128)(2,1)}, bf16[2048,1024]{1,0:T(8,128)(2,1)}...) custom-call(s32[1]{0:T(128)} %get-tuple-element.176.refs_0_, ...), custom_call_target="tpu_custom_call", output_to_operand_aliasing={{0}: (8, {}), {1}: (9, {}), {2}: (10, {}), {3}: (11, {}), {... | custom-call | flops 1 | bytes 1 | tf_op jit(solution)/shard_map/pallas_call | solution.py:42
  289.8 3.2 collective-permute-done.14.refs_1_
  293.9 18.4 %shard_map.301 = (bf16[1536,1024]{1,0:T(8,128)(2,1)}, bf16[1024,1536]{1,0:T(8,128)(2,1)}, bf16[1024,1536]{1,0:T(8,128)(2,1)}, bf16[2048,1024]{1,0:T(8,128)(2,1)}...) custom-call(s32[1]{0:T(128)} %get-tuple-element.178.refs_0_, ...), custom_call_target="tpu_custom_call", output_to_operand_aliasing={{0}: (8, {}), {1}: (9, {}), {2}: (10, {}), {3}: (11, {}), {... | custom-call | flops 1 | bytes 1 | tf_op jit(solution)/shard_map/pallas_call | solution.py:42
  315.1 18.1 %shard_map.303.refs_3_ = bf16[2,6,2048,256]{3,2,1,0:T(8,128)(2,1)} custom-call(bf16[2048,1024]{1,0:T(8,128)(2,1)} %get-tuple-element.122.refs_0_, bf16[1024,1536]{1,0:T(8,128)(2,1)} %get-tuple-element.123.refs_1_, bf16[1024,1536]{1,0:T(8,128)(2,1)} %get-tuple-element.124.refs_2_, bf16[1,256,2176]{2,1,0:T(8,128)(2,1)} %shard_map.302.refs_3_), custom_call_target="tpu_custom_call" | custom-call | flops 1 | bytes 1 | tf_op jit(solution)/shard_map/pallas_call | solution.py:42
  333.2 8.2 %shard_map.304.refs_2_ = bf16[4,192,2048]{2,1,0:T(8,128)(2,1)} custom-call(s32[4]{0:T(128)} %get-tuple-element.175.refs_0_, bf16[1536,1024]{1,0:T(8,128)(2,1)} %get-tuple-element.121.refs_1_, bf16[4,1024,512]{2,1,0:T(8,128)(2,1)} %all-gather.4.cloned.1.call-done.refs_2_.refs_7_, bf16[2,6,2048,256]{3,2,1,0:T(8,128)(2,1)} %shard_map.303.refs_3_), custom_call_target="tpu_custom_call" | custom-call | flops 1 | bytes 1 | tf_op jit(solution)/shard_map/pallas_call | solution.py:42
  343.1 2.5 shard_map.305.refs_3_
  345.6 8.2 %shard_map.306.refs_2_.refs_0_ = bf16[4,192,2048]{2,1,0:T(8,128)(2,1)} custom-call(s32[4]{0:T(128)} %get-tuple-element.174.refs_0_, bf16[1536,1024]{1,0:T(8,128)(2,1)} %get-tuple-element.121.refs_1_, bf16[4,1024,512]{2,1,0:T(8,128)(2,1)} %all-gather.4.cloned.1.call-done.refs_2_.refs_7_, bf16[1,256,2176]{2,1,0:T(8,128)(2,1)} %shard_map.305.refs_3_), custom_call_target="tpu_custom_call" | custom-call | flops 1 | bytes 1 | tf_op jit(solution)/shard_map/pallas_call | solution.py:42
  353.8 20.4 %collective-permute-done.16 = bf16[256,2176]{1,0:T(8,128)(2,1)S(1)} collective-permute-done((bf16[256,2176]{1,0:T(8,128)(2,1)}, bf16[256,2176]{1,0:T(8,128)(2,1)S(1)}, u32[]{:S(2)}, u32[]{:S(2)}) %collective-permute-start.16) | collective-permute-done | bytes 1114144 | tf_op jit(solution)/shard_map/ppermute | solution.py:80
  375.2 2.5 shard_map.307.refs_2_
  377.9 4.8 shard_map.308
  382.7 22.9 %collective-permute-done.17.refs_2_ = bf16[256,2176]{1,0:T(8,128)(2,1)S(1)} collective-permute-done((bf16[256,2176]{1,0:T(8,128)(2,1)}, bf16[256,2176]{1,0:T(8,128)(2,1)S(1)}, u32[]{:S(2)}, u32[]{:S(2)}) %collective-permute-start.17) | collective-permute-done | bytes 1114144 | tf_op jit(solution)/shard_map/ppermute | solution.py:80
  406.6 11.8 %shard_map.309 = (bf16[256,2048]{1,0:T(8,128)(2,1)}, f32[8,2048]{1,0:T(8,128)}, bf16[256,512]{1,0:T(8,128)(2,1)}, bf16[256,512]{1,0:T(8,128)(2,1)}, bf16[256,512]{1,0:T(8,128)(2,1)}, /*index=5*/bf16[256,512]{1,0:T(8,128)(2,1)}) custom-call(s32[1]{0:T(128)} %bitcast.23.refs_0_, bf16[256,2176]{1,0:T(8,128)(2,1)} %get-tuple-element.116.refs_1_, ...), custom_call_target="tpu_custom_call" | custom-call | flops 1 | bytes 1 | tf_op jit(solution)/shard_map/pallas_call | solution.py:42
  418.5 3.7 collective-permute-start.21
  422.8 3.0 collective-permute-start.23
  425.8 3.9 collective-permute-done.19.refs_2_
  429.7 8.2 %collective-permute-done.20.refs_3_ = bf16[256,512]{1,0:T(8,128)(2,1)S(1)} collective-permute-done((bf16[256,512]{1,0:T(8,128)(2,1)}, bf16[256,512]{1,0:T(8,128)(2,1)S(1)}, u32[]{:S(2)}, u32[]{:S(2)}) %collective-permute-start.20) | collective-permute-done | bytes 262176 | tf_op jit(solution)/shard_map/ppermute | solution.py:80
  438.7 3.4 shard_map.310
  442.1 5.1 collective-permute-start.27
  447.2 2.4 collective-permute-done.22.refs_1_
  450.8 3.1 shard_map.311
  456.0 17.5 %shard_map.312 = (f32[1024,512]{1,0:T(8,128)}, f32[1024,512]{1,0:T(8,128)}, bf16[1024,512]{1,0:T(8,128)(2,1)}, f32[8,512]{1,0:T(8,128)}, f32[8,1024]{1,0:T(8,128)}) custom-call(s32[1]{0:T(128)S(6)} %copy.79.refs_0_, f32[1024,512]{1,0:T(8,128)} %get-tuple-element.87.refs_1_.refs_0_, f32[1024,512]{1,0:T(8,128)} %get-tuple-element.88.refs_2_.refs_1_, ...), custom_call_target="tpu_custom_call" | custom-call | flops 1 | bytes 1 | tf_op jit(solution)/shard_map/pallas_call | solution.py:42
  474.8 2.4 collective-permute-start.25
  487.7 6.9 shard_map.315
  494.6 12.2 %shard_map.316 = (bf16[2048,1536]{1,0:T(8,128)(2,1)}, f32[8,2048]{1,0:T(8,128)}) custom-call(bf16[1024,2048]{1,0:T(8,128)(2,1)} %get-tuple-element.91.refs_12_.refs_0_, bf16[1024,1536]{1,0:T(8,128)(2,1)} %get-tuple-element.146.refs_1_, bf16[2048,1536]{1,0:T(8,128)(2,1)} %bitcast.78), custom_call_target="tpu_custom_call" | custom-call | flops 1 | bytes 1 | tf_op jit(solution)/shard_map/pallas_call | solution.py:42
  515.8 21.9 %collective-permute-done.33.refs_5_.refs_11_ = bf16[256,2048]{1,0:T(8,128)(2,1)S(1)} collective-permute-done((bf16[256,2048]{1,0:T(8,128)(2,1)}, bf16[256,2048]{1,0:T(8,128)(2,1)S(1)}, u32[]{:S(2)}, u32[]{:S(2)}) %collective-permute-start.33) | collective-permute-done | bytes 1048608 | tf_op jit(solution)/shard_map/ppermute | solution.py:80
  538.8 7.1 shard_map.319.refs_1_
  548.0 6.2 shard_map.321.refs_2_
  558.3 2.7 shard_map.322.refs_4_
  563.1 19.8 %collective-permute-done.36.refs_1_ = bf16[2,192,1024]{2,1,0:T(8,128)(2,1)S(1)} collective-permute-done((bf16[2,192,1024]{2,1,0:T(8,128)(2,1)S(1)}, bf16[2,192,1024]{2,1,0:T(8,128)(2,1)S(1)}, u32[]{:S(2)}, u32[]{:S(2)}) %collective-permute-start.36) | collective-permute-done | bytes 786464 | tf_op jit(solution)/shard_map/ppermute | solution.py:99
  585.6 3.1 shard_map.323.refs_4_.refs_1_
  589.7 6.8 shard_map.324.refs_1_
  596.5 14.0 %shard_map.325 = (f32[6,2048,256]{2,1,0:T(8,128)}, f32[6,2048,256]{2,1,0:T(8,128)}) custom-call(bf16[2,6,2048,256]{3,2,1,0:T(8,128)(2,1)} %all-reduce.8.cloned.1.call-done.refs_2_.refs_0_, bf16[1024,512]{1,0:T(8,128)(2,1)} %shard_map.324.refs_1_), custom_call_target="tpu_custom_call" | custom-call | flops 1 | bytes 1 | tf_op jit(solution)/shard_map/pallas_call | solution.py:42
  611.5 3.1 shard_map.326.refs_4_
  616.2 14.5 %collective-permute-done.39.refs_3_ = bf16[1024,512]{1,0:T(8,128)(2,1)S(1)} collective-permute-done((bf16[1024,512]{1,0:T(8,128)(2,1)}, bf16[1024,512]{1,0:T(8,128)(2,1)S(1)}, u32[]{:S(2)}, u32[]{:S(2)}) %collective-permute-start.39) | collective-permute-done | bytes 1048608 | tf_op jit(solution)/shard_map/ppermute | solution.py:80
  631.7 6.3 shard_map.327.refs_3_
  638.0 15.2 %collective-permute-done.38.refs_2_ = bf16[1024,512]{1,0:T(8,128)(2,1)S(1)} collective-permute-done((bf16[1024,512]{1,0:T(8,128)(2,1)}, bf16[1024,512]{1,0:T(8,128)(2,1)S(1)}, u32[]{:S(2)}, u32[]{:S(2)}) %collective-permute-start.38) | collective-permute-done | bytes 1048608 | tf_op jit(solution)/shard_map/ppermute | solution.py:80
  654.1 3.0 shard_map.328.refs_12_
  658.4 17.3 %collective-permute-done.42.refs_3_ = bf16[1024,512]{1,0:T(8,128)(2,1)S(1)} collective-permute-done((bf16[1024,512]{1,0:T(8,128)(2,1)}, bf16[1024,512]{1,0:T(8,128)(2,1)S(1)}, u32[]{:S(2)}, u32[]{:S(2)}) %collective-permute-start.42) | collective-permute-done | bytes 1048608 | tf_op jit(solution)/shard_map/ppermute | solution.py:80
  676.6 7.8 %shard_map.329.refs_3_ = f32[1024,512]{1,0:T(8,128)} custom-call(s32[4]{0:T(128)} %and_select_fusion.refs_0_, bf16[1024,1536]{1,0:T(8,128)(2,1)} %get-tuple-element.146.refs_1_, bf16[2048,1536]{1,0:T(8,128)(2,1)} %bitcast.82, bf16[1024,512]{1,0:T(8,128)(2,1)} %copy-done.19, bf16[1024,512]{1,0:T(8,128)(2,1)} %refs_4_.1, ...), custom_call_target="tpu_custom_call" | custom-call | flops 1 | bytes 1 | tf_op jit(solution)/shard_map/pallas_call | solution.py:42
  684.4 10.6 %shard_map.330.refs_3_ = f32[1536,2048]{1,0:T(8,128)} custom-call(s32[8]{0:T(128)} %gather_fusion, bf16[4,192,2048]{2,1,0:T(8,128)(2,1)} %shard_map.323.refs_4_.refs_1_, bf16[4,192,2048]{2,1,0:T(8,128)(2,1)} %collective-permute-done.41.refs_2_, f32[1024,512]{1,0:T(8,128)} %shard_map.329.refs_3_), custom_call_target="tpu_custom_call" | custom-call | flops 1 | bytes 1 | tf_op jit(solution)/shard_map/pallas_call | solution.py:42
  697.5 3.1 shard_map.331.refs_1_
  707.6 9.7 %shard_map.333 = (f32[2048,512]{1,0:T(8,128)}, f32[2048,512]{1,0:T(8,128)}, f32[2048,512]{1,0:T(8,128)}) custom-call(bf16[2048,1536]{1,0:T(8,128)(2,1)} %get-tuple-element.161.refs_0_, bf16[1,32,1536]{2,1,0:T(8,128)(2,1)} %shard_map.332.refs_1_), custom_call_target="tpu_custom_call" | custom-call | flops 1 | bytes 1 | tf_op jit(solution)/shard_map/pallas_call | solution.py:42
  717.3 2.5 convert_element_type.28
  (267 shorter events, 100.6 us)
Async XLA Ops:
  7.2 194.4 %all-gather.6.cloned.1.call-start = ((), (), s32[]{:S(2)}) async-start(), calls=%async_computation.2 | async-start | bytes 9437184 | tf_op jit(solution)/shard_map/all_gather | solution.py:1138
  9.5 12.8 %collective-permute-start.3 = (bf16[80,2048]{1,0:T(8,128)(2,1)S(1)}, bf16[80,2048]{1,0:T(8,128)(2,1)S(1)}, u32[]{:S(2)}, u32[]{:S(2)}) collective-permute-start(bf16[80,2048]{1,0:T(8,128)(2,1)S(1)} %fusion.18), channel_id=1, source_target_pairs={{0,1},{1,2},{2,3},{3,0},{4,5},{5,6},{6,7},{7,4},{8,9},{9,10},{10,1... | collective-permute-start | bytes 983048 | tf_op jit(solution)/shard_map/ppermute | solution.py:80
  12.8 31.2 %copy-start.4 = (bf16[1024,512]{1,0:T(8,128)(2,1)S(1)}, bf16[1024,512]{1,0:T(8,128)(2,1)}, u32[]{:S(2)}) copy-start(bf16[1024,512]{1,0:T(8,128)(2,1)} %refs_4_.1) | copy-start | bytes 3145732
  12.8 31.3 %copy-start.50 = (s32[1,3072]{1,0:T(1,128)S(1)}, s32[1,3072]{1,0:T(1,128)}, u32[]{:S(2)}) copy-start(s32[1,3072]{1,0:T(1,128)} %param.35) | copy-start | bytes 36868
  12.8 31.5 %copy-start.60 = (s32[1024,3]{0,1:T(4,128)S(1)}, s32[1024,3]{0,1:T(4,128)}, u32[]{:S(2)}) copy-start(s32[1024,3]{0,1:T(4,128)} %param.33) | copy-start | bytes 36868
  22.4 10.7 %collective-permute-start.4 = (bf16[80,2048]{1,0:T(8,128)(2,1)S(1)}, bf16[80,2048]{1,0:T(8,128)(2,1)S(1)}, u32[]{:S(2)}, u32[]{:S(2)}) collective-permute-start(bf16[80,2048]{1,0:T(8,128)(2,1)S(1)} %collective-permute-done.3), channel_id=1, source_target_pairs={{0,1},{1,2},{2,3},{3,0},{4,5},{5,6},{6,7},{7,4},{8,9},{9,10},{10,1... | collective-permute-start | bytes 983048 | tf_op jit(solution)/shard_map/ppermute | solution.py:80
  33.1 9.8 %collective-permute-start.5 = (bf16[80,2048]{1,0:T(8,128)(2,1)S(1)}, bf16[80,2048]{1,0:T(8,128)(2,1)S(1)}, u32[]{:S(2)}, u32[]{:S(2)}) collective-permute-start(bf16[80,2048]{1,0:T(8,128)(2,1)S(1)} %collective-permute-done.4), channel_id=1, source_target_pairs={{0,1},{1,2},{2,3},{3,0},{4,5},{5,6},{6,7},{7,4},{8,9},{9,10},{10,1... | collective-permute-start | bytes 983048 | tf_op jit(solution)/shard_map/ppermute | solution.py:80
  43.9 167.8 %all-gather.4.cloned.1.call-start = ((), (), s32[]{:S(2)}) async-start(), calls=%async_computation | async-start | bytes 5242880 | tf_op jit(solution)/shard_map/all_gather | solution.py:1151
  44.0 24.4 %collective-permute-start = (bf16[1024,512]{1,0:T(8,128)(2,1)S(1)}, bf16[1024,512]{1,0:T(8,128)(2,1)S(1)}, u32[]{:S(2)}, u32[]{:S(2)}) collective-permute-start(bf16[1024,512]{1,0:T(8,128)(2,1)S(1)} %copy-done.4), channel_id=1, source_target_pairs={{0,1},{1,2},{2,3},{3,0},{4,5},{5,6},{6,7},{7,4},{8,9},{9,10},{10,1... | collective-permute-start | bytes 3145736 | tf_op jit(solution)/shard_map/ppermute | solution.py:80
  68.3 23.4 %collective-permute-start.1 = (bf16[1024,512]{1,0:T(8,128)(2,1)S(1)}, bf16[1024,512]{1,0:T(8,128)(2,1)S(1)}, u32[]{:S(2)}, u32[]{:S(2)}) collective-permute-start(bf16[1024,512]{1,0:T(8,128)(2,1)S(1)} %collective-permute-done.refs_2_.refs_6_), channel_id=1, source_target_pairs={{0,1},{1,2},{2,3},{3,0},{4,5},{5,6},{6,7},{7,4},{8,9},{9,10},{10,1... | collective-permute-start | bytes 3145736 | tf_op jit(solution)/shard_map/ppermute | solution.py:80
  69.7 9.3 %copy-start.35 = (f32[3072,8]{0,1:T(8,128)S(1)}, f32[3072,8]{0,1:T(8,128)}, u32[]{:S(2)}) copy-start(f32[3072,8]{0,1:T(8,128)} %copy-done.34) | copy-start | bytes 294916
  94.8 34.4 %collective-permute-start.2 = (bf16[1024,512]{1,0:T(8,128)(2,1)}, bf16[1024,512]{1,0:T(8,128)(2,1)S(1)}, u32[]{:S(2)}, u32[]{:S(2)}) collective-permute-start(bf16[1024,512]{1,0:T(8,128)(2,1)} %copy-done.7), channel_id=1, source_target_pairs={{0,1},{1,2},{2,3},{3,0},{4,5},{5,6},{6,7},{7,4},{8,9},{9,10},{10,1... | collective-permute-start | bytes 3145736 | tf_op jit(solution)/shard_map/ppermute | solution.py:80
  96.0 52.1 %copy-start.56 = (bf16[512]{0:T(512)(128)(2,1)S(1)}, bf16[512]{0:T(512)(128)(2,1)}, u32[]{:S(2)}) copy-start(bf16[512]{0:T(512)(128)(2,1)} %param.25) | copy-start | bytes 3076
  96.0 52.7 %copy-start.57 = (bf16[512]{0:T(512)(128)(2,1)S(1)}, bf16[512]{0:T(512)(128)(2,1)}, u32[]{:S(2)}) copy-start(bf16[512]{0:T(512)(128)(2,1)} %param.26) | copy-start | bytes 3076
  143.7 6.7 collective-permute-start.6
  143.8 7.6 %collective-permute-start.7 = (f32[8,1024]{1,0:T(8,128)}, f32[8,1024]{1,0:T(8,128)S(1)}, u32[]{:S(2)}, u32[]{:S(2)}) collective-permute-start(f32[8,1024]{1,0:T(8,128)} %get-tuple-element.90.refs_8_.refs_12_.refs_7_.refs_5_), channel_id=1, source_target_pairs={{0,2},{1,3},{2,0},{3,1},{4,6},{5,7},{6,4},{7,5},{8,10},{9,11},{10,... | collective-permute-start | bytes 98312 | tf_op jit(solution)/shard_map/ppermute | solution.py:80
  145.7 8.3 %collective-permute-start.8 = (f32[8,1024]{1,0:T(8,128)}, f32[8,1024]{1,0:T(8,128)S(1)}, u32[]{:S(2)}, u32[]{:S(2)}) collective-permute-start(f32[8,1024]{1,0:T(8,128)} %get-tuple-element.90.refs_8_.refs_12_.refs_7_.refs_5_), channel_id=1, source_target_pairs={{0,3},{1,0},{2,1},{3,2},{4,7},{5,4},{6,5},{7,6},{8,11},{9,8},{10,9... | collective-permute-start | bytes 98312 | tf_op jit(solution)/shard_map/ppermute | solution.py:80
  169.8 31.8 %collective-permute-start.10 = (bf16[256,512]{1,0:T(8,128)(2,1)S(1)}, bf16[256,512]{1,0:T(8,128)(2,1)S(1)}, u32[]{:S(2)}, u32[]{:S(2)}) collective-permute-start(bf16[256,512]{1,0:T(8,128)(2,1)S(1)} %get-tuple-element.164), channel_id=1, source_target_pairs={{0,2},{1,3},{2,0},{3,1},{4,6},{5,7},{6,4},{7,5},{8,10},{9,11},{10,... | collective-permute-start | bytes 786440 | tf_op jit(solution)/shard_map/ppermute | solution.py:80
  169.9 31.7 %collective-permute-start.11 = (bf16[256,512]{1,0:T(8,128)(2,1)S(1)}, bf16[256,512]{1,0:T(8,128)(2,1)S(1)}, u32[]{:S(2)}, u32[]{:S(2)}) collective-permute-start(bf16[256,512]{1,0:T(8,128)(2,1)S(1)} %get-tuple-element.163), channel_id=1, source_target_pairs={{0,3},{1,0},{2,1},{3,2},{4,7},{5,4},{6,5},{7,6},{8,11},{9,8},{10,9... | collective-permute-start | bytes 786440 | tf_op jit(solution)/shard_map/ppermute | solution.py:80
  171.7 29.9 %collective-permute-start.9 = (bf16[256,512]{1,0:T(8,128)(2,1)S(1)}, bf16[256,512]{1,0:T(8,128)(2,1)S(1)}, u32[]{:S(2)}, u32[]{:S(2)}) collective-permute-start(bf16[256,512]{1,0:T(8,128)(2,1)S(1)} %get-tuple-element.165), channel_id=1, source_target_pairs={{0,1},{1,2},{2,3},{3,0},{4,5},{5,6},{6,7},{7,4},{8,9},{9,10},{10,1... | collective-permute-start | bytes 786440 | tf_op jit(solution)/shard_map/ppermute | solution.py:80
  211.7 11.0 %copy-start.51 = (s32[4]{0:T(128)S(1)}, s32[4]{0:T(128)}, u32[]{:S(2)}) copy-start(s32[4]{0:T(128)} %and_select_fusion.refs_0_) | copy-start | bytes 52
  213.8 28.7 %collective-permute-start.12 = (bf16[256,2048]{1,0:T(8,128)(2,1)}, bf16[256,2048]{1,0:T(8,128)(2,1)S(1)}, u32[]{:S(2)}, u32[]{:S(2)}) collective-permute-start(bf16[256,2048]{1,0:T(8,128)(2,1)} %bitcast.88), channel_id=1, source_target_pairs={{0,1},{1,2},{2,3},{3,0},{4,5},{5,6},{6,7},{7,4},{8,9},{9,10},{10,1... | collective-permute-start | bytes 3145736 | tf_op jit(solution)/shard_map/ppermute | solution.py:80
  245.6 22.6 %collective-permute-start.13 = (bf16[256,2048]{1,0:T(8,128)(2,1)}, bf16[256,2048]{1,0:T(8,128)(2,1)S(1)}, u32[]{:S(2)}, u32[]{:S(2)}) collective-permute-start(bf16[256,2048]{1,0:T(8,128)(2,1)} %bitcast.99), channel_id=1, source_target_pairs={{0,1},{1,2},{2,3},{3,0},{4,5},{5,6},{6,7},{7,4},{8,9},{9,10},{10,1... | collective-permute-start | bytes 3145736 | tf_op jit(solution)/shard_map/ppermute | solution.py:80
  271.1 21.8 %collective-permute-start.14 = (bf16[256,2048]{1,0:T(8,128)(2,1)}, bf16[256,2048]{1,0:T(8,128)(2,1)S(1)}, u32[]{:S(2)}, u32[]{:S(2)}) collective-permute-start(bf16[256,2048]{1,0:T(8,128)(2,1)} %bitcast.98), channel_id=1, source_target_pairs={{0,1},{1,2},{2,3},{3,0},{4,5},{5,6},{6,7},{7,4},{8,9},{9,10},{10,1... | collective-permute-start | bytes 3145736 | tf_op jit(solution)/shard_map/ppermute | solution.py:80
  293.9 20.5 %copy-start.2 = (s32[8]{0:T(128)S(1)}, s32[8]{0:T(128)}, u32[]{:S(2)}) copy-start(s32[8]{0:T(128)} %constant.112.clone) | copy-start | bytes 100
  314.5 27.7 %collective-permute-start.15 = (bf16[256,2176]{1,0:T(8,128)(2,1)}, bf16[256,2176]{1,0:T(8,128)(2,1)S(1)}, u32[]{:S(2)}, u32[]{:S(2)}) collective-permute-start(bf16[256,2176]{1,0:T(8,128)(2,1)} %bitcast.94), channel_id=1, source_target_pairs={{0,1},{1,2},{2,3},{3,0},{4,5},{5,6},{6,7},{7,4},{8,9},{9,10},{10,1... | collective-permute-start | bytes 3342344 | tf_op jit(solution)/shard_map/ppermute | solution.py:80
  341.4 205.1 %all-reduce.8.cloned.1.call-start = ((), (), s32[]{:S(2)}) async-start(), calls=%async_computation.1 | async-start | bytes 25165824 | tf_op jit(solution)/shard_map/psum | solution.py:1192
  341.4 36.5 %collective-permute-start.18 = (bf16[4,192,2048]{2,1,0:T(8,128)(2,1)}, bf16[4,192,2048]{2,1,0:T(8,128)(2,1)}, u32[]{:S(2)}, u32[]{:S(2)}) collective-permute-start(bf16[4,192,2048]{2,1,0:T(8,128)(2,1)} %shard_map.304.refs_2_), channel_id=1, source_target_pairs={{0,4},{4,0},{8,12},{12,8},{16,20},{20,16},{24,28},{28,24},{1,5},{5... | collective-permute-start | bytes 9437192 | tf_op jit(solution)/shard_map/ppermute | solution.py:99
  345.6 28.6 %collective-permute-start.16 = (bf16[256,2176]{1,0:T(8,128)(2,1)}, bf16[256,2176]{1,0:T(8,128)(2,1)S(1)}, u32[]{:S(2)}, u32[]{:S(2)}) collective-permute-start(bf16[256,2176]{1,0:T(8,128)(2,1)} %bitcast.104), channel_id=1, source_target_pairs={{0,1},{1,2},{2,3},{3,0},{4,5},{5,6},{6,7},{7,4},{8,9},{9,10},{10,1... | collective-permute-start | bytes 3342344 | tf_op jit(solution)/shard_map/ppermute | solution.py:80
  377.7 27.9 %collective-permute-start.17 = (bf16[256,2176]{1,0:T(8,128)(2,1)}, bf16[256,2176]{1,0:T(8,128)(2,1)S(1)}, u32[]{:S(2)}, u32[]{:S(2)}) collective-permute-start(bf16[256,2176]{1,0:T(8,128)(2,1)} %bitcast.93), channel_id=1, source_target_pairs={{0,1},{1,2},{2,3},{3,0},{4,5},{5,6},{6,7},{7,4},{8,9},{9,10},{10,1... | collective-permute-start | bytes 3342344 | tf_op jit(solution)/shard_map/ppermute | solution.py:80
  382.7 39.5 %copy-start.26 = (bf16[2,192,1024]{2,1,0:T(8,128)(2,1)S(1)}, bf16[2,192,1024]{2,1,0:T(8,128)(2,1)}, u32[]{:S(2)}) copy-start(bf16[2,192,1024]{2,1,0:T(8,128)(2,1)} %get-tuple-element.125.refs_10_) | copy-start | bytes 2359300
  382.7 40.1 %copy-start.59 = (bf16[2,192,1024]{2,1,0:T(8,128)(2,1)S(1)}, bf16[2,192,1024]{2,1,0:T(8,128)(2,1)}, u32[]{:S(2)}) copy-start(bf16[2,192,1024]{2,1,0:T(8,128)(2,1)} %get-tuple-element.135) | copy-start | bytes 2359300
  418.4 11.3 %collective-permute-start.19 = (bf16[256,512]{1,0:T(8,128)(2,1)}, bf16[256,512]{1,0:T(8,128)(2,1)S(1)}, u32[]{:S(2)}, u32[]{:S(2)}) collective-permute-start(bf16[256,512]{1,0:T(8,128)(2,1)} %get-tuple-element.127), channel_id=1, source_target_pairs={{0,1},{1,2},{2,3},{3,0},{4,5},{5,6},{6,7},{7,4},{8,9},{9,10},{10,1... | collective-permute-start | bytes 786440 | tf_op jit(solution)/shard_map/ppermute | solution.py:80
  418.4 19.5 %collective-permute-start.20 = (bf16[256,512]{1,0:T(8,128)(2,1)}, bf16[256,512]{1,0:T(8,128)(2,1)S(1)}, u32[]{:S(2)}, u32[]{:S(2)}) collective-permute-start(bf16[256,512]{1,0:T(8,128)(2,1)} %get-tuple-element.128), channel_id=1, source_target_pairs={{0,2},{1,3},{2,0},{3,1},{4,6},{5,7},{6,4},{7,5},{8,10},{9,11},{10,... | collective-permute-start | bytes 786440 | tf_op jit(solution)/shard_map/ppermute | solution.py:80
  418.5 19.4 %collective-permute-start.21 = (bf16[256,512]{1,0:T(8,128)(2,1)}, bf16[256,512]{1,0:T(8,128)(2,1)S(1)}, u32[]{:S(2)}, u32[]{:S(2)}) collective-permute-start(bf16[256,512]{1,0:T(8,128)(2,1)} %get-tuple-element.129), channel_id=1, source_target_pairs={{0,3},{1,0},{2,1},{3,2},{4,7},{5,4},{6,5},{7,6},{8,11},{9,8},{10,9... | collective-permute-start | bytes 786440 | tf_op jit(solution)/shard_map/ppermute | solution.py:80
  422.2 27.4 %collective-permute-start.22 = (bf16[2,192,1024]{2,1,0:T(8,128)(2,1)S(1)}, bf16[2,192,1024]{2,1,0:T(8,128)(2,1)S(1)}, u32[]{:S(2)}, u32[]{:S(2)}) collective-permute-start(bf16[2,192,1024]{2,1,0:T(8,128)(2,1)S(1)} %copy-done.26), channel_id=1, source_target_pairs={{0,8},{4,12},{8,0},{12,4},{16,24},{20,28},{24,16},{28,20},{1,9},{5... | collective-permute-start | bytes 2359304 | tf_op jit(solution)/shard_map/ppermute | solution.py:99
  422.8 26.8 %collective-permute-start.23 = (bf16[2,192,1024]{2,1,0:T(8,128)(2,1)S(1)}, bf16[2,192,1024]{2,1,0:T(8,128)(2,1)S(1)}, u32[]{:S(2)}, u32[]{:S(2)}) collective-permute-start(bf16[2,192,1024]{2,1,0:T(8,128)(2,1)S(1)} %copy-done.59), channel_id=1, source_target_pairs={{0,16},{4,20},{8,24},{12,28},{16,0},{20,4},{24,8},{28,12},{1,17},{... | collective-permute-start | bytes 2359304 | tf_op jit(solution)/shard_map/ppermute | solution.py:99
  429.7 8.2 %copy-start.44 = (bf16[256,512]{1,0:T(8,128)(2,1)}, bf16[256,512]{1,0:T(8,128)(2,1)S(1)}, u32[]{:S(2)}) copy-start(bf16[256,512]{1,0:T(8,128)(2,1)S(1)} %collective-permute-done.19.refs_2_) | copy-start | bytes 786436
  442.1 39.6 %collective-permute-start.27 = (bf16[256,2048]{1,0:T(8,128)(2,1)}, bf16[256,2048]{1,0:T(8,128)(2,1)S(1)}, u32[]{:S(2)}, u32[]{:S(2)}) collective-permute-start(bf16[256,2048]{1,0:T(8,128)(2,1)} %get-tuple-element.141.refs_2_.refs_8_), channel_id=1, source_target_pairs={{0,1},{1,2},{2,3},{3,0},{4,5},{5,6},{6,7},{7,4},{8,9},{9,10},{10,1... | collective-permute-start | bytes 3145736 | tf_op jit(solution)/shard_map/ppermute | solution.py:80
  453.9 23.3 %collective-permute-start.28 = (bf16[1,192,1024]{2,1,0:T(8,128)(2,1)}, bf16[1,192,1024]{2,1,0:T(8,128)(2,1)S(1)}, u32[]{:S(2)}, u32[]{:S(2)}) collective-permute-start(bf16[1,192,1024]{2,1,0:T(8,128)(2,1)} %get-tuple-element.136.refs_16_), channel_id=1, source_target_pairs={{0,16},{4,20},{8,24},{12,28},{16,0},{20,4},{24,8},{28,12},{1,17},{... | collective-permute-start | bytes 1179656 | tf_op jit(solution)/shard_map/ppermute | solution.py:99
  455.3 23.3 %collective-permute-start.29 = (bf16[1,192,1024]{2,1,0:T(8,128)(2,1)}, bf16[1,192,1024]{2,1,0:T(8,128)(2,1)S(1)}, u32[]{:S(2)}, u32[]{:S(2)}) collective-permute-start(bf16[1,192,1024]{2,1,0:T(8,128)(2,1)} %get-tuple-element.144), channel_id=1, source_target_pairs={{0,8},{4,12},{8,0},{12,4},{16,24},{20,28},{24,16},{28,20},{1,9},{5... | collective-permute-start | bytes 1179656 | tf_op jit(solution)/shard_map/ppermute | solution.py:99
  473.5 8.1 %collective-permute-start.24 = (f32[8,1024]{1,0:T(8,128)}, f32[8,1024]{1,0:T(8,128)S(1)}, u32[]{:S(2)}, u32[]{:S(2)}) collective-permute-start(f32[8,1024]{1,0:T(8,128)} %get-tuple-element.140.refs_11_), channel_id=1, source_target_pairs={{0,1},{1,2},{2,3},{3,0},{4,5},{5,6},{6,7},{7,4},{8,9},{9,10},{10,1... | collective-permute-start | bytes 98312 | tf_op jit(solution)/shard_map/ppermute | solution.py:80
  474.8 6.9 collective-permute-start.25
  477.2 4.5 collective-permute-start.26
  484.7 25.5 %collective-permute-start.30 = (bf16[256,2048]{1,0:T(8,128)(2,1)}, bf16[256,2048]{1,0:T(8,128)(2,1)S(1)}, u32[]{:S(2)}, u32[]{:S(2)}) collective-permute-start(bf16[256,2048]{1,0:T(8,128)(2,1)} %bitcast.95), channel_id=1, source_target_pairs={{0,1},{1,2},{2,3},{3,0},{4,5},{5,6},{6,7},{7,4},{8,9},{9,10},{10,1... | collective-permute-start | bytes 3145736 | tf_op jit(solution)/shard_map/ppermute | solution.py:80
  485.3 21.6 %collective-permute-start.31 = (bf16[1,192,1024]{2,1,0:T(8,128)(2,1)}, bf16[1,192,1024]{2,1,0:T(8,128)(2,1)S(1)}, u32[]{:S(2)}, u32[]{:S(2)}) collective-permute-start(bf16[1,192,1024]{2,1,0:T(8,128)(2,1)} %get-tuple-element.145.refs_1_.refs_0_), channel_id=1, source_target_pairs={{0,16},{4,20},{8,24},{12,28},{16,0},{20,4},{24,8},{28,12},{1,17},{... | collective-permute-start | bytes 1179656 | tf_op jit(solution)/shard_map/ppermute | solution.py:99
  486.6 20.2 %collective-permute-start.32 = (bf16[1,192,1024]{2,1,0:T(8,128)(2,1)}, bf16[1,192,1024]{2,1,0:T(8,128)(2,1)S(1)}, u32[]{:S(2)}, u32[]{:S(2)}) collective-permute-start(bf16[1,192,1024]{2,1,0:T(8,128)(2,1)} %get-tuple-element.150.refs_2_), channel_id=1, source_target_pairs={{0,8},{4,12},{8,0},{12,4},{16,24},{20,28},{24,16},{28,20},{1,9},{5... | collective-permute-start | bytes 1179656 | tf_op jit(solution)/shard_map/ppermute | solution.py:99
  513.2 24.6 %collective-permute-start.33 = (bf16[256,2048]{1,0:T(8,128)(2,1)}, bf16[256,2048]{1,0:T(8,128)(2,1)S(1)}, u32[]{:S(2)}, u32[]{:S(2)}) collective-permute-start(bf16[256,2048]{1,0:T(8,128)(2,1)} %bitcast.100), channel_id=1, source_target_pairs={{0,1},{1,2},{2,3},{3,0},{4,5},{5,6},{6,7},{7,4},{8,9},{9,10},{10,1... | collective-permute-start | bytes 3145736 | tf_op jit(solution)/shard_map/ppermute | solution.py:80
  554.1 146.5 %all-reduce.10.cloned.1.call-start = ((), (), s32[]{:S(2)}) async-start(), calls=%async_computation.3 | async-start | bytes 16973824 | tf_op jit(solution)/shard_map/psum | solution.py:1225
  555.3 27.6 %collective-permute-start.36 = (bf16[2,192,1024]{2,1,0:T(8,128)(2,1)S(1)}, bf16[2,192,1024]{2,1,0:T(8,128)(2,1)S(1)}, u32[]{:S(2)}, u32[]{:S(2)}) collective-permute-start(bf16[2,192,1024]{2,1,0:T(8,128)(2,1)S(1)} %copy-done.13), channel_id=1, source_target_pairs={{0,8},{4,12},{8,0},{12,4},{16,24},{20,28},{24,16},{28,20},{1,9},{5... | collective-permute-start | bytes 2359304 | tf_op jit(solution)/shard_map/ppermute | solution.py:99
  556.3 28.4 %collective-permute-start.37 = (bf16[2,192,1024]{2,1,0:T(8,128)(2,1)S(1)}, bf16[2,192,1024]{2,1,0:T(8,128)(2,1)S(1)}, u32[]{:S(2)}, u32[]{:S(2)}) collective-permute-start(bf16[2,192,1024]{2,1,0:T(8,128)(2,1)S(1)} %copy-done.27), channel_id=1, source_target_pairs={{0,16},{4,20},{8,24},{12,28},{16,0},{20,4},{24,8},{28,12},{1,17},{... | collective-permute-start | bytes 2359304 | tf_op jit(solution)/shard_map/ppermute | solution.py:99
  557.6 31.1 %collective-permute-start.35 = (bf16[1024,512]{1,0:T(8,128)(2,1)S(1)}, bf16[1024,512]{1,0:T(8,128)(2,1)S(1)}, u32[]{:S(2)}, u32[]{:S(2)}) collective-permute-start(bf16[1024,512]{1,0:T(8,128)(2,1)S(1)} %copy-done.18), channel_id=1, source_target_pairs={{0,1},{1,2},{2,3},{3,0},{4,5},{5,6},{6,7},{7,4},{8,9},{9,10},{10,1... | collective-permute-start | bytes 3145736 | tf_op jit(solution)/shard_map/ppermute | solution.py:80
  561.1 49.4 %collective-permute-start.34 = (bf16[1024,512]{1,0:T(8,128)(2,1)}, bf16[1024,512]{1,0:T(8,128)(2,1)S(1)}, u32[]{:S(2)}, u32[]{:S(2)}) collective-permute-start(bf16[1024,512]{1,0:T(8,128)(2,1)} %shard_map.322.refs_4_), channel_id=1, source_target_pairs={{0,1},{1,2},{2,3},{3,0},{4,5},{5,6},{6,7},{7,4},{8,9},{9,10},{10,1... | collective-permute-start | bytes 3145736 | tf_op jit(solution)/shard_map/ppermute | solution.py:80
  588.7 95.8 %collective-permute-start.41 = (bf16[4,192,2048]{2,1,0:T(8,128)(2,1)}, bf16[4,192,2048]{2,1,0:T(8,128)(2,1)}, u32[]{:S(2)}, u32[]{:S(2)}) collective-permute-start(bf16[4,192,2048]{2,1,0:T(8,128)(2,1)} %shard_map.323.refs_4_.refs_1_), channel_id=1, source_target_pairs={{0,4},{4,0},{8,12},{12,8},{16,20},{20,16},{24,28},{28,24},{1,5},{5... | collective-permute-start | bytes 9437192 | tf_op jit(solution)/shard_map/ppermute | solution.py:99
  596.5 34.2 %collective-permute-start.39 = (bf16[1024,512]{1,0:T(8,128)(2,1)}, bf16[1024,512]{1,0:T(8,128)(2,1)S(1)}, u32[]{:S(2)}, u32[]{:S(2)}) collective-permute-start(bf16[1024,512]{1,0:T(8,128)(2,1)} %shard_map.324.refs_1_), channel_id=1, source_target_pairs={{0,1},{1,2},{2,3},{3,0},{4,5},{5,6},{6,7},{7,4},{8,9},{9,10},{10,1... | collective-permute-start | bytes 3145736 | tf_op jit(solution)/shard_map/ppermute | solution.py:80
  614.5 38.6 %collective-permute-start.38 = (bf16[1024,512]{1,0:T(8,128)(2,1)}, bf16[1024,512]{1,0:T(8,128)(2,1)S(1)}, u32[]{:S(2)}, u32[]{:S(2)}) collective-permute-start(bf16[1024,512]{1,0:T(8,128)(2,1)} %shard_map.326.refs_4_), channel_id=1, source_target_pairs={{0,1},{1,2},{2,3},{3,0},{4,5},{5,6},{6,7},{7,4},{8,9},{9,10},{10,1... | collective-permute-start | bytes 3145736 | tf_op jit(solution)/shard_map/ppermute | solution.py:80
  638.0 19.2 %copy-start.3 = (s32[8]{0:T(128)S(1)}, s32[8]{0:T(128)}, u32[]{:S(2)}) copy-start(s32[8]{0:T(128)} %constant.112.clone) | copy-start | bytes 100
  638.0 37.7 %collective-permute-start.42 = (bf16[1024,512]{1,0:T(8,128)(2,1)}, bf16[1024,512]{1,0:T(8,128)(2,1)S(1)}, u32[]{:S(2)}, u32[]{:S(2)}) collective-permute-start(bf16[1024,512]{1,0:T(8,128)(2,1)} %shard_map.327.refs_3_), channel_id=1, source_target_pairs={{0,1},{1,2},{2,3},{3,0},{4,5},{5,6},{6,7},{7,4},{8,9},{9,10},{10,1... | collective-permute-start | bytes 3145736 | tf_op jit(solution)/shard_map/ppermute | solution.py:80
  657.2 39.4 %collective-permute-start.40 = (bf16[1024,512]{1,0:T(8,128)(2,1)}, bf16[1024,512]{1,0:T(8,128)(2,1)S(1)}, u32[]{:S(2)}, u32[]{:S(2)}) collective-permute-start(bf16[1024,512]{1,0:T(8,128)(2,1)} %shard_map.328.refs_12_), channel_id=1, source_target_pairs={{0,1},{1,2},{2,3},{3,0},{4,5},{5,6},{6,7},{7,4},{8,9},{9,10},{10,1... | collective-permute-start | bytes 3145736 | tf_op jit(solution)/shard_map/ppermute | solution.py:80
  703.1 16.7 %collective-permute-start.43 = (f32[8,2048]{1,0:T(8,128)S(1)}, f32[8,2048]{1,0:T(8,128)S(1)}, u32[]{:S(2)}, u32[]{:S(2)}) collective-permute-start(f32[8,2048]{1,0:T(8,128)S(1)} %slice.101), channel_id=1, source_target_pairs={{0,1},{1,2},{2,3},{3,0},{4,5},{5,6},{6,7},{7,4},{8,9},{9,10},{10,1... | collective-permute-start | bytes 196616 | tf_op jit(solution)/shard_map/ppermute | solution.py:80
  703.2 16.7 %collective-permute-start.44 = (f32[8,2048]{1,0:T(8,128)S(1)}, f32[8,2048]{1,0:T(8,128)S(1)}, u32[]{:S(2)}, u32[]{:S(2)}) collective-permute-start(f32[8,2048]{1,0:T(8,128)S(1)} %slice.101), channel_id=1, source_target_pairs={{0,2},{1,3},{2,0},{3,1},{4,6},{5,7},{6,4},{7,5},{8,10},{9,11},{10,... | collective-permute-start | bytes 196616 | tf_op jit(solution)/shard_map/ppermute | solution.py:80
  705.1 14.7 %collective-permute-start.45 = (f32[8,2048]{1,0:T(8,128)S(1)}, f32[8,2048]{1,0:T(8,128)S(1)}, u32[]{:S(2)}, u32[]{:S(2)}) collective-permute-start(f32[8,2048]{1,0:T(8,128)S(1)} %slice.101), channel_id=1, source_target_pairs={{0,3},{1,0},{2,1},{3,2},{4,7},{5,4},{6,5},{7,6},{8,11},{9,8},{10,9... | collective-permute-start | bytes 196616 | tf_op jit(solution)/shard_map/ppermute | solution.py:80
  707.6 9.7 %copy-start.15 = (bf16[512,2048]{1,0:T(8,128)(2,1)S(1)}, bf16[512,2048]{1,0:T(8,128)(2,1)}, u32[]{:S(2)}) copy-start(bf16[512,2048]{1,0:T(8,128)(2,1)} %get-tuple-element.162) | copy-start | bytes 6291460
  707.6 14.1 %copy-start.1 = (bf16[512,2048]{1,0:T(8,128)(2,1)S(1)}, bf16[512,2048]{1,0:T(8,128)(2,1)}, u32[]{:S(2)}) copy-start(bf16[512,2048]{1,0:T(8,128)(2,1)} %param.27) | copy-start | bytes 6291460
  (47 other events, 76.8 us)
Sparse Core Ops, SparseCore 0:
  44.0 52.0 all-gather.5
  98.3 112.3 all-gather.3
  346.3 200.1 all-reduce.7
  559.8 136.2 all-reduce.9

commit v5 on v4

--- a/solution.py
+++ b/solution.py
@@ -244,9 +244,9 @@
         return self.keep, self.flying[0]
 
 
-def qkv_kernel(owners_ref, *refs):
-    blocks, refs = refs[:-9], refs[-9:]
-    gain_ref, wq_ref, wk_ref, wv_ref, n1_ref, q_ref, k_ref, v_ref, sums_ref = refs
+def query_key_kernel(owners_ref, *refs):
+    blocks, refs = refs[:-7], refs[-7:]
+    gain_ref, wq_ref, wk_ref, n1_ref, q_ref, k_ref, sums_ref = refs
     rows, cols = blocks[0].shape
     full = len(blocks) * cols
     fields = [block[...].astype(F32) for block in blocks]
@@ -260,12 +260,11 @@
         first = pl.multiple_of(at * cols, 128)
         normed = (field * scale * gain).astype(BF)
         n1_ref[:, pl.ds(first, cols)] = normed
-        terms = [dot(normed, ref[pl.ds(first, cols), :]) for ref in (wq_ref, wk_ref, wv_ref)]
+        terms = [dot(normed, ref[pl.ds(first, cols), :]) for ref in (wq_ref, wk_ref)]
         total = terms if k == 0 else [a + b for a, b in zip(total, terms, strict=True)]
-    query, key, value = total
+    query, key = total
     q_ref[...] = query
     k_ref[...] = key
-    v_ref[...] = value.astype(BF)
     which = lax.broadcasted_iota(jnp.int32, (8, rows), 0)
     sums_ref[...] = jnp.where(
         which == 0,
@@ -274,7 +273,7 @@
     )
 
 
-def qkv_call(owners, blocks, gains, wq, wk, wv):
+def query_key_call(owners, blocks, gains, wq, wk):
     length, cols = blocks[0].shape
     full = cols * len(blocks)
     out = wq.shape[1]
@@ -282,26 +281,45 @@
     whole = pl.BlockSpec((full, out), lambda g, o: (0, 0))
     tile = pl.BlockSpec((rows, out), lambda g, o: (g, 0))
     return launch(
-        qkv_kernel,
-        [owners, *blocks, gains, wq, wk, wv],
+        query_key_kernel,
+        [owners, *blocks, gains, wq, wk],
         prefetch=1,
         grid=(length // rows,),
         in_specs=[pl.BlockSpec((rows, cols), lambda g, o: (g, 0))] * len(blocks)
-        + [pl.BlockSpec((len(blocks), 16, cols), lambda g, o: (0, 0, 0)), whole, whole, whole],
+        + [pl.BlockSpec((len(blocks), 16, cols), lambda g, o: (0, 0, 0)), whole, whole],
         out_specs=[
             pl.BlockSpec((rows, full), lambda g, o: (g, 0)),
             tile,
             tile,
-            tile,
             pl.BlockSpec((8, rows), lambda g, o: (0, g)),
         ],
         out_shape=[
             jax.ShapeDtypeStruct((length, full), BF),
             jax.ShapeDtypeStruct((length, out), F32),
             jax.ShapeDtypeStruct((length, out), F32),
-            jax.ShapeDtypeStruct((length, out), BF),
             jax.ShapeDtypeStruct((8, length), F32),
         ],
+    )
+
+
+def value_kernel(n1_ref, wv_ref, v_ref):
+    v_ref[...] = dot(n1_ref[...], wv_ref[...]).astype(BF)
+
+
+def value_call(normed, wv):
+    length, full = normed.shape
+    out = wv.shape[1]
+    rows = min(256, length)
+    return launch(
+        value_kernel,
+        [normed, wv],
+        grid=(length // rows,),
+        in_specs=[
+            pl.BlockSpec((rows, full), lambda g: (g, 0)),
+            pl.BlockSpec((full, out), lambda g: (0, 0)),
+        ],
+        out_specs=pl.BlockSpec((rows, out), lambda g: (g, 0)),
+        out_shape=jax.ShapeDtypeStruct((length, out), BF),
     )
 
 
@@ -1149,10 +1167,9 @@
         x_blocks.append(send(x_blocks[-1], 1, size))
     late_cot = copied(cotangent, (x_blocks[-2], keep, router_wide, cosine, sine))
     cot = lax.all_gather(late_cot, "tensor", axis=0)
-    normed_one, q_pre, k_pre, v_rows, own_sums = qkv_call(
-        owners, x_blocks, gains, w_query, w_key, w_value
-    )
+    normed_one, q_pre, k_pre, own_sums = query_key_call(owners, x_blocks, gains, w_query, w_key)
     sums = [own_sums] + [send(own_sums, step, size) for step in steps]
+    v_rows = value_call(normed_one, w_value)
 
     gq, gk = query_gain[None], key_gain[None]
     attended, lse, q_rot, k_rot = attn_forward(

time: 739 us -> 739 us (level)
    pallas_call x44 -> x45, Pallas kernels: 322 us -> 325 us  [launch(): pl.pallas_call(kernel, grid_spec=pltpu.PrefetchScalarGridSpec(num_scalar_...]
  transfers between devices with their start and end apart: 50 -> 50, of which waited for: 25 -> 23; matrix products, arithmetic and copies ran while one was open for 4% -> 4% of each run, Pallas kernels for 39% -> 40%
where the time goes in v5:
time: 739 us; the launch traced here: 729 us
  Pallas kernels  325 us (44%)
  waiting for transfers between devices  272 us (37%)
  starting transfers between devices  55.6 us (8%)
  local copies, waits for them, and re-layouts  41.1 us (6%)
  between operations  15.6 us (2%)
  other arithmetic  12.8 us (2%)
    pallas_call x45, Pallas kernels, launch(): pl.pallas_call(kernel, grid_spec=pltpu.PrefetchScalarGridSpec(num_scalar_...  325 us
    ppermute x36, waiting for transfers between devices, send(): lax.ppermute(value, 'tensor', [(at, (at + step) % size) for at in range(s...  247 us
    ppermute x36, starting transfers between devices, send(): lax.ppermute(value, 'tensor', [(at, (at + step) % size) for at in range(s...  44.5 us
    unnamed x124, local copies, waits for them, and re-layouts  25.9 us
    ppermute x10, waiting for transfers between devices, swap(): return lax.ppermute(field, 'dp', [(at, at ^ mask) for at in range(n)])  24.7 us
  transfers between devices with their start and end apart: 50, of which 23 were waited for; matrix products, arithmetic and copies ran while one was open for 4% of the time, Pallas kernels for 40%

profile of v5, /device:TPU:0, one launch (start us, length us, event | category | flops | bytes accessed | tf_op | source)
XLA Modules:
  0.0 728.6 jit_solution(3278267795964861751)
XLA Ops:
  9.5 3.1 collective-permute-start.3
  13.9 8.5 %collective-permute-done.3 = bf16[80,2048]{1,0:T(8,128)(2,1)S(1)} collective-permute-done((bf16[80,2048]{1,0:T(8,128)(2,1)S(1)}, bf16[80,2048]{1,0:T(8,128)(2,1)S(1)}, u32[]{:S(2)}, u32[]{:S(2)}) %collective-permute-start.3) | collective-permute-done | bytes 327712 | tf_op jit(solution)/shard_map/ppermute | solution.py:80
  22.4 10.7 %collective-permute-done.4 = bf16[80,2048]{1,0:T(8,128)(2,1)S(1)} collective-permute-done((bf16[80,2048]{1,0:T(8,128)(2,1)S(1)}, bf16[80,2048]{1,0:T(8,128)(2,1)S(1)}, u32[]{:S(2)}, u32[]{:S(2)}) %collective-permute-start.4) | collective-permute-done | bytes 327712 | tf_op jit(solution)/shard_map/ppermute | solution.py:80
  33.1 9.7 %collective-permute-done.5 = bf16[80,2048]{1,0:T(8,128)(2,1)S(1)} collective-permute-done((bf16[80,2048]{1,0:T(8,128)(2,1)S(1)}, bf16[80,2048]{1,0:T(8,128)(2,1)S(1)}, u32[]{:S(2)}, u32[]{:S(2)}) %collective-permute-start.5) | collective-permute-done | bytes 327712 | tf_op jit(solution)/shard_map/ppermute | solution.py:80
  44.3 2.4 fusion.11
  47.4 4.3 reduce-window.6
  54.1 14.2 %collective-permute-done.refs_2_.refs_6_ = bf16[1024,512]{1,0:T(8,128)(2,1)S(1)} collective-permute-done((bf16[1024,512]{1,0:T(8,128)(2,1)S(1)}, bf16[1024,512]{1,0:T(8,128)(2,1)S(1)}, u32[]{:S(2)}, u32[]{:S(2)}) %collective-permute-start) | collective-permute-done | bytes 1048608 | tf_op jit(solution)/shard_map/ppermute | solution.py:80
  69.7 5.5 shard_map.290.refs_1_
  79.0 3.2 fusion.4.refs_3_.refs_4_
  82.2 9.6 %collective-permute-done.1.refs_2_.refs_3_.refs_7_ = bf16[1024,512]{1,0:T(8,128)(2,1)S(1)} collective-permute-done((bf16[1024,512]{1,0:T(8,128)(2,1)S(1)}, bf16[1024,512]{1,0:T(8,128)(2,1)S(1)}, u32[]{:S(2)}, u32[]{:S(2)}) %collective-permute-start.1) | collective-permute-done | bytes 1048608 | tf_op jit(solution)/shard_map/ppermute | solution.py:80
  96.0 33.2 %collective-permute-done.2.refs_4_.refs_8_ = bf16[1024,512]{1,0:T(8,128)(2,1)S(1)} collective-permute-done((bf16[1024,512]{1,0:T(8,128)(2,1)}, bf16[1024,512]{1,0:T(8,128)(2,1)S(1)}, u32[]{:S(2)}, u32[]{:S(2)}) %collective-permute-start.2) | collective-permute-done | bytes 1048608 | tf_op jit(solution)/shard_map/ppermute | solution.py:80
  130.1 11.2 %shard_map.292 = (bf16[1024,2048]{1,0:T(8,128)(2,1)}, f32[1024,512]{1,0:T(8,128)}, f32[1024,512]{1,0:T(8,128)}, f32[8,1024]{1,0:T(8,128)}) custom-call(s32[4]{0:T(128)} %and_select_fusion.refs_0_, bf16[1024,512]{1,0:T(8,128)(2,1)} %refs_4_.1, bf16[1024,512]{1,0:T(8,128)(2,1)} %copy-done.8, bf16[1024,512]{1,0:T(8,128)(2,1)} %copy-done.7, ...), custom_call_target="tpu_custom_call" | custom-call | flops 1 | bytes 1 | tf_op jit(solution)/shard_map/pallas_call | solution.py:42
  147.5 6.2 shard_map.293.refs_3_.refs_5_
  154.3 14.0 %shard_map.294 = (bf16[1024,512]{1,0:T(8,128)(2,1)}, f32[1024,512]{1,0:T(8,128)}, bf16[1024,512]{1,0:T(8,128)(2,1)}, bf16[1024,512]{1,0:T(8,128)(2,1)}) custom-call(s32[1]{0:T(128)S(6)} %copy.79.refs_0_, f32[1024,512]{1,0:T(8,128)} %get-tuple-element.86.refs_1_.refs_0_, f32[1024,512]{1,0:T(8,128)} %get-tuple-element.87.refs_2_.refs_1_, ...), custom_call_target="tpu_custom_call" | custom-call | flops 1 | bytes 1 | tf_op jit(solution)/shard_map/pallas_call | solution.py:42
  173.7 27.9 %collective-permute-done.10.refs_3_ = bf16[256,512]{1,0:T(8,128)(2,1)S(1)} collective-permute-done((bf16[256,512]{1,0:T(8,128)(2,1)S(1)}, bf16[256,512]{1,0:T(8,128)(2,1)S(1)}, u32[]{:S(2)}, u32[]{:S(2)}) %collective-permute-start.10) | collective-permute-done | bytes 262176 | tf_op jit(solution)/shard_map/ppermute | solution.py:80
  202.6 9.3 %shard_map.295 = (f32[256,2048]{1,0:T(8,128)}, bf16[256,2048]{1,0:T(8,128)(2,1)}) custom-call(s32[4]{0:T(128)} %and_select_fusion.refs_0_, bf16[1024,512]{1,0:T(8,128)(2,1)} %get-tuple-element.90.refs_1_, bf16[256,512]{1,0:T(8,128)(2,1)} %copy-done.43, bf16[256,512]{1,0:T(8,128)(2,1)} %copy-done.41, bf16[256,512]{1,0:T(8,128)(2,1)} %copy-done.42, ...), custom_call_target="tpu_custom_call" | custom-call | flops 1 | bytes 1 | tf_op jit(solution)/shard_map/pallas_call | solution.py:42
  214.0 8.8 %collective-permute-start.12 = (bf16[256,2048]{1,0:T(8,128)(2,1)}, bf16[256,2048]{1,0:T(8,128)(2,1)S(1)}, u32[]{:S(2)}, u32[]{:S(2)}) collective-permute-start(bf16[256,2048]{1,0:T(8,128)(2,1)} %bitcast.88), channel_id=1, source_target_pairs={{0,1},{1,2},{2,3},{3,0},{4,5},{5,6},{6,7},{7,4},{8,9},{9,10},{10,1... | collective-permute-start | bytes 3145736 | tf_op jit(solution)/shard_map/ppermute | solution.py:80
  223.4 19.2 %shard_map.297 = (bf16[1536,1024]{1,0:T(8,128)(2,1)}, bf16[1024,1536]{1,0:T(8,128)(2,1)}, bf16[1024,1536]{1,0:T(8,128)(2,1)}, bf16[2048,1024]{1,0:T(8,128)(2,1)}...) custom-call(s32[1]{0:T(128)} %get-tuple-element.177.refs_0_, ...), custom_call_target="tpu_custom_call" | custom-call | flops 1 | bytes 1 | tf_op jit(solution)/shard_map/pallas_call | solution.py:42
  245.8 18.5 %shard_map.299 = (bf16[1536,1024]{1,0:T(8,128)(2,1)}, bf16[1024,1536]{1,0:T(8,128)(2,1)}, bf16[1024,1536]{1,0:T(8,128)(2,1)}, bf16[2048,1024]{1,0:T(8,128)(2,1)}...) custom-call(s32[1]{0:T(128)} %get-tuple-element.175.refs_0_, ...), custom_call_target="tpu_custom_call", output_to_operand_aliasing={{0}: (8, {}), {1}: (9, {}), {2}: (10, {}), {3}: (11, {}), {... | custom-call | flops 1 | bytes 1 | tf_op jit(solution)/shard_map/pallas_call | solution.py:42
  264.3 3.7 collective-permute-done.13.refs_1_
  271.0 18.4 %shard_map.301 = (bf16[1536,1024]{1,0:T(8,128)(2,1)}, bf16[1024,1536]{1,0:T(8,128)(2,1)}, bf16[1024,1536]{1,0:T(8,128)(2,1)}, bf16[2048,1024]{1,0:T(8,128)(2,1)}...) custom-call(s32[1]{0:T(128)} %get-tuple-element.174.refs_0_, ...), custom_call_target="tpu_custom_call", output_to_operand_aliasing={{0}: (8, {}), {1}: (9, {}), {2}: (10, {}), {3}: (11, {}), {... | custom-call | flops 1 | bytes 1 | tf_op jit(solution)/shard_map/pallas_call | solution.py:42
  289.4 2.8 collective-permute-done.14.refs_1_
  293.3 18.4 %shard_map.302 = (bf16[1536,1024]{1,0:T(8,128)(2,1)}, bf16[1024,1536]{1,0:T(8,128)(2,1)}, bf16[1024,1536]{1,0:T(8,128)(2,1)}, bf16[2048,1024]{1,0:T(8,128)(2,1)}...) custom-call(s32[1]{0:T(128)} %get-tuple-element.176.refs_0_, ...), custom_call_target="tpu_custom_call", output_to_operand_aliasing={{0}: (8, {}), {1}: (9, {}), {2}: (10, {}), {3}: (11, {}), {... | custom-call | flops 1 | bytes 1 | tf_op jit(solution)/shard_map/pallas_call | solution.py:42
  314.4 18.1 %shard_map.304.refs_3_ = bf16[2,6,2048,256]{3,2,1,0:T(8,128)(2,1)} custom-call(bf16[2048,1024]{1,0:T(8,128)(2,1)} %get-tuple-element.120.refs_0_, bf16[1024,1536]{1,0:T(8,128)(2,1)} %get-tuple-element.121.refs_1_, bf16[1024,1536]{1,0:T(8,128)(2,1)} %get-tuple-element.122.refs_2_, bf16[1,256,2176]{2,1,0:T(8,128)(2,1)} %shard_map.303.refs_3_), custom_call_target="tpu_custom_call" | custom-call | flops 1 | bytes 1 | tf_op jit(solution)/shard_map/pallas_call | solution.py:42
  332.5 8.2 %shard_map.305.refs_2_ = bf16[4,192,2048]{2,1,0:T(8,128)(2,1)} custom-call(s32[4]{0:T(128)} %get-tuple-element.173.refs_0_, bf16[1536,1024]{1,0:T(8,128)(2,1)} %get-tuple-element.119.refs_1_, bf16[4,1024,512]{2,1,0:T(8,128)(2,1)} %all-gather.4.cloned.1.call-done.refs_2_.refs_7_, bf16[2,6,2048,256]{3,2,1,0:T(8,128)(2,1)} %shard_map.304.refs_3_), custom_call_target="tpu_custom_call" | custom-call | flops 1 | bytes 1 | tf_op jit(solution)/shard_map/pallas_call | solution.py:42
  342.5 2.5 shard_map.306.refs_3_
  344.9 8.2 %shard_map.307.refs_2_.refs_0_ = bf16[4,192,2048]{2,1,0:T(8,128)(2,1)} custom-call(s32[4]{0:T(128)} %get-tuple-element.172.refs_0_, bf16[1536,1024]{1,0:T(8,128)(2,1)} %get-tuple-element.119.refs_1_, bf16[4,1024,512]{2,1,0:T(8,128)(2,1)} %all-gather.4.cloned.1.call-done.refs_2_.refs_7_, bf16[1,256,2176]{2,1,0:T(8,128)(2,1)} %shard_map.306.refs_3_), custom_call_target="tpu_custom_call" | custom-call | flops 1 | bytes 1 | tf_op jit(solution)/shard_map/pallas_call | solution.py:42
  353.1 20.6 %collective-permute-done.16 = bf16[256,2176]{1,0:T(8,128)(2,1)S(1)} collective-permute-done((bf16[256,2176]{1,0:T(8,128)(2,1)}, bf16[256,2176]{1,0:T(8,128)(2,1)S(1)}, u32[]{:S(2)}, u32[]{:S(2)}) %collective-permute-start.16) | collective-permute-done | bytes 1114144 | tf_op jit(solution)/shard_map/ppermute | solution.py:80
  374.8 2.5 shard_map.308.refs_2_
  377.3 4.8 shard_map.309
  382.1 23.2 %collective-permute-done.17.refs_2_ = bf16[256,2176]{1,0:T(8,128)(2,1)S(1)} collective-permute-done((bf16[256,2176]{1,0:T(8,128)(2,1)}, bf16[256,2176]{1,0:T(8,128)(2,1)S(1)}, u32[]{:S(2)}, u32[]{:S(2)}) %collective-permute-start.17) | collective-permute-done | bytes 1114144 | tf_op jit(solution)/shard_map/ppermute | solution.py:80
  406.3 12.0 %shard_map.310 = (bf16[256,2048]{1,0:T(8,128)(2,1)}, f32[8,2048]{1,0:T(8,128)}, bf16[256,512]{1,0:T(8,128)(2,1)}, bf16[256,512]{1,0:T(8,128)(2,1)}, bf16[256,512]{1,0:T(8,128)(2,1)}, /*index=5*/bf16[256,512]{1,0:T(8,128)(2,1)}) custom-call(s32[1]{0:T(128)} %bitcast.23.refs_0_, bf16[256,2176]{1,0:T(8,128)(2,1)} %get-tuple-element.114.refs_1_, ...), custom_call_target="tpu_custom_call" | custom-call | flops 1 | bytes 1 | tf_op jit(solution)/shard_map/pallas_call | solution.py:42
  418.4 3.7 collective-permute-start.21
  422.1 2.7 collective-permute-start.22
  426.1 3.5 collective-permute-done.19.refs_2_
  429.6 8.3 %collective-permute-done.20.refs_3_ = bf16[256,512]{1,0:T(8,128)(2,1)S(1)} collective-permute-done((bf16[256,512]{1,0:T(8,128)(2,1)}, bf16[256,512]{1,0:T(8,128)(2,1)S(1)}, u32[]{:S(2)}, u32[]{:S(2)}) %collective-permute-start.20) | collective-permute-done | bytes 262176 | tf_op jit(solution)/shard_map/ppermute | solution.py:80
  438.7 3.4 shard_map.311
  442.1 5.1 collective-permute-start.27
  447.2 2.5 collective-permute-done.22.refs_1_
  450.9 3.4 shard_map.312
  457.1 17.4 %shard_map.313 = (f32[1024,512]{1,0:T(8,128)}, f32[1024,512]{1,0:T(8,128)}, bf16[1024,512]{1,0:T(8,128)(2,1)}, f32[8,512]{1,0:T(8,128)}, f32[8,1024]{1,0:T(8,128)}) custom-call(s32[1]{0:T(128)S(6)} %copy.79.refs_0_, f32[1024,512]{1,0:T(8,128)} %get-tuple-element.86.refs_1_.refs_0_, f32[1024,512]{1,0:T(8,128)} %get-tuple-element.87.refs_2_.refs_1_, ...), custom_call_target="tpu_custom_call" | custom-call | flops 1 | bytes 1 | tf_op jit(solution)/shard_map/pallas_call | solution.py:42
  475.0 2.4 collective-permute-start.25
  487.8 6.7 shard_map.316
  494.5 12.2 %shard_map.317 = (bf16[2048,1536]{1,0:T(8,128)(2,1)}, f32[8,2048]{1,0:T(8,128)}) custom-call(bf16[1024,2048]{1,0:T(8,128)(2,1)} %get-tuple-element.88.refs_0_, bf16[1024,1536]{1,0:T(8,128)(2,1)} %get-tuple-element.144.refs_1_, bf16[2048,1536]{1,0:T(8,128)(2,1)} %bitcast.78), custom_call_target="tpu_custom_call" | custom-call | flops 1 | bytes 1 | tf_op jit(solution)/shard_map/pallas_call | solution.py:42
  507.6 2.4 shard_map.318
  515.9 22.5 %collective-permute-done.33.refs_5_.refs_11_ = bf16[256,2048]{1,0:T(8,128)(2,1)S(1)} collective-permute-done((bf16[256,2048]{1,0:T(8,128)(2,1)}, bf16[256,2048]{1,0:T(8,128)(2,1)S(1)}, u32[]{:S(2)}, u32[]{:S(2)}) %collective-permute-start.33) | collective-permute-done | bytes 1048608 | tf_op jit(solution)/shard_map/ppermute | solution.py:80
  539.4 7.1 shard_map.320.refs_1_
  548.1 6.2 shard_map.322.refs_2_
  558.2 2.7 shard_map.323.refs_4_
  562.9 20.2 %collective-permute-done.36.refs_1_ = bf16[2,192,1024]{2,1,0:T(8,128)(2,1)S(1)} collective-permute-done((bf16[2,192,1024]{2,1,0:T(8,128)(2,1)S(1)}, bf16[2,192,1024]{2,1,0:T(8,128)(2,1)S(1)}, u32[]{:S(2)}, u32[]{:S(2)}) %collective-permute-start.36) | collective-permute-done | bytes 786464 | tf_op jit(solution)/shard_map/ppermute | solution.py:99
  586.0 3.1 shard_map.324.refs_4_.refs_1_
  590.1 6.7 shard_map.325.refs_1_
  596.7 14.0 %shard_map.326 = (f32[6,2048,256]{2,1,0:T(8,128)}, f32[6,2048,256]{2,1,0:T(8,128)}) custom-call(bf16[2,6,2048,256]{3,2,1,0:T(8,128)(2,1)} %all-reduce.8.cloned.1.call-done.refs_2_.refs_0_, bf16[1024,512]{1,0:T(8,128)(2,1)} %shard_map.325.refs_1_), custom_call_target="tpu_custom_call" | custom-call | flops 1 | bytes 1 | tf_op jit(solution)/shard_map/pallas_call | solution.py:42
  611.7 3.1 shard_map.327.refs_4_
  616.8 13.7 %collective-permute-done.39.refs_3_ = bf16[1024,512]{1,0:T(8,128)(2,1)S(1)} collective-permute-done((bf16[1024,512]{1,0:T(8,128)(2,1)}, bf16[1024,512]{1,0:T(8,128)(2,1)S(1)}, u32[]{:S(2)}, u32[]{:S(2)}) %collective-permute-start.39) | collective-permute-done | bytes 1048608 | tf_op jit(solution)/shard_map/ppermute | solution.py:80
  631.5 6.3 shard_map.328.refs_3_
  637.8 15.2 %collective-permute-done.38.refs_2_ = bf16[1024,512]{1,0:T(8,128)(2,1)S(1)} collective-permute-done((bf16[1024,512]{1,0:T(8,128)(2,1)}, bf16[1024,512]{1,0:T(8,128)(2,1)S(1)}, u32[]{:S(2)}, u32[]{:S(2)}) %collective-permute-start.38) | collective-permute-done | bytes 1048608 | tf_op jit(solution)/shard_map/ppermute | solution.py:80
  654.0 3.0 shard_map.329.refs_12_
  658.2 17.3 %collective-permute-done.42.refs_3_ = bf16[1024,512]{1,0:T(8,128)(2,1)S(1)} collective-permute-done((bf16[1024,512]{1,0:T(8,128)(2,1)}, bf16[1024,512]{1,0:T(8,128)(2,1)S(1)}, u32[]{:S(2)}, u32[]{:S(2)}) %collective-permute-start.42) | collective-permute-done | bytes 1048608 | tf_op jit(solution)/shard_map/ppermute | solution.py:80
  676.5 7.8 %shard_map.330.refs_3_ = f32[1024,512]{1,0:T(8,128)} custom-call(s32[4]{0:T(128)} %and_select_fusion.refs_0_, bf16[1024,1536]{1,0:T(8,128)(2,1)} %get-tuple-element.144.refs_1_, bf16[2048,1536]{1,0:T(8,128)(2,1)} %bitcast.82, bf16[1024,512]{1,0:T(8,128)(2,1)} %copy-done.19, bf16[1024,512]{1,0:T(8,128)(2,1)} %refs_4_.1, ...), custom_call_target="tpu_custom_call" | custom-call | flops 1 | bytes 1 | tf_op jit(solution)/shard_map/pallas_call | solution.py:42
  684.3 10.6 %shard_map.331.refs_3_ = f32[1536,2048]{1,0:T(8,128)} custom-call(s32[8]{0:T(128)} %gather_fusion, bf16[4,192,2048]{2,1,0:T(8,128)(2,1)} %shard_map.324.refs_4_.refs_1_, bf16[4,192,2048]{2,1,0:T(8,128)(2,1)} %collective-permute-done.41.refs_2_, f32[1024,512]{1,0:T(8,128)} %shard_map.330.refs_3_), custom_call_target="tpu_custom_call" | custom-call | flops 1 | bytes 1 | tf_op jit(solution)/shard_map/pallas_call | solution.py:42
  697.4 3.1 shard_map.332.refs_1_
  707.5 9.7 %shard_map.334 = (f32[2048,512]{1,0:T(8,128)}, f32[2048,512]{1,0:T(8,128)}, f32[2048,512]{1,0:T(8,128)}) custom-call(bf16[2048,1536]{1,0:T(8,128)(2,1)} %get-tuple-element.159.refs_0_, bf16[1,32,1536]{2,1,0:T(8,128)(2,1)} %shard_map.333.refs_1_), custom_call_target="tpu_custom_call" | custom-call | flops 1 | bytes 1 | tf_op jit(solution)/shard_map/pallas_call | solution.py:42
  717.2 2.5 convert_element_type.28
  (268 shorter events, 101.5 us)
Async XLA Ops:
  7.2 194.7 %all-gather.6.cloned.1.call-start = ((), (), s32[]{:S(2)}) async-start(), calls=%async_computation.2 | async-start | bytes 9437184 | tf_op jit(solution)/shard_map/all_gather | solution.py:1156
  9.5 12.8 %collective-permute-start.3 = (bf16[80,2048]{1,0:T(8,128)(2,1)S(1)}, bf16[80,2048]{1,0:T(8,128)(2,1)S(1)}, u32[]{:S(2)}, u32[]{:S(2)}) collective-permute-start(bf16[80,2048]{1,0:T(8,128)(2,1)S(1)} %fusion.18), channel_id=1, source_target_pairs={{0,1},{1,2},{2,3},{3,0},{4,5},{5,6},{6,7},{7,4},{8,9},{9,10},{10,1... | collective-permute-start | bytes 983048 | tf_op jit(solution)/shard_map/ppermute | solution.py:80
  12.8 31.2 %copy-start.4 = (bf16[1024,512]{1,0:T(8,128)(2,1)S(1)}, bf16[1024,512]{1,0:T(8,128)(2,1)}, u32[]{:S(2)}) copy-start(bf16[1024,512]{1,0:T(8,128)(2,1)} %refs_4_.1) | copy-start | bytes 3145732
  12.8 31.3 %copy-start.50 = (s32[1,3072]{1,0:T(1,128)S(1)}, s32[1,3072]{1,0:T(1,128)}, u32[]{:S(2)}) copy-start(s32[1,3072]{1,0:T(1,128)} %param.35) | copy-start | bytes 36868
  12.8 31.5 %copy-start.60 = (s32[1024,3]{0,1:T(4,128)S(1)}, s32[1024,3]{0,1:T(4,128)}, u32[]{:S(2)}) copy-start(s32[1024,3]{0,1:T(4,128)} %param.33) | copy-start | bytes 36868
  22.4 10.7 %collective-permute-start.4 = (bf16[80,2048]{1,0:T(8,128)(2,1)S(1)}, bf16[80,2048]{1,0:T(8,128)(2,1)S(1)}, u32[]{:S(2)}, u32[]{:S(2)}) collective-permute-start(bf16[80,2048]{1,0:T(8,128)(2,1)S(1)} %collective-permute-done.3), channel_id=1, source_target_pairs={{0,1},{1,2},{2,3},{3,0},{4,5},{5,6},{6,7},{7,4},{8,9},{9,10},{10,1... | collective-permute-start | bytes 983048 | tf_op jit(solution)/shard_map/ppermute | solution.py:80
  33.1 9.8 %collective-permute-start.5 = (bf16[80,2048]{1,0:T(8,128)(2,1)S(1)}, bf16[80,2048]{1,0:T(8,128)(2,1)S(1)}, u32[]{:S(2)}, u32[]{:S(2)}) collective-permute-start(bf16[80,2048]{1,0:T(8,128)(2,1)S(1)} %collective-permute-done.4), channel_id=1, source_target_pairs={{0,1},{1,2},{2,3},{3,0},{4,5},{5,6},{6,7},{7,4},{8,9},{9,10},{10,1... | collective-permute-start | bytes 983048 | tf_op jit(solution)/shard_map/ppermute | solution.py:80
  43.9 168.0 %all-gather.4.cloned.1.call-start = ((), (), s32[]{:S(2)}) async-start(), calls=%async_computation | async-start | bytes 5242880 | tf_op jit(solution)/shard_map/all_gather | solution.py:1169
  44.0 24.4 %collective-permute-start = (bf16[1024,512]{1,0:T(8,128)(2,1)S(1)}, bf16[1024,512]{1,0:T(8,128)(2,1)S(1)}, u32[]{:S(2)}, u32[]{:S(2)}) collective-permute-start(bf16[1024,512]{1,0:T(8,128)(2,1)S(1)} %copy-done.4), channel_id=1, source_target_pairs={{0,1},{1,2},{2,3},{3,0},{4,5},{5,6},{6,7},{7,4},{8,9},{9,10},{10,1... | collective-permute-start | bytes 3145736 | tf_op jit(solution)/shard_map/ppermute | solution.py:80
  68.3 23.4 %collective-permute-start.1 = (bf16[1024,512]{1,0:T(8,128)(2,1)S(1)}, bf16[1024,512]{1,0:T(8,128)(2,1)S(1)}, u32[]{:S(2)}, u32[]{:S(2)}) collective-permute-start(bf16[1024,512]{1,0:T(8,128)(2,1)S(1)} %collective-permute-done.refs_2_.refs_6_), channel_id=1, source_target_pairs={{0,1},{1,2},{2,3},{3,0},{4,5},{5,6},{6,7},{7,4},{8,9},{9,10},{10,1... | collective-permute-start | bytes 3145736 | tf_op jit(solution)/shard_map/ppermute | solution.py:80
  69.7 9.3 %copy-start.35 = (f32[3072,8]{0,1:T(8,128)S(1)}, f32[3072,8]{0,1:T(8,128)}, u32[]{:S(2)}) copy-start(f32[3072,8]{0,1:T(8,128)} %copy-done.34) | copy-start | bytes 294916
  94.8 34.4 %collective-permute-start.2 = (bf16[1024,512]{1,0:T(8,128)(2,1)}, bf16[1024,512]{1,0:T(8,128)(2,1)S(1)}, u32[]{:S(2)}, u32[]{:S(2)}) collective-permute-start(bf16[1024,512]{1,0:T(8,128)(2,1)} %copy-done.7), channel_id=1, source_target_pairs={{0,1},{1,2},{2,3},{3,0},{4,5},{5,6},{6,7},{7,4},{8,9},{9,10},{10,1... | collective-permute-start | bytes 3145736 | tf_op jit(solution)/shard_map/ppermute | solution.py:80
  96.0 49.7 %copy-start.56 = (bf16[512]{0:T(512)(128)(2,1)S(1)}, bf16[512]{0:T(512)(128)(2,1)}, u32[]{:S(2)}) copy-start(bf16[512]{0:T(512)(128)(2,1)} %param.25) | copy-start | bytes 3076
  96.0 50.3 %copy-start.57 = (bf16[512]{0:T(512)(128)(2,1)S(1)}, bf16[512]{0:T(512)(128)(2,1)}, u32[]{:S(2)}) copy-start(bf16[512]{0:T(512)(128)(2,1)} %param.26) | copy-start | bytes 3076
  141.3 12.3 %collective-permute-start.6 = (f32[8,1024]{1,0:T(8,128)}, f32[8,1024]{1,0:T(8,128)S(1)}, u32[]{:S(2)}, u32[]{:S(2)}) collective-permute-start(f32[8,1024]{1,0:T(8,128)} %get-tuple-element.89.refs_8_.refs_12_.refs_7_.refs_5_), channel_id=1, source_target_pairs={{0,1},{1,2},{2,3},{3,0},{4,5},{5,6},{6,7},{7,4},{8,9},{9,10},{10,1... | collective-permute-start | bytes 98312 | tf_op jit(solution)/shard_map/ppermute | solution.py:80
  141.4 12.3 %collective-permute-start.7 = (f32[8,1024]{1,0:T(8,128)}, f32[8,1024]{1,0:T(8,128)S(1)}, u32[]{:S(2)}, u32[]{:S(2)}) collective-permute-start(f32[8,1024]{1,0:T(8,128)} %get-tuple-element.89.refs_8_.refs_12_.refs_7_.refs_5_), channel_id=1, source_target_pairs={{0,2},{1,3},{2,0},{3,1},{4,6},{5,7},{6,4},{7,5},{8,10},{9,11},{10,... | collective-permute-start | bytes 98312 | tf_op jit(solution)/shard_map/ppermute | solution.py:80
  143.3 10.4 %collective-permute-start.8 = (f32[8,1024]{1,0:T(8,128)}, f32[8,1024]{1,0:T(8,128)S(1)}, u32[]{:S(2)}, u32[]{:S(2)}) collective-permute-start(f32[8,1024]{1,0:T(8,128)} %get-tuple-element.89.refs_8_.refs_12_.refs_7_.refs_5_), channel_id=1, source_target_pairs={{0,3},{1,0},{2,1},{3,2},{4,7},{5,4},{6,5},{7,6},{8,11},{9,8},{10,9... | collective-permute-start | bytes 98312 | tf_op jit(solution)/shard_map/ppermute | solution.py:80
  169.5 32.0 %collective-permute-start.10 = (bf16[256,512]{1,0:T(8,128)(2,1)S(1)}, bf16[256,512]{1,0:T(8,128)(2,1)S(1)}, u32[]{:S(2)}, u32[]{:S(2)}) collective-permute-start(bf16[256,512]{1,0:T(8,128)(2,1)S(1)} %get-tuple-element.162), channel_id=1, source_target_pairs={{0,2},{1,3},{2,0},{3,1},{4,6},{5,7},{6,4},{7,5},{8,10},{9,11},{10,... | collective-permute-start | bytes 786440 | tf_op jit(solution)/shard_map/ppermute | solution.py:80
  171.7 29.9 %collective-permute-start.11 = (bf16[256,512]{1,0:T(8,128)(2,1)S(1)}, bf16[256,512]{1,0:T(8,128)(2,1)S(1)}, u32[]{:S(2)}, u32[]{:S(2)}) collective-permute-start(bf16[256,512]{1,0:T(8,128)(2,1)S(1)} %get-tuple-element.161), channel_id=1, source_target_pairs={{0,3},{1,0},{2,1},{3,2},{4,7},{5,4},{6,5},{7,6},{8,11},{9,8},{10,9... | collective-permute-start | bytes 786440 | tf_op jit(solution)/shard_map/ppermute | solution.py:80
  172.6 29.3 %collective-permute-start.9 = (bf16[256,512]{1,0:T(8,128)(2,1)S(1)}, bf16[256,512]{1,0:T(8,128)(2,1)S(1)}, u32[]{:S(2)}, u32[]{:S(2)}) collective-permute-start(bf16[256,512]{1,0:T(8,128)(2,1)S(1)} %get-tuple-element.163), channel_id=1, source_target_pairs={{0,1},{1,2},{2,3},{3,0},{4,5},{5,6},{6,7},{7,4},{8,9},{9,10},{10,1... | collective-permute-start | bytes 786440 | tf_op jit(solution)/shard_map/ppermute | solution.py:80
  211.9 10.9 %copy-start.51 = (s32[4]{0:T(128)S(1)}, s32[4]{0:T(128)}, u32[]{:S(2)}) copy-start(s32[4]{0:T(128)} %and_select_fusion.refs_0_) | copy-start | bytes 52
  214.0 28.7 %collective-permute-start.12 = (bf16[256,2048]{1,0:T(8,128)(2,1)}, bf16[256,2048]{1,0:T(8,128)(2,1)S(1)}, u32[]{:S(2)}, u32[]{:S(2)}) collective-permute-start(bf16[256,2048]{1,0:T(8,128)(2,1)} %bitcast.88), channel_id=1, source_target_pairs={{0,1},{1,2},{2,3},{3,0},{4,5},{5,6},{6,7},{7,4},{8,9},{9,10},{10,1... | collective-permute-start | bytes 3145736 | tf_op jit(solution)/shard_map/ppermute | solution.py:80
  245.7 22.3 %collective-permute-start.13 = (bf16[256,2048]{1,0:T(8,128)(2,1)}, bf16[256,2048]{1,0:T(8,128)(2,1)S(1)}, u32[]{:S(2)}, u32[]{:S(2)}) collective-permute-start(bf16[256,2048]{1,0:T(8,128)(2,1)} %bitcast.99), channel_id=1, source_target_pairs={{0,1},{1,2},{2,3},{3,0},{4,5},{5,6},{6,7},{7,4},{8,9},{9,10},{10,1... | collective-permute-start | bytes 3145736 | tf_op jit(solution)/shard_map/ppermute | solution.py:80
  271.0 21.3 %collective-permute-start.14 = (bf16[256,2048]{1,0:T(8,128)(2,1)}, bf16[256,2048]{1,0:T(8,128)(2,1)S(1)}, u32[]{:S(2)}, u32[]{:S(2)}) collective-permute-start(bf16[256,2048]{1,0:T(8,128)(2,1)} %bitcast.98), channel_id=1, source_target_pairs={{0,1},{1,2},{2,3},{3,0},{4,5},{5,6},{6,7},{7,4},{8,9},{9,10},{10,1... | collective-permute-start | bytes 3145736 | tf_op jit(solution)/shard_map/ppermute | solution.py:80
  293.3 20.5 %copy-start.2 = (s32[8]{0:T(128)S(1)}, s32[8]{0:T(128)}, u32[]{:S(2)}) copy-start(s32[8]{0:T(128)} %constant.112.clone) | copy-start | bytes 100
  313.8 27.7 %collective-permute-start.15 = (bf16[256,2176]{1,0:T(8,128)(2,1)}, bf16[256,2176]{1,0:T(8,128)(2,1)S(1)}, u32[]{:S(2)}, u32[]{:S(2)}) collective-permute-start(bf16[256,2176]{1,0:T(8,128)(2,1)} %bitcast.94), channel_id=1, source_target_pairs={{0,1},{1,2},{2,3},{3,0},{4,5},{5,6},{6,7},{7,4},{8,9},{9,10},{10,1... | collective-permute-start | bytes 3342344 | tf_op jit(solution)/shard_map/ppermute | solution.py:80
  340.7 205.9 %all-reduce.8.cloned.1.call-start = ((), (), s32[]{:S(2)}) async-start(), calls=%async_computation.1 | async-start | bytes 25165824 | tf_op jit(solution)/shard_map/psum | solution.py:1209
  340.9 36.3 %collective-permute-start.18 = (bf16[4,192,2048]{2,1,0:T(8,128)(2,1)}, bf16[4,192,2048]{2,1,0:T(8,128)(2,1)}, u32[]{:S(2)}, u32[]{:S(2)}) collective-permute-start(bf16[4,192,2048]{2,1,0:T(8,128)(2,1)} %shard_map.305.refs_2_), channel_id=1, source_target_pairs={{0,4},{4,0},{8,12},{12,8},{16,20},{20,16},{24,28},{28,24},{1,5},{5... | collective-permute-start | bytes 9437192 | tf_op jit(solution)/shard_map/ppermute | solution.py:99
  344.9 28.8 %collective-permute-start.16 = (bf16[256,2176]{1,0:T(8,128)(2,1)}, bf16[256,2176]{1,0:T(8,128)(2,1)S(1)}, u32[]{:S(2)}, u32[]{:S(2)}) collective-permute-start(bf16[256,2176]{1,0:T(8,128)(2,1)} %bitcast.104), channel_id=1, source_target_pairs={{0,1},{1,2},{2,3},{3,0},{4,5},{5,6},{6,7},{7,4},{8,9},{9,10},{10,1... | collective-permute-start | bytes 3342344 | tf_op jit(solution)/shard_map/ppermute | solution.py:80
  377.3 28.1 %collective-permute-start.17 = (bf16[256,2176]{1,0:T(8,128)(2,1)}, bf16[256,2176]{1,0:T(8,128)(2,1)S(1)}, u32[]{:S(2)}, u32[]{:S(2)}) collective-permute-start(bf16[256,2176]{1,0:T(8,128)(2,1)} %bitcast.93), channel_id=1, source_target_pairs={{0,1},{1,2},{2,3},{3,0},{4,5},{5,6},{6,7},{7,4},{8,9},{9,10},{10,1... | collective-permute-start | bytes 3342344 | tf_op jit(solution)/shard_map/ppermute | solution.py:80
  382.1 40.0 %copy-start.26 = (bf16[2,192,1024]{2,1,0:T(8,128)(2,1)S(1)}, bf16[2,192,1024]{2,1,0:T(8,128)(2,1)}, u32[]{:S(2)}) copy-start(bf16[2,192,1024]{2,1,0:T(8,128)(2,1)} %get-tuple-element.123.refs_10_) | copy-start | bytes 2359300
  382.1 42.7 %copy-start.59 = (bf16[2,192,1024]{2,1,0:T(8,128)(2,1)S(1)}, bf16[2,192,1024]{2,1,0:T(8,128)(2,1)}, u32[]{:S(2)}) copy-start(bf16[2,192,1024]{2,1,0:T(8,128)(2,1)} %get-tuple-element.133) | copy-start | bytes 2359300
  418.3 11.3 %collective-permute-start.19 = (bf16[256,512]{1,0:T(8,128)(2,1)}, bf16[256,512]{1,0:T(8,128)(2,1)S(1)}, u32[]{:S(2)}, u32[]{:S(2)}) collective-permute-start(bf16[256,512]{1,0:T(8,128)(2,1)} %get-tuple-element.125), channel_id=1, source_target_pairs={{0,1},{1,2},{2,3},{3,0},{4,5},{5,6},{6,7},{7,4},{8,9},{9,10},{10,1... | collective-permute-start | bytes 786440 | tf_op jit(solution)/shard_map/ppermute | solution.py:80
  418.3 19.6 %collective-permute-start.20 = (bf16[256,512]{1,0:T(8,128)(2,1)}, bf16[256,512]{1,0:T(8,128)(2,1)S(1)}, u32[]{:S(2)}, u32[]{:S(2)}) collective-permute-start(bf16[256,512]{1,0:T(8,128)(2,1)} %get-tuple-element.126), channel_id=1, source_target_pairs={{0,2},{1,3},{2,0},{3,1},{4,6},{5,7},{6,4},{7,5},{8,10},{9,11},{10,... | collective-permute-start | bytes 786440 | tf_op jit(solution)/shard_map/ppermute | solution.py:80
  418.4 19.5 %collective-permute-start.21 = (bf16[256,512]{1,0:T(8,128)(2,1)}, bf16[256,512]{1,0:T(8,128)(2,1)S(1)}, u32[]{:S(2)}, u32[]{:S(2)}) collective-permute-start(bf16[256,512]{1,0:T(8,128)(2,1)} %get-tuple-element.127), channel_id=1, source_target_pairs={{0,3},{1,0},{2,1},{3,2},{4,7},{5,4},{6,5},{7,6},{8,11},{9,8},{10,9... | collective-permute-start | bytes 786440 | tf_op jit(solution)/shard_map/ppermute | solution.py:80
  422.1 27.6 %collective-permute-start.22 = (bf16[2,192,1024]{2,1,0:T(8,128)(2,1)S(1)}, bf16[2,192,1024]{2,1,0:T(8,128)(2,1)S(1)}, u32[]{:S(2)}, u32[]{:S(2)}) collective-permute-start(bf16[2,192,1024]{2,1,0:T(8,128)(2,1)S(1)} %copy-done.26), channel_id=1, source_target_pairs={{0,8},{4,12},{8,0},{12,4},{16,24},{20,28},{24,16},{28,20},{1,9},{5... | collective-permute-start | bytes 2359304 | tf_op jit(solution)/shard_map/ppermute | solution.py:99
  424.8 24.9 %collective-permute-start.23 = (bf16[2,192,1024]{2,1,0:T(8,128)(2,1)S(1)}, bf16[2,192,1024]{2,1,0:T(8,128)(2,1)S(1)}, u32[]{:S(2)}, u32[]{:S(2)}) collective-permute-start(bf16[2,192,1024]{2,1,0:T(8,128)(2,1)S(1)} %copy-done.59), channel_id=1, source_target_pairs={{0,16},{4,20},{8,24},{12,28},{16,0},{20,4},{24,8},{28,12},{1,17},{... | collective-permute-start | bytes 2359304 | tf_op jit(solution)/shard_map/ppermute | solution.py:99
  429.6 8.3 %copy-start.44 = (bf16[256,512]{1,0:T(8,128)(2,1)}, bf16[256,512]{1,0:T(8,128)(2,1)S(1)}, u32[]{:S(2)}) copy-start(bf16[256,512]{1,0:T(8,128)(2,1)S(1)} %collective-permute-done.19.refs_2_) | copy-start | bytes 786436
  442.1 39.9 %collective-permute-start.27 = (bf16[256,2048]{1,0:T(8,128)(2,1)}, bf16[256,2048]{1,0:T(8,128)(2,1)S(1)}, u32[]{:S(2)}, u32[]{:S(2)}) collective-permute-start(bf16[256,2048]{1,0:T(8,128)(2,1)} %get-tuple-element.139.refs_2_.refs_8_), channel_id=1, source_target_pairs={{0,1},{1,2},{2,3},{3,0},{4,5},{5,6},{6,7},{7,4},{8,9},{9,10},{10,1... | collective-permute-start | bytes 3145736 | tf_op jit(solution)/shard_map/ppermute | solution.py:80
  454.2 23.2 %collective-permute-start.28 = (bf16[1,192,1024]{2,1,0:T(8,128)(2,1)}, bf16[1,192,1024]{2,1,0:T(8,128)(2,1)S(1)}, u32[]{:S(2)}, u32[]{:S(2)}) collective-permute-start(bf16[1,192,1024]{2,1,0:T(8,128)(2,1)} %get-tuple-element.134.refs_16_), channel_id=1, source_target_pairs={{0,16},{4,20},{8,24},{12,28},{16,0},{20,4},{24,8},{28,12},{1,17},{... | collective-permute-start | bytes 1179656 | tf_op jit(solution)/shard_map/ppermute | solution.py:99
  455.9 23.0 %collective-permute-start.29 = (bf16[1,192,1024]{2,1,0:T(8,128)(2,1)}, bf16[1,192,1024]{2,1,0:T(8,128)(2,1)S(1)}, u32[]{:S(2)}, u32[]{:S(2)}) collective-permute-start(bf16[1,192,1024]{2,1,0:T(8,128)(2,1)} %get-tuple-element.142), channel_id=1, source_target_pairs={{0,8},{4,12},{8,0},{12,4},{16,24},{20,28},{24,16},{28,20},{1,9},{5... | collective-permute-start | bytes 1179656 | tf_op jit(solution)/shard_map/ppermute | solution.py:99
  474.6 7.3 %collective-permute-start.24 = (f32[8,1024]{1,0:T(8,128)}, f32[8,1024]{1,0:T(8,128)S(1)}, u32[]{:S(2)}, u32[]{:S(2)}) collective-permute-start(f32[8,1024]{1,0:T(8,128)} %get-tuple-element.138.refs_11_), channel_id=1, source_target_pairs={{0,1},{1,2},{2,3},{3,0},{4,5},{5,6},{6,7},{7,4},{8,9},{9,10},{10,1... | collective-permute-start | bytes 98312 | tf_op jit(solution)/shard_map/ppermute | solution.py:80
  475.0 6.9 collective-permute-start.25
  477.4 4.5 collective-permute-start.26
  485.0 25.0 %collective-permute-start.30 = (bf16[256,2048]{1,0:T(8,128)(2,1)}, bf16[256,2048]{1,0:T(8,128)(2,1)S(1)}, u32[]{:S(2)}, u32[]{:S(2)}) collective-permute-start(bf16[256,2048]{1,0:T(8,128)(2,1)} %bitcast.95), channel_id=1, source_target_pairs={{0,1},{1,2},{2,3},{3,0},{4,5},{5,6},{6,7},{7,4},{8,9},{9,10},{10,1... | collective-permute-start | bytes 3145736 | tf_op jit(solution)/shard_map/ppermute | solution.py:80
  486.2 20.5 %collective-permute-start.31 = (bf16[1,192,1024]{2,1,0:T(8,128)(2,1)}, bf16[1,192,1024]{2,1,0:T(8,128)(2,1)S(1)}, u32[]{:S(2)}, u32[]{:S(2)}) collective-permute-start(bf16[1,192,1024]{2,1,0:T(8,128)(2,1)} %get-tuple-element.143.refs_1_.refs_0_), channel_id=1, source_target_pairs={{0,16},{4,20},{8,24},{12,28},{16,0},{20,4},{24,8},{28,12},{1,17},{... | collective-permute-start | bytes 1179656 | tf_op jit(solution)/shard_map/ppermute | solution.py:99
  486.9 19.8 %collective-permute-start.32 = (bf16[1,192,1024]{2,1,0:T(8,128)(2,1)}, bf16[1,192,1024]{2,1,0:T(8,128)(2,1)S(1)}, u32[]{:S(2)}, u32[]{:S(2)}) collective-permute-start(bf16[1,192,1024]{2,1,0:T(8,128)(2,1)} %get-tuple-element.148.refs_2_), channel_id=1, source_target_pairs={{0,8},{4,12},{8,0},{12,4},{16,24},{20,28},{24,16},{28,20},{1,9},{5... | collective-permute-start | bytes 1179656 | tf_op jit(solution)/shard_map/ppermute | solution.py:99
  513.0 25.4 %collective-permute-start.33 = (bf16[256,2048]{1,0:T(8,128)(2,1)}, bf16[256,2048]{1,0:T(8,128)(2,1)S(1)}, u32[]{:S(2)}, u32[]{:S(2)}) collective-permute-start(bf16[256,2048]{1,0:T(8,128)(2,1)} %bitcast.100), channel_id=1, source_target_pairs={{0,1},{1,2},{2,3},{3,0},{4,5},{5,6},{6,7},{7,4},{8,9},{9,10},{10,1... | collective-permute-start | bytes 3145736 | tf_op jit(solution)/shard_map/ppermute | solution.py:80
  554.3 146.2 %all-reduce.10.cloned.1.call-start = ((), (), s32[]{:S(2)}) async-start(), calls=%async_computation.3 | async-start | bytes 16973824 | tf_op jit(solution)/shard_map/psum | solution.py:1242
  555.4 27.7 %collective-permute-start.36 = (bf16[2,192,1024]{2,1,0:T(8,128)(2,1)S(1)}, bf16[2,192,1024]{2,1,0:T(8,128)(2,1)S(1)}, u32[]{:S(2)}, u32[]{:S(2)}) collective-permute-start(bf16[2,192,1024]{2,1,0:T(8,128)(2,1)S(1)} %copy-done.13), channel_id=1, source_target_pairs={{0,8},{4,12},{8,0},{12,4},{16,24},{20,28},{24,16},{28,20},{1,9},{5... | collective-permute-start | bytes 2359304 | tf_op jit(solution)/shard_map/ppermute | solution.py:99
  556.5 28.6 %collective-permute-start.37 = (bf16[2,192,1024]{2,1,0:T(8,128)(2,1)S(1)}, bf16[2,192,1024]{2,1,0:T(8,128)(2,1)S(1)}, u32[]{:S(2)}, u32[]{:S(2)}) collective-permute-start(bf16[2,192,1024]{2,1,0:T(8,128)(2,1)S(1)} %copy-done.27), channel_id=1, source_target_pairs={{0,16},{4,20},{8,24},{12,28},{16,0},{20,4},{24,8},{28,12},{1,17},{... | collective-permute-start | bytes 2359304 | tf_op jit(solution)/shard_map/ppermute | solution.py:99
  557.7 31.4 %collective-permute-start.35 = (bf16[1024,512]{1,0:T(8,128)(2,1)S(1)}, bf16[1024,512]{1,0:T(8,128)(2,1)S(1)}, u32[]{:S(2)}, u32[]{:S(2)}) collective-permute-start(bf16[1024,512]{1,0:T(8,128)(2,1)S(1)} %copy-done.18), channel_id=1, source_target_pairs={{0,1},{1,2},{2,3},{3,0},{4,5},{5,6},{6,7},{7,4},{8,9},{9,10},{10,1... | collective-permute-start | bytes 3145736 | tf_op jit(solution)/shard_map/ppermute | solution.py:80
  560.9 49.8 %collective-permute-start.34 = (bf16[1024,512]{1,0:T(8,128)(2,1)}, bf16[1024,512]{1,0:T(8,128)(2,1)S(1)}, u32[]{:S(2)}, u32[]{:S(2)}) collective-permute-start(bf16[1024,512]{1,0:T(8,128)(2,1)} %shard_map.323.refs_4_), channel_id=1, source_target_pairs={{0,1},{1,2},{2,3},{3,0},{4,5},{5,6},{6,7},{7,4},{8,9},{9,10},{10,1... | collective-permute-start | bytes 3145736 | tf_op jit(solution)/shard_map/ppermute | solution.py:80
  589.1 95.2 %collective-permute-start.41 = (bf16[4,192,2048]{2,1,0:T(8,128)(2,1)}, bf16[4,192,2048]{2,1,0:T(8,128)(2,1)}, u32[]{:S(2)}, u32[]{:S(2)}) collective-permute-start(bf16[4,192,2048]{2,1,0:T(8,128)(2,1)} %shard_map.324.refs_4_.refs_1_), channel_id=1, source_target_pairs={{0,4},{4,0},{8,12},{12,8},{16,20},{20,16},{24,28},{28,24},{1,5},{5... | collective-permute-start | bytes 9437192 | tf_op jit(solution)/shard_map/ppermute | solution.py:99
  596.7 33.8 %collective-permute-start.39 = (bf16[1024,512]{1,0:T(8,128)(2,1)}, bf16[1024,512]{1,0:T(8,128)(2,1)S(1)}, u32[]{:S(2)}, u32[]{:S(2)}) collective-permute-start(bf16[1024,512]{1,0:T(8,128)(2,1)} %shard_map.325.refs_1_), channel_id=1, source_target_pairs={{0,1},{1,2},{2,3},{3,0},{4,5},{5,6},{6,7},{7,4},{8,9},{9,10},{10,1... | collective-permute-start | bytes 3145736 | tf_op jit(solution)/shard_map/ppermute | solution.py:80
  614.8 38.2 %collective-permute-start.38 = (bf16[1024,512]{1,0:T(8,128)(2,1)}, bf16[1024,512]{1,0:T(8,128)(2,1)S(1)}, u32[]{:S(2)}, u32[]{:S(2)}) collective-permute-start(bf16[1024,512]{1,0:T(8,128)(2,1)} %shard_map.327.refs_4_), channel_id=1, source_target_pairs={{0,1},{1,2},{2,3},{3,0},{4,5},{5,6},{6,7},{7,4},{8,9},{9,10},{10,1... | collective-permute-start | bytes 3145736 | tf_op jit(solution)/shard_map/ppermute | solution.py:80
  637.8 19.3 %copy-start.3 = (s32[8]{0:T(128)S(1)}, s32[8]{0:T(128)}, u32[]{:S(2)}) copy-start(s32[8]{0:T(128)} %constant.112.clone) | copy-start | bytes 100
  637.8 37.7 %collective-permute-start.42 = (bf16[1024,512]{1,0:T(8,128)(2,1)}, bf16[1024,512]{1,0:T(8,128)(2,1)S(1)}, u32[]{:S(2)}, u32[]{:S(2)}) collective-permute-start(bf16[1024,512]{1,0:T(8,128)(2,1)} %shard_map.328.refs_3_), channel_id=1, source_target_pairs={{0,1},{1,2},{2,3},{3,0},{4,5},{5,6},{6,7},{7,4},{8,9},{9,10},{10,1... | collective-permute-start | bytes 3145736 | tf_op jit(solution)/shard_map/ppermute | solution.py:80
  657.0 39.4 %collective-permute-start.40 = (bf16[1024,512]{1,0:T(8,128)(2,1)}, bf16[1024,512]{1,0:T(8,128)(2,1)S(1)}, u32[]{:S(2)}, u32[]{:S(2)}) collective-permute-start(bf16[1024,512]{1,0:T(8,128)(2,1)} %shard_map.329.refs_12_), channel_id=1, source_target_pairs={{0,1},{1,2},{2,3},{3,0},{4,5},{5,6},{6,7},{7,4},{8,9},{9,10},{10,1... | collective-permute-start | bytes 3145736 | tf_op jit(solution)/shard_map/ppermute | solution.py:80
  703.0 16.7 %collective-permute-start.43 = (f32[8,2048]{1,0:T(8,128)S(1)}, f32[8,2048]{1,0:T(8,128)S(1)}, u32[]{:S(2)}, u32[]{:S(2)}) collective-permute-start(f32[8,2048]{1,0:T(8,128)S(1)} %slice.101), channel_id=1, source_target_pairs={{0,1},{1,2},{2,3},{3,0},{4,5},{5,6},{6,7},{7,4},{8,9},{9,10},{10,1... | collective-permute-start | bytes 196616 | tf_op jit(solution)/shard_map/ppermute | solution.py:80
  703.1 16.7 %collective-permute-start.44 = (f32[8,2048]{1,0:T(8,128)S(1)}, f32[8,2048]{1,0:T(8,128)S(1)}, u32[]{:S(2)}, u32[]{:S(2)}) collective-permute-start(f32[8,2048]{1,0:T(8,128)S(1)} %slice.101), channel_id=1, source_target_pairs={{0,2},{1,3},{2,0},{3,1},{4,6},{5,7},{6,4},{7,5},{8,10},{9,11},{10,... | collective-permute-start | bytes 196616 | tf_op jit(solution)/shard_map/ppermute | solution.py:80
  705.0 14.8 %collective-permute-start.45 = (f32[8,2048]{1,0:T(8,128)S(1)}, f32[8,2048]{1,0:T(8,128)S(1)}, u32[]{:S(2)}, u32[]{:S(2)}) collective-permute-start(f32[8,2048]{1,0:T(8,128)S(1)} %slice.101), channel_id=1, source_target_pairs={{0,3},{1,0},{2,1},{3,2},{4,7},{5,4},{6,5},{7,6},{8,11},{9,8},{10,9... | collective-permute-start | bytes 196616 | tf_op jit(solution)/shard_map/ppermute | solution.py:80
  707.5 9.7 %copy-start.15 = (bf16[512,2048]{1,0:T(8,128)(2,1)S(1)}, bf16[512,2048]{1,0:T(8,128)(2,1)}, u32[]{:S(2)}) copy-start(bf16[512,2048]{1,0:T(8,128)(2,1)} %get-tuple-element.160) | copy-start | bytes 6291460
  707.5 14.1 %copy-start.1 = (bf16[512,2048]{1,0:T(8,128)(2,1)S(1)}, bf16[512,2048]{1,0:T(8,128)(2,1)}, u32[]{:S(2)}) copy-start(bf16[512,2048]{1,0:T(8,128)(2,1)} %param.27) | copy-start | bytes 6291460
  (47 other events, 72.4 us)
Sparse Core Ops, SparseCore 0:
  44.0 52.0 all-gather.5
  98.3 112.3 all-gather.3
  345.6 201.0 all-reduce.7
  559.9 136.1 all-reduce.9
